TPU v7x, 32 devices: a whole 2x2x4 slice. The times are simulated.
32 devices in a mesh: box: 16 (over z, x, core), rhs: 2 (over y).
Axes of the slice: x: 2, y: 2, z: 4, core: 2. Of those that a mesh axis runs over, the one named last changes fastest.
Arguments:
- basis: float32 [8, 16, 131072], P(None, 'rhs', 'box')
- facet_centres: float32 [3, 131072], P(None, 'box'), as said below
- normals: float32 [3, 131072], P(None, 'box'), as said below
- areas: float32 [131072], P('box'), may hold values from 0.2 to 2
- contrast: float32 [131072], P('box'), may hold values from -0.9 to 0.9
- facet_counts: int32 [512], P('box'), may hold values from 64 to 256, as said below
- box_centres: float32 [3, 512], P(None, 'box'), as said below
- near_boxes: int32 [512, 27], P('box'), may hold values from -1 to 511, as said below
- far_boxes: int32 [512, 189], P('box'), may hold values from -1 to 511, as said below
Outputs:
- next_vector: float32 [16, 131072], P('rhs', 'box')
- hessenberg: float32 [9, 16], P(None, 'rhs')
Inputs may be any that keep to these rules, and one draw needn't show every extreme that they name: Live facets of box b occupy its first facet_counts[b] slots; at least one box in five is full. `box_centres`: box b stands for the lattice code c(b) = 32 * (b div 32) + p(b mod 32), p a permutation of 0 to 31 drawn for each aligned block of 32 boxes. With l = c mod 64: x = bit 0 of l + 2 * bit 3 of l, y = bit 1 + 2 * bit 4, z = bit 2 + 2 * bit 5 + 4 * (c div 64); the lattice is 4 by 4 by 32 boxes. Box b's centre lies within 0.1 in each coordinate of its lattice point. `near_boxes`: row b holds b itself first, then the boxes at the 26 lattice points next to b's (Chebyshev distance 1) in an order drawn for each row, -1 where a neighbour lies outside the lattice. `far_boxes`: row b holds the octree interaction list of b: the boxes at the children of the neighbours of b's parent (lattice point divided by 2) that are not lattice neighbours of b, in an order drawn for each row, -1 where one lies outside the lattice. `facet_centres`: each facet lies within 0.45 in each coordinate of its box's centre. `normals`: unit vectors.
All inputs are finite; a program needn't handle non-finite values.
Results may differ from a plain program's by a relative error of at most 0.00034.
Values may be sent and summed in bfloat16 or wider, within the bound.
No kernel may reach another device: no remote copies, remote signals or barrier semaphores. Data moves between devices by JAX's collectives and lax.ppermute only.
A program may use at most 64 MiB of HBM per device.

v0:
```python
import jax
import jax.numpy as jnp
from jax import lax
from jax.sharding import PartitionSpec as P

soften = 0.0025
epsilon = 1e-06
largest_index = lax.Precision.HIGHEST


def extended_2(cells, sides, width):
    for axis, dim in sides:
        count = lax.axis_size(axis)
        ends = count - 1
        head = lax.slice_in_dim(cells, 0, width, axis=dim)
        tail = lax.slice_in_dim(cells, cells.shape[dim] - width, cells.shape[dim], axis=dim)
        cells = jnp.concatenate(
            [
                lax.ppermute(tail, axis, [(i, (i + 1) % count) for i in range(ends)]),
                cells,
                lax.ppermute(head, axis, [((i + 1) % count, i) for i in range(ends)]),
            ],
            axis=dim,
        )
    return cells


def passed_along(x, axis, by):
    length = lax.axis_size(axis)
    pairs = [(i, i + by) for i in range(length) if 0 <= i + by < length]
    return lax.ppermute(x, axis, pairs)


def near_block(target_centres, target_normals, source_centres, source_charges):
    diff_x = target_centres[0][:, :, None] - source_centres[0][:, None, :]
    diff_y = target_centres[1][:, :, None] - source_centres[1][:, None, :]
    diff_z = target_centres[2][:, :, None] - source_centres[2][:, None, :]
    normal_part = (
        diff_x * target_normals[0][:, :, None]
        + diff_y * target_normals[1][:, :, None]
        + diff_z * target_normals[2][:, :, None]
    )
    spread = diff_x * diff_x + diff_y * diff_y + diff_z * diff_z + soften
    kernel = (normal_part / (spread * jnp.sqrt(spread))).astype(jnp.bfloat16)
    return jnp.einsum("bij,rbj->rbi", kernel, source_charges, preferred_element_type=jnp.float32)


def near_field(charges_halo, centres_halo, target_centres, target_normals, near_lists, first_box):
    box_count = near_lists.shape[0]
    row_count = charges_halo.shape[0]
    per_box = target_centres.shape[2]
    charge_boxes = charges_halo.reshape(row_count, -1, per_box)
    centre_boxes = centres_halo.reshape(3, -1, per_box)

    def add_slot(slot_number, running):
        box_ids = lax.dynamic_index_in_dim(near_lists, slot_number, 1, keepdims=False)
        is_valid = box_ids >= 0
        local_box = jnp.where(is_valid, box_ids - first_box, 0)
        source_centres = jnp.take(centre_boxes, local_box, axis=1)
        source_charges = jnp.take(charge_boxes, local_box, axis=1) * is_valid[None, :, None].astype(
            jnp.bfloat16
        )
        return running + near_block(target_centres, target_normals, source_centres, source_charges)

    start_value = jnp.zeros((row_count, box_count, per_box), jnp.float32)
    return lax.fori_loop(0, near_lists.shape[1], add_slot, start_value)


def far_coeffs(target_centres, target_normals, centres_far):
    offsets = [
        target_centres[axis_number][:, None, :] - centres_far[axis_number][:, :, None]
        for axis_number in range(3)
    ]
    distance = offsets[0] * offsets[0] + offsets[1] * offsets[1] + offsets[2] * offsets[2] + soften
    inverse_cube = 1.0 / (distance * jnp.sqrt(distance))
    normal_part = (
        offsets[0] * target_normals[0][:, None, :]
        + offsets[1] * target_normals[1][:, None, :]
        + offsets[2] * target_normals[2][:, None, :]
    )
    coeff_list = [normal_part * inverse_cube]
    for axis_number in range(3):
        coeff_list.append(
            3.0 * normal_part * offsets[axis_number] * inverse_cube / distance
            - target_normals[axis_number][:, None, :] * inverse_cube
        )
    return jnp.stack(coeff_list)


def on_device(
    basis, facet_centres, normals, areas, contrast, facet_counts, box_centres, near_boxes, far_boxes
):
    krylov_count, rhs_local, facet_local = basis.shape
    boxes_here = facet_counts.shape[0]
    per_box = facet_local // boxes_here
    total_facets = lax.axis_size("box") * facet_local
    first_box = (lax.axis_index("box") - 1) * boxes_here
    slot_index = lax.broadcasted_iota(jnp.int32, (boxes_here, per_box), 1)
    live_mask = (slot_index < facet_counts[:, None]).astype(jnp.float32).reshape(facet_local)
    current = basis[krylov_count - 1]
    weighted = current * (areas * live_mask / per_box)[None, :]
    charges_low = weighted.astype(jnp.bfloat16)
    target_centres = facet_centres.reshape(3, boxes_here, per_box)
    target_normals = normals.reshape(3, boxes_here, per_box)
    centres_halo = extended_2(facet_centres, (("box", 1),), facet_local)
    charges_halo = extended_2(charges_low, (("box", 1),), facet_local)
    near_flat = near_field(
        charges_halo, centres_halo, target_centres, target_normals, near_boxes, first_box
    ).reshape(rhs_local, facet_local)
    weighted_boxes = weighted.reshape(rhs_local, boxes_here, per_box)
    relative = target_centres - box_centres[:, :, None]
    monopole = jnp.sum(weighted_boxes, axis=2)
    dipole = jnp.einsum("rbj,abj->arb", weighted_boxes, relative, precision=largest_index)
    moments = jnp.concatenate([monopole[None], dipole], 0).reshape(4 * rhs_local, boxes_here)
    stacked = jnp.concatenate([moments, box_centres], 0)
    shifted = {}
    for shift_by in (2, 1, -1, -2):
        shifted[shift_by] = passed_along(stacked, "box", shift_by)
    extended = jnp.concatenate([shifted[2], shifted[1], stacked, shifted[-1], shifted[-2]], 1)
    all_moments = extended[: 4 * rhs_local]
    all_centres = extended[4 * rhs_local :]
    far_first = (lax.axis_index("box") - 2) * boxes_here
    group_size = 2
    group_count = boxes_here // group_size

    def far_group(group_number):
        start_box = group_number * group_size
        group_centres = lax.dynamic_slice_in_dim(target_centres, start_box, group_size, 1)
        group_normals = lax.dynamic_slice_in_dim(target_normals, start_box, group_size, 1)
        group_lists = lax.dynamic_slice_in_dim(far_boxes, start_box, group_size, 0)
        is_valid = group_lists >= 0
        safe_ids = jnp.where(is_valid, group_lists - far_first, 0).reshape(-1)
        picked = jnp.take(all_moments, safe_ids, axis=1).reshape(4, rhs_local, group_size, -1)
        picked = picked * is_valid[None, None].astype(jnp.float32)
        centres_far = jnp.take(all_centres, safe_ids, axis=1).reshape(3, group_size, -1)
        coeffs = far_coeffs(group_centres, group_normals, centres_far)
        return jnp.einsum("mbki,mrbk->rbi", coeffs, picked, precision=largest_index)

    far_parts = lax.map(far_group, jnp.arange(group_count, dtype=jnp.int32))
    far_flat = jnp.transpose(far_parts, (1, 0, 2, 3)).reshape(rhs_local, facet_local)
    image_vector = live_mask[None, :] * (current - 2.0 * contrast[None, :] * (near_flat + far_flat))
    basis_masked_rows = basis * live_mask[None, None, :]
    partial_result = jnp.einsum(
        "lbe,be->lb", basis_masked_rows, image_vector, precision=largest_index
    )
    raw_sums = lax.psum(partial_result, "box")
    basis_projections = raw_sums / total_facets
    residual_vector = image_vector - jnp.einsum(
        "zo,zov->ov", basis_projections, basis_masked_rows, precision=largest_index
    )
    remaining = lax.psum(jnp.sum(residual_vector * residual_vector, axis=1), "box")
    norm_scale = jnp.sqrt(remaining / total_facets + epsilon)
    next_vector = residual_vector / norm_scale[:, None]
    hessenberg = jnp.concatenate([basis_projections, norm_scale[None, :]], 0)
    return (next_vector, hessenberg)


def solution(mesh):
    return jax.shard_map(
        on_device,
        mesh=mesh,
        in_specs=(
            P(None, "rhs", "box"),
            P(None, "box"),
            P(None, "box"),
            P("box"),
            P("box"),
            P("box"),
            P(None, "box"),
            P("box", None),
            P("box", None),
        ),
        out_specs=(P("rhs", "box"), P(None, "rhs")),
        check_vma=False,
    )
```

profile of v0, /device:TPU:0, one launch (start us, length us, event | category | flops | bytes accessed | tf_op | source)
XLA Modules:
  0.0 767.8 jit_solution(6374527010060955192)
XLA Ops:
  6.1 4.8 collective-permute-start.4
  16.6 5.3 collective-permute-start
  27.0 4.9 collective-permute-start.2
  34.8 232.3 %while.24 = (s32[]{:T(128)}, f32[16,8,2,256]{3,1,2,0:T(8,128)}, s32[16]{0:T(128)}, s32[32,189]{1,0:T(8,128)}, s32[]{:T(128)}, /*index=5*/f32[32,160]{0,1:T(8,128...) while((s32[]{:T(128)}, f32[16,8,2,256]{3,1,2,0:T(8,128)}, ...), condition=%wide.region_4.5_spmd, body=%wide.region_3.4_spmd.sunk | while | flops 41547012 | bytes 3676191 | solution.py:139
  38.2 2.0 gather_fusion
  46.9 2.5 fusion.86
  52.7 2.0 gather_fusion
  61.4 2.5 fusion.86
  67.2 2.0 gather_fusion
  75.9 2.5 fusion.86
  81.7 2.0 gather_fusion
  90.4 2.5 fusion.86
  96.2 2.0 gather_fusion
  104.9 2.5 fusion.86
  110.8 2.0 gather_fusion
  119.5 2.5 fusion.86
  125.3 2.0 gather_fusion
  134.0 2.5 fusion.86
  139.8 2.0 gather_fusion
  148.5 2.5 fusion.86
  154.3 2.0 gather_fusion
  163.0 2.5 fusion.86
  168.9 2.0 gather_fusion
  177.5 2.5 fusion.86
  183.4 2.0 gather_fusion
  192.1 2.5 fusion.86
  197.9 2.0 gather_fusion
  206.6 2.5 fusion.86
  221.1 2.5 fusion.86
  235.6 2.5 fusion.86
  250.1 2.5 fusion.86
  264.7 2.5 fusion.86
  269.4 420.7 %while.25 = (s32[]{:T(128)}, f32[8,32,256]{2,0,1:T(8,128)}, s32[32,27]{0,1:T(8,128)}, s32[]{:T(128)}, bf16[8,96,256]{2,0,1:T(8,128)(2,1)S(1)}, /*index=5*/f32[3,...) while((s32[]{:T(128)}, f32[8,32,256]{2,0,1:T(8,128)}, ...), condition=%wide.region_1.2_spmd.clone, body=%wide.region_0.1_spmd.clone.sunk | while | flops 69494080 | bytes 2397143 | solution.py:66
  272.4 12.1 %fusion.90 = f32[8,32,256]{2,0,1:T(8,128)} fusion(f32[32,256]{1,0:T(8,128)S(1)} %get-tuple-element.500, f32[32,256]{1,0:T(8,128)S(1)} %get-tuple-element.505, f32[32,256]{1,0:T(8,128)S(1)} %get-tuple-element.506, f32[32,256]{1,0:T(8,128)S(1)} %get-tuple-element.507, f32[32,256]{1,0:T(8,128)S(1)} %get-tuple-element.508, ...), kind=kOutput, calls=%fused_computation.20.clone.1 | convolution fusion | flops 69468160 | bytes 950369 | tf_op jit(solution)/shard_map/while/body/eval_jaxpr/bij,rbj->rbi/dot_general | solution.py:45
  287.5 12.6 %fusion.90 = f32[8,32,256]{2,0,1:T(8,128)} fusion(f32[32,256]{1,0:T(8,128)S(1)} %get-tuple-element.500, f32[32,256]{1,0:T(8,128)S(1)} %get-tuple-element.505, f32[32,256]{1,0:T(8,128)S(1)} %get-tuple-element.506, f32[32,256]{1,0:T(8,128)S(1)} %get-tuple-element.507, f32[32,256]{1,0:T(8,128)S(1)} %get-tuple-element.508, ...), kind=kOutput, calls=%fused_computation.20.clone.1 | convolution fusion | flops 69468160 | bytes 950369 | tf_op jit(solution)/shard_map/while/body/eval_jaxpr/bij,rbj->rbi/dot_general | solution.py:45
  303.1 12.6 %fusion.90 = f32[8,32,256]{2,0,1:T(8,128)} fusion(f32[32,256]{1,0:T(8,128)S(1)} %get-tuple-element.500, f32[32,256]{1,0:T(8,128)S(1)} %get-tuple-element.505, f32[32,256]{1,0:T(8,128)S(1)} %get-tuple-element.506, f32[32,256]{1,0:T(8,128)S(1)} %get-tuple-element.507, f32[32,256]{1,0:T(8,128)S(1)} %get-tuple-element.508, ...), kind=kOutput, calls=%fused_computation.20.clone.1 | convolution fusion | flops 69468160 | bytes 950369 | tf_op jit(solution)/shard_map/while/body/eval_jaxpr/bij,rbj->rbi/dot_general | solution.py:45
  318.7 12.6 %fusion.90 = f32[8,32,256]{2,0,1:T(8,128)} fusion(f32[32,256]{1,0:T(8,128)S(1)} %get-tuple-element.500, f32[32,256]{1,0:T(8,128)S(1)} %get-tuple-element.505, f32[32,256]{1,0:T(8,128)S(1)} %get-tuple-element.506, f32[32,256]{1,0:T(8,128)S(1)} %get-tuple-element.507, f32[32,256]{1,0:T(8,128)S(1)} %get-tuple-element.508, ...), kind=kOutput, calls=%fused_computation.20.clone.1 | convolution fusion | flops 69468160 | bytes 950369 | tf_op jit(solution)/shard_map/while/body/eval_jaxpr/bij,rbj->rbi/dot_general | solution.py:45
  334.3 12.6 %fusion.90 = f32[8,32,256]{2,0,1:T(8,128)} fusion(f32[32,256]{1,0:T(8,128)S(1)} %get-tuple-element.500, f32[32,256]{1,0:T(8,128)S(1)} %get-tuple-element.505, f32[32,256]{1,0:T(8,128)S(1)} %get-tuple-element.506, f32[32,256]{1,0:T(8,128)S(1)} %get-tuple-element.507, f32[32,256]{1,0:T(8,128)S(1)} %get-tuple-element.508, ...), kind=kOutput, calls=%fused_computation.20.clone.1 | convolution fusion | flops 69468160 | bytes 950369 | tf_op jit(solution)/shard_map/while/body/eval_jaxpr/bij,rbj->rbi/dot_general | solution.py:45
  349.9 12.6 %fusion.90 = f32[8,32,256]{2,0,1:T(8,128)} fusion(f32[32,256]{1,0:T(8,128)S(1)} %get-tuple-element.500, f32[32,256]{1,0:T(8,128)S(1)} %get-tuple-element.505, f32[32,256]{1,0:T(8,128)S(1)} %get-tuple-element.506, f32[32,256]{1,0:T(8,128)S(1)} %get-tuple-element.507, f32[32,256]{1,0:T(8,128)S(1)} %get-tuple-element.508, ...), kind=kOutput, calls=%fused_computation.20.clone.1 | convolution fusion | flops 69468160 | bytes 950369 | tf_op jit(solution)/shard_map/while/body/eval_jaxpr/bij,rbj->rbi/dot_general | solution.py:45
  365.5 12.6 %fusion.90 = f32[8,32,256]{2,0,1:T(8,128)} fusion(f32[32,256]{1,0:T(8,128)S(1)} %get-tuple-element.500, f32[32,256]{1,0:T(8,128)S(1)} %get-tuple-element.505, f32[32,256]{1,0:T(8,128)S(1)} %get-tuple-element.506, f32[32,256]{1,0:T(8,128)S(1)} %get-tuple-element.507, f32[32,256]{1,0:T(8,128)S(1)} %get-tuple-element.508, ...), kind=kOutput, calls=%fused_computation.20.clone.1 | convolution fusion | flops 69468160 | bytes 950369 | tf_op jit(solution)/shard_map/while/body/eval_jaxpr/bij,rbj->rbi/dot_general | solution.py:45
  381.1 12.6 %fusion.90 = f32[8,32,256]{2,0,1:T(8,128)} fusion(f32[32,256]{1,0:T(8,128)S(1)} %get-tuple-element.500, f32[32,256]{1,0:T(8,128)S(1)} %get-tuple-element.505, f32[32,256]{1,0:T(8,128)S(1)} %get-tuple-element.506, f32[32,256]{1,0:T(8,128)S(1)} %get-tuple-element.507, f32[32,256]{1,0:T(8,128)S(1)} %get-tuple-element.508, ...), kind=kOutput, calls=%fused_computation.20.clone.1 | convolution fusion | flops 69468160 | bytes 950369 | tf_op jit(solution)/shard_map/while/body/eval_jaxpr/bij,rbj->rbi/dot_general | solution.py:45
  396.7 12.6 %fusion.90 = f32[8,32,256]{2,0,1:T(8,128)} fusion(f32[32,256]{1,0:T(8,128)S(1)} %get-tuple-element.500, f32[32,256]{1,0:T(8,128)S(1)} %get-tuple-element.505, f32[32,256]{1,0:T(8,128)S(1)} %get-tuple-element.506, f32[32,256]{1,0:T(8,128)S(1)} %get-tuple-element.507, f32[32,256]{1,0:T(8,128)S(1)} %get-tuple-element.508, ...), kind=kOutput, calls=%fused_computation.20.clone.1 | convolution fusion | flops 69468160 | bytes 950369 | tf_op jit(solution)/shard_map/while/body/eval_jaxpr/bij,rbj->rbi/dot_general | solution.py:45
  412.3 12.6 %fusion.90 = f32[8,32,256]{2,0,1:T(8,128)} fusion(f32[32,256]{1,0:T(8,128)S(1)} %get-tuple-element.500, f32[32,256]{1,0:T(8,128)S(1)} %get-tuple-element.505, f32[32,256]{1,0:T(8,128)S(1)} %get-tuple-element.506, f32[32,256]{1,0:T(8,128)S(1)} %get-tuple-element.507, f32[32,256]{1,0:T(8,128)S(1)} %get-tuple-element.508, ...), kind=kOutput, calls=%fused_computation.20.clone.1 | convolution fusion | flops 69468160 | bytes 950369 | tf_op jit(solution)/shard_map/while/body/eval_jaxpr/bij,rbj->rbi/dot_general | solution.py:45
  427.9 12.6 %fusion.90 = f32[8,32,256]{2,0,1:T(8,128)} fusion(f32[32,256]{1,0:T(8,128)S(1)} %get-tuple-element.500, f32[32,256]{1,0:T(8,128)S(1)} %get-tuple-element.505, f32[32,256]{1,0:T(8,128)S(1)} %get-tuple-element.506, f32[32,256]{1,0:T(8,128)S(1)} %get-tuple-element.507, f32[32,256]{1,0:T(8,128)S(1)} %get-tuple-element.508, ...), kind=kOutput, calls=%fused_computation.20.clone.1 | convolution fusion | flops 69468160 | bytes 950369 | tf_op jit(solution)/shard_map/while/body/eval_jaxpr/bij,rbj->rbi/dot_general | solution.py:45
  443.5 12.6 %fusion.90 = f32[8,32,256]{2,0,1:T(8,128)} fusion(f32[32,256]{1,0:T(8,128)S(1)} %get-tuple-element.500, f32[32,256]{1,0:T(8,128)S(1)} %get-tuple-element.505, f32[32,256]{1,0:T(8,128)S(1)} %get-tuple-element.506, f32[32,256]{1,0:T(8,128)S(1)} %get-tuple-element.507, f32[32,256]{1,0:T(8,128)S(1)} %get-tuple-element.508, ...), kind=kOutput, calls=%fused_computation.20.clone.1 | convolution fusion | flops 69468160 | bytes 950369 | tf_op jit(solution)/shard_map/while/body/eval_jaxpr/bij,rbj->rbi/dot_general | solution.py:45
  459.1 12.6 %fusion.90 = f32[8,32,256]{2,0,1:T(8,128)} fusion(f32[32,256]{1,0:T(8,128)S(1)} %get-tuple-element.500, f32[32,256]{1,0:T(8,128)S(1)} %get-tuple-element.505, f32[32,256]{1,0:T(8,128)S(1)} %get-tuple-element.506, f32[32,256]{1,0:T(8,128)S(1)} %get-tuple-element.507, f32[32,256]{1,0:T(8,128)S(1)} %get-tuple-element.508, ...), kind=kOutput, calls=%fused_computation.20.clone.1 | convolution fusion | flops 69468160 | bytes 950369 | tf_op jit(solution)/shard_map/while/body/eval_jaxpr/bij,rbj->rbi/dot_general | solution.py:45
  474.7 12.6 %fusion.90 = f32[8,32,256]{2,0,1:T(8,128)} fusion(f32[32,256]{1,0:T(8,128)S(1)} %get-tuple-element.500, f32[32,256]{1,0:T(8,128)S(1)} %get-tuple-element.505, f32[32,256]{1,0:T(8,128)S(1)} %get-tuple-element.506, f32[32,256]{1,0:T(8,128)S(1)} %get-tuple-element.507, f32[32,256]{1,0:T(8,128)S(1)} %get-tuple-element.508, ...), kind=kOutput, calls=%fused_computation.20.clone.1 | convolution fusion | flops 69468160 | bytes 950369 | tf_op jit(solution)/shard_map/while/body/eval_jaxpr/bij,rbj->rbi/dot_general | solution.py:45
  490.4 12.6 %fusion.90 = f32[8,32,256]{2,0,1:T(8,128)} fusion(f32[32,256]{1,0:T(8,128)S(1)} %get-tuple-element.500, f32[32,256]{1,0:T(8,128)S(1)} %get-tuple-element.505, f32[32,256]{1,0:T(8,128)S(1)} %get-tuple-element.506, f32[32,256]{1,0:T(8,128)S(1)} %get-tuple-element.507, f32[32,256]{1,0:T(8,128)S(1)} %get-tuple-element.508, ...), kind=kOutput, calls=%fused_computation.20.clone.1 | convolution fusion | flops 69468160 | bytes 950369 | tf_op jit(solution)/shard_map/while/body/eval_jaxpr/bij,rbj->rbi/dot_general | solution.py:45
  506.0 12.6 %fusion.90 = f32[8,32,256]{2,0,1:T(8,128)} fusion(f32[32,256]{1,0:T(8,128)S(1)} %get-tuple-element.500, f32[32,256]{1,0:T(8,128)S(1)} %get-tuple-element.505, f32[32,256]{1,0:T(8,128)S(1)} %get-tuple-element.506, f32[32,256]{1,0:T(8,128)S(1)} %get-tuple-element.507, f32[32,256]{1,0:T(8,128)S(1)} %get-tuple-element.508, ...), kind=kOutput, calls=%fused_computation.20.clone.1 | convolution fusion | flops 69468160 | bytes 950369 | tf_op jit(solution)/shard_map/while/body/eval_jaxpr/bij,rbj->rbi/dot_general | solution.py:45
  521.6 12.6 %fusion.90 = f32[8,32,256]{2,0,1:T(8,128)} fusion(f32[32,256]{1,0:T(8,128)S(1)} %get-tuple-element.500, f32[32,256]{1,0:T(8,128)S(1)} %get-tuple-element.505, f32[32,256]{1,0:T(8,128)S(1)} %get-tuple-element.506, f32[32,256]{1,0:T(8,128)S(1)} %get-tuple-element.507, f32[32,256]{1,0:T(8,128)S(1)} %get-tuple-element.508, ...), kind=kOutput, calls=%fused_computation.20.clone.1 | convolution fusion | flops 69468160 | bytes 950369 | tf_op jit(solution)/shard_map/while/body/eval_jaxpr/bij,rbj->rbi/dot_general | solution.py:45
  537.1 12.6 %fusion.90 = f32[8,32,256]{2,0,1:T(8,128)} fusion(f32[32,256]{1,0:T(8,128)S(1)} %get-tuple-element.500, f32[32,256]{1,0:T(8,128)S(1)} %get-tuple-element.505, f32[32,256]{1,0:T(8,128)S(1)} %get-tuple-element.506, f32[32,256]{1,0:T(8,128)S(1)} %get-tuple-element.507, f32[32,256]{1,0:T(8,128)S(1)} %get-tuple-element.508, ...), kind=kOutput, calls=%fused_computation.20.clone.1 | convolution fusion | flops 69468160 | bytes 950369 | tf_op jit(solution)/shard_map/while/body/eval_jaxpr/bij,rbj->rbi/dot_general | solution.py:45
  552.7 12.6 %fusion.90 = f32[8,32,256]{2,0,1:T(8,128)} fusion(f32[32,256]{1,0:T(8,128)S(1)} %get-tuple-element.500, f32[32,256]{1,0:T(8,128)S(1)} %get-tuple-element.505, f32[32,256]{1,0:T(8,128)S(1)} %get-tuple-element.506, f32[32,256]{1,0:T(8,128)S(1)} %get-tuple-element.507, f32[32,256]{1,0:T(8,128)S(1)} %get-tuple-element.508, ...), kind=kOutput, calls=%fused_computation.20.clone.1 | convolution fusion | flops 69468160 | bytes 950369 | tf_op jit(solution)/shard_map/while/body/eval_jaxpr/bij,rbj->rbi/dot_general | solution.py:45
  568.3 12.6 %fusion.90 = f32[8,32,256]{2,0,1:T(8,128)} fusion(f32[32,256]{1,0:T(8,128)S(1)} %get-tuple-element.500, f32[32,256]{1,0:T(8,128)S(1)} %get-tuple-element.505, f32[32,256]{1,0:T(8,128)S(1)} %get-tuple-element.506, f32[32,256]{1,0:T(8,128)S(1)} %get-tuple-element.507, f32[32,256]{1,0:T(8,128)S(1)} %get-tuple-element.508, ...), kind=kOutput, calls=%fused_computation.20.clone.1 | convolution fusion | flops 69468160 | bytes 950369 | tf_op jit(solution)/shard_map/while/body/eval_jaxpr/bij,rbj->rbi/dot_general | solution.py:45
  583.9 12.6 %fusion.90 = f32[8,32,256]{2,0,1:T(8,128)} fusion(f32[32,256]{1,0:T(8,128)S(1)} %get-tuple-element.500, f32[32,256]{1,0:T(8,128)S(1)} %get-tuple-element.505, f32[32,256]{1,0:T(8,128)S(1)} %get-tuple-element.506, f32[32,256]{1,0:T(8,128)S(1)} %get-tuple-element.507, f32[32,256]{1,0:T(8,128)S(1)} %get-tuple-element.508, ...), kind=kOutput, calls=%fused_computation.20.clone.1 | convolution fusion | flops 69468160 | bytes 950369 | tf_op jit(solution)/shard_map/while/body/eval_jaxpr/bij,rbj->rbi/dot_general | solution.py:45
  599.5 12.6 %fusion.90 = f32[8,32,256]{2,0,1:T(8,128)} fusion(f32[32,256]{1,0:T(8,128)S(1)} %get-tuple-element.500, f32[32,256]{1,0:T(8,128)S(1)} %get-tuple-element.505, f32[32,256]{1,0:T(8,128)S(1)} %get-tuple-element.506, f32[32,256]{1,0:T(8,128)S(1)} %get-tuple-element.507, f32[32,256]{1,0:T(8,128)S(1)} %get-tuple-element.508, ...), kind=kOutput, calls=%fused_computation.20.clone.1 | convolution fusion | flops 69468160 | bytes 950369 | tf_op jit(solution)/shard_map/while/body/eval_jaxpr/bij,rbj->rbi/dot_general | solution.py:45
  615.1 12.6 %fusion.90 = f32[8,32,256]{2,0,1:T(8,128)} fusion(f32[32,256]{1,0:T(8,128)S(1)} %get-tuple-element.500, f32[32,256]{1,0:T(8,128)S(1)} %get-tuple-element.505, f32[32,256]{1,0:T(8,128)S(1)} %get-tuple-element.506, f32[32,256]{1,0:T(8,128)S(1)} %get-tuple-element.507, f32[32,256]{1,0:T(8,128)S(1)} %get-tuple-element.508, ...), kind=kOutput, calls=%fused_computation.20.clone.1 | convolution fusion | flops 69468160 | bytes 950369 | tf_op jit(solution)/shard_map/while/body/eval_jaxpr/bij,rbj->rbi/dot_general | solution.py:45
  630.7 12.6 %fusion.90 = f32[8,32,256]{2,0,1:T(8,128)} fusion(f32[32,256]{1,0:T(8,128)S(1)} %get-tuple-element.500, f32[32,256]{1,0:T(8,128)S(1)} %get-tuple-element.505, f32[32,256]{1,0:T(8,128)S(1)} %get-tuple-element.506, f32[32,256]{1,0:T(8,128)S(1)} %get-tuple-element.507, f32[32,256]{1,0:T(8,128)S(1)} %get-tuple-element.508, ...), kind=kOutput, calls=%fused_computation.20.clone.1 | convolution fusion | flops 69468160 | bytes 950369 | tf_op jit(solution)/shard_map/while/body/eval_jaxpr/bij,rbj->rbi/dot_general | solution.py:45
  646.2 12.6 %fusion.90 = f32[8,32,256]{2,0,1:T(8,128)} fusion(f32[32,256]{1,0:T(8,128)S(1)} %get-tuple-element.500, f32[32,256]{1,0:T(8,128)S(1)} %get-tuple-element.505, f32[32,256]{1,0:T(8,128)S(1)} %get-tuple-element.506, f32[32,256]{1,0:T(8,128)S(1)} %get-tuple-element.507, f32[32,256]{1,0:T(8,128)S(1)} %get-tuple-element.508, ...), kind=kOutput, calls=%fused_computation.20.clone.1 | convolution fusion | flops 69468160 | bytes 950369 | tf_op jit(solution)/shard_map/while/body/eval_jaxpr/bij,rbj->rbi/dot_general | solution.py:45
  661.8 12.6 %fusion.90 = f32[8,32,256]{2,0,1:T(8,128)} fusion(f32[32,256]{1,0:T(8,128)S(1)} %get-tuple-element.500, f32[32,256]{1,0:T(8,128)S(1)} %get-tuple-element.505, f32[32,256]{1,0:T(8,128)S(1)} %get-tuple-element.506, f32[32,256]{1,0:T(8,128)S(1)} %get-tuple-element.507, f32[32,256]{1,0:T(8,128)S(1)} %get-tuple-element.508, ...), kind=kOutput, calls=%fused_computation.20.clone.1 | convolution fusion | flops 69468160 | bytes 950369 | tf_op jit(solution)/shard_map/while/body/eval_jaxpr/bij,rbj->rbi/dot_general | solution.py:45
  677.4 12.6 %fusion.90 = f32[8,32,256]{2,0,1:T(8,128)} fusion(f32[32,256]{1,0:T(8,128)S(1)} %get-tuple-element.500, f32[32,256]{1,0:T(8,128)S(1)} %get-tuple-element.505, f32[32,256]{1,0:T(8,128)S(1)} %get-tuple-element.506, f32[32,256]{1,0:T(8,128)S(1)} %get-tuple-element.507, f32[32,256]{1,0:T(8,128)S(1)} %get-tuple-element.508, ...), kind=kOutput, calls=%fused_computation.20.clone.1 | convolution fusion | flops 69468160 | bytes 950369 | tf_op jit(solution)/shard_map/while/body/eval_jaxpr/bij,rbj->rbi/dot_general | solution.py:45
  691.2 5.9 fusion.62
  697.1 36.4 %psum.14 = f32[8,8]{0,1:T(8,128)S(1)} all-reduce(f32[8,8]{0,1:T(8,128)S(1)} %bitcast.141), channel_id=1, replica_groups=mesh['box'=16,'rhs'=2] {'box'}, use_global_device_ids=true, to_apply=%region_5.6 | all-reduce | flops 64 | bytes 512 | tf_op jit(solution)/shard_map/psum | solution.py:146
  733.6 2.8 fusion.60
  736.7 29.5 %psum.15 = f32[8]{0:T(128)S(1)} all-reduce(f32[8]{0:T(128)S(1)} %multiply_reduce_fusion), channel_id=1, replica_groups=mesh['box'=16,'rhs'=2] {'box'}, use_global_device_ids=true, to_apply=%region_7.8 | all-reduce | flops 8 | bytes 64 | tf_op jit(solution)/shard_map/psum | solution.py:151
  (627 shorter events, 260.6 us)
Async XLA Ops:
  6.1 19.6 %collective-permute-start.4 = (f32[35,32]{1,0:T(8,128)S(1)}, f32[35,32]{1,0:T(8,128)S(1)}, u32[]{:S(2)}, u32[]{:S(2)}) collective-permute-start(f32[35,32]{1,0:T(8,128)S(1)} %pad_maximum_fusion.2), channel_id=1, source_target_pairs={{0,4},{2,6},{4,8},{6,10},{8,12},{10,14},{12,16},{14,18},{16,20},{1... | collective-permute-start | bytes 13448 | tf_op jit(solution)/shard_map/ppermute | solution.py:31
  10.9 16.1 %collective-permute-start.5 = (f32[35,32]{1,0:T(8,128)S(1)}, f32[35,32]{1,0:T(8,128)S(1)}, u32[]{:S(2)}, u32[]{:S(2)}) collective-permute-start(f32[35,32]{1,0:T(8,128)S(1)} %pad_maximum_fusion.2), channel_id=1, source_target_pairs={{0,2},{2,4},{4,6},{6,8},{8,10},{10,12},{12,14},{14,16},{16,18},{18... | collective-permute-start | bytes 13448 | tf_op jit(solution)/shard_map/ppermute | solution.py:31
  12.4 19.5 %collective-permute-start.6 = (f32[35,32]{1,0:T(8,128)S(1)}, f32[35,32]{1,0:T(8,128)S(1)}, u32[]{:S(2)}, u32[]{:S(2)}) collective-permute-start(f32[35,32]{1,0:T(8,128)S(1)} %pad_maximum_fusion.2), channel_id=1, source_target_pairs={{2,0},{4,2},{6,4},{8,6},{10,8},{12,10},{14,12},{16,14},{18,16},{20... | collective-permute-start | bytes 13448 | tf_op jit(solution)/shard_map/ppermute | solution.py:31
  13.7 19.5 %collective-permute-start.7 = (f32[35,32]{1,0:T(8,128)S(1)}, f32[35,32]{1,0:T(8,128)S(1)}, u32[]{:S(2)}, u32[]{:S(2)}) collective-permute-start(f32[35,32]{1,0:T(8,128)S(1)} %pad_maximum_fusion.2), channel_id=1, source_target_pairs={{4,0},{6,2},{8,4},{10,6},{12,8},{14,10},{16,12},{18,14},{20,16},{2... | collective-permute-start | bytes 13448 | tf_op jit(solution)/shard_map/ppermute | solution.py:31
  16.6 251.6 %collective-permute-start = (bf16[8,8192]{1,0:T(8,128)(2,1)}, bf16[8,8192]{1,0:T(8,128)(2,1)}, u32[]{:S(2)}, u32[]{:S(2)}) collective-permute-start(bf16[8,8192]{1,0:T(8,128)(2,1)} %fusion.64), channel_id=1, source_target_pairs={{0,2},{2,4},{4,6},{6,8},{8,10},{10,12},{12,14},{14,16},{16,18},{18... | collective-permute-start | bytes 393224 | tf_op jit(solution)/shard_map/ppermute | solution.py:19
  21.9 1.8 copy-start.1
  21.9 1.8 copy-start.5
  21.9 2.5 copy-start.3
  21.9 3.1 copy-start.6
  25.7 242.6 %collective-permute-start.1 = (bf16[8,8192]{1,0:T(8,128)(2,1)}, bf16[8,8192]{1,0:T(8,128)(2,1)}, u32[]{:S(2)}, u32[]{:S(2)}) collective-permute-start(bf16[8,8192]{1,0:T(8,128)(2,1)} %fusion.64), channel_id=1, source_target_pairs={{2,0},{4,2},{6,4},{8,6},{10,8},{12,10},{14,12},{16,14},{18,16},{20... | collective-permute-start | bytes 393224 | tf_op jit(solution)/shard_map/ppermute | solution.py:21
  27.0 240.1 %collective-permute-start.2 = (f32[3,8192]{1,0:T(4,128)}, f32[3,8192]{1,0:T(4,128)}, u32[]{:S(2)}, u32[]{:S(2)}) collective-permute-start(f32[3,8192]{1,0:T(4,128)} %param.14), channel_id=1, source_target_pairs={{0,2},{2,4},{4,6},{6,8},{8,10},{10,12},{12,14},{14,16},{16,18},{18... | collective-permute-start | bytes 294920 | tf_op jit(solution)/shard_map/ppermute | solution.py:19
  31.9 235.2 %collective-permute-start.3 = (f32[3,8192]{1,0:T(4,128)}, f32[3,8192]{1,0:T(4,128)}, u32[]{:S(2)}, u32[]{:S(2)}) collective-permute-start(f32[3,8192]{1,0:T(4,128)} %param.14), channel_id=1, source_target_pairs={{2,0},{4,2},{6,4},{8,6},{10,8},{12,10},{14,12},{16,14},{18,16},{20... | collective-permute-start | bytes 294920 | tf_op jit(solution)/shard_map/ppermute | solution.py:21
  38.1 3.7 copy-start
  52.7 3.7 copy-start
  67.2 3.7 copy-start
  81.7 3.7 copy-start
  96.2 3.7 copy-start
  110.7 3.7 copy-start
  125.3 3.7 copy-start
  139.8 3.7 copy-start
  154.3 3.7 copy-start
  168.8 3.7 copy-start
  183.4 3.7 copy-start
  197.9 3.7 copy-start
  212.4 3.7 copy-start
  226.9 3.7 copy-start
  241.4 3.7 copy-start
  256.0 3.7 copy-start
  269.4 420.7 %copy-start.2 = (f32[8192]{0:T(1024)S(1)}, f32[8192]{0:T(1024)}, u32[]{:S(2)}) copy-start(f32[8192]{0:T(1024)} %copy-done.1) | copy-start | bytes 98308
  269.4 420.7 %copy-start.4 = (f32[8192]{0:T(1024)S(1)}, f32[8192]{0:T(1024)}, u32[]{:S(2)}) copy-start(f32[8192]{0:T(1024)} %broadcast_multiply_fusion.1) | copy-start | bytes 98308
where the time goes:
time: 777 us; the launch traced here: 768 us
  matrix products  389 us (50%)
  local copies, waits for them, and re-layouts  185 us (24%)
  other arithmetic  92.1 us (12%)
  blocking collectives  65.9 us (8%)
  starting transfers between devices  21.6 us (3%)
  loops' own time  13.2 us (2%)
    dot_general x27, matrix products, near_block(): jnp.einsum('bij,rbj->rbi', kernel, source_charges, preferred_element_type...  340 us
    gather x48, local copies, waits for them, and re-layouts, far_group(): jnp.take(all_moments, safe_ids, axis=1)  46.1 us
    dot_general x16, matrix products, far_group(): return jnp.einsum('mbki,mrbk->rbi', coeffs, picked, precision=largest_index)  39.5 us
    psum x1, blocking collectives, on_device(): raw_sums = lax.psum(partial_result, 'box')  36.4 us
    gather x16, local copies, waits for them, and re-layouts, far_group(): jnp.take(all_centres, safe_ids, axis=1).reshape(3, group_size, -1)  32.1 us
    psum x1, blocking collectives, on_device(): lax.psum(jnp.sum(residual_vector * residual_vector, axis=1), 'box')  29.5 us
    mul x27, local copies, waits for them, and re-layouts, near_block(): diff_x * target_normals[0][:, :, None]  23.1 us
    mul x16, other arithmetic, far_coeffs(): coeff_list = [normal_part * inverse_cube]  22.6 us
  transfers between devices with their start and end apart: 8, of which 0 were waited for; matrix products, arithmetic and copies ran while one was open for 30% of the time, Pallas kernels for 0%

commit v1 on v0

v1 whole, which is shorter than its diff:
```python
import functools

import jax
import jax.numpy as jnp
from jax import lax
from jax.experimental import pallas as pl
from jax.experimental.pallas import tpu as pltpu
from jax.sharding import PartitionSpec as P

soften = 0.0025
epsilon = 1e-06
f32 = jnp.float32
bf16 = jnp.bfloat16
box_rows = 24
plane_boxes = 16
tail = plane_boxes * box_rows
pack_rows = tail + 16
depth = 128


def lattice(centres_s, b):
    x = (centres_s[0, b] + 0.5).astype(jnp.int32)
    y = (centres_s[1, b] + 0.5).astype(jnp.int32)
    z = (centres_s[2, b] + 0.5).astype(jnp.int32)
    return x, y, z


def wide_row(ref, b):
    return jnp.concatenate([ref[pl.ds(2 * b, 1), :], ref[pl.ds(2 * b + 1, 1), :]], axis=1)


def live_row(counts_s, b, per_box):
    slots = lax.broadcasted_iota(jnp.int32, (1, per_box), 1)
    return (slots < counts_s[b]).astype(f32)


def prep_kernel(centres_s, counts_s, current_ref, facets_ref, areas_ref, low_ref, high_ref, packs):
    boxes = counts_s.shape[0]
    per_box = current_ref.shape[2] // boxes
    lane = lax.broadcasted_iota(jnp.int32, (8, 128), 1)
    row = lax.broadcasted_iota(jnp.int32, (8, 128), 0)

    def one_box(b, carry):
        moments, centres = carry
        x, y, z = lattice(centres_s, b)
        plane = z & 1
        place = y * 4 + x
        slot = plane * plane_boxes + place
        lanes = pl.ds(pl.multiple_of(b * per_box, per_box), per_box)
        facets = facets_ref[:, lanes]
        live = live_row(counts_s, b, per_box)
        weighted = current_ref[0, :, lanes] * (wide_row(areas_ref, b) * live / per_box)
        charges = weighted.astype(bf16).astype(f32)
        start = pl.multiple_of(plane * pack_rows + place * box_rows, 8)
        packs[pl.ds(start, 8), :] = charges[:, :128]
        packs[pl.ds(start + 8, 8), :] = charges[:, 128:]
        packs[pl.ds(start + 16, 8), :] = jnp.concatenate(
            [facets[:, :128], facets[:, 128:], jnp.zeros((2, 128), f32)], axis=0
        )
        moments += jnp.where(lane == slot, jnp.sum(weighted, axis=1, keepdims=True), 0.0)
        for a in range(3):
            dipole = jnp.sum(weighted * (facets[a : a + 1] - centres_s[a, b]), axis=1, keepdims=True)
            moments += jnp.where(lane == 32 * (a + 1) + slot, dipole, 0.0)
            centres += jnp.where((lane == slot) & (row == a), centres_s[a, b], 0.0)
        return moments, centres

    zeros = jnp.zeros((8, 128), f32)
    moments, centres = lax.fori_loop(0, boxes, one_box, (zeros, zeros), unroll=4)
    low_ref[:tail] = packs[:tail]
    high_ref[:tail] = packs[pack_rows : pack_rows + tail]
    for ref in (low_ref, high_ref):
        ref[tail : tail + 8] = moments
        ref[tail + 8 :] = centres


def thirds(x):
    high = x.astype(bf16).astype(f32)
    rest = x - high
    middle = rest.astype(bf16).astype(f32)
    return high, middle, (rest - middle).astype(bf16).astype(f32)


def stacked_rows(parts, width):
    zeros = jnp.zeros((depth - 8 * len(parts), width), f32)
    return jnp.concatenate([*parts, zeros], axis=0)


def local_facets(pack_ref, place, origin):
    start = pl.multiple_of(place * box_rows + 16, 8)
    tile = pack_ref[pl.ds(start, 8), :]
    both = jnp.concatenate([tile[0:3], tile[3:6]], axis=1)
    return jnp.concatenate([both - origin, jnp.zeros((5, 256), f32)], axis=0)


def field_kernel(
    centres_s, counts_s, prev_ref, low_ref, high_ref, next_ref, normals_ref, contrast_ref, basis_ref,
    image_ref, sums_ref, left, right, field, far_centres
):
    boxes = counts_s.shape[0]
    krylov = basis_ref.shape[0]
    per_box = image_ref.shape[1] // boxes
    packs = (prev_ref, low_ref, high_ref, next_ref)
    row = lax.broadcasted_iota(jnp.int32, (8, per_box), 0)
    _, _, z = lattice(centres_s, 0)
    base_z = (z - (z & 1)).astype(f32) + 0.5
    axis_row = lax.broadcasted_iota(jnp.int32, (3, 1), 0)
    origin = jnp.where(axis_row == 2, base_z, 1.5)

    for plane, pack in enumerate(packs):

        def source_features(place, _, plane=plane, pack=pack):
            local = local_facets(pack, place, origin)
            square = jnp.sum(local * local, axis=0, keepdims=True)
            features = jnp.where(row == 3, square, jnp.where(row == 4, 1.0, local))
            high, middle, low = thirds(features)
            columns = stacked_rows((high, high, high, middle, middle, low), per_box)
            start = pl.multiple_of((plane * plane_boxes + place) * per_box, per_box)
            left[pl.ds(start, per_box), :] = jnp.transpose(columns).astype(bf16)
            return 0

        lax.fori_loop(0, plane_boxes, source_features, 0, unroll=2)

    for group, pack in enumerate((prev_ref, low_ref, next_ref)):
        columns = jnp.transpose(pack[tail + 8 : tail + 16, :])[:32]
        for a in range(3):
            shift = base_z if a == 2 else 1.5
            far_centres[(group * 3 + a) * 32 : (group * 3 + a + 1) * 32, :] = jnp.broadcast_to(
                columns[:, a : a + 1] - shift, (32, 128)
            )
    far_moments = jnp.concatenate([pack[tail : tail + 8, :] for pack in (prev_ref, low_ref, next_ref)], axis=1)
    far_high = far_moments.astype(bf16).astype(f32)
    far_both = jnp.concatenate([far_high, far_moments - far_high], axis=0)
    far_lane = lax.broadcasted_iota(jnp.int32, (1, 384), 1)
    lane_x = far_lane & 3
    lane_y = (far_lane >> 2) & 3
    lane_z = 2 * (far_lane >> 7) - 2 + ((far_lane >> 4) & 1)

    def target(b, _):
        x, y, z = lattice(centres_s, b)
        plane = z & 1
        place = y * 4 + x
        slot = plane * plane_boxes + place
        lanes = pl.ds(pl.multiple_of(b * per_box, per_box), per_box)
        start = pl.multiple_of(place * box_rows + 16, 8)
        tile = jnp.where(plane == 0, low_ref[pl.ds(start, 8), :], high_ref[pl.ds(start, 8), :])
        local = jnp.concatenate([tile[0:3], tile[3:6]], axis=1) - origin
        normal = normals_ref[:, lanes]
        five = jnp.zeros((5, per_box), f32)
        local_8 = jnp.concatenate([local, five], axis=0)
        normal_8 = jnp.concatenate([normal, five], axis=0)
        square = jnp.sum(local_8 * local_8, axis=0, keepdims=True) + soften
        along = jnp.sum(local_8 * normal_8, axis=0, keepdims=True)
        distance = jnp.where(row == 3, 1.0, jnp.where(row == 4, square, -2.0 * local_8))
        slope = jnp.where(row == 4, along, -normal_8)
        both = jnp.concatenate([distance, slope], axis=1)
        high, middle, low = thirds(both)
        rows = stacked_rows((high, middle, low, high, middle, high), 2 * per_box)
        right[pl.ds(pl.multiple_of(slot * depth, depth), depth), :] = rows.astype(bf16)

        coefficients = []
        for group in range(3):
            d = []
            for a in range(3):
                centre = far_centres[(group * 3 + a) * 32 : (group * 3 + a + 1) * 32, :]
                d.append(local[a : a + 1] - jnp.concatenate([centre, centre], axis=1))
            q = d[0] * d[0] + d[1] * d[1] + d[2] * d[2] + soften
            inverse = lax.rsqrt(q)
            inverse_2 = inverse * inverse
            inverse_3 = inverse_2 * inverse
            t = d[0] * normal[0:1] + d[1] * normal[1:2] + d[2] * normal[2:3]
            single = t * inverse_3
            coefficients.append(single)
            steep = 3.0 * single * inverse_2
            for a in range(3):
                coefficients.append(steep * d[a] - normal[a : a + 1] * inverse_3)
        whole = jnp.concatenate(coefficients, axis=0)
        upper = whole.astype(bf16)
        lower = (whole - upper.astype(f32)).astype(bf16)
        near = (
            (jnp.abs(lane_x - x) <= 1) & (jnp.abs(lane_y - y) <= 1) & (jnp.abs(lane_z - plane) <= 1)
        )
        picked = jnp.where(near, 0.0, far_both).astype(bf16)
        first = jnp.dot(picked, upper, preferred_element_type=f32)
        second = jnp.dot(picked, lower, preferred_element_type=f32)
        field[pl.ds(pl.multiple_of(slot * 8, 8), 8), :] = first[:8] + first[8:] + second[:8]
        return 0

    lax.fori_loop(0, boxes, target, 0)

    for step in range(3):
        for plane in range(2):
            pack = packs[plane + step]

            def near_rows(item, _, plane=plane, step=step, pack=pack):
                target_y = (item + 1) // 3
                source_y = target_y + lax.rem(item + 1, 3) - 1
                source_start = pl.multiple_of((plane + step) * plane_boxes * per_box + source_y * 4 * per_box, per_box)
                charges = []
                for x in range(4):
                    start = pl.multiple_of((source_y * 4 + x) * box_rows, 8)
                    charges.append(
                        jnp.concatenate(
                            [pack[pl.ds(start, 8), :], pack[pl.ds(start + 8, 8), :]], axis=1
                        ).astype(bf16)
                    )
                for x in range(4):
                    slot = plane * plane_boxes + target_y * 4 + x
                    weights = right[pl.ds(pl.multiple_of(slot * depth, depth), depth), :]
                    total = None
                    for source_x in range(max(x - 1, 0), min(x + 2, 4)):
                        facets = left[pl.ds(source_start + source_x * per_box, per_box), :]
                        geometry = jnp.dot(facets, weights, preferred_element_type=f32)
                        inverse = lax.rsqrt(geometry[:, :per_box])
                        kernel = (geometry[:, per_box:] * inverse) * (inverse * inverse)
                        part = jnp.dot(charges[source_x], kernel.astype(bf16), preferred_element_type=f32)
                        total = part if total is None else total + part
                    field[pl.ds(pl.multiple_of(slot * 8, 8), 8), :] += total
                return 0

            lax.fori_loop(0, 10, near_rows, 0)

    def image_box(b, carry):
        x, y, z = lattice(centres_s, b)
        slot = (z & 1) * plane_boxes + y * 4 + x
        lanes = pl.ds(pl.multiple_of(b * per_box, per_box), per_box)
        live = live_row(counts_s, b, per_box)
        current = basis_ref[krylov - 1, :, lanes]
        part = field[pl.ds(pl.multiple_of(slot * 8, 8), 8), :]
        image = live * (current - 2.0 * wide_row(contrast_ref, b) * part)
        image_ref[:, lanes] = image
        sums = []
        for m in range(krylov + 1):
            product = image * (basis_ref[m, :, lanes] if m < krylov else image)
            sums.append(carry[m] + product[:, :128] + product[:, 128:])
        return tuple(sums)

    zeros = jnp.zeros((8, 128), f32)
    sums = lax.fori_loop(0, boxes, image_box, (zeros,) * (krylov + 1))
    pairs = [(m, n) for m in range(krylov) for n in range(m + 1)]

    def gram_box(b, carry):
        lanes = pl.ds(pl.multiple_of(b * per_box, per_box), per_box)
        live = live_row(counts_s, b, per_box)
        rows = [basis_ref[m, :, lanes] * live for m in range(krylov)]
        out = []
        for k, (m, n) in enumerate(pairs):
            product = rows[m] * rows[n]
            out.append(carry[k] + product[:, :128] + product[:, 128:])
        return tuple(out)

    gram = lax.fori_loop(0, boxes, gram_box, (zeros,) * len(pairs))
    lane = lax.broadcasted_iota(jnp.int32, (8, 128), 1)
    total = zeros
    for k, value in enumerate([*sums, *gram]):
        total = jnp.where(lane == k, jnp.sum(value, axis=1, keepdims=True), total)
    sums_ref[...] = total


def two_sum(a, b):
    s = a + b
    c = s - a
    return s, (a - (s - c)) + (b - c)


def halves(a):
    c = a * 4097.0
    high = c - (c - a)
    return high, a - high


def two_product(a, b):
    p = a * b
    a_high, a_low = halves(a)
    b_high, b_low = halves(b)
    return p, ((a_high * b_high - p) + a_high * b_low + a_low * b_high) + a_low * b_low


def finish_kernel(total_facets, counts_s, sums_ref, rest_ref, image_ref, basis_ref, next_ref, hessenberg_ref):
    boxes = counts_s.shape[0]
    krylov = basis_ref.shape[0]
    per_box = image_ref.shape[1] // boxes
    lane = lax.broadcasted_iota(jnp.int32, (8, 128), 1)
    sums = sums_ref[...]
    rest = rest_ref[...]
    exact = sums + rest
    projections = [exact[:, m : m + 1] / total_facets for m in range(krylov)]
    pairs = [(m, n) for m in range(krylov) for n in range(m + 1)]
    first = jnp.where(lane == krylov, 1.0, 0.0)
    second = jnp.where(lane <= krylov, 1.0, 0.0)
    for m in range(krylov):
        first = jnp.where(lane == m, -2.0 * projections[m], first)
    for k, (m, n) in enumerate(pairs):
        at = lane == krylov + 1 + k
        scale = 1.0 if m == n else 2.0
        first = jnp.where(at, scale * projections[m], first)
        second = jnp.where(at, projections[n], second)
    factor, factor_rest = two_product(first, second)
    value, value_rest = two_product(factor, sums)
    value_rest = value_rest + (factor * rest + factor_rest * sums)
    for shift in (64, 32, 16, 8, 4, 2, 1):
        other = pltpu.roll(value, shift, 1)
        other_rest = pltpu.roll(value_rest, shift, 1)
        value, error = two_sum(value, other)
        value_rest = (value_rest + other_rest) + error
    remaining = jnp.maximum(value + value_rest, 0.0)
    norm = jnp.sqrt(remaining / total_facets + epsilon)
    heads = jnp.where(lane == krylov, norm, 0.0)
    for m in range(krylov):
        heads = jnp.where(lane == m, projections[m], heads)
    hessenberg_ref[...] = jnp.transpose(heads)[: krylov + 1]
    wide = [jnp.broadcast_to(p, (8, per_box)) for p in projections]
    scale = jnp.concatenate([1.0 / norm] * (per_box // 128), axis=1)

    def one_box(b, _):
        lanes = pl.ds(pl.multiple_of(b * per_box, per_box), per_box)
        live = live_row(counts_s, b, per_box)
        sent = wide[0] * basis_ref[0, :, lanes]
        for m in range(1, krylov):
            sent += wide[m] * basis_ref[m, :, lanes]
        next_ref[:, lanes] = (image_ref[:, lanes] - sent * live) * scale
        return 0

    lax.fori_loop(0, boxes, one_box, 0, unroll=4)


smem = pl.BlockSpec(memory_space=pltpu.SMEM)
vmem = pl.BlockSpec(memory_space=pltpu.VMEM)


def summed(value, axis):
    count = lax.axis_size(axis)
    rest = jnp.zeros_like(value)
    step = 1
    while step < count:
        pairs = [(i, i ^ step) for i in range(count)]
        if step == 1:
            value, rest = two_sum(value, lax.ppermute(value, axis, pairs))
        else:
            other = lax.ppermute(jnp.stack([value, rest]), axis, pairs)
            value, error = two_sum(value, other[0])
            rest = (rest + other[1]) + error
        step *= 2
    return value, rest


def on_device(
    basis, facet_centres, normals, areas, contrast, facet_counts, box_centres, near_boxes, far_boxes
):
    krylov, rhs_local, facet_local = basis.shape
    boxes = facet_counts.shape[0]
    per_box = facet_local // boxes
    count = lax.axis_size("box")
    total_facets = count * facet_local
    areas = areas.reshape(-1, 128)
    contrast = contrast.reshape(-1, 128)
    pack = jax.ShapeDtypeStruct((pack_rows, 128), f32)
    low, high = pl.pallas_call(
        prep_kernel,
        grid=(1,),
        out_shape=(pack, pack),
        in_specs=[
            smem,
            smem,
            pl.BlockSpec((1, rhs_local, facet_local), lambda i: (krylov - 1, 0, 0)),
            vmem,
            vmem,
        ],
        out_specs=(vmem, vmem),
        scratch_shapes=[pltpu.VMEM((2 * pack_rows, 128), f32)],
        name="prepare",
    )(box_centres, facet_counts, basis, facet_centres, areas)
    below = lax.ppermute(high, "box", [(i, i + 1) for i in range(count - 1)])
    above = lax.ppermute(low, "box", [(i + 1, i) for i in range(count - 1)])
    image, sums = pl.pallas_call(
        field_kernel,
        out_shape=(
            jax.ShapeDtypeStruct((rhs_local, facet_local), f32),
            jax.ShapeDtypeStruct((8, 128), f32),
        ),
        in_specs=[smem, smem] + [vmem] * 7,
        out_specs=(vmem, vmem),
        scratch_shapes=[
            pltpu.VMEM((4 * plane_boxes * per_box, depth), bf16),
            pltpu.VMEM((boxes * depth, 2 * per_box), bf16),
            pltpu.VMEM((boxes * 8, per_box), f32),
            pltpu.VMEM((9 * 32, 128), f32),
        ],
        compiler_params=pltpu.CompilerParams(vmem_limit_bytes=48 * 1024 * 1024),
        name="fields",
    )(box_centres, facet_counts, below, low, high, above, normals, contrast, basis)
    value, rest = summed(sums, "box")
    return tuple(
        pl.pallas_call(
            functools.partial(finish_kernel, total_facets),
            out_shape=(
                jax.ShapeDtypeStruct((rhs_local, facet_local), f32),
                jax.ShapeDtypeStruct((krylov + 1, rhs_local), f32),
            ),
            in_specs=[smem] + [vmem] * 4,
            out_specs=(vmem, vmem),
            compiler_params=pltpu.CompilerParams(vmem_limit_bytes=16 * 1024 * 1024),
            name="finish",
        )(facet_counts, value, rest, image, basis)
    )


def solution(mesh):
    return jax.shard_map(
        on_device,
        mesh=mesh,
        in_specs=(
            P(None, "rhs", "box"),
            P(None, "box"),
            P(None, "box"),
            P("box"),
            P("box"),
            P("box"),
            P(None, "box"),
            P("box", None),
            P("box", None),
        ),
        out_specs=(P("rhs", "box"), P(None, "rhs")),
        check_vma=False,
    )
```

time: 777 us -> 148 us (0.19); the launches traced: 768 us -> 147 us
  matrix products: 389 us -> 0 us
  local copies, waits for them, and re-layouts: 185 us -> 2.55 us
  Pallas kernels: 0 us -> 118 us
  other arithmetic: 92.1 us -> 0.05 us
  blocking collectives: 65.9 us -> 0 us
  loops' own time: 13.2 us -> 0 us
  waiting for transfers between devices: 0.02 us -> 10.8 us
    dot_general x46 -> x0, matrix products: 389 us -> none  [the longest x27 340 us: near_block(): jnp.einsum('bij,rbj->rbi', kernel, source_charges, preferred_element_type...]
    pallas_call x0 -> x3, Pallas kernels: none -> 118 us  [the longest x1 114 us: on_device(): pl.pallas_call(field_kernel, out_shape=(jax.ShapeDtypeStruct((rhs_local,...]
    gather x118 -> x0, local copies, waits for them, and re-layouts: 111 us -> none  [the longest x48 46.1 us: far_group(): jnp.take(all_moments, safe_ids, axis=1)]
    psum x2 -> x0, blocking collectives: 65.9 us -> none  [the longest x1 36.4 us: on_device(): raw_sums = lax.psum(partial_result, 'box')]
    mul x35 -> x0, other arithmetic: 37.7 us -> none  [the longest x16 22.6 us: far_coeffs(): coeff_list = [normal_part * inverse_cube]]
    mul x44 -> x0, local copies, waits for them, and re-layouts: 35.9 us -> none  [the longest x27 23.1 us: near_block(): diff_x * target_normals[0][:, :, None]]
    and x32 -> x0, other arithmetic: 21.1 us -> none  [far_group(): jnp.take(all_moments, safe_ids, axis=1)]
    dynamic_slice x16 -> x0, local copies, waits for them, and re-layouts: 20.1 us -> none  [on_device(): far_parts = lax.map(far_group, jnp.arange(group_count, dtype=jnp.int32))]
  transfers between devices with their start and end apart: 8 -> 6, of which waited for: 0 -> 5; matrix products, arithmetic and copies ran while one was open for 30% -> 0% of each run, Pallas kernels for 0% -> 0%
where the time goes in v1:
time: 148 us; the launch traced here: 147 us
  Pallas kernels  118 us (80%)
  starting transfers between devices  14.7 us (10%)
  waiting for transfers between devices  10.8 us (7%)
  local copies, waits for them, and re-layouts  2.55 us (2%)
    pallas_call x1, Pallas kernels, on_device(): pl.pallas_call(field_kernel, out_shape=(jax.ShapeDtypeStruct((rhs_local,...  114 us
    ppermute x3, starting transfers between devices, summed(): other = lax.ppermute(jnp.stack([value, rest]), axis, pairs)  6.78 us
    ppermute x3, waiting for transfers between devices, summed(): other = lax.ppermute(jnp.stack([value, rest]), axis, pairs)  5.64 us
    ppermute x1, waiting for transfers between devices, on_device(): above = lax.ppermute(low, 'box', [(i + 1, i) for i in range(count - 1)])  4.34 us
    ppermute x1, starting transfers between devices, summed(): value, rest = two_sum(value, lax.ppermute(value, axis, pairs))  4.29 us
  transfers between devices with their start and end apart: 6, of which 5 were waited for; matrix products, arithmetic and copies ran while one was open for 0% of the time, Pallas kernels for 0%

profile of v1, /device:TPU:0, one launch (start us, length us, event | category | flops | bytes accessed | tf_op | source)
XLA Modules:
  0.0 147.3 jit_solution(14119449685264593732)
XLA Ops:
  0.6 0.0 copy-start.6
  0.6 0.0 copy-start
  0.7 0.0 copy-start.5
  0.7 0.0 copy-start.4
  0.7 0.0 copy-start.3
  0.7 2.8 %prepare.1 = (f32[400,128]{1,0:T(8,128)}, f32[400,128]{1,0:T(8,128)}) custom-call(f32[3,32]{1,0:T(4,128)} %centres_s.3, s32[32]{0:T(128)} %counts_s.5, f32[8,8,8192]{2,1,0:T(8,128)} %basis_ref.3, f32[3,8192]{1,0:T(4,128)} %facets_ref.1, f32[64,128]{1,0:T(8,128)} %bitcast.70), custom_call_target="tpu_custom_call" | custom-call | tf_op jit(solution)/shard_map/prepare/pallas_call | solution.py:357
  3.5 2.4 %collective-permute-start = (f32[400,128]{1,0:T(8,128)}, f32[400,128]{1,0:T(8,128)S(1)}, u32[]{:S(2)}, u32[]{:S(2)}) collective-permute-start(f32[400,128]{1,0:T(8,128)} %get-tuple-element.6.high_ref), channel_id=1, source_target_pairs={{0,2},{2,4},{4,6},{6,8},{8,10},{10,12},{12,14},{14,16},{16,18},{18... | collective-permute-start | bytes 614408 | tf_op jit(solution)/shard_map/ppermute | solution.py:372
  5.8 1.3 collective-permute-start.1
  7.1 0.0 collective-permute-done.prev_ref
  7.2 4.3 %collective-permute-done.1.next_ref = f32[400,128]{1,0:T(8,128)S(1)} collective-permute-done((f32[400,128]{1,0:T(8,128)}, f32[400,128]{1,0:T(8,128)S(1)}, u32[]{:S(2)}, u32[]{:S(2)}) %collective-permute-start.1) | collective-permute-done | bytes 204832 | tf_op jit(solution)/shard_map/ppermute | solution.py:373
  11.5 0.0 copy-done.6
  11.5 0.0 copy-done
  11.5 0.0 copy-done.5
  11.5 0.0 copy-done.4
  11.5 0.0 copy-done.3
  11.5 0.0 copy-start.1
  11.5 0.9 copy-done.1
  12.5 0.0 copy-start.2
  12.5 0.9 copy-done.2
  13.4 113.5 %fields.1 = (f32[8,8192]{1,0:T(8,128)S(1)}, f32[8,128]{1,0:T(8,128)S(1)}) custom-call(f32[3,32]{1,0:T(4,128)S(1)} %copy-done.5, s32[32]{0:T(128)S(1)} %copy-done.6, f32[400,128]{1,0:T(8,128)S(1)} %collective-permute-done.prev_ref, f32[400,128]{1,0:T(8,128)S(1)} %copy-done.1, f32[400,128]{1,0:T(8,128)S(1)} %copy-done.2, ...), custom_call_target="tpu_custom_call" | custom-call | tf_op jit(solution)/shard_map/fields/pallas_call | solution.py:374
  126.9 4.3 %collective-permute-start.2 = (f32[8,128]{1,0:T(8,128)S(1)}, f32[8,128]{1,0:T(8,128)S(1)}, u32[]{:S(2)}, u32[]{:S(2)}) collective-permute-start(f32[8,128]{1,0:T(8,128)S(1)} %get-tuple-element.8), channel_id=1, source_target_pairs={{0,2},{2,0},{4,6},{6,4},{8,10},{10,8},{12,14},{14,12},{16,18},{18,... | collective-permute-start | bytes 12296 | tf_op jit(solution)/shard_map/ppermute | solution.py:337
  131.2 0.8 collective-permute-done.2
  132.0 2.5 %collective-permute-start.3 = (f32[2,8,128]{2,1,0:T(8,128)S(1)}, f32[2,8,128]{2,1,0:T(8,128)S(1)}, u32[]{:S(2)}, u32[]{:S(2)}) collective-permute-start(f32[2,8,128]{2,1,0:T(8,128)S(1)} %pad_maximum_fusion), channel_id=1, source_target_pairs={{0,4},{2,6},{4,0},{6,2},{8,12},{10,14},{12,8},{14,10},{16,20},{18,... | collective-permute-start | bytes 24584 | tf_op jit(solution)/shard_map/ppermute | solution.py:339
  134.5 1.6 %collective-permute-done.3 = f32[2,8,128]{2,1,0:T(8,128)S(1)} collective-permute-done((f32[2,8,128]{2,1,0:T(8,128)S(1)}, f32[2,8,128]{2,1,0:T(8,128)S(1)}, u32[]{:S(2)}, u32[]{:S(2)}) %collective-permute-start.3) | collective-permute-done | bytes 8224 | tf_op jit(solution)/shard_map/ppermute | solution.py:339
  136.2 1.6 %collective-permute-start.4 = (f32[2,8,128]{2,1,0:T(8,128)S(1)}, f32[2,8,128]{2,1,0:T(8,128)S(1)}, u32[]{:S(2)}, u32[]{:S(2)}) collective-permute-start(f32[2,8,128]{2,1,0:T(8,128)S(1)} %pad_maximum_fusion.1), channel_id=1, source_target_pairs={{0,8},{2,10},{4,12},{6,14},{8,0},{10,2},{12,4},{14,6},{16,24},{18,... | collective-permute-start | bytes 24584 | tf_op jit(solution)/shard_map/ppermute | solution.py:339
  137.8 2.1 %collective-permute-done.4 = f32[2,8,128]{2,1,0:T(8,128)S(1)} collective-permute-done((f32[2,8,128]{2,1,0:T(8,128)S(1)}, f32[2,8,128]{2,1,0:T(8,128)S(1)}, u32[]{:S(2)}, u32[]{:S(2)}) %collective-permute-start.4) | collective-permute-done | bytes 8224 | tf_op jit(solution)/shard_map/ppermute | solution.py:339
  139.9 2.7 %collective-permute-start.5 = (f32[2,8,128]{2,1,0:T(8,128)S(1)}, f32[2,8,128]{2,1,0:T(8,128)S(1)}, u32[]{:S(2)}, u32[]{:S(2)}) collective-permute-start(f32[2,8,128]{2,1,0:T(8,128)S(1)} %pad_maximum_fusion.2), channel_id=1, source_target_pairs={{0,16},{2,18},{4,20},{6,22},{8,24},{10,26},{12,28},{14,30},{16,0},... | collective-permute-start | bytes 24584 | tf_op jit(solution)/shard_map/ppermute | solution.py:339
  142.5 2.0 %collective-permute-done.5 = f32[2,8,128]{2,1,0:T(8,128)S(1)} collective-permute-done((f32[2,8,128]{2,1,0:T(8,128)S(1)}, f32[2,8,128]{2,1,0:T(8,128)S(1)}, u32[]{:S(2)}, u32[]{:S(2)}) %collective-permute-start.5) | collective-permute-done | bytes 8224 | tf_op jit(solution)/shard_map/ppermute | solution.py:339
  144.5 2.2 %finish.1 = (f32[8,8192]{1,0:T(8,128)}, f32[9,8]{1,0:T(8,128)S(1)}) custom-call(s32[32]{0:T(128)S(1)} %copy-done.6, f32[8,128]{1,0:T(8,128)S(1)} %get-tuple-element.17.sums_ref, f32[8,128]{1,0:T(8,128)S(1)} %get-tuple-element.16.rest_ref, f32[8,8192]{1,0:T(8,128)S(1)} %get-tuple-element.9.image_ref, f32[8,8,8192]{2,1,0:T(8,128)S(1)} %copy-done), custom_call_target="tpu_custom_call" | custom-call | tf_op jit(solution)/shard_map/finish/pallas_call | solution.py:393
  146.7 0.7 copy.9
  (7 shorter events, 0.1 us)
Async XLA Ops:
  0.6 10.9 %copy-start.6 = (s32[32]{0:T(128)S(1)}, s32[32]{0:T(128)}, u32[]{:S(2)}) copy-start(s32[32]{0:T(128)} %counts_s.5) | copy-start | bytes 388
  0.6 10.9 %copy-start = (f32[8,8,8192]{2,1,0:T(8,128)S(1)}, f32[8,8,8192]{2,1,0:T(8,128)}, u32[]{:S(2)}) copy-start(f32[8,8,8192]{2,1,0:T(8,128)} %basis_ref.3) | copy-start | bytes 6291460
  0.7 10.8 %copy-start.5 = (f32[3,32]{1,0:T(4,128)S(1)}, f32[3,32]{1,0:T(4,128)}, u32[]{:S(2)}) copy-start(f32[3,32]{1,0:T(4,128)} %centres_s.3) | copy-start | bytes 1156
  0.7 10.8 %copy-start.4 = (f32[8192]{0:T(1024)S(1)}, f32[8192]{0:T(1024)}, u32[]{:S(2)}) copy-start(f32[8192]{0:T(1024)} %param.13) | copy-start | bytes 98308
  0.7 10.8 %copy-start.3 = (f32[3,8192]{1,0:T(4,128)S(1)}, f32[3,8192]{1,0:T(4,128)}, u32[]{:S(2)}) copy-start(f32[3,8192]{1,0:T(4,128)} %normals_ref.1) | copy-start | bytes 294916
  3.5 3.7 %collective-permute-start = (f32[400,128]{1,0:T(8,128)}, f32[400,128]{1,0:T(8,128)S(1)}, u32[]{:S(2)}, u32[]{:S(2)}) collective-permute-start(f32[400,128]{1,0:T(8,128)} %get-tuple-element.6.high_ref), channel_id=1, source_target_pairs={{0,2},{2,4},{4,6},{6,8},{8,10},{10,12},{12,14},{14,16},{16,18},{18... | collective-permute-start | bytes 614408 | tf_op jit(solution)/shard_map/ppermute | solution.py:372
  5.8 5.7 %collective-permute-start.1 = (f32[400,128]{1,0:T(8,128)}, f32[400,128]{1,0:T(8,128)S(1)}, u32[]{:S(2)}, u32[]{:S(2)}) collective-permute-start(f32[400,128]{1,0:T(8,128)} %get-tuple-element.7.low_ref), channel_id=1, source_target_pairs={{2,0},{4,2},{6,4},{8,6},{10,8},{12,10},{14,12},{16,14},{18,16},{20... | collective-permute-start | bytes 614408 | tf_op jit(solution)/shard_map/ppermute | solution.py:373
  11.5 0.9 copy-start.1
  12.5 0.9 copy-start.2
  126.9 5.1 %collective-permute-start.2 = (f32[8,128]{1,0:T(8,128)S(1)}, f32[8,128]{1,0:T(8,128)S(1)}, u32[]{:S(2)}, u32[]{:S(2)}) collective-permute-start(f32[8,128]{1,0:T(8,128)S(1)} %get-tuple-element.8), channel_id=1, source_target_pairs={{0,2},{2,0},{4,6},{6,4},{8,10},{10,8},{12,14},{14,12},{16,18},{18,... | collective-permute-start | bytes 12296 | tf_op jit(solution)/shard_map/ppermute | solution.py:337
  132.0 4.1 %collective-permute-start.3 = (f32[2,8,128]{2,1,0:T(8,128)S(1)}, f32[2,8,128]{2,1,0:T(8,128)S(1)}, u32[]{:S(2)}, u32[]{:S(2)}) collective-permute-start(f32[2,8,128]{2,1,0:T(8,128)S(1)} %pad_maximum_fusion), channel_id=1, source_target_pairs={{0,4},{2,6},{4,0},{6,2},{8,12},{10,14},{12,8},{14,10},{16,20},{18,... | collective-permute-start | bytes 24584 | tf_op jit(solution)/shard_map/ppermute | solution.py:339
  136.2 3.7 %collective-permute-start.4 = (f32[2,8,128]{2,1,0:T(8,128)S(1)}, f32[2,8,128]{2,1,0:T(8,128)S(1)}, u32[]{:S(2)}, u32[]{:S(2)}) collective-permute-start(f32[2,8,128]{2,1,0:T(8,128)S(1)} %pad_maximum_fusion.1), channel_id=1, source_target_pairs={{0,8},{2,10},{4,12},{6,14},{8,0},{10,2},{12,4},{14,6},{16,24},{18,... | collective-permute-start | bytes 24584 | tf_op jit(solution)/shard_map/ppermute | solution.py:339
  139.9 4.6 %collective-permute-start.5 = (f32[2,8,128]{2,1,0:T(8,128)S(1)}, f32[2,8,128]{2,1,0:T(8,128)S(1)}, u32[]{:S(2)}, u32[]{:S(2)}) collective-permute-start(f32[2,8,128]{2,1,0:T(8,128)S(1)} %pad_maximum_fusion.2), channel_id=1, source_target_pairs={{0,16},{2,18},{4,20},{6,22},{8,24},{10,26},{12,28},{14,30},{16,0},... | collective-permute-start | bytes 24584 | tf_op jit(solution)/shard_map/ppermute | solution.py:339

commit v2 on v1

v2 whole, which is shorter than its diff:
```python
import functools

import jax
import jax.numpy as jnp
from jax import lax
from jax.experimental import pallas as pl
from jax.experimental.pallas import tpu as pltpu
from jax.sharding import PartitionSpec as P

soften = 0.0025
epsilon = 1e-06
f32 = jnp.float32
bf16 = jnp.bfloat16
box_rows = 24
plane_boxes = 16
per_box = 256
tail = plane_boxes * box_rows
pack_rows = tail + 16
depth = 128


def lattice(centres_s, b):
    x = (centres_s[0, b] + 0.5).astype(jnp.int32)
    y = (centres_s[1, b] + 0.5).astype(jnp.int32)
    z = (centres_s[2, b] + 0.5).astype(jnp.int32)
    return x, y, z


def wide_row(ref, b):
    return jnp.concatenate([ref[pl.ds(2 * b, 1), :], ref[pl.ds(2 * b + 1, 1), :]], axis=1)


def live_row(counts_s, b):
    slots = lax.broadcasted_iota(jnp.int32, (1, per_box), 1)
    return (slots < counts_s[b]).astype(f32)


def prep_kernel(centres_s, counts_s, current_ref, facets_ref, areas_ref, low_ref, high_ref, packs):
    boxes = counts_s.shape[0]
    lane = lax.broadcasted_iota(jnp.int32, (8, 128), 1)
    row = lax.broadcasted_iota(jnp.int32, (8, 128), 0)

    def one_box(b, carry):
        moments, centres = carry
        x, y, z = lattice(centres_s, b)
        plane = z & 1
        place = y * 4 + x
        slot = plane * plane_boxes + place
        lanes = pl.ds(pl.multiple_of(b * per_box, per_box), per_box)
        facets = facets_ref[:, lanes]
        live = live_row(counts_s, b)
        weighted = current_ref[0, :, lanes] * (wide_row(areas_ref, b) * live / per_box)
        charges = weighted.astype(bf16).astype(f32)
        start = pl.multiple_of(plane * pack_rows + place * box_rows, 8)
        packs[pl.ds(start, 8), :] = charges[:, :128]
        packs[pl.ds(start + 8, 8), :] = charges[:, 128:]
        packs[pl.ds(start + 16, 8), :] = jnp.concatenate(
            [facets[:, :128], facets[:, 128:], jnp.zeros((2, 128), f32)], axis=0
        )
        moments += jnp.where(lane == slot, jnp.sum(weighted, axis=1, keepdims=True), 0.0)
        for a in range(3):
            dipole = jnp.sum(weighted * (facets[a : a + 1] - centres_s[a, b]), axis=1, keepdims=True)
            moments += jnp.where(lane == 32 * (a + 1) + slot, dipole, 0.0)
            centres += jnp.where((lane == slot) & (row == a), centres_s[a, b], 0.0)
        return moments, centres

    zeros = jnp.zeros((8, 128), f32)
    moments, centres = lax.fori_loop(0, boxes, one_box, (zeros, zeros), unroll=4)
    low_ref[:tail] = packs[:tail]
    high_ref[:tail] = packs[pack_rows : pack_rows + tail]
    for ref in (low_ref, high_ref):
        ref[tail : tail + 8] = moments
        ref[tail + 8 :] = centres


def thirds(x):
    high = x.astype(bf16).astype(f32)
    rest = x - high
    middle = rest.astype(bf16).astype(f32)
    return high, middle, (rest - middle).astype(bf16).astype(f32)


def stacked_rows(parts, width):
    zeros = jnp.zeros((depth - 8 * len(parts), width), f32)
    return jnp.concatenate([*parts, zeros], axis=0)


def local_facets(pack_ref, place, origin):
    start = pl.multiple_of(place * box_rows + 16, 8)
    tile = pack_ref[pl.ds(start, 8), :]
    both = jnp.concatenate([tile[0:3], tile[3:6]], axis=1)
    return jnp.concatenate([both - origin, jnp.zeros((5, 256), f32)], axis=0)


def slab_origin(centres_s):
    _, _, z = lattice(centres_s, 0)
    base_z = (z - (z & 1)).astype(f32) + 0.5
    axis_row = lax.broadcasted_iota(jnp.int32, (3, 1), 0)
    return jnp.where(axis_row == 2, base_z, 1.5), base_z


def store_source_features(pack, origin, left, first):
    row = lax.broadcasted_iota(jnp.int32, (8, per_box), 0)

    def one_box(place, _):
        local = local_facets(pack, place, origin)
        square = jnp.sum(local * local, axis=0, keepdims=True)
        features = jnp.where(row == 3, square, jnp.where(row == 4, 1.0, local))
        high, middle, low = thirds(features)
        columns = stacked_rows((high, high, high, middle, middle, low), per_box)
        start = pl.multiple_of(first + place * per_box, per_box)
        left[pl.ds(start, per_box), :] = jnp.transpose(columns).astype(bf16)
        return 0

    lax.fori_loop(0, plane_boxes, one_box, 0, unroll=2)


def target_place(centres_s, b):
    x, y, z = lattice(centres_s, b)
    plane = z & 1
    place = y * 4 + x
    return x, y, plane, place, plane * plane_boxes + place


def facets_at(low_ref, high_ref, plane, place, origin):
    start = pl.multiple_of(place * box_rows + 16, 8)
    tile = jnp.where(plane == 0, low_ref[pl.ds(start, 8), :], high_ref[pl.ds(start, 8), :])
    return jnp.concatenate([tile[0:3], tile[3:6]], axis=1) - origin


def feature_kernel(centres_s, low_ref, high_ref, normals_ref, left, right):
    boxes = centres_s.shape[1]
    row = lax.broadcasted_iota(jnp.int32, (8, per_box), 0)
    origin, _ = slab_origin(centres_s)
    store_source_features(low_ref, origin, left, 0)
    store_source_features(high_ref, origin, left, plane_boxes * per_box)

    def target(b, _):
        _, _, plane, place, slot = target_place(centres_s, b)
        local = facets_at(low_ref, high_ref, plane, place, origin)
        normal = normals_ref[:, pl.ds(pl.multiple_of(b * per_box, per_box), per_box)]
        five = jnp.zeros((5, per_box), f32)
        local_8 = jnp.concatenate([local, five], axis=0)
        normal_8 = jnp.concatenate([normal, five], axis=0)
        square = jnp.sum(local_8 * local_8, axis=0, keepdims=True) + soften
        along = jnp.sum(local_8 * normal_8, axis=0, keepdims=True)
        distance = jnp.where(row == 3, 1.0, jnp.where(row == 4, square, -2.0 * local_8))
        slope = jnp.where(row == 4, along, -normal_8)
        both = jnp.concatenate([distance, slope], axis=1)
        high, middle, low = thirds(both)
        rows = stacked_rows((high, middle, low, high, middle, high), 2 * per_box)
        right[pl.ds(pl.multiple_of(slot * depth, depth), depth), :] = rows.astype(bf16)
        return 0

    lax.fori_loop(0, boxes, target, 0, unroll=2)


def near_plane(pack, left, first, right, plane, field):
    def near_rows(item, _):
        target_y = (item + 1) // 3
        source_y = target_y + lax.rem(item + 1, 3) - 1
        source_start = pl.multiple_of(first + source_y * 4 * per_box, per_box)
        charges = []
        for x in range(4):
            start = pl.multiple_of((source_y * 4 + x) * box_rows, 8)
            charges.append(
                jnp.concatenate([pack[pl.ds(start, 8), :], pack[pl.ds(start + 8, 8), :]], axis=1).astype(bf16)
            )
        for x in range(4):
            slot = plane * plane_boxes + target_y * 4 + x
            weights = right[pl.ds(pl.multiple_of(slot * depth, depth), depth), :]
            low, high = max(x - 1, 0), min(x + 2, 4)
            facets = left[pl.ds(source_start + low * per_box, (high - low) * per_box), :]
            geometry = jnp.dot(facets, weights, preferred_element_type=f32)
            inverse = lax.rsqrt(geometry[:, :per_box])
            kernel = ((geometry[:, per_box:] * inverse) * (inverse * inverse)).astype(bf16)
            row_charges = jnp.concatenate(charges[low:high], axis=1)
            total = jnp.dot(row_charges, kernel, preferred_element_type=f32)
            field[pl.ds(pl.multiple_of(slot * 8, 8), 8), :] += total
        return 0

    lax.fori_loop(0, 10, near_rows, 0)


def own_kernel(low_ref, high_ref, left, right, field):
    field[...] = jnp.zeros_like(field)
    for plane in range(2):
        near_plane(low_ref, left, 0, right, plane, field)
        near_plane(high_ref, left, plane_boxes * per_box, right, plane, field)


def halo_kernel(
    centres_s, counts_s, prev_ref, low_ref, high_ref, next_ref, normals_ref, contrast_ref, basis_ref, right,
    own_field, image_ref, sums_ref, left, field, far_centres
):
    boxes = counts_s.shape[0]
    krylov = basis_ref.shape[0]
    origin, base_z = slab_origin(centres_s)
    field[...] = own_field[...]
    store_source_features(prev_ref, origin, left, 0)
    store_source_features(next_ref, origin, left, plane_boxes * per_box)
    near_plane(prev_ref, left, 0, right, 0, field)
    near_plane(next_ref, left, plane_boxes * per_box, right, 1, field)

    for group, pack in enumerate((prev_ref, low_ref, next_ref)):
        columns = jnp.transpose(pack[tail + 8 : tail + 16, :])[:32]
        for a in range(3):
            shift = base_z if a == 2 else 1.5
            far_centres[(group * 3 + a) * 32 : (group * 3 + a + 1) * 32, :] = jnp.broadcast_to(
                columns[:, a : a + 1] - shift, (32, 128)
            )
    far_moments = jnp.concatenate([pack[tail : tail + 8, :] for pack in (prev_ref, low_ref, next_ref)], axis=1)
    far_high = far_moments.astype(bf16).astype(f32)
    far_both = jnp.concatenate([far_high, far_moments - far_high], axis=0)
    far_lane = lax.broadcasted_iota(jnp.int32, (1, 384), 1)
    lane_x = far_lane & 3
    lane_y = (far_lane >> 2) & 3
    lane_z = 2 * (far_lane >> 7) - 2 + ((far_lane >> 4) & 1)

    def far_box(b, _):
        x, y, plane, place, slot = target_place(centres_s, b)
        local = facets_at(low_ref, high_ref, plane, place, origin)
        normal = normals_ref[:, pl.ds(pl.multiple_of(b * per_box, per_box), per_box)]
        coefficients = []
        for group in range(3):
            d = []
            for a in range(3):
                centre = far_centres[(group * 3 + a) * 32 : (group * 3 + a + 1) * 32, :]
                d.append(local[a : a + 1] - jnp.concatenate([centre, centre], axis=1))
            q = d[0] * d[0] + d[1] * d[1] + d[2] * d[2] + soften
            inverse = lax.rsqrt(q)
            inverse_2 = inverse * inverse
            inverse_3 = inverse_2 * inverse
            t = d[0] * normal[0:1] + d[1] * normal[1:2] + d[2] * normal[2:3]
            single = t * inverse_3
            coefficients.append(single)
            steep = 3.0 * single * inverse_2
            for a in range(3):
                coefficients.append(steep * d[a] - normal[a : a + 1] * inverse_3)
        whole = jnp.concatenate(coefficients, axis=0)
        upper = whole.astype(bf16)
        lower = (whole - upper.astype(f32)).astype(bf16)
        near = (jnp.abs(lane_x - x) <= 1) & (jnp.abs(lane_y - y) <= 1) & (jnp.abs(lane_z - plane) <= 1)
        picked = jnp.where(near, 0.0, far_both).astype(bf16)
        first = jnp.dot(picked, upper, preferred_element_type=f32)
        second = jnp.dot(picked, lower, preferred_element_type=f32)
        field[pl.ds(pl.multiple_of(slot * 8, 8), 8), :] += first[:8] + first[8:] + second[:8]
        return 0

    lax.fori_loop(0, boxes, far_box, 0)

    def image_box(b, carry):
        _, _, _, _, slot = target_place(centres_s, b)
        lanes = pl.ds(pl.multiple_of(b * per_box, per_box), per_box)
        live = live_row(counts_s, b)
        current = basis_ref[krylov - 1, :, lanes]
        part = field[pl.ds(pl.multiple_of(slot * 8, 8), 8), :]
        image = live * (current - 2.0 * wide_row(contrast_ref, b) * part)
        image_ref[:, lanes] = image
        sums = []
        for m in range(krylov + 1):
            product = image * (basis_ref[m, :, lanes] if m < krylov else image)
            sums.append(carry[m] + product[:, :128] + product[:, 128:])
        return tuple(sums)

    zeros = jnp.zeros((8, 128), f32)
    sums = lax.fori_loop(0, boxes, image_box, (zeros,) * (krylov + 1), unroll=2)
    pairs = [(m, n) for m in range(krylov) for n in range(m + 1)]

    def gram_box(b, carry):
        lanes = pl.ds(pl.multiple_of(b * per_box, per_box), per_box)
        live = live_row(counts_s, b)
        rows = [basis_ref[m, :, lanes] * live for m in range(krylov)]
        out = []
        for k, (m, n) in enumerate(pairs):
            product = rows[m] * rows[n]
            out.append(carry[k] + product[:, :128] + product[:, 128:])
        return tuple(out)

    gram = lax.fori_loop(0, boxes, gram_box, (zeros,) * len(pairs))
    lane = lax.broadcasted_iota(jnp.int32, (8, 128), 1)
    total = zeros
    for k, value in enumerate([*sums, *gram]):
        total = jnp.where(lane == k, jnp.sum(value, axis=1, keepdims=True), total)
    sums_ref[...] = jnp.broadcast_to(total[None], sums_ref.shape)


def two_sum(a, b):
    s = a + b
    c = s - a
    return s, (a - (s - c)) + (b - c)


def halves(a):
    c = a * 4097.0
    high = c - (c - a)
    return high, a - high


def two_product(a, b):
    p = a * b
    a_high, a_low = halves(a)
    b_high, b_low = halves(b)
    return p, ((a_high * b_high - p) + a_high * b_low + a_low * b_high) + a_low * b_low


def finish_kernel(total_facets, counts_s, tiles_ref, image_ref, basis_ref, next_ref, hessenberg_ref):
    boxes = counts_s.shape[0]
    krylov = basis_ref.shape[0]
    lane = lax.broadcasted_iota(jnp.int32, (8, 128), 1)

    def add_tile(i, carry):
        value, error = two_sum(carry[0], tiles_ref[i])
        return value, carry[1] + error

    sums, rest = lax.fori_loop(0, tiles_ref.shape[0], add_tile, (jnp.zeros((8, 128), f32),) * 2, unroll=8)
    exact = sums + rest
    projections = [exact[:, m : m + 1] / total_facets for m in range(krylov)]
    pairs = [(m, n) for m in range(krylov) for n in range(m + 1)]
    first = jnp.where(lane == krylov, 1.0, 0.0)
    second = jnp.where(lane <= krylov, 1.0, 0.0)
    for m in range(krylov):
        first = jnp.where(lane == m, -2.0 * projections[m], first)
    for k, (m, n) in enumerate(pairs):
        at = lane == krylov + 1 + k
        scale = 1.0 if m == n else 2.0
        first = jnp.where(at, scale * projections[m], first)
        second = jnp.where(at, projections[n], second)
    factor, factor_rest = two_product(first, second)
    value, value_rest = two_product(factor, sums)
    value_rest = value_rest + (factor * rest + factor_rest * sums)
    for shift in (64, 32, 16, 8, 4, 2, 1):
        other = pltpu.roll(value, shift, 1)
        other_rest = pltpu.roll(value_rest, shift, 1)
        value, error = two_sum(value, other)
        value_rest = (value_rest + other_rest) + error
    remaining = jnp.maximum(value + value_rest, 0.0)
    norm = jnp.sqrt(remaining / total_facets + epsilon)
    heads = jnp.where(lane == krylov, norm, 0.0)
    for m in range(krylov):
        heads = jnp.where(lane == m, projections[m], heads)
    hessenberg_ref[...] = heads[:, : krylov + 1]
    wide = [jnp.broadcast_to(p, (8, per_box)) for p in projections]
    scale = jnp.concatenate([1.0 / norm] * (per_box // 128), axis=1)

    def one_box(b, _):
        lanes = pl.ds(pl.multiple_of(b * per_box, per_box), per_box)
        live = live_row(counts_s, b)
        sent = wide[0] * basis_ref[0, :, lanes]
        for m in range(1, krylov):
            sent += wide[m] * basis_ref[m, :, lanes]
        next_ref[:, lanes] = (image_ref[:, lanes] - sent * live) * scale
        return 0

    lax.fori_loop(0, boxes, one_box, 0, unroll=4)


smem = pl.BlockSpec(memory_space=pltpu.SMEM)
vmem = pl.BlockSpec(memory_space=pltpu.VMEM)


def on_device(
    basis, facet_centres, normals, areas, contrast, facet_counts, box_centres, near_boxes, far_boxes
):
    krylov, rhs_local, facet_local = basis.shape
    boxes = facet_counts.shape[0]
    count = lax.axis_size("box")
    total_facets = count * facet_local
    areas = areas.reshape(-1, 128)
    contrast = contrast.reshape(-1, 128)
    pack = jax.ShapeDtypeStruct((pack_rows, 128), f32)
    low, high = pl.pallas_call(
        prep_kernel,
        grid=(1,),
        out_shape=(pack, pack),
        in_specs=[
            smem,
            smem,
            pl.BlockSpec((1, rhs_local, facet_local), lambda i: (krylov - 1, 0, 0)),
            vmem,
            vmem,
        ],
        out_specs=(vmem, vmem),
        scratch_shapes=[pltpu.VMEM((2 * pack_rows, 128), f32)],
        name="prepare",
    )(box_centres, facet_counts, basis, facet_centres, areas)
    below = lax.ppermute(high, "box", [(i, i + 1) for i in range(count - 1)])
    above = lax.ppermute(low, "box", [(i + 1, i) for i in range(count - 1)])
    slots = boxes * per_box
    left, right = pl.pallas_call(
        feature_kernel,
        out_shape=(
            jax.ShapeDtypeStruct((slots, depth), bf16),
            jax.ShapeDtypeStruct((boxes * depth, 2 * per_box), bf16),
        ),
        in_specs=[smem] + [vmem] * 3,
        out_specs=(vmem, vmem),
        compiler_params=pltpu.CompilerParams(vmem_limit_bytes=16 * 1024 * 1024),
        name="features",
    )(box_centres, low, high, normals)
    own_field = pl.pallas_call(
        own_kernel,
        out_shape=jax.ShapeDtypeStruct((boxes * 8, per_box), f32),
        in_specs=[vmem] * 4,
        out_specs=vmem,
        compiler_params=pltpu.CompilerParams(vmem_limit_bytes=24 * 1024 * 1024),
        name="own",
    )(low, high, left, right)
    image, tiles = pl.pallas_call(
        halo_kernel,
        out_shape=(
            jax.ShapeDtypeStruct((rhs_local, facet_local), f32),
            jax.ShapeDtypeStruct((count, 8, 128), f32),
        ),
        in_specs=[smem, smem] + [vmem] * 9,
        out_specs=(vmem, vmem),
        scratch_shapes=[
            pltpu.VMEM((slots, depth), bf16),
            pltpu.VMEM((boxes * 8, per_box), f32),
            pltpu.VMEM((9 * 32, 128), f32),
        ],
        compiler_params=pltpu.CompilerParams(vmem_limit_bytes=32 * 1024 * 1024),
        name="halo",
    )(box_centres, facet_counts, below, low, high, above, normals, contrast, basis, right, own_field)
    tiles = lax.all_to_all(tiles, "box", 0, 0, tiled=True)
    next_vector, hessenberg = pl.pallas_call(
        functools.partial(finish_kernel, total_facets),
        out_shape=(
            jax.ShapeDtypeStruct((rhs_local, facet_local), f32),
            jax.ShapeDtypeStruct((rhs_local, krylov + 1), f32),
        ),
        in_specs=[smem] + [vmem] * 3,
        out_specs=(vmem, vmem),
        compiler_params=pltpu.CompilerParams(vmem_limit_bytes=16 * 1024 * 1024),
        name="finish",
    )(facet_counts, tiles, image, basis)
    return next_vector, hessenberg.T


def solution(mesh):
    return jax.shard_map(
        on_device,
        mesh=mesh,
        in_specs=(
            P(None, "rhs", "box"),
            P(None, "box"),
            P(None, "box"),
            P("box"),
            P("box"),
            P("box"),
            P(None, "box"),
            P("box", None),
            P("box", None),
        ),
        out_specs=(P("rhs", "box"), P(None, "rhs")),
        check_vma=False,
    )
```

time: 148 us -> 127 us (0.86)
  blocking collectives: 0 us -> 16.3 us
  Pallas kernels: 118 us -> 102 us
  starting transfers between devices: 14.7 us -> 3.65 us
  waiting for transfers between devices: 10.8 us -> 0.05 us
    pallas_call x1 -> x3, Pallas kernels: 114 us -> 97.1 us  [the longest x1 53.9 us: on_device(): pl.pallas_call(own_kernel, out_shape=jax.ShapeDtypeStruct((boxes * 8, per...]
    all_to_all x0 -> x1, blocking collectives: none -> 16.3 us  [on_device(): tiles = lax.all_to_all(tiles, 'box', 0, 0, tiled=True)]
    ppermute x4 -> x0, starting transfers between devices: 11.1 us -> none  [the longest x3 6.78 us: summed(): other = lax.ppermute(jnp.stack([value, rest]), axis, pairs)]
    ppermute x4 -> x0, waiting for transfers between devices: 6.46 us -> none  [the longest x3 5.64 us: summed(): other = lax.ppermute(jnp.stack([value, rest]), axis, pairs)]
    ppermute x1, waiting for transfers between devices: 4.34 us -> 0.05 us  [on_device(): above = lax.ppermute(low, 'box', [(i + 1, i) for i in range(count - 1)])]
    unnamed x14 -> x22, local copies, waits for them, and re-layouts: 1.88 us -> 3.74 us
  transfers between devices with their start and end apart: 6 -> 2, of which waited for: 5 -> 0; matrix products, arithmetic and copies ran while one was open for 0% -> 0% of each run, Pallas kernels for 0% -> 45%
where the time goes in v2:
time: 127 us; the launch traced here: 126 us
  Pallas kernels  102 us (80%)
  blocking collectives  16.3 us (13%)
  local copies, waits for them, and re-layouts  3.74 us (3%)
  starting transfers between devices  3.65 us (3%)
    pallas_call x1, Pallas kernels, on_device(): pl.pallas_call(own_kernel, out_shape=jax.ShapeDtypeStruct((boxes * 8, per...  53.9 us
    pallas_call x1, Pallas kernels, on_device(): pl.pallas_call(halo_kernel, out_shape=(jax.ShapeDtypeStruct((rhs_local, f...  40 us
    all_to_all x1, blocking collectives, on_device(): tiles = lax.all_to_all(tiles, 'box', 0, 0, tiled=True)  16.3 us
    unnamed x22, local copies, waits for them, and re-layouts  3.74 us
    pallas_call x1, Pallas kernels, on_device(): pl.pallas_call(feature_kernel, out_shape=(jax.ShapeDtypeStruct((slots, de...  3.28 us
    pallas_call x1, Pallas kernels, on_device(): pl.pallas_call(prep_kernel, grid=(1,), out_shape=(pack, pack), in_specs=[...  2.68 us
  transfers between devices with their start and end apart: 2, of which 0 were waited for; matrix products, arithmetic and copies ran while one was open for 0% of the time, Pallas kernels for 45%

profile of v2, /device:TPU:0, one launch (start us, length us, event | category | flops | bytes accessed | tf_op | source)
XLA Modules:
  0.0 126.5 jit_solution(138486679977149098)
XLA Ops:
  0.6 0.0 copy-start.9
  0.6 0.0 copy-start.7
  0.7 2.7 %prepare.1 = (f32[400,128]{1,0:T(8,128)}, f32[400,128]{1,0:T(8,128)}) custom-call(f32[3,32]{1,0:T(4,128)} %centres_s.5, s32[32]{0:T(128)} %counts_s.5, f32[8,8,8192]{2,1,0:T(8,128)} %basis_ref.3, f32[3,8192]{1,0:T(4,128)} %facets_ref.1, f32[64,128]{1,0:T(8,128)} %bitcast.4), custom_call_target="tpu_custom_call" | custom-call | tf_op jit(solution)/shard_map/prepare/pallas_call | solution.py:372
  3.3 2.4 %collective-permute-start = (f32[400,128]{1,0:T(8,128)}, f32[400,128]{1,0:T(8,128)S(1)}, u32[]{:S(2)}, u32[]{:S(2)}) collective-permute-start(f32[400,128]{1,0:T(8,128)} %get-tuple-element.10.high_ref), channel_id=1, source_target_pairs={{0,2},{2,4},{4,6},{6,8},{8,10},{10,12},{12,14},{14,16},{16,18},{18... | collective-permute-start | bytes 614408 | tf_op jit(solution)/shard_map/ppermute | solution.py:387
  5.7 1.3 %collective-permute-start.1 = (f32[400,128]{1,0:T(8,128)}, f32[400,128]{1,0:T(8,128)S(1)}, u32[]{:S(2)}, u32[]{:S(2)}) collective-permute-start(f32[400,128]{1,0:T(8,128)} %get-tuple-element.11.low_ref), channel_id=1, source_target_pairs={{2,0},{4,2},{6,4},{8,6},{10,8},{12,10},{14,12},{16,14},{18,16},{20... | collective-permute-start | bytes 614408 | tf_op jit(solution)/shard_map/ppermute | solution.py:388
  7.0 0.0 copy-done.9
  7.0 0.0 copy-done.7
  7.0 0.0 copy-start.1
  7.0 0.9 copy-done.1
  8.0 0.0 copy-start.4
  8.0 0.9 copy-done.4
  8.9 3.3 %features.1 = (bf16[8192,128]{1,0:T(8,128)(2,1)S(1)}, bf16[4096,512]{1,0:T(8,128)(2,1)S(1)}) custom-call(f32[3,32]{1,0:T(4,128)S(1)} %copy-done.9, f32[400,128]{1,0:T(8,128)S(1)} %copy-done.1, f32[400,128]{1,0:T(8,128)S(1)} %copy-done.4, f32[3,8192]{1,0:T(4,128)S(1)} %copy-done.7), custom_call_target="tpu_custom_call" | custom-call | tf_op jit(solution)/shard_map/features/pallas_call | solution.py:390
  12.2 0.0 copy-start.2
  12.2 0.9 copy-done.2
  13.1 0.0 copy-start.5
  13.1 0.9 copy-done.5
  14.0 0.0 copy-start
  14.0 0.0 copy-start.3
  14.0 0.0 copy-start.6
  14.0 0.0 copy-start.8
  14.0 0.0 copy-start.10
  14.1 53.9 %own.1.own_field = f32[256,256]{1,0:T(8,128)S(1)} custom-call(f32[400,128]{1,0:T(8,128)S(1)} %copy-done.2, f32[400,128]{1,0:T(8,128)S(1)} %copy-done.5, bf16[8192,128]{1,0:T(8,128)(2,1)S(1)} %get-tuple-element.13.left, bf16[4096,512]{1,0:T(8,128)(2,1)S(1)} %get-tuple-element.12.right), custom_call_target="tpu_custom_call" | custom-call | tf_op jit(solution)/shard_map/own/pallas_call | solution.py:401
  67.9 0.0 collective-permute-done.prev_ref
  67.9 0.0 collective-permute-done.1.next_ref
  68.0 0.0 copy-done
  68.0 0.0 copy-done.3
  68.0 0.0 copy-done.6
  68.0 0.0 copy-done.8
  68.0 0.0 copy-done.10
  68.0 40.0 %halo.1 = (f32[8,8192]{1,0:T(8,128)S(1)}, f32[16,8,128]{2,1,0:T(8,128)S(1)}) custom-call(f32[3,32]{1,0:T(4,128)S(1)} %copy-done.9, s32[32]{0:T(128)S(1)} %copy-done.10, f32[400,128]{1,0:T(8,128)S(1)} %collective-permute-done.prev_ref, f32[400,128]{1,0:T(8,128)S(1)} %copy-done.3, f32[400,128]{1,0:T(8,128)S(1)} %copy-done.6, ...), custom_call_target="tpu_custom_call" | custom-call | tf_op jit(solution)/shard_map/halo/pallas_call | solution.py:409
  108.0 16.3 %all_to_all.5.tiles_ref = f32[16,8,128]{2,1,0:T(8,128)S(1)} all-to-all(f32[16,8,128]{2,1,0:T(8,128)S(1)} %get-tuple-element.14), channel_id=1, replica_groups=mesh['box'=16,'rhs'=2] {'box'}, dimensions={0} | all-to-all | bytes 131072 | tf_op jit(solution)/shard_map/all_to_all | solution.py:425
  124.3 2.1 %finish.1 = (f32[8,8192]{1,0:T(8,128)}, f32[8,9]{1,0:T(8,128)}) custom-call(s32[32]{0:T(128)S(1)} %copy-done.10, f32[16,8,128]{2,1,0:T(8,128)S(1)} %all_to_all.5.tiles_ref, f32[8,8192]{1,0:T(8,128)S(1)} %get-tuple-element.15.image_ref, f32[8,8,8192]{2,1,0:T(8,128)S(1)} %copy-done), custom_call_target="tpu_custom_call" | custom-call | tf_op jit(solution)/shard_map/finish/pallas_call | solution.py:426
Async XLA Ops:
  0.6 6.4 %copy-start.9 = (f32[3,32]{1,0:T(4,128)S(1)}, f32[3,32]{1,0:T(4,128)}, u32[]{:S(2)}) copy-start(f32[3,32]{1,0:T(4,128)} %centres_s.5) | copy-start | bytes 1156
  0.6 6.4 %copy-start.7 = (f32[3,8192]{1,0:T(4,128)S(1)}, f32[3,8192]{1,0:T(4,128)}, u32[]{:S(2)}) copy-start(f32[3,8192]{1,0:T(4,128)} %normals_ref.3) | copy-start | bytes 294916
  3.3 64.6 %collective-permute-start = (f32[400,128]{1,0:T(8,128)}, f32[400,128]{1,0:T(8,128)S(1)}, u32[]{:S(2)}, u32[]{:S(2)}) collective-permute-start(f32[400,128]{1,0:T(8,128)} %get-tuple-element.10.high_ref), channel_id=1, source_target_pairs={{0,2},{2,4},{4,6},{6,8},{8,10},{10,12},{12,14},{14,16},{16,18},{18... | collective-permute-start | bytes 614408 | tf_op jit(solution)/shard_map/ppermute | solution.py:387
  5.7 62.3 %collective-permute-start.1 = (f32[400,128]{1,0:T(8,128)}, f32[400,128]{1,0:T(8,128)S(1)}, u32[]{:S(2)}, u32[]{:S(2)}) collective-permute-start(f32[400,128]{1,0:T(8,128)} %get-tuple-element.11.low_ref), channel_id=1, source_target_pairs={{2,0},{4,2},{6,4},{8,6},{10,8},{12,10},{14,12},{16,14},{18,16},{20... | collective-permute-start | bytes 614408 | tf_op jit(solution)/shard_map/ppermute | solution.py:388
  7.0 0.9 copy-start.1
  8.0 0.9 copy-start.4
  12.2 0.9 copy-start.2
  13.1 0.9 copy-start.5
  14.0 54.0 %copy-start = (f32[8,8,8192]{2,1,0:T(8,128)S(1)}, f32[8,8,8192]{2,1,0:T(8,128)}, u32[]{:S(2)}) copy-start(f32[8,8,8192]{2,1,0:T(8,128)} %basis_ref.3) | copy-start | bytes 6291460
  14.0 54.0 %copy-start.3 = (f32[400,128]{1,0:T(8,128)S(1)}, f32[400,128]{1,0:T(8,128)}, u32[]{:S(2)}) copy-start(f32[400,128]{1,0:T(8,128)} %get-tuple-element.11.low_ref) | copy-start | bytes 614404
  14.0 54.0 %copy-start.6 = (f32[400,128]{1,0:T(8,128)S(1)}, f32[400,128]{1,0:T(8,128)}, u32[]{:S(2)}) copy-start(f32[400,128]{1,0:T(8,128)} %get-tuple-element.10.high_ref) | copy-start | bytes 614404
  14.0 54.0 %copy-start.8 = (f32[8192]{0:T(1024)S(1)}, f32[8192]{0:T(1024)}, u32[]{:S(2)}) copy-start(f32[8192]{0:T(1024)} %param.13) | copy-start | bytes 98308
  14.0 54.0 %copy-start.10 = (s32[32]{0:T(128)S(1)}, s32[32]{0:T(128)}, u32[]{:S(2)}) copy-start(s32[32]{0:T(128)} %counts_s.5) | copy-start | bytes 388

commit v3 on v2

--- a/solution.py
+++ b/solution.py
@@ -35,7 +35,7 @@
     return (slots < counts_s[b]).astype(f32)
 
 
-def prep_kernel(centres_s, counts_s, current_ref, facets_ref, areas_ref, low_ref, high_ref, packs):
+def prep_kernel(centres_s, counts_s, current_ref, facets_ref, areas_ref, low_ref, high_ref, own_low, own_high, packs):
     boxes = counts_s.shape[0]
     lane = lax.broadcasted_iota(jnp.int32, (8, 128), 1)
     row = lax.broadcasted_iota(jnp.int32, (8, 128), 0)
@@ -66,9 +66,8 @@
 
     zeros = jnp.zeros((8, 128), f32)
     moments, centres = lax.fori_loop(0, boxes, one_box, (zeros, zeros), unroll=4)
-    low_ref[:tail] = packs[:tail]
-    high_ref[:tail] = packs[pack_rows : pack_rows + tail]
-    for ref in (low_ref, high_ref):
+    for ref, first in ((low_ref, 0), (high_ref, pack_rows), (own_low, 0), (own_high, pack_rows)):
+        ref[:tail] = packs[first : first + tail]
         ref[tail : tail + 8] = moments
         ref[tail + 8 :] = centres
 
@@ -99,7 +98,7 @@
     return jnp.where(axis_row == 2, base_z, 1.5), base_z
 
 
-def store_source_features(pack, origin, left, first):
+def store_source_features(pack, origin, left, columns, first):
     row = lax.broadcasted_iota(jnp.int32, (8, per_box), 0)
 
     def one_box(place, _):
@@ -107,9 +106,11 @@
         square = jnp.sum(local * local, axis=0, keepdims=True)
         features = jnp.where(row == 3, square, jnp.where(row == 4, 1.0, local))
         high, middle, low = thirds(features)
-        columns = stacked_rows((high, high, high, middle, middle, low), per_box)
+        rows = stacked_rows((high, high, high, middle, middle, low, features), per_box)
         start = pl.multiple_of(first + place * per_box, per_box)
-        left[pl.ds(start, per_box), :] = jnp.transpose(columns).astype(bf16)
+        turned = jnp.transpose(rows)
+        left[pl.ds(start, per_box), :] = turned.astype(bf16)
+        columns[pl.ds(start, per_box), :] = turned
         return 0
 
     lax.fori_loop(0, plane_boxes, one_box, 0, unroll=2)
@@ -128,12 +129,12 @@
     return jnp.concatenate([tile[0:3], tile[3:6]], axis=1) - origin
 
 
-def feature_kernel(centres_s, low_ref, high_ref, normals_ref, left, right):
+def own_kernel(centres_s, low_ref, high_ref, normals_ref, right, planes, field, left, columns):
     boxes = centres_s.shape[1]
     row = lax.broadcasted_iota(jnp.int32, (8, per_box), 0)
     origin, _ = slab_origin(centres_s)
-    store_source_features(low_ref, origin, left, 0)
-    store_source_features(high_ref, origin, left, plane_boxes * per_box)
+    store_source_features(low_ref, origin, left, columns, 0)
+    store_source_features(high_ref, origin, left, columns, plane_boxes * per_box)
 
     def target(b, _):
         _, _, plane, place, slot = target_place(centres_s, b)
@@ -145,62 +146,71 @@
         square = jnp.sum(local_8 * local_8, axis=0, keepdims=True) + soften
         along = jnp.sum(local_8 * normal_8, axis=0, keepdims=True)
         distance = jnp.where(row == 3, 1.0, jnp.where(row == 4, square, -2.0 * local_8))
-        slope = jnp.where(row == 4, along, -normal_8)
-        both = jnp.concatenate([distance, slope], axis=1)
-        high, middle, low = thirds(both)
-        rows = stacked_rows((high, middle, low, high, middle, high), 2 * per_box)
+        high, middle, low = thirds(distance)
+        rows = stacked_rows((high, middle, low, high, middle, high), per_box)
         right[pl.ds(pl.multiple_of(slot * depth, depth), depth), :] = rows.astype(bf16)
+        planes[pl.ds(pl.multiple_of(slot * 8, 8), 8), :] = jnp.where(row == 3, along, normal_8)
         return 0
 
     lax.fori_loop(0, boxes, target, 0, unroll=2)
-
-
-def near_plane(pack, left, first, right, plane, field):
+    field[...] = jnp.zeros_like(field)
+    for plane in range(2):
+        near_plane(low_ref, left, columns, 0, right, planes, plane, field)
+        near_plane(high_ref, left, columns, plane_boxes * per_box, right, planes, plane, field)
+
+
+def near_plane(pack, left, columns, first, right, planes, plane, field):
     def near_rows(item, _):
         target_y = (item + 1) // 3
         source_y = target_y + lax.rem(item + 1, 3) - 1
         source_start = pl.multiple_of(first + source_y * 4 * per_box, per_box)
         charges = []
+        spread = []
         for x in range(4):
             start = pl.multiple_of((source_y * 4 + x) * box_rows, 8)
             charges.append(
                 jnp.concatenate([pack[pl.ds(start, 8), :], pack[pl.ds(start + 8, 8), :]], axis=1).astype(bf16)
             )
+            column = columns[pl.ds(source_start + x * per_box, per_box), :]
+            spread.append([jnp.broadcast_to(column[:, 48 + a : 49 + a], (per_box, 128)) for a in range(3)])
         for x in range(4):
             slot = plane * plane_boxes + target_y * 4 + x
             weights = right[pl.ds(pl.multiple_of(slot * depth, depth), depth), :]
+            side = planes[pl.ds(pl.multiple_of(slot * 8, 8), 8), :]
             low, high = max(x - 1, 0), min(x + 2, 4)
             facets = left[pl.ds(source_start + low * per_box, (high - low) * per_box), :]
-            geometry = jnp.dot(facets, weights, preferred_element_type=f32)
-            inverse = lax.rsqrt(geometry[:, :per_box])
-            kernel = ((geometry[:, per_box:] * inverse) * (inverse * inverse)).astype(bf16)
+            distance = jnp.dot(facets, weights, preferred_element_type=f32)
+            kernels = []
+            for source_x in range(low, high):
+                begin = (source_x - low) * per_box
+                halves_of = []
+                for lanes in (slice(0, 128), slice(128, 256)):
+                    inverse = lax.rsqrt(distance[begin : begin + per_box, lanes])
+                    slope = side[3:4, lanes] - spread[source_x][0] * side[0:1, lanes]
+                    slope = slope - spread[source_x][1] * side[1:2, lanes]
+                    slope = slope - spread[source_x][2] * side[2:3, lanes]
+                    halves_of.append(((slope * inverse) * (inverse * inverse)).astype(bf16))
+                kernels.append(jnp.concatenate(halves_of, axis=1))
             row_charges = jnp.concatenate(charges[low:high], axis=1)
-            total = jnp.dot(row_charges, kernel, preferred_element_type=f32)
+            total = jnp.dot(row_charges, jnp.concatenate(kernels, axis=0), preferred_element_type=f32)
             field[pl.ds(pl.multiple_of(slot * 8, 8), 8), :] += total
         return 0
 
     lax.fori_loop(0, 10, near_rows, 0)
 
 
-def own_kernel(low_ref, high_ref, left, right, field):
-    field[...] = jnp.zeros_like(field)
-    for plane in range(2):
-        near_plane(low_ref, left, 0, right, plane, field)
-        near_plane(high_ref, left, plane_boxes * per_box, right, plane, field)
-
-
 def halo_kernel(
     centres_s, counts_s, prev_ref, low_ref, high_ref, next_ref, normals_ref, contrast_ref, basis_ref, right,
-    own_field, image_ref, sums_ref, left, field, far_centres
+    planes, own_field, image_ref, sums_ref, left, columns, field, far_centres
 ):
     boxes = counts_s.shape[0]
     krylov = basis_ref.shape[0]
     origin, base_z = slab_origin(centres_s)
     field[...] = own_field[...]
-    store_source_features(prev_ref, origin, left, 0)
-    store_source_features(next_ref, origin, left, plane_boxes * per_box)
-    near_plane(prev_ref, left, 0, right, 0, field)
-    near_plane(next_ref, left, plane_boxes * per_box, right, 1, field)
+    store_source_features(prev_ref, origin, left, columns, 0)
+    store_source_features(next_ref, origin, left, columns, plane_boxes * per_box)
+    near_plane(prev_ref, left, columns, 0, right, planes, 0, field)
+    near_plane(next_ref, left, columns, plane_boxes * per_box, right, planes, 1, field)
 
     for group, pack in enumerate((prev_ref, low_ref, next_ref)):
         columns = jnp.transpose(pack[tail + 8 : tail + 16, :])[:32]
@@ -369,10 +379,10 @@
     areas = areas.reshape(-1, 128)
     contrast = contrast.reshape(-1, 128)
     pack = jax.ShapeDtypeStruct((pack_rows, 128), f32)
-    low, high = pl.pallas_call(
+    sent_low, sent_high, low, high = pl.pallas_call(
         prep_kernel,
         grid=(1,),
-        out_shape=(pack, pack),
+        out_shape=(pack,) * 4,
         in_specs=[
             smem,
             smem,
@@ -380,48 +390,43 @@
             vmem,
             vmem,
         ],
-        out_specs=(vmem, vmem),
+        out_specs=(vmem,) * 4,
         scratch_shapes=[pltpu.VMEM((2 * pack_rows, 128), f32)],
         name="prepare",
     )(box_centres, facet_counts, basis, facet_centres, areas)
-    below = lax.ppermute(high, "box", [(i, i + 1) for i in range(count - 1)])
-    above = lax.ppermute(low, "box", [(i + 1, i) for i in range(count - 1)])
+    below = lax.ppermute(sent_high, "box", [(i, i + 1) for i in range(count - 1)])
+    above = lax.ppermute(sent_low, "box", [(i + 1, i) for i in range(count - 1)])
     slots = boxes * per_box
-    left, right = pl.pallas_call(
-        feature_kernel,
+    right, planes, own_field = pl.pallas_call(
+        own_kernel,
         out_shape=(
-            jax.ShapeDtypeStruct((slots, depth), bf16),
-            jax.ShapeDtypeStruct((boxes * depth, 2 * per_box), bf16),
+            jax.ShapeDtypeStruct((boxes * depth, per_box), bf16),
+            jax.ShapeDtypeStruct((boxes * 8, per_box), f32),
+            jax.ShapeDtypeStruct((boxes * 8, per_box), f32),
         ),
         in_specs=[smem] + [vmem] * 3,
-        out_specs=(vmem, vmem),
-        compiler_params=pltpu.CompilerParams(vmem_limit_bytes=16 * 1024 * 1024),
-        name="features",
+        out_specs=(vmem,) * 3,
+        scratch_shapes=[pltpu.VMEM((slots, depth), bf16), pltpu.VMEM((slots, depth), f32)],
+        compiler_params=pltpu.CompilerParams(vmem_limit_bytes=32 * 1024 * 1024),
+        name="own",
     )(box_centres, low, high, normals)
-    own_field = pl.pallas_call(
-        own_kernel,
-        out_shape=jax.ShapeDtypeStruct((boxes * 8, per_box), f32),
-        in_specs=[vmem] * 4,
-        out_specs=vmem,
-        compiler_params=pltpu.CompilerParams(vmem_limit_bytes=24 * 1024 * 1024),
-        name="own",
-    )(low, high, left, right)
     image, tiles = pl.pallas_call(
         halo_kernel,
         out_shape=(
             jax.ShapeDtypeStruct((rhs_local, facet_local), f32),
             jax.ShapeDtypeStruct((count, 8, 128), f32),
         ),
-        in_specs=[smem, smem] + [vmem] * 9,
+        in_specs=[smem, smem] + [vmem] * 10,
         out_specs=(vmem, vmem),
         scratch_shapes=[
             pltpu.VMEM((slots, depth), bf16),
+            pltpu.VMEM((slots, depth), f32),
             pltpu.VMEM((boxes * 8, per_box), f32),
             pltpu.VMEM((9 * 32, 128), f32),
         ],
         compiler_params=pltpu.CompilerParams(vmem_limit_bytes=32 * 1024 * 1024),
         name="halo",
-    )(box_centres, facet_counts, below, low, high, above, normals, contrast, basis, right, own_field)
+    )(box_centres, facet_counts, below, low, high, above, normals, contrast, basis, right, planes, own_field)
     tiles = lax.all_to_all(tiles, "box", 0, 0, tiled=True)
     next_vector, hessenberg = pl.pallas_call(
         functools.partial(finish_kernel, total_facets),

time: 127 us -> 141 us (1.11)
  Pallas kernels: 102 us -> 117 us
    pallas_call x3 -> x2, Pallas kernels: 59.8 us -> 70 us  [the longest x1 67 us: on_device(): pl.pallas_call(own_kernel, out_shape=(jax.ShapeDtypeStruct((boxes * depth...]
    pallas_call x1, Pallas kernels: 40 us -> 45 us  [on_device(): pl.pallas_call(halo_kernel, out_shape=(jax.ShapeDtypeStruct((rhs_local, f...]
    unnamed x22 -> x16, local copies, waits for them, and re-layouts: 3.74 us -> 2.8 us
  transfers between devices with their start and end apart: 2 -> 2, of which waited for: 0 -> 0; matrix products, arithmetic and copies ran while one was open for 0% -> 0% of each run, Pallas kernels for 45% -> 48%
where the time goes in v3:
time: 141 us; the launch traced here: 140 us
  Pallas kernels  117 us (83%)
  blocking collectives  16 us (11%)
  starting transfers between devices  3.65 us (3%)
  local copies, waits for them, and re-layouts  2.8 us (2%)
    pallas_call x1, Pallas kernels, on_device(): pl.pallas_call(own_kernel, out_shape=(jax.ShapeDtypeStruct((boxes * depth...  67 us
    pallas_call x1, Pallas kernels, on_device(): pl.pallas_call(halo_kernel, out_shape=(jax.ShapeDtypeStruct((rhs_local, f...  45 us
    all_to_all x1, blocking collectives, on_device(): tiles = lax.all_to_all(tiles, 'box', 0, 0, tiled=True)  16 us
    pallas_call x1, Pallas kernels, on_device(): pl.pallas_call(prep_kernel, grid=(1,), out_shape=(pack,) * 4, in_specs=[s...  2.97 us
  transfers between devices with their start and end apart: 2, of which 0 were waited for; matrix products, arithmetic and copies ran while one was open for 0% of the time, Pallas kernels for 48%

profile of v3, /device:TPU:0, one launch (start us, length us, event | category | flops | bytes accessed | tf_op | source)
XLA Modules:
  0.0 140.3 jit_solution(11598137045271676016)
XLA Ops:
  0.6 0.0 copy-start.6
  0.6 0.0 copy-start.7
  0.7 0.0 copy-start
  0.7 0.0 copy-start.4
  0.7 0.0 copy-start.5
  0.7 3.0 %prepare.1 = (f32[400,128]{1,0:T(8,128)}, f32[400,128]{1,0:T(8,128)}, f32[400,128]{1,0:T(8,128)}, f32[400,128]{1,0:T(8,128)}) custom-call(f32[3,32]{1,0:T(4,128)} %centres_s.5, s32[32]{0:T(128)} %counts_s.5, f32[8,8,8192]{2,1,0:T(8,128)} %basis_ref.3, f32[3,8192]{1,0:T(4,128)} %facets_ref.1, f32[64,128]{1,0:T(8,128)} %bitcast.4), custom_call_target="tpu_custom_call" | custom-call | tf_op jit(solution)/shard_map/prepare/pallas_call | solution.py:382
  3.7 2.4 %collective-permute-start = (f32[400,128]{1,0:T(8,128)}, f32[400,128]{1,0:T(8,128)S(1)}, u32[]{:S(2)}, u32[]{:S(2)}) collective-permute-start(f32[400,128]{1,0:T(8,128)} %get-tuple-element.13), channel_id=1, source_target_pairs={{0,2},{2,4},{4,6},{6,8},{8,10},{10,12},{12,14},{14,16},{16,18},{18... | collective-permute-start | bytes 614408 | tf_op jit(solution)/shard_map/ppermute | solution.py:397
  6.0 1.3 collective-permute-start.1
  7.3 0.0 copy-done.6
  7.3 0.0 copy-done.4
  7.3 0.0 copy-start.1
  7.4 0.9 copy-done.1
  8.3 0.0 copy-start.3
  8.3 0.9 copy-done.3
  9.2 67.0 %own.1 = (bf16[4096,256]{1,0:T(8,128)(2,1)S(1)}, f32[256,256]{1,0:T(8,128)S(1)}, f32[256,256]{1,0:T(8,128)S(1)}) custom-call(f32[3,32]{1,0:T(4,128)S(1)} %copy-done.6, f32[400,128]{1,0:T(8,128)S(1)} %copy-done.1, f32[400,128]{1,0:T(8,128)S(1)} %copy-done.3, f32[3,8192]{1,0:T(4,128)S(1)} %copy-done.4), custom_call_target="tpu_custom_call" | custom-call | tf_op jit(solution)/shard_map/own/pallas_call | solution.py:400
  76.2 0.0 collective-permute-done.prev_ref
  76.2 0.0 collective-permute-done.1.next_ref
  76.3 0.0 copy-done.7
  76.3 0.0 copy-done
  76.3 0.0 copy-done.5
  76.3 0.0 copy-start.2
  76.3 0.9 copy-done.2
  77.2 45.0 %halo.1 = (f32[8,8192]{1,0:T(8,128)S(1)}, f32[16,8,128]{2,1,0:T(8,128)S(1)}) custom-call(f32[3,32]{1,0:T(4,128)S(1)} %copy-done.6, s32[32]{0:T(128)S(1)} %copy-done.7, f32[400,128]{1,0:T(8,128)S(1)} %collective-permute-done.prev_ref, f32[400,128]{1,0:T(8,128)S(1)} %copy-done.2, f32[400,128]{1,0:T(8,128)S(1)} %copy-done.3, ...), custom_call_target="tpu_custom_call" | custom-call | tf_op jit(solution)/shard_map/halo/pallas_call | solution.py:413
  122.2 16.0 %all_to_all.5.tiles_ref = f32[16,8,128]{2,1,0:T(8,128)S(1)} all-to-all(f32[16,8,128]{2,1,0:T(8,128)S(1)} %get-tuple-element.20), channel_id=1, replica_groups=mesh['box'=16,'rhs'=2] {'box'}, dimensions={0} | all-to-all | bytes 131072 | tf_op jit(solution)/shard_map/all_to_all | solution.py:430
  138.2 2.1 %finish.1 = (f32[8,8192]{1,0:T(8,128)}, f32[8,9]{1,0:T(8,128)}) custom-call(s32[32]{0:T(128)S(1)} %copy-done.7, f32[16,8,128]{2,1,0:T(8,128)S(1)} %all_to_all.5.tiles_ref, f32[8,8192]{1,0:T(8,128)S(1)} %get-tuple-element.21.image_ref, f32[8,8,8192]{2,1,0:T(8,128)S(1)} %copy-done), custom_call_target="tpu_custom_call" | custom-call | tf_op jit(solution)/shard_map/finish/pallas_call | solution.py:431
Async XLA Ops:
  0.6 6.7 %copy-start.6 = (f32[3,32]{1,0:T(4,128)S(1)}, f32[3,32]{1,0:T(4,128)}, u32[]{:S(2)}) copy-start(f32[3,32]{1,0:T(4,128)} %centres_s.5) | copy-start | bytes 1156
  0.6 75.6 %copy-start.7 = (s32[32]{0:T(128)S(1)}, s32[32]{0:T(128)}, u32[]{:S(2)}) copy-start(s32[32]{0:T(128)} %counts_s.5) | copy-start | bytes 388
  0.7 75.6 %copy-start = (f32[8,8,8192]{2,1,0:T(8,128)S(1)}, f32[8,8,8192]{2,1,0:T(8,128)}, u32[]{:S(2)}) copy-start(f32[8,8,8192]{2,1,0:T(8,128)} %basis_ref.3) | copy-start | bytes 6291460
  0.7 6.7 %copy-start.4 = (f32[3,8192]{1,0:T(4,128)S(1)}, f32[3,8192]{1,0:T(4,128)}, u32[]{:S(2)}) copy-start(f32[3,8192]{1,0:T(4,128)} %normals_ref.3) | copy-start | bytes 294916
  0.7 75.6 %copy-start.5 = (f32[8192]{0:T(1024)S(1)}, f32[8192]{0:T(1024)}, u32[]{:S(2)}) copy-start(f32[8192]{0:T(1024)} %param.13) | copy-start | bytes 98308
  3.7 72.5 %collective-permute-start = (f32[400,128]{1,0:T(8,128)}, f32[400,128]{1,0:T(8,128)S(1)}, u32[]{:S(2)}, u32[]{:S(2)}) collective-permute-start(f32[400,128]{1,0:T(8,128)} %get-tuple-element.13), channel_id=1, source_target_pairs={{0,2},{2,4},{4,6},{6,8},{8,10},{10,12},{12,14},{14,16},{16,18},{18... | collective-permute-start | bytes 614408 | tf_op jit(solution)/shard_map/ppermute | solution.py:397
  6.0 70.2 %collective-permute-start.1 = (f32[400,128]{1,0:T(8,128)}, f32[400,128]{1,0:T(8,128)S(1)}, u32[]{:S(2)}, u32[]{:S(2)}) collective-permute-start(f32[400,128]{1,0:T(8,128)} %get-tuple-element.16), channel_id=1, source_target_pairs={{2,0},{4,2},{6,4},{8,6},{10,8},{12,10},{14,12},{16,14},{18,16},{20... | collective-permute-start | bytes 614408 | tf_op jit(solution)/shard_map/ppermute | solution.py:398
  7.3 0.9 copy-start.1
  8.3 0.9 copy-start.3
  76.3 0.9 copy-start.2

commit v4 on v3

--- a/solution.py
+++ b/solution.py
@@ -98,7 +98,7 @@
     return jnp.where(axis_row == 2, base_z, 1.5), base_z
 
 
-def store_source_features(pack, origin, left, columns, first):
+def store_source_features(pack, origin, geometry, strengths, first):
     row = lax.broadcasted_iota(jnp.int32, (8, per_box), 0)
 
     def one_box(place, _):
@@ -106,11 +106,13 @@
         square = jnp.sum(local * local, axis=0, keepdims=True)
         features = jnp.where(row == 3, square, jnp.where(row == 4, 1.0, local))
         high, middle, low = thirds(features)
-        rows = stacked_rows((high, high, high, middle, middle, low, features), per_box)
-        start = pl.multiple_of(first + place * per_box, per_box)
-        turned = jnp.transpose(rows)
-        left[pl.ds(start, per_box), :] = turned.astype(bf16)
-        columns[pl.ds(start, per_box), :] = turned
+        rows = stacked_rows((high, high, high, middle, middle, low), per_box)
+        geometry[pl.ds(pl.multiple_of((first + place) * depth, depth), depth), :] = rows.astype(bf16)
+        start = pl.multiple_of(place * box_rows, 8)
+        charges = jnp.concatenate([pack[pl.ds(start, 8), :], pack[pl.ds(start + 8, 8), :]], axis=1)
+        products = jnp.concatenate([charges] + [charges * local[a : a + 1] for a in range(3)], axis=0)
+        rows = jnp.concatenate([*thirds(products), jnp.zeros((32, per_box), f32)], axis=0)
+        strengths[pl.ds(pl.multiple_of((first + place) * per_box, per_box), per_box), :] = jnp.transpose(rows).astype(bf16)
         return 0
 
     lax.fori_loop(0, plane_boxes, one_box, 0, unroll=2)
@@ -159,58 +161,83 @@
         near_plane(high_ref, left, columns, plane_boxes * per_box, right, planes, plane, field)
 
 
-def near_plane(pack, left, columns, first, right, planes, plane, field):
+def near_planes(sources, geometry, strengths, targets, total):
     def near_rows(item, _):
         target_y = (item + 1) // 3
         source_y = target_y + lax.rem(item + 1, 3) - 1
-        source_start = pl.multiple_of(first + source_y * 4 * per_box, per_box)
-        charges = []
-        spread = []
-        for x in range(4):
-            start = pl.multiple_of((source_y * 4 + x) * box_rows, 8)
-            charges.append(
-                jnp.concatenate([pack[pl.ds(start, 8), :], pack[pl.ds(start + 8, 8), :]], axis=1).astype(bf16)
-            )
-            column = columns[pl.ds(source_start + x * per_box, per_box), :]
-            spread.append([jnp.broadcast_to(column[:, 48 + a : 49 + a], (per_box, 128)) for a in range(3)])
-        for x in range(4):
-            slot = plane * plane_boxes + target_y * 4 + x
-            weights = right[pl.ds(pl.multiple_of(slot * depth, depth), depth), :]
-            side = planes[pl.ds(pl.multiple_of(slot * 8, 8), 8), :]
-            low, high = max(x - 1, 0), min(x + 2, 4)
-            facets = left[pl.ds(source_start + low * per_box, (high - low) * per_box), :]
-            distance = jnp.dot(facets, weights, preferred_element_type=f32)
-            kernels = []
-            for source_x in range(low, high):
-                begin = (source_x - low) * per_box
-                halves_of = []
-                for lanes in (slice(0, 128), slice(128, 256)):
-                    inverse = lax.rsqrt(distance[begin : begin + per_box, lanes])
-                    slope = side[3:4, lanes] - spread[source_x][0] * side[0:1, lanes]
-                    slope = slope - spread[source_x][1] * side[1:2, lanes]
-                    slope = slope - spread[source_x][2] * side[2:3, lanes]
-                    halves_of.append(((slope * inverse) * (inverse * inverse)).astype(bf16))
-                kernels.append(jnp.concatenate(halves_of, axis=1))
-            row_charges = jnp.concatenate(charges[low:high], axis=1)
-            total = jnp.dot(row_charges, jnp.concatenate(kernels, axis=0), preferred_element_type=f32)
-            field[pl.ds(pl.multiple_of(slot * 8, 8), 8), :] += total
+        for first, planes in sources:
+            for x in range(4):
+                box = first + source_y * 4 + x
+                low, high = max(x - 1, 0), min(x + 2, 4)
+                size = (high - low) * per_box
+                starts = [
+                    pl.multiple_of((plane * plane_boxes + target_y * 4 + low) * per_box, per_box) for plane in planes
+                ]
+                facets = jnp.concatenate([targets[pl.ds(start, size), :] for start in starts], axis=0)
+                weights = geometry[pl.ds(pl.multiple_of(box * depth, depth), depth), :]
+                inverse = lax.rsqrt(jnp.dot(facets, weights, preferred_element_type=f32))
+                cubed = (inverse * inverse * inverse).astype(bf16)
+                given = strengths[pl.ds(pl.multiple_of(box * per_box, per_box), per_box), :]
+                part = jnp.dot(cubed, given, preferred_element_type=f32)
+                for k, start in enumerate(starts):
+                    total[pl.ds(start, size), :] += part[k * size : (k + 1) * size]
         return 0
 
     lax.fori_loop(0, 10, near_rows, 0)
 
 
+def own_kernel(centres_s, low_ref, high_ref, normals_ref, targets, planes, total, geometry, strengths):
+    boxes = centres_s.shape[1]
+    row = lax.broadcasted_iota(jnp.int32, (8, per_box), 0)
+    origin, _ = slab_origin(centres_s)
+    store_source_features(low_ref, origin, geometry, strengths, 0)
+    store_source_features(high_ref, origin, geometry, strengths, plane_boxes)
+
+    def target(b, _):
+        _, _, plane, place, slot = target_place(centres_s, b)
+        local = facets_at(low_ref, high_ref, plane, place, origin)
+        normal = normals_ref[:, pl.ds(pl.multiple_of(b * per_box, per_box), per_box)]
+        five = jnp.zeros((5, per_box), f32)
+        local_8 = jnp.concatenate([local, five], axis=0)
+        normal_8 = jnp.concatenate([normal, five], axis=0)
+        square = jnp.sum(local_8 * local_8, axis=0, keepdims=True) + soften
+        along = jnp.sum(local_8 * normal_8, axis=0, keepdims=True)
+        distance = jnp.where(row == 3, 1.0, jnp.where(row == 4, square, -2.0 * local_8))
+        high, middle, low = thirds(distance)
+        rows = stacked_rows((high, middle, low, high, middle, high), per_box)
+        start = pl.multiple_of(slot * per_box, per_box)
+        targets[pl.ds(start, per_box), :] = jnp.transpose(rows).astype(bf16)
+        planes[pl.ds(pl.multiple_of(slot * 8, 8), 8), :] = jnp.where(row == 3, along, normal_8)
+        return 0
+
+    lax.fori_loop(0, boxes, target, 0, unroll=2)
+    total[...] = jnp.zeros_like(total)
+    near_planes(((0, (0, 1)), (plane_boxes, (0, 1))), geometry, strengths, targets, total)
+
+
 def halo_kernel(
-    centres_s, counts_s, prev_ref, low_ref, high_ref, next_ref, normals_ref, contrast_ref, basis_ref, right,
-    planes, own_field, image_ref, sums_ref, left, columns, field, far_centres
+    centres_s, counts_s, prev_ref, low_ref, high_ref, next_ref, normals_ref, contrast_ref, basis_ref, targets,
+    planes, own_total, image_ref, sums_ref, geometry, strengths, total, field, far_centres
 ):
     boxes = counts_s.shape[0]
     krylov = basis_ref.shape[0]
     origin, base_z = slab_origin(centres_s)
-    field[...] = own_field[...]
-    store_source_features(prev_ref, origin, left, columns, 0)
-    store_source_features(next_ref, origin, left, columns, plane_boxes * per_box)
-    near_plane(prev_ref, left, columns, 0, right, planes, 0, field)
-    near_plane(next_ref, left, columns, plane_boxes * per_box, right, planes, 1, field)
+    store_source_features(prev_ref, origin, geometry, strengths, 0)
+    store_source_features(next_ref, origin, geometry, strengths, plane_boxes)
+    total[...] = jnp.zeros_like(total)
+    near_planes(((0, (0,)), (plane_boxes, (1,))), geometry, strengths, targets, total)
+
+    def near_field(slot, _):
+        rows = pl.ds(pl.multiple_of(slot * per_box, per_box), per_box)
+        turned = jnp.transpose(total[rows, :] + own_total[rows, :])
+        sums = turned[:32] + (turned[32:64] + turned[64:96])
+        side = planes[pl.ds(pl.multiple_of(slot * 8, 8), 8), :]
+        value = side[3:4] * sums[:8] - side[0:1] * sums[8:16]
+        value = value - side[1:2] * sums[16:24] - side[2:3] * sums[24:32]
+        field[pl.ds(pl.multiple_of(slot * 8, 8), 8), :] = value
+        return 0
+
+    lax.fori_loop(0, boxes, near_field, 0, unroll=2)
 
     for group, pack in enumerate((prev_ref, low_ref, next_ref)):
         columns = jnp.transpose(pack[tail + 8 : tail + 16, :])[:32]
@@ -397,17 +424,17 @@
     below = lax.ppermute(sent_high, "box", [(i, i + 1) for i in range(count - 1)])
     above = lax.ppermute(sent_low, "box", [(i + 1, i) for i in range(count - 1)])
     slots = boxes * per_box
-    right, planes, own_field = pl.pallas_call(
+    targets, planes, own_total = pl.pallas_call(
         own_kernel,
         out_shape=(
-            jax.ShapeDtypeStruct((boxes * depth, per_box), bf16),
+            jax.ShapeDtypeStruct((slots, depth), bf16),
             jax.ShapeDtypeStruct((boxes * 8, per_box), f32),
-            jax.ShapeDtypeStruct((boxes * 8, per_box), f32),
+            jax.ShapeDtypeStruct((slots, 128), f32),
         ),
         in_specs=[smem] + [vmem] * 3,
         out_specs=(vmem,) * 3,
-        scratch_shapes=[pltpu.VMEM((slots, depth), bf16), pltpu.VMEM((slots, depth), f32)],
-        compiler_params=pltpu.CompilerParams(vmem_limit_bytes=32 * 1024 * 1024),
+        scratch_shapes=[pltpu.VMEM((boxes * depth, per_box), bf16), pltpu.VMEM((slots, 128), bf16)],
+        compiler_params=pltpu.CompilerParams(vmem_limit_bytes=24 * 1024 * 1024),
         name="own",
     )(box_centres, low, high, normals)
     image, tiles = pl.pallas_call(
@@ -419,14 +446,15 @@
         in_specs=[smem, smem] + [vmem] * 10,
         out_specs=(vmem, vmem),
         scratch_shapes=[
-            pltpu.VMEM((slots, depth), bf16),
-            pltpu.VMEM((slots, depth), f32),
+            pltpu.VMEM((boxes * depth, per_box), bf16),
+            pltpu.VMEM((slots, 128), bf16),
+            pltpu.VMEM((slots, 128), f32),
             pltpu.VMEM((boxes * 8, per_box), f32),
             pltpu.VMEM((9 * 32, 128), f32),
         ],
         compiler_params=pltpu.CompilerParams(vmem_limit_bytes=32 * 1024 * 1024),
         name="halo",
-    )(box_centres, facet_counts, below, low, high, above, normals, contrast, basis, right, planes, own_field)
+    )(box_centres, facet_counts, below, low, high, above, normals, contrast, basis, targets, planes, own_total)
     tiles = lax.all_to_all(tiles, "box", 0, 0, tiled=True)
     next_vector, hessenberg = pl.pallas_call(
         functools.partial(finish_kernel, total_facets),

time: 141 us -> 96.5 us (0.68)
  Pallas kernels: 117 us -> 72 us
    pallas_call x1, Pallas kernels: 67 us -> 35.1 us  [on_device(): pl.pallas_call(own_kernel, out_shape=(jax.ShapeDtypeStruct((slots, depth)...]
    pallas_call x1, Pallas kernels: 45 us -> 31.9 us  [on_device(): pl.pallas_call(halo_kernel, out_shape=(jax.ShapeDtypeStruct((rhs_local, f...]
    unnamed x16 -> x18, local copies, waits for them, and re-layouts: 2.8 us -> 3.73 us
  transfers between devices with their start and end apart: 2 -> 2, of which waited for: 0 -> 0; matrix products, arithmetic and copies ran while one was open for 0% -> 0% of each run, Pallas kernels for 48% -> 36%
where the time goes in v4:
time: 96.5 us; the launch traced here: 96.2 us
  Pallas kernels  72 us (75%)
  blocking collectives  16 us (17%)
  local copies, waits for them, and re-layouts  3.73 us (4%)
  starting transfers between devices  3.65 us (4%)
    pallas_call x1, Pallas kernels, on_device(): pl.pallas_call(own_kernel, out_shape=(jax.ShapeDtypeStruct((slots, depth)...  35.1 us
    pallas_call x1, Pallas kernels, on_device(): pl.pallas_call(halo_kernel, out_shape=(jax.ShapeDtypeStruct((rhs_local, f...  31.9 us
    all_to_all x1, blocking collectives, on_device(): tiles = lax.all_to_all(tiles, 'box', 0, 0, tiled=True)  16 us
    unnamed x18, local copies, waits for them, and re-layouts  3.73 us
    pallas_call x1, Pallas kernels, on_device(): pl.pallas_call(prep_kernel, grid=(1,), out_shape=(pack,) * 4, in_specs=[s...  2.97 us
    ppermute x1, starting transfers between devices, on_device(): lax.ppermute(sent_high, 'box', [(i, i + 1) for i in range(count - 1)])  2.36 us
    pallas_call x1, Pallas kernels, on_device(): pl.pallas_call(functools.partial(finish_kernel, total_facets), out_shape=...  2.14 us
  transfers between devices with their start and end apart: 2, of which 0 were waited for; matrix products, arithmetic and copies ran while one was open for 0% of the time, Pallas kernels for 36%

profile of v4, /device:TPU:0, one launch (start us, length us, event | category | flops | bytes accessed | tf_op | source)
XLA Modules:
  0.0 96.2 jit_solution(11494243211867544343)
XLA Ops:
  0.6 0.0 copy-start.7
  0.6 0.0 copy-start.8
  0.7 0.0 copy-start
  0.7 0.0 copy-start.5
  0.7 0.0 copy-start.6
  0.7 3.0 %prepare.1 = (f32[400,128]{1,0:T(8,128)}, f32[400,128]{1,0:T(8,128)}, f32[400,128]{1,0:T(8,128)}, f32[400,128]{1,0:T(8,128)}) custom-call(f32[3,32]{1,0:T(4,128)} %centres_s.5, s32[32]{0:T(128)} %counts_s.5, f32[8,8,8192]{2,1,0:T(8,128)} %basis_ref.3, f32[3,8192]{1,0:T(4,128)} %facets_ref.1, f32[64,128]{1,0:T(8,128)} %bitcast.4), custom_call_target="tpu_custom_call" | custom-call | tf_op jit(solution)/shard_map/prepare/pallas_call | solution.py:409
  3.7 2.4 %collective-permute-start = (f32[400,128]{1,0:T(8,128)}, f32[400,128]{1,0:T(8,128)S(1)}, u32[]{:S(2)}, u32[]{:S(2)}) collective-permute-start(f32[400,128]{1,0:T(8,128)} %get-tuple-element.13), channel_id=1, source_target_pairs={{0,2},{2,4},{4,6},{6,8},{8,10},{10,12},{12,14},{14,16},{16,18},{18... | collective-permute-start | bytes 614408 | tf_op jit(solution)/shard_map/ppermute | solution.py:424
  6.0 1.3 %collective-permute-start.1 = (f32[400,128]{1,0:T(8,128)}, f32[400,128]{1,0:T(8,128)S(1)}, u32[]{:S(2)}, u32[]{:S(2)}) collective-permute-start(f32[400,128]{1,0:T(8,128)} %get-tuple-element.16), channel_id=1, source_target_pairs={{2,0},{4,2},{6,4},{8,6},{10,8},{12,10},{14,12},{16,14},{18,16},{20... | collective-permute-start | bytes 614408 | tf_op jit(solution)/shard_map/ppermute | solution.py:425
  7.3 0.0 copy-done.7
  7.3 0.0 copy-done.5
  7.3 0.0 copy-start.1
  7.3 0.9 copy-done.1
  8.3 0.0 copy-start.3
  8.3 0.9 copy-done.3
  9.2 35.1 %own.1 = (bf16[8192,128]{1,0:T(8,128)(2,1)S(1)}, f32[256,256]{1,0:T(8,128)S(1)}, f32[8192,128]{1,0:T(8,128)S(1)}) custom-call(f32[3,32]{1,0:T(4,128)S(1)} %copy-done.7, f32[400,128]{1,0:T(8,128)S(1)} %copy-done.1, f32[400,128]{1,0:T(8,128)S(1)} %copy-done.3, f32[3,8192]{1,0:T(4,128)S(1)} %copy-done.5), custom_call_target="tpu_custom_call" | custom-call | tf_op jit(solution)/shard_map/own/pallas_call | solution.py:427
  44.3 0.0 collective-permute-done.prev_ref
  44.3 0.0 collective-permute-done.1.next_ref
  44.3 0.0 copy-done.8
  44.3 0.0 copy-done
  44.3 0.0 copy-done.6
  44.3 0.0 copy-start.2
  44.3 0.9 copy-done.2
  45.2 0.0 copy-start.4
  45.2 0.9 copy-done.4
  46.2 31.9 %halo.1 = (f32[8,8192]{1,0:T(8,128)S(1)}, f32[16,8,128]{2,1,0:T(8,128)S(1)}) custom-call(f32[3,32]{1,0:T(4,128)S(1)} %copy-done.7, s32[32]{0:T(128)S(1)} %copy-done.8, f32[400,128]{1,0:T(8,128)S(1)} %collective-permute-done.prev_ref, f32[400,128]{1,0:T(8,128)S(1)} %copy-done.2, f32[400,128]{1,0:T(8,128)S(1)} %copy-done.4, ...), custom_call_target="tpu_custom_call" | custom-call | tf_op jit(solution)/shard_map/halo/pallas_call | solution.py:440
  78.1 16.0 %all_to_all.5.tiles_ref = f32[16,8,128]{2,1,0:T(8,128)S(1)} all-to-all(f32[16,8,128]{2,1,0:T(8,128)S(1)} %get-tuple-element.20), channel_id=1, replica_groups=mesh['box'=16,'rhs'=2] {'box'}, dimensions={0} | all-to-all | bytes 131072 | tf_op jit(solution)/shard_map/all_to_all | solution.py:458
  94.0 2.1 %finish.1 = (f32[8,8192]{1,0:T(8,128)}, f32[8,9]{1,0:T(8,128)}) custom-call(s32[32]{0:T(128)S(1)} %copy-done.8, f32[16,8,128]{2,1,0:T(8,128)S(1)} %all_to_all.5.tiles_ref, f32[8,8192]{1,0:T(8,128)S(1)} %get-tuple-element.21.image_ref, f32[8,8,8192]{2,1,0:T(8,128)S(1)} %copy-done), custom_call_target="tpu_custom_call" | custom-call | tf_op jit(solution)/shard_map/finish/pallas_call | solution.py:459
Async XLA Ops:
  0.6 6.7 %copy-start.7 = (f32[3,32]{1,0:T(4,128)S(1)}, f32[3,32]{1,0:T(4,128)}, u32[]{:S(2)}) copy-start(f32[3,32]{1,0:T(4,128)} %centres_s.5) | copy-start | bytes 1156
  0.6 43.6 %copy-start.8 = (s32[32]{0:T(128)S(1)}, s32[32]{0:T(128)}, u32[]{:S(2)}) copy-start(s32[32]{0:T(128)} %counts_s.5) | copy-start | bytes 388
  0.7 43.6 %copy-start = (f32[8,8,8192]{2,1,0:T(8,128)S(1)}, f32[8,8,8192]{2,1,0:T(8,128)}, u32[]{:S(2)}) copy-start(f32[8,8,8192]{2,1,0:T(8,128)} %basis_ref.3) | copy-start | bytes 6291460
  0.7 6.7 %copy-start.5 = (f32[3,8192]{1,0:T(4,128)S(1)}, f32[3,8192]{1,0:T(4,128)}, u32[]{:S(2)}) copy-start(f32[3,8192]{1,0:T(4,128)} %normals_ref.3) | copy-start | bytes 294916
  0.7 43.6 %copy-start.6 = (f32[8192]{0:T(1024)S(1)}, f32[8192]{0:T(1024)}, u32[]{:S(2)}) copy-start(f32[8192]{0:T(1024)} %param.13) | copy-start | bytes 98308
  3.7 40.6 %collective-permute-start = (f32[400,128]{1,0:T(8,128)}, f32[400,128]{1,0:T(8,128)S(1)}, u32[]{:S(2)}, u32[]{:S(2)}) collective-permute-start(f32[400,128]{1,0:T(8,128)} %get-tuple-element.13), channel_id=1, source_target_pairs={{0,2},{2,4},{4,6},{6,8},{8,10},{10,12},{12,14},{14,16},{16,18},{18... | collective-permute-start | bytes 614408 | tf_op jit(solution)/shard_map/ppermute | solution.py:424
  6.0 38.3 %collective-permute-start.1 = (f32[400,128]{1,0:T(8,128)}, f32[400,128]{1,0:T(8,128)S(1)}, u32[]{:S(2)}, u32[]{:S(2)}) collective-permute-start(f32[400,128]{1,0:T(8,128)} %get-tuple-element.16), channel_id=1, source_target_pairs={{2,0},{4,2},{6,4},{8,6},{10,8},{12,10},{14,12},{16,14},{18,16},{20... | collective-permute-start | bytes 614408 | tf_op jit(solution)/shard_map/ppermute | solution.py:425
  7.3 0.9 copy-start.1
  8.3 0.9 copy-start.3
  44.3 0.9 copy-start.2
  45.2 0.9 copy-start.4

commit v5 on v4

--- a/solution.py
+++ b/solution.py
@@ -35,7 +35,7 @@
     return (slots < counts_s[b]).astype(f32)
 
 
-def prep_kernel(centres_s, counts_s, current_ref, facets_ref, areas_ref, low_ref, high_ref, own_low, own_high, packs):
+def prep_kernel(centres_s, counts_s, current_ref, facets_ref, areas_ref, low_ref, high_ref, packs):
     boxes = counts_s.shape[0]
     lane = lax.broadcasted_iota(jnp.int32, (8, 128), 1)
     row = lax.broadcasted_iota(jnp.int32, (8, 128), 0)
@@ -66,7 +66,7 @@
 
     zeros = jnp.zeros((8, 128), f32)
     moments, centres = lax.fori_loop(0, boxes, one_box, (zeros, zeros), unroll=4)
-    for ref, first in ((low_ref, 0), (high_ref, pack_rows), (own_low, 0), (own_high, pack_rows)):
+    for ref, first in ((low_ref, 0), (high_ref, pack_rows)):
         ref[:tail] = packs[first : first + tail]
         ref[tail : tail + 8] = moments
         ref[tail + 8 :] = centres
@@ -129,6 +129,69 @@
     start = pl.multiple_of(place * box_rows + 16, 8)
     tile = jnp.where(plane == 0, low_ref[pl.ds(start, 8), :], high_ref[pl.ds(start, 8), :])
     return jnp.concatenate([tile[0:3], tile[3:6]], axis=1) - origin
+
+
+def own_kernel(centres_s, low_ref, high_ref, normals_ref, right, planes, field, left, columns):
+    boxes = centres_s.shape[1]
+    row = lax.broadcasted_iota(jnp.int32, (8, per_box), 0)
+    origin, _ = slab_origin(centres_s)
+    store_source_features(low_ref, origin, left, columns, 0)
+    store_source_features(high_ref, origin, left, columns, plane_boxes * per_box)
+
+    def target(b, _):
+        _, _, plane, place, slot = target_place(centres_s, b)
+        local = facets_at(low_ref, high_ref, plane, place, origin)
+        normal = normals_ref[:, pl.ds(pl.multiple_of(b * per_box, per_box), per_box)]
+        five = jnp.zeros((5, per_box), f32)
+        local_8 = jnp.concatenate([local, five], axis=0)
+        normal_8 = jnp.concatenate([normal, five], axis=0)
+        square = jnp.sum(local_8 * local_8, axis=0, keepdims=True) + soften
+        along = jnp.sum(local_8 * normal_8, axis=0, keepdims=True)
+        distance = jnp.where(row == 3, 1.0, jnp.where(row == 4, square, -2.0 * local_8))
+        high, middle, low = thirds(distance)
+        rows = stacked_rows((high, middle, low, high, middle, high), per_box)
+        right[pl.ds(pl.multiple_of(slot * depth, depth), depth), :] = rows.astype(bf16)
+        planes[pl.ds(pl.multiple_of(slot * 8, 8), 8), :] = jnp.where(row == 3, along, normal_8)
+        return 0
+
+    lax.fori_loop(0, boxes, target, 0, unroll=2)
+    field[...] = jnp.zeros_like(field)
+    for plane in range(2):
+        near_plane(low_ref, left, columns, 0, right, planes, plane, field)
+        near_plane(high_ref, left, columns, plane_boxes * per_box, right, planes, plane, field)
+
+
+def near_planes(sources, geometry, strengths, targets, total):
+    def source_row(source_y, target_y, rows):
+        for first, planes in sources:
+            for x in range(4):
+                box = first + source_y * 4 + x
+                low, high = max(x - 1, 0), min(x + 2, 4)
+                size = (high - low) * per_box
+                starts = [
+                    pl.multiple_of((plane * plane_boxes + (target_y + k) * 4 + low) * per_box, per_box)
+                    for plane in planes
+                    for k in range(rows)
+                ]
+                facets = jnp.concatenate([targets[pl.ds(start, size), :] for start in starts], axis=0)
+                weights = geometry[pl.ds(pl.multiple_of(box * depth, depth), depth), :]
+                inverse = lax.rsqrt(jnp.dot(facets, weights, preferred_element_type=f32))
+                cubed = (inverse * inverse * inverse).astype(bf16)
+                given = strengths[pl.ds(pl.multiple_of(box * per_box, per_box), per_box), :]
+                part = jnp.dot(cubed, given, preferred_element_type=f32)
+                for k, start in enumerate(starts):
+                    total[pl.ds(start, size), :] += part[k * size : (k + 1) * size]
+
+    def outer(i, _):
+        source_row(3 * i, 2 * i, 2)
+        return 0
+
+    def inner(i, _):
+        source_row(i + 1, i, 3)
+        return 0
+
+    lax.fori_loop(0, 2, outer, 0)
+    lax.fori_loop(0, 2, inner, 0)
 
 
 def own_kernel(centres_s, low_ref, high_ref, normals_ref, right, planes, field, left, columns):
@@ -284,7 +347,7 @@
         field[pl.ds(pl.multiple_of(slot * 8, 8), 8), :] += first[:8] + first[8:] + second[:8]
         return 0
 
-    lax.fori_loop(0, boxes, far_box, 0)
+    lax.fori_loop(0, boxes, far_box, 0, unroll=2)
 
     def image_box(b, carry):
         _, _, _, _, slot = target_place(centres_s, b)
@@ -406,10 +469,10 @@
     areas = areas.reshape(-1, 128)
     contrast = contrast.reshape(-1, 128)
     pack = jax.ShapeDtypeStruct((pack_rows, 128), f32)
-    sent_low, sent_high, low, high = pl.pallas_call(
+    low, high = pl.pallas_call(
         prep_kernel,
         grid=(1,),
-        out_shape=(pack,) * 4,
+        out_shape=(pack, pack),
         in_specs=[
             smem,
             smem,
@@ -417,12 +480,13 @@
             vmem,
             vmem,
         ],
-        out_specs=(vmem,) * 4,
+        out_specs=(vmem, vmem),
         scratch_shapes=[pltpu.VMEM((2 * pack_rows, 128), f32)],
+        compiler_params=pltpu.CompilerParams(vmem_limit_bytes=8 * 1024 * 1024),
         name="prepare",
     )(box_centres, facet_counts, basis, facet_centres, areas)
-    below = lax.ppermute(sent_high, "box", [(i, i + 1) for i in range(count - 1)])
-    above = lax.ppermute(sent_low, "box", [(i + 1, i) for i in range(count - 1)])
+    below = lax.ppermute(high, "box", [(i, i + 1) for i in range(count - 1)])
+    above = lax.ppermute(low, "box", [(i + 1, i) for i in range(count - 1)])
     slots = boxes * per_box
     targets, planes, own_total = pl.pallas_call(
         own_kernel,

time: 96.5 us -> 93.9 us (0.973)
  Pallas kernels: 72 us -> 68.5 us
    pallas_call x1, Pallas kernels: 31.9 us -> 29.9 us  [on_device(): pl.pallas_call(halo_kernel, out_shape=(jax.ShapeDtypeStruct((rhs_local, f...]
    pallas_call x1, Pallas kernels: 2.97 us -> 1.44 us  [on_device(): pl.pallas_call(prep_kernel, grid=(1,), out_shape=(pack, pack), in_specs=[...]
    unnamed x18 -> x20, local copies, waits for them, and re-layouts: 3.73 us -> 4.61 us
  transfers between devices with their start and end apart: 2 -> 2, of which waited for: 0 -> 0; matrix products, arithmetic and copies ran while one was open for 0% -> 0% of each run, Pallas kernels for 36% -> 37%
where the time goes in v5:
time: 93.9 us; the launch traced here: 93.5 us
  Pallas kernels  68.5 us (73%)
  blocking collectives  16 us (17%)
  local copies, waits for them, and re-layouts  4.61 us (5%)
  starting transfers between devices  3.66 us (4%)
    pallas_call x1, Pallas kernels, on_device(): pl.pallas_call(own_kernel, out_shape=(jax.ShapeDtypeStruct((slots, depth)...  35.1 us
    pallas_call x1, Pallas kernels, on_device(): pl.pallas_call(halo_kernel, out_shape=(jax.ShapeDtypeStruct((rhs_local, f...  29.9 us
    all_to_all x1, blocking collectives, on_device(): tiles = lax.all_to_all(tiles, 'box', 0, 0, tiled=True)  16 us
    unnamed x20, local copies, waits for them, and re-layouts  4.61 us
    ppermute x1, starting transfers between devices, on_device(): below = lax.ppermute(high, 'box', [(i, i + 1) for i in range(count - 1)])  2.37 us
    pallas_call x1, Pallas kernels, on_device(): pl.pallas_call(functools.partial(finish_kernel, total_facets), out_shape=...  2.14 us
  transfers between devices with their start and end apart: 2, of which 0 were waited for; matrix products, arithmetic and copies ran while one was open for 0% of the time, Pallas kernels for 37%

profile of v5, /device:TPU:0, one launch (start us, length us, event | category | flops | bytes accessed | tf_op | source)
XLA Modules:
  0.0 93.5 jit_solution(8434507203580410894)
XLA Ops:
  0.6 0.0 copy-start.9
  0.6 0.0 copy-start
  0.7 1.6 %copy-done = f32[8,8,8192]{2,1,0:T(8,128)S(1)} copy-done((f32[8,8,8192]{2,1,0:T(8,128)S(1)}, f32[8,8,8192]{2,1,0:T(8,128)}, u32[]{:S(2)}) %copy-start) | copy-done | bytes 2097176
  2.2 0.0 copy-start.3
  2.2 0.9 copy-done.3
  3.1 0.0 copy-start.4
  3.1 0.8 copy-done.4
  3.9 0.0 copy-start.6
  3.9 0.7 copy-done.6
  4.6 0.0 copy-start.8
  4.6 0.7 copy-done.8
  5.2 0.0 copy-start.2
  5.2 0.0 copy-start.7
  5.2 0.0 copy-start.1
  5.2 0.0 copy-start.5
  5.3 1.4 %prepare.1 = (f32[400,128]{1,0:T(8,128)S(1)}, f32[400,128]{1,0:T(8,128)S(1)}) custom-call(f32[3,32]{1,0:T(4,128)S(1)} %copy-done.6, s32[32]{0:T(128)S(1)} %copy-done.8, f32[8,8,8192]{2,1,0:T(8,128)S(1)} %copy-done, f32[3,8192]{1,0:T(4,128)S(1)} %copy-done.3, f32[64,128]{1,0:T(8,128)S(1)} %bitcast.3), custom_call_target="tpu_custom_call" | custom-call | tf_op jit(solution)/shard_map/prepare/pallas_call | solution.py:472
  6.7 2.4 %collective-permute-start = (f32[400,128]{1,0:T(8,128)S(1)}, f32[400,128]{1,0:T(8,128)S(1)}, u32[]{:S(2)}, u32[]{:S(2)}) collective-permute-start(f32[400,128]{1,0:T(8,128)S(1)} %get-tuple-element.11.high_ref), channel_id=1, source_target_pairs={{0,2},{2,4},{4,6},{6,8},{8,10},{10,12},{12,14},{14,16},{16,18},{18... | collective-permute-start | bytes 614408 | tf_op jit(solution)/shard_map/ppermute | solution.py:488
  9.1 1.3 %collective-permute-start.1 = (f32[400,128]{1,0:T(8,128)S(1)}, f32[400,128]{1,0:T(8,128)S(1)}, u32[]{:S(2)}, u32[]{:S(2)}) collective-permute-start(f32[400,128]{1,0:T(8,128)S(1)} %get-tuple-element.12.low_ref), channel_id=1, source_target_pairs={{2,0},{4,2},{6,4},{8,6},{10,8},{12,10},{14,12},{16,14},{18,16},{20... | collective-permute-start | bytes 614408 | tf_op jit(solution)/shard_map/ppermute | solution.py:489
  10.4 0.0 copy-done.2
  10.4 0.0 copy-done.7
  10.4 35.1 %own.1 = (bf16[8192,128]{1,0:T(8,128)(2,1)S(1)}, f32[256,256]{1,0:T(8,128)S(1)}, f32[8192,128]{1,0:T(8,128)S(1)}) custom-call(f32[3,32]{1,0:T(4,128)S(1)} %copy-done.7, f32[400,128]{1,0:T(8,128)S(1)} %get-tuple-element.12.low_ref, f32[400,128]{1,0:T(8,128)S(1)} %get-tuple-element.11.high_ref, f32[3,8192]{1,0:T(4,128)S(1)} %copy-done.2), custom_call_target="tpu_custom_call" | custom-call | tf_op jit(solution)/shard_map/own/pallas_call | solution.py:491
  45.5 0.0 collective-permute-done.prev_ref
  45.5 0.0 collective-permute-done.1.next_ref
  45.5 0.0 copy-done.9
  45.5 0.0 copy-done.1
  45.5 0.0 copy-done.5
  45.5 29.9 %halo.1 = (f32[8,8192]{1,0:T(8,128)S(1)}, f32[16,8,128]{2,1,0:T(8,128)S(1)}) custom-call(f32[3,32]{1,0:T(4,128)S(1)} %copy-done.7, s32[32]{0:T(128)S(1)} %copy-done.9, f32[400,128]{1,0:T(8,128)S(1)} %collective-permute-done.prev_ref, f32[400,128]{1,0:T(8,128)S(1)} %get-tuple-element.12.low_ref, f32[400,128]{1,0:T(8,128)S(1)} %get-tuple-element.11.high_ref, ...), custom_call_target="tpu_custom_call" | custom-call | tf_op jit(solution)/shard_map/halo/pallas_call | solution.py:504
  75.4 16.0 %all_to_all.5.tiles_ref = f32[16,8,128]{2,1,0:T(8,128)S(1)} all-to-all(f32[16,8,128]{2,1,0:T(8,128)S(1)} %get-tuple-element.16), channel_id=1, replica_groups=mesh['box'=16,'rhs'=2] {'box'}, dimensions={0} | all-to-all | bytes 131072 | tf_op jit(solution)/shard_map/all_to_all | solution.py:522
  91.4 2.1 %finish.1 = (f32[8,8192]{1,0:T(8,128)}, f32[8,9]{1,0:T(8,128)}) custom-call(s32[32]{0:T(128)S(1)} %copy-done.9, f32[16,8,128]{2,1,0:T(8,128)S(1)} %all_to_all.5.tiles_ref, f32[8,8192]{1,0:T(8,128)S(1)} %get-tuple-element.17.image_ref, f32[8,8,8192]{2,1,0:T(8,128)S(1)} %copy-done.1), custom_call_target="tpu_custom_call" | custom-call | tf_op jit(solution)/shard_map/finish/pallas_call | solution.py:523
Async XLA Ops:
  0.6 44.8 %copy-start.9 = (s32[32]{0:T(128)S(1)}, s32[32]{0:T(128)}, u32[]{:S(2)}) copy-start(s32[32]{0:T(128)} %counts_s.5) | copy-start | bytes 388
  0.6 1.6 %copy-start = (f32[8,8,8192]{2,1,0:T(8,128)S(1)}, f32[8,8,8192]{2,1,0:T(8,128)}, u32[]{:S(2)}) copy-start(f32[8,8,8192]{2,1,0:T(8,128)} %basis_ref.3) | copy-start | bytes 6291460
  2.2 0.9 copy-start.3
  3.1 0.8 copy-start.4
  3.9 0.7 copy-start.6
  4.6 0.7 copy-start.8
  5.2 5.1 %copy-start.2 = (f32[3,8192]{1,0:T(4,128)S(1)}, f32[3,8192]{1,0:T(4,128)}, u32[]{:S(2)}) copy-start(f32[3,8192]{1,0:T(4,128)} %normals_ref.3) | copy-start | bytes 294916
  5.2 5.1 %copy-start.7 = (f32[3,32]{1,0:T(4,128)S(1)}, f32[3,32]{1,0:T(4,128)}, u32[]{:S(2)}) copy-start(f32[3,32]{1,0:T(4,128)} %centres_s.5) | copy-start | bytes 1156
  5.2 40.2 %copy-start.1 = (f32[8,8,8192]{2,1,0:T(8,128)S(1)}, f32[8,8,8192]{2,1,0:T(8,128)}, u32[]{:S(2)}) copy-start(f32[8,8,8192]{2,1,0:T(8,128)} %basis_ref.3) | copy-start | bytes 6291460
  5.2 40.2 %copy-start.5 = (f32[8192]{0:T(1024)S(1)}, f32[8192]{0:T(1024)}, u32[]{:S(2)}) copy-start(f32[8192]{0:T(1024)} %param.13) | copy-start | bytes 98308
  6.7 38.8 %collective-permute-start = (f32[400,128]{1,0:T(8,128)S(1)}, f32[400,128]{1,0:T(8,128)S(1)}, u32[]{:S(2)}, u32[]{:S(2)}) collective-permute-start(f32[400,128]{1,0:T(8,128)S(1)} %get-tuple-element.11.high_ref), channel_id=1, source_target_pairs={{0,2},{2,4},{4,6},{6,8},{8,10},{10,12},{12,14},{14,16},{16,18},{18... | collective-permute-start | bytes 614408 | tf_op jit(solution)/shard_map/ppermute | solution.py:488
  9.1 36.4 %collective-permute-start.1 = (f32[400,128]{1,0:T(8,128)S(1)}, f32[400,128]{1,0:T(8,128)S(1)}, u32[]{:S(2)}, u32[]{:S(2)}) collective-permute-start(f32[400,128]{1,0:T(8,128)S(1)} %get-tuple-element.12.low_ref), channel_id=1, source_target_pairs={{2,0},{4,2},{6,4},{8,6},{10,8},{12,10},{14,12},{16,14},{18,16},{20... | collective-permute-start | bytes 614408 | tf_op jit(solution)/shard_map/ppermute | solution.py:489

commit v6 on v5

--- a/solution.py
+++ b/solution.py
@@ -35,8 +35,23 @@
     return (slots < counts_s[b]).astype(f32)
 
 
-def prep_kernel(centres_s, counts_s, current_ref, facets_ref, areas_ref, low_ref, high_ref, packs):
+def prep_kernel(
+    centres_h, counts_h, basis_h, facets_h, areas_h, low_ref, high_ref,
+    packs, centres_s, counts_s, current_ref, facets_ref, areas_ref, arrived
+):
     boxes = counts_s.shape[0]
+    moves = [
+        (basis_h.at[basis_h.shape[0] - 1], current_ref),
+        (facets_h, facets_ref),
+        (areas_h, areas_ref),
+        (centres_h, centres_s),
+        (counts_h, counts_s),
+    ]
+    copies = [pltpu.make_async_copy(a, b, arrived.at[k]) for k, (a, b) in enumerate(moves)]
+    for copy in copies:
+        copy.start()
+    for copy in copies:
+        copy.wait()
     lane = lax.broadcasted_iota(jnp.int32, (8, 128), 1)
     row = lax.broadcasted_iota(jnp.int32, (8, 128), 0)
 
@@ -49,7 +64,7 @@
         lanes = pl.ds(pl.multiple_of(b * per_box, per_box), per_box)
         facets = facets_ref[:, lanes]
         live = live_row(counts_s, b)
-        weighted = current_ref[0, :, lanes] * (wide_row(areas_ref, b) * live / per_box)
+        weighted = current_ref[:, lanes] * (wide_row(areas_ref, b) * live / per_box)
         charges = weighted.astype(bf16).astype(f32)
         start = pl.multiple_of(plane * pack_rows + place * box_rows, 8)
         packs[pl.ds(start, 8), :] = charges[:, :128]
@@ -163,24 +178,29 @@
 
 def near_planes(sources, geometry, strengths, targets, total):
     def source_row(source_y, target_y, rows):
+        runs = []
         for first, planes in sources:
             for x in range(4):
-                box = first + source_y * 4 + x
-                low, high = max(x - 1, 0), min(x + 2, 4)
-                size = (high - low) * per_box
-                starts = [
-                    pl.multiple_of((plane * plane_boxes + (target_y + k) * 4 + low) * per_box, per_box)
-                    for plane in planes
-                    for k in range(rows)
-                ]
-                facets = jnp.concatenate([targets[pl.ds(start, size), :] for start in starts], axis=0)
-                weights = geometry[pl.ds(pl.multiple_of(box * depth, depth), depth), :]
-                inverse = lax.rsqrt(jnp.dot(facets, weights, preferred_element_type=f32))
-                cubed = (inverse * inverse * inverse).astype(bf16)
-                given = strengths[pl.ds(pl.multiple_of(box * per_box, per_box), per_box), :]
-                part = jnp.dot(cubed, given, preferred_element_type=f32)
-                for k, start in enumerate(starts):
-                    total[pl.ds(start, size), :] += part[k * size : (k + 1) * size]
+                for plane in planes:
+                    for k in range(rows):
+                        low, high = max(x - 1, 0), min(x + 2, 4)
+                        start = (plane * plane_boxes + (target_y + k) * 4 + low) * per_box
+                        rows_of = pl.ds(pl.multiple_of(start, per_box), (high - low) * per_box)
+                        runs.append((first + source_y * 4 + x, rows_of))
+
+        def distances(box, rows_of):
+            weights = geometry[pl.ds(pl.multiple_of(box * depth, depth), depth), :]
+            return jnp.dot(targets[rows_of, :], weights, preferred_element_type=f32)
+
+        ahead = distances(*runs[0])
+        for i, (box, rows_of) in enumerate(runs):
+            here = ahead
+            if i + 1 < len(runs):
+                ahead = distances(*runs[i + 1])
+            inverse = lax.rsqrt(here)
+            cubed = (inverse * inverse * inverse).astype(bf16)
+            given = strengths[pl.ds(pl.multiple_of(box * per_box, per_box), per_box), :]
+            total[rows_of, :] += jnp.dot(cubed, given, preferred_element_type=f32)
 
     def outer(i, _):
         source_row(3 * i, 2 * i, 2)
@@ -471,17 +491,18 @@
     pack = jax.ShapeDtypeStruct((pack_rows, 128), f32)
     low, high = pl.pallas_call(
         prep_kernel,
-        grid=(1,),
         out_shape=(pack, pack),
-        in_specs=[
-            smem,
-            smem,
-            pl.BlockSpec((1, rhs_local, facet_local), lambda i: (krylov - 1, 0, 0)),
-            vmem,
-            vmem,
+        in_specs=[pl.BlockSpec(memory_space=pltpu.HBM)] * 5,
+        out_specs=(vmem, vmem),
+        scratch_shapes=[
+            pltpu.VMEM((2 * pack_rows, 128), f32),
+            pltpu.SMEM(box_centres.shape, f32),
+            pltpu.SMEM(facet_counts.shape, jnp.int32),
+            pltpu.VMEM((rhs_local, facet_local), f32),
+            pltpu.VMEM(facet_centres.shape, f32),
+            pltpu.VMEM(areas.shape, f32),
+            pltpu.SemaphoreType.DMA((5,)),
         ],
-        out_specs=(vmem, vmem),
-        scratch_shapes=[pltpu.VMEM((2 * pack_rows, 128), f32)],
         compiler_params=pltpu.CompilerParams(vmem_limit_bytes=8 * 1024 * 1024),
         name="prepare",
     )(box_centres, facet_counts, basis, facet_centres, areas)

time: 93.9 us -> 94.1 us (level)
  no operation moved by 1% of the time
where the time goes in v6:
time: 94.1 us; the launch traced here: 93.8 us
  Pallas kernels  68.8 us (73%)
  blocking collectives  16 us (17%)
  local copies, waits for them, and re-layouts  4.61 us (5%)
  starting transfers between devices  3.66 us (4%)
    pallas_call x1, Pallas kernels, on_device(): pl.pallas_call(own_kernel, out_shape=(jax.ShapeDtypeStruct((slots, depth)...  35.1 us
    pallas_call x1, Pallas kernels, on_device(): pl.pallas_call(halo_kernel, out_shape=(jax.ShapeDtypeStruct((rhs_local, f...  29.9 us
    all_to_all x1, blocking collectives, on_device(): tiles = lax.all_to_all(tiles, 'box', 0, 0, tiled=True)  16 us
    unnamed x20, local copies, waits for them, and re-layouts  4.61 us
    ppermute x1, starting transfers between devices, on_device(): below = lax.ppermute(high, 'box', [(i, i + 1) for i in range(count - 1)])  2.37 us
    pallas_call x1, Pallas kernels, on_device(): pl.pallas_call(functools.partial(finish_kernel, total_facets), out_shape=...  2.14 us
  transfers between devices with their start and end apart: 2, of which 0 were waited for; matrix products, arithmetic and copies ran while one was open for 0% of the time, Pallas kernels for 37%

profile of v6, /device:TPU:0, one launch (start us, length us, event | category | flops | bytes accessed | tf_op | source)
XLA Modules:
  0.0 93.8 jit_solution(16418507618530781506)
XLA Ops:
  0.6 0.0 copy-start.9
  0.6 0.0 copy-start
  0.7 1.6 %copy-done = f32[8,8,8192]{2,1,0:T(8,128)S(1)} copy-done((f32[8,8,8192]{2,1,0:T(8,128)S(1)}, f32[8,8,8192]{2,1,0:T(8,128)}, u32[]{:S(2)}) %copy-start) | copy-done | bytes 2097176
  2.2 0.0 copy-start.3
  2.2 0.9 copy-done.3
  3.1 0.0 copy-start.4
  3.1 0.8 copy-done.4
  3.9 0.0 copy-start.6
  3.9 0.7 copy-done.6
  4.6 0.0 copy-start.8
  4.6 0.7 copy-done.8
  5.2 0.0 copy-start.2
  5.2 0.0 copy-start.7
  5.2 0.0 copy-start.1
  5.2 0.0 copy-start.5
  5.3 1.7 %prepare.1 = (f32[400,128]{1,0:T(8,128)S(1)}, f32[400,128]{1,0:T(8,128)S(1)}) custom-call(f32[3,32]{1,0:T(4,128)S(1)} %copy-done.6, s32[32]{0:T(128)S(1)} %copy-done.8, f32[8,8,8192]{2,1,0:T(8,128)S(1)} %copy-done, f32[3,8192]{1,0:T(4,128)S(1)} %copy-done.3, f32[64,128]{1,0:T(8,128)S(1)} %bitcast.3), custom_call_target="tpu_custom_call" | custom-call | tf_op jit(solution)/shard_map/prepare/pallas_call | solution.py:492
  7.0 2.4 %collective-permute-start = (f32[400,128]{1,0:T(8,128)S(1)}, f32[400,128]{1,0:T(8,128)S(1)}, u32[]{:S(2)}, u32[]{:S(2)}) collective-permute-start(f32[400,128]{1,0:T(8,128)S(1)} %get-tuple-element.11.high_ref), channel_id=1, source_target_pairs={{0,2},{2,4},{4,6},{6,8},{8,10},{10,12},{12,14},{14,16},{16,18},{18... | collective-permute-start | bytes 614408 | tf_op jit(solution)/shard_map/ppermute | solution.py:509
  9.4 1.3 %collective-permute-start.1 = (f32[400,128]{1,0:T(8,128)S(1)}, f32[400,128]{1,0:T(8,128)S(1)}, u32[]{:S(2)}, u32[]{:S(2)}) collective-permute-start(f32[400,128]{1,0:T(8,128)S(1)} %get-tuple-element.12.low_ref), channel_id=1, source_target_pairs={{2,0},{4,2},{6,4},{8,6},{10,8},{12,10},{14,12},{16,14},{18,16},{20... | collective-permute-start | bytes 614408 | tf_op jit(solution)/shard_map/ppermute | solution.py:510
  10.7 0.0 copy-done.2
  10.7 0.0 copy-done.7
  10.7 35.1 %own.1 = (bf16[8192,128]{1,0:T(8,128)(2,1)S(1)}, f32[256,256]{1,0:T(8,128)S(1)}, f32[8192,128]{1,0:T(8,128)S(1)}) custom-call(f32[3,32]{1,0:T(4,128)S(1)} %copy-done.7, f32[400,128]{1,0:T(8,128)S(1)} %get-tuple-element.12.low_ref, f32[400,128]{1,0:T(8,128)S(1)} %get-tuple-element.11.high_ref, f32[3,8192]{1,0:T(4,128)S(1)} %copy-done.2), custom_call_target="tpu_custom_call" | custom-call | tf_op jit(solution)/shard_map/own/pallas_call | solution.py:512
  45.7 0.0 collective-permute-done.prev_ref
  45.7 0.0 collective-permute-done.1.next_ref
  45.8 0.0 copy-done.9
  45.8 0.0 copy-done.1
  45.8 0.0 copy-done.5
  45.8 29.9 %halo.1 = (f32[8,8192]{1,0:T(8,128)S(1)}, f32[16,8,128]{2,1,0:T(8,128)S(1)}) custom-call(f32[3,32]{1,0:T(4,128)S(1)} %copy-done.7, s32[32]{0:T(128)S(1)} %copy-done.9, f32[400,128]{1,0:T(8,128)S(1)} %collective-permute-done.prev_ref, f32[400,128]{1,0:T(8,128)S(1)} %get-tuple-element.12.low_ref, f32[400,128]{1,0:T(8,128)S(1)} %get-tuple-element.11.high_ref, ...), custom_call_target="tpu_custom_call" | custom-call | tf_op jit(solution)/shard_map/halo/pallas_call | solution.py:525
  75.7 16.0 %all_to_all.5.tiles_ref = f32[16,8,128]{2,1,0:T(8,128)S(1)} all-to-all(f32[16,8,128]{2,1,0:T(8,128)S(1)} %get-tuple-element.16), channel_id=1, replica_groups=mesh['box'=16,'rhs'=2] {'box'}, dimensions={0} | all-to-all | bytes 131072 | tf_op jit(solution)/shard_map/all_to_all | solution.py:543
  91.7 2.1 %finish.1 = (f32[8,8192]{1,0:T(8,128)}, f32[8,9]{1,0:T(8,128)}) custom-call(s32[32]{0:T(128)S(1)} %copy-done.9, f32[16,8,128]{2,1,0:T(8,128)S(1)} %all_to_all.5.tiles_ref, f32[8,8192]{1,0:T(8,128)S(1)} %get-tuple-element.17.image_ref, f32[8,8,8192]{2,1,0:T(8,128)S(1)} %copy-done.1), custom_call_target="tpu_custom_call" | custom-call | tf_op jit(solution)/shard_map/finish/pallas_call | solution.py:544
Async XLA Ops:
  0.6 45.1 %copy-start.9 = (s32[32]{0:T(128)S(1)}, s32[32]{0:T(128)}, u32[]{:S(2)}) copy-start(s32[32]{0:T(128)} %counts_s.3) | copy-start | bytes 388
  0.6 1.6 %copy-start = (f32[8,8,8192]{2,1,0:T(8,128)S(1)}, f32[8,8,8192]{2,1,0:T(8,128)}, u32[]{:S(2)}) copy-start(f32[8,8,8192]{2,1,0:T(8,128)} %basis_ref.3) | copy-start | bytes 6291460
  2.2 0.9 copy-start.3
  3.1 0.8 copy-start.4
  3.9 0.7 copy-start.6
  4.6 0.7 copy-start.8
  5.2 5.4 %copy-start.2 = (f32[3,8192]{1,0:T(4,128)S(1)}, f32[3,8192]{1,0:T(4,128)}, u32[]{:S(2)}) copy-start(f32[3,8192]{1,0:T(4,128)} %normals_ref.3) | copy-start | bytes 294916
  5.2 5.4 %copy-start.7 = (f32[3,32]{1,0:T(4,128)S(1)}, f32[3,32]{1,0:T(4,128)}, u32[]{:S(2)}) copy-start(f32[3,32]{1,0:T(4,128)} %centres_s.3) | copy-start | bytes 1156
  5.2 40.5 %copy-start.1 = (f32[8,8,8192]{2,1,0:T(8,128)S(1)}, f32[8,8,8192]{2,1,0:T(8,128)}, u32[]{:S(2)}) copy-start(f32[8,8,8192]{2,1,0:T(8,128)} %basis_ref.3) | copy-start | bytes 6291460
  5.2 40.5 %copy-start.5 = (f32[8192]{0:T(1024)S(1)}, f32[8192]{0:T(1024)}, u32[]{:S(2)}) copy-start(f32[8192]{0:T(1024)} %param.13) | copy-start | bytes 98308
  7.0 38.8 %collective-permute-start = (f32[400,128]{1,0:T(8,128)S(1)}, f32[400,128]{1,0:T(8,128)S(1)}, u32[]{:S(2)}, u32[]{:S(2)}) collective-permute-start(f32[400,128]{1,0:T(8,128)S(1)} %get-tuple-element.11.high_ref), channel_id=1, source_target_pairs={{0,2},{2,4},{4,6},{6,8},{8,10},{10,12},{12,14},{14,16},{16,18},{18... | collective-permute-start | bytes 614408 | tf_op jit(solution)/shard_map/ppermute | solution.py:509
  9.4 36.4 %collective-permute-start.1 = (f32[400,128]{1,0:T(8,128)S(1)}, f32[400,128]{1,0:T(8,128)S(1)}, u32[]{:S(2)}, u32[]{:S(2)}) collective-permute-start(f32[400,128]{1,0:T(8,128)S(1)} %get-tuple-element.12.low_ref), channel_id=1, source_target_pairs={{2,0},{4,2},{6,4},{8,6},{10,8},{12,10},{14,12},{16,14},{18,16},{20... | collective-permute-start | bytes 614408 | tf_op jit(solution)/shard_map/ppermute | solution.py:510

commit v7 on v6

--- a/solution.py
+++ b/solution.py
@@ -36,7 +36,7 @@
 
 
 def prep_kernel(
-    centres_h, counts_h, basis_h, facets_h, areas_h, low_ref, high_ref,
+    centres_h, counts_h, basis_h, facets_h, areas_h, low_ref, high_ref, tail_ref,
     packs, centres_s, counts_s, current_ref, facets_ref, areas_ref, arrived
 ):
     boxes = counts_s.shape[0]
@@ -85,6 +85,8 @@
         ref[:tail] = packs[first : first + tail]
         ref[tail : tail + 8] = moments
         ref[tail + 8 :] = centres
+    tail_ref[:8] = moments
+    tail_ref[8:] = centres
 
 
 def thirds(x):
@@ -113,21 +115,23 @@
     return jnp.where(axis_row == 2, base_z, 1.5), base_z
 
 
-def store_source_features(pack, origin, geometry, strengths, first):
+def store_source_features(local, charges, box, geometry, strengths):
     row = lax.broadcasted_iota(jnp.int32, (8, per_box), 0)
-
+    square = jnp.sum(local * local, axis=0, keepdims=True)
+    features = jnp.where(row == 3, square, jnp.where(row == 4, 1.0, local))
+    high, middle, low = thirds(features)
+    rows = stacked_rows((high, high, high, middle, middle, low), per_box)
+    geometry[pl.ds(pl.multiple_of(box * depth, depth), depth), :] = rows.astype(bf16)
+    products = jnp.concatenate([charges] + [charges * local[a : a + 1] for a in range(3)], axis=0)
+    rows = jnp.concatenate([*thirds(products), jnp.zeros((32, per_box), f32)], axis=0)
+    strengths[pl.ds(pl.multiple_of(box * per_box, per_box), per_box), :] = jnp.transpose(rows).astype(bf16)
+
+
+def store_pack_features(pack, origin, geometry, strengths, first):
     def one_box(place, _):
-        local = local_facets(pack, place, origin)
-        square = jnp.sum(local * local, axis=0, keepdims=True)
-        features = jnp.where(row == 3, square, jnp.where(row == 4, 1.0, local))
-        high, middle, low = thirds(features)
-        rows = stacked_rows((high, high, high, middle, middle, low), per_box)
-        geometry[pl.ds(pl.multiple_of((first + place) * depth, depth), depth), :] = rows.astype(bf16)
         start = pl.multiple_of(place * box_rows, 8)
         charges = jnp.concatenate([pack[pl.ds(start, 8), :], pack[pl.ds(start + 8, 8), :]], axis=1)
-        products = jnp.concatenate([charges] + [charges * local[a : a + 1] for a in range(3)], axis=0)
-        rows = jnp.concatenate([*thirds(products), jnp.zeros((32, per_box), f32)], axis=0)
-        strengths[pl.ds(pl.multiple_of((first + place) * per_box, per_box), per_box), :] = jnp.transpose(rows).astype(bf16)
+        store_source_features(local_facets(pack, place, origin), charges, first + place, geometry, strengths)
         return 0
 
     lax.fori_loop(0, plane_boxes, one_box, 0, unroll=2)
@@ -140,53 +144,17 @@
     return x, y, plane, place, plane * plane_boxes + place
 
 
-def facets_at(low_ref, high_ref, plane, place, origin):
-    start = pl.multiple_of(place * box_rows + 16, 8)
-    tile = jnp.where(plane == 0, low_ref[pl.ds(start, 8), :], high_ref[pl.ds(start, 8), :])
-    return jnp.concatenate([tile[0:3], tile[3:6]], axis=1) - origin
-
-
-def own_kernel(centres_s, low_ref, high_ref, normals_ref, right, planes, field, left, columns):
-    boxes = centres_s.shape[1]
-    row = lax.broadcasted_iota(jnp.int32, (8, per_box), 0)
-    origin, _ = slab_origin(centres_s)
-    store_source_features(low_ref, origin, left, columns, 0)
-    store_source_features(high_ref, origin, left, columns, plane_boxes * per_box)
-
-    def target(b, _):
-        _, _, plane, place, slot = target_place(centres_s, b)
-        local = facets_at(low_ref, high_ref, plane, place, origin)
-        normal = normals_ref[:, pl.ds(pl.multiple_of(b * per_box, per_box), per_box)]
-        five = jnp.zeros((5, per_box), f32)
-        local_8 = jnp.concatenate([local, five], axis=0)
-        normal_8 = jnp.concatenate([normal, five], axis=0)
-        square = jnp.sum(local_8 * local_8, axis=0, keepdims=True) + soften
-        along = jnp.sum(local_8 * normal_8, axis=0, keepdims=True)
-        distance = jnp.where(row == 3, 1.0, jnp.where(row == 4, square, -2.0 * local_8))
-        high, middle, low = thirds(distance)
-        rows = stacked_rows((high, middle, low, high, middle, high), per_box)
-        right[pl.ds(pl.multiple_of(slot * depth, depth), depth), :] = rows.astype(bf16)
-        planes[pl.ds(pl.multiple_of(slot * 8, 8), 8), :] = jnp.where(row == 3, along, normal_8)
-        return 0
-
-    lax.fori_loop(0, boxes, target, 0, unroll=2)
-    field[...] = jnp.zeros_like(field)
-    for plane in range(2):
-        near_plane(low_ref, left, columns, 0, right, planes, plane, field)
-        near_plane(high_ref, left, columns, plane_boxes * per_box, right, planes, plane, field)
-
-
 def near_planes(sources, geometry, strengths, targets, total):
-    def source_row(source_y, target_y, rows):
+    def near_rows(item, _):
+        target_y = (item + 1) // 3
+        source_y = target_y + lax.rem(item + 1, 3) - 1
         runs = []
         for first, planes in sources:
             for x in range(4):
                 for plane in planes:
-                    for k in range(rows):
-                        low, high = max(x - 1, 0), min(x + 2, 4)
-                        start = (plane * plane_boxes + (target_y + k) * 4 + low) * per_box
-                        rows_of = pl.ds(pl.multiple_of(start, per_box), (high - low) * per_box)
-                        runs.append((first + source_y * 4 + x, rows_of))
+                    for near_x in range(max(x - 1, 0), min(x + 2, 4)):
+                        start = (plane * plane_boxes + target_y * 4 + near_x) * per_box
+                        runs.append((first + source_y * 4 + x, pl.ds(pl.multiple_of(start, per_box), per_box)))
 
         def distances(box, rows_of):
             weights = geometry[pl.ds(pl.multiple_of(box * depth, depth), depth), :]
@@ -202,87 +170,29 @@
             given = strengths[pl.ds(pl.multiple_of(box * per_box, per_box), per_box), :]
             total[rows_of, :] += jnp.dot(cubed, given, preferred_element_type=f32)
 
-    def outer(i, _):
-        source_row(3 * i, 2 * i, 2)
-        return 0
-
-    def inner(i, _):
-        source_row(i + 1, i, 3)
-        return 0
-
-    lax.fori_loop(0, 2, outer, 0)
-    lax.fori_loop(0, 2, inner, 0)
-
-
-def own_kernel(centres_s, low_ref, high_ref, normals_ref, right, planes, field, left, columns):
-    boxes = centres_s.shape[1]
+        return 0
+
+    lax.fori_loop(0, 10, near_rows, 0)
+
+
+def own_kernel(
+    centres_s, counts_s, basis_ref, facets_ref, areas_ref, normals_ref, targets, planes, total, geometry, strengths
+):
+    boxes = counts_s.shape[0]
+    krylov = basis_ref.shape[0]
     row = lax.broadcasted_iota(jnp.int32, (8, per_box), 0)
     origin, _ = slab_origin(centres_s)
-    store_source_features(low_ref, origin, left, columns, 0)
-    store_source_features(high_ref, origin, left, columns, plane_boxes * per_box)
 
     def target(b, _):
-        _, _, plane, place, slot = target_place(centres_s, b)
-        local = facets_at(low_ref, high_ref, plane, place, origin)
-        normal = normals_ref[:, pl.ds(pl.multiple_of(b * per_box, per_box), per_box)]
+        _, _, _, _, slot = target_place(centres_s, b)
+        lanes = pl.ds(pl.multiple_of(b * per_box, per_box), per_box)
+        normal = normals_ref[:, lanes]
         five = jnp.zeros((5, per_box), f32)
-        local_8 = jnp.concatenate([local, five], axis=0)
+        local_8 = jnp.concatenate([facets_ref[:, lanes] - origin, five], axis=0)
         normal_8 = jnp.concatenate([normal, five], axis=0)
-        square = jnp.sum(local_8 * local_8, axis=0, keepdims=True) + soften
-        along = jnp.sum(local_8 * normal_8, axis=0, keepdims=True)
-        distance = jnp.where(row == 3, 1.0, jnp.where(row == 4, square, -2.0 * local_8))
-        high, middle, low = thirds(distance)
-        rows = stacked_rows((high, middle, low, high, middle, high), per_box)
-        right[pl.ds(pl.multiple_of(slot * depth, depth), depth), :] = rows.astype(bf16)
-        planes[pl.ds(pl.multiple_of(slot * 8, 8), 8), :] = jnp.where(row == 3, along, normal_8)
-        return 0
-
-    lax.fori_loop(0, boxes, target, 0, unroll=2)
-    field[...] = jnp.zeros_like(field)
-    for plane in range(2):
-        near_plane(low_ref, left, columns, 0, right, planes, plane, field)
-        near_plane(high_ref, left, columns, plane_boxes * per_box, right, planes, plane, field)
-
-
-def near_planes(sources, geometry, strengths, targets, total):
-    def near_rows(item, _):
-        target_y = (item + 1) // 3
-        source_y = target_y + lax.rem(item + 1, 3) - 1
-        for first, planes in sources:
-            for x in range(4):
-                box = first + source_y * 4 + x
-                low, high = max(x - 1, 0), min(x + 2, 4)
-                size = (high - low) * per_box
-                starts = [
-                    pl.multiple_of((plane * plane_boxes + target_y * 4 + low) * per_box, per_box) for plane in planes
-                ]
-                facets = jnp.concatenate([targets[pl.ds(start, size), :] for start in starts], axis=0)
-                weights = geometry[pl.ds(pl.multiple_of(box * depth, depth), depth), :]
-                inverse = lax.rsqrt(jnp.dot(facets, weights, preferred_element_type=f32))
-                cubed = (inverse * inverse * inverse).astype(bf16)
-                given = strengths[pl.ds(pl.multiple_of(box * per_box, per_box), per_box), :]
-                part = jnp.dot(cubed, given, preferred_element_type=f32)
-                for k, start in enumerate(starts):
-                    total[pl.ds(start, size), :] += part[k * size : (k + 1) * size]
-        return 0
-
-    lax.fori_loop(0, 10, near_rows, 0)
-
-
-def own_kernel(centres_s, low_ref, high_ref, normals_ref, targets, planes, total, geometry, strengths):
-    boxes = centres_s.shape[1]
-    row = lax.broadcasted_iota(jnp.int32, (8, per_box), 0)
-    origin, _ = slab_origin(centres_s)
-    store_source_features(low_ref, origin, geometry, strengths, 0)
-    store_source_features(high_ref, origin, geometry, strengths, plane_boxes)
-
-    def target(b, _):
-        _, _, plane, place, slot = target_place(centres_s, b)
-        local = facets_at(low_ref, high_ref, plane, place, origin)
-        normal = normals_ref[:, pl.ds(pl.multiple_of(b * per_box, per_box), per_box)]
-        five = jnp.zeros((5, per_box), f32)
-        local_8 = jnp.concatenate([local, five], axis=0)
-        normal_8 = jnp.concatenate([normal, five], axis=0)
+        live = live_row(counts_s, b)
+        weighted = basis_ref[krylov - 1, :, lanes] * (wide_row(areas_ref, b) * live / per_box)
+        store_source_features(local_8, weighted.astype(bf16).astype(f32), slot, geometry, strengths)
         square = jnp.sum(local_8 * local_8, axis=0, keepdims=True) + soften
         along = jnp.sum(local_8 * normal_8, axis=0, keepdims=True)
         distance = jnp.where(row == 3, 1.0, jnp.where(row == 4, square, -2.0 * local_8))
@@ -299,14 +209,14 @@
 
 
 def halo_kernel(
-    centres_s, counts_s, prev_ref, low_ref, high_ref, next_ref, normals_ref, contrast_ref, basis_ref, targets,
+    centres_s, counts_s, prev_ref, tail_ref, next_ref, facets_ref, normals_ref, contrast_ref, basis_ref, targets,
     planes, own_total, image_ref, sums_ref, geometry, strengths, total, field, far_centres
 ):
     boxes = counts_s.shape[0]
     krylov = basis_ref.shape[0]
     origin, base_z = slab_origin(centres_s)
-    store_source_features(prev_ref, origin, geometry, strengths, 0)
-    store_source_features(next_ref, origin, geometry, strengths, plane_boxes)
+    store_pack_features(prev_ref, origin, geometry, strengths, 0)
+    store_pack_features(next_ref, origin, geometry, strengths, plane_boxes)
     total[...] = jnp.zeros_like(total)
     near_planes(((0, (0,)), (plane_boxes, (1,))), geometry, strengths, targets, total)
 
@@ -322,14 +232,15 @@
 
     lax.fori_loop(0, boxes, near_field, 0, unroll=2)
 
-    for group, pack in enumerate((prev_ref, low_ref, next_ref)):
-        columns = jnp.transpose(pack[tail + 8 : tail + 16, :])[:32]
+    tails = (prev_ref[tail:, :], tail_ref[...], next_ref[tail:, :])
+    for group in range(3):
+        columns = jnp.transpose(tails[group][8:])[:32]
         for a in range(3):
             shift = base_z if a == 2 else 1.5
             far_centres[(group * 3 + a) * 32 : (group * 3 + a + 1) * 32, :] = jnp.broadcast_to(
                 columns[:, a : a + 1] - shift, (32, 128)
             )
-    far_moments = jnp.concatenate([pack[tail : tail + 8, :] for pack in (prev_ref, low_ref, next_ref)], axis=1)
+    far_moments = jnp.concatenate([part[:8] for part in tails], axis=1)
     far_high = far_moments.astype(bf16).astype(f32)
     far_both = jnp.concatenate([far_high, far_moments - far_high], axis=0)
     far_lane = lax.broadcasted_iota(jnp.int32, (1, 384), 1)
@@ -338,9 +249,10 @@
     lane_z = 2 * (far_lane >> 7) - 2 + ((far_lane >> 4) & 1)
 
     def far_box(b, _):
-        x, y, plane, place, slot = target_place(centres_s, b)
-        local = facets_at(low_ref, high_ref, plane, place, origin)
-        normal = normals_ref[:, pl.ds(pl.multiple_of(b * per_box, per_box), per_box)]
+        x, y, plane, _, slot = target_place(centres_s, b)
+        lanes = pl.ds(pl.multiple_of(b * per_box, per_box), per_box)
+        local = facets_ref[:, lanes] - origin
+        normal = normals_ref[:, lanes]
         coefficients = []
         for group in range(3):
             d = []
@@ -489,11 +401,11 @@
     areas = areas.reshape(-1, 128)
     contrast = contrast.reshape(-1, 128)
     pack = jax.ShapeDtypeStruct((pack_rows, 128), f32)
-    low, high = pl.pallas_call(
+    low, high, own_tail = pl.pallas_call(
         prep_kernel,
-        out_shape=(pack, pack),
-        in_specs=[pl.BlockSpec(memory_space=pltpu.HBM)] * 5,
-        out_specs=(vmem, vmem),
+        out_shape=(pack, pack, jax.ShapeDtypeStruct((16, 128), f32)),
+        in_specs=[pl.BlockSpec(memory_space=pl.ANY)] * 5,
+        out_specs=(vmem,) * 3,
         scratch_shapes=[
             pltpu.VMEM((2 * pack_rows, 128), f32),
             pltpu.SMEM(box_centres.shape, f32),
@@ -503,7 +415,6 @@
             pltpu.VMEM(areas.shape, f32),
             pltpu.SemaphoreType.DMA((5,)),
         ],
-        compiler_params=pltpu.CompilerParams(vmem_limit_bytes=8 * 1024 * 1024),
         name="prepare",
     )(box_centres, facet_counts, basis, facet_centres, areas)
     below = lax.ppermute(high, "box", [(i, i + 1) for i in range(count - 1)])
@@ -516,12 +427,12 @@
             jax.ShapeDtypeStruct((boxes * 8, per_box), f32),
             jax.ShapeDtypeStruct((slots, 128), f32),
         ),
-        in_specs=[smem] + [vmem] * 3,
+        in_specs=[smem, smem] + [vmem] * 4,
         out_specs=(vmem,) * 3,
         scratch_shapes=[pltpu.VMEM((boxes * depth, per_box), bf16), pltpu.VMEM((slots, 128), bf16)],
         compiler_params=pltpu.CompilerParams(vmem_limit_bytes=24 * 1024 * 1024),
         name="own",
-    )(box_centres, low, high, normals)
+    )(box_centres, facet_counts, basis, facet_centres, areas, normals)
     image, tiles = pl.pallas_call(
         halo_kernel,
         out_shape=(
@@ -539,7 +450,9 @@
         ],
         compiler_params=pltpu.CompilerParams(vmem_limit_bytes=32 * 1024 * 1024),
         name="halo",
-    )(box_centres, facet_counts, below, low, high, above, normals, contrast, basis, targets, planes, own_total)
+    )(
+        box_centres, facet_counts, below, own_tail, above, facet_centres, normals, contrast, basis, targets, planes, own_total
+    )
     tiles = lax.all_to_all(tiles, "box", 0, 0, tiled=True)
     next_vector, hessenberg = pl.pallas_call(
         functools.partial(finish_kernel, total_facets),

time: 94.1 us -> 89.3 us (0.949)
  local copies, waits for them, and re-layouts: 4.61 us -> 0.93 us
  Pallas kernels: 68.8 us -> 67.7 us
    unnamed x20 -> x18, local copies, waits for them, and re-layouts: 4.61 us -> 0.93 us
    pallas_call x1, Pallas kernels: 35.1 us -> 33.2 us  [on_device(): pl.pallas_call(own_kernel, out_shape=(jax.ShapeDtypeStruct((slots, depth)...]
    pallas_call x1, Pallas kernels: 1.72 us -> 2.82 us  [on_device(): pl.pallas_call(prep_kernel, out_shape=(pack, pack, jax.ShapeDtypeStruct((...]
where the time goes in v7:
time: 89.3 us; the launch traced here: 89.1 us
  Pallas kernels  67.7 us (76%)
  blocking collectives  16 us (18%)
  starting transfers between devices  3.66 us (4%)
  local copies, waits for them, and re-layouts  0.93 us (1%)
    pallas_call x1, Pallas kernels, on_device(): pl.pallas_call(own_kernel, out_shape=(jax.ShapeDtypeStruct((slots, depth)...  33.2 us
    pallas_call x1, Pallas kernels, on_device(): pl.pallas_call(halo_kernel, out_shape=(jax.ShapeDtypeStruct((rhs_local, f...  29.5 us
    all_to_all x1, blocking collectives, on_device(): tiles = lax.all_to_all(tiles, 'box', 0, 0, tiled=True)  16 us
    pallas_call x1, Pallas kernels, on_device(): pl.pallas_call(prep_kernel, out_shape=(pack, pack, jax.ShapeDtypeStruct((...  2.82 us
    ppermute x1, starting transfers between devices, on_device(): below = lax.ppermute(high, 'box', [(i, i + 1) for i in range(count - 1)])  2.37 us
    pallas_call x1, Pallas kernels, on_device(): pl.pallas_call(functools.partial(finish_kernel, total_facets), out_shape=...  2.14 us
  transfers between devices with their start and end apart: 2, of which 0 were waited for; matrix products, arithmetic and copies ran while one was open for 0% of the time, Pallas kernels for 37%

profile of v7, /device:TPU:0, one launch (start us, length us, event | category | flops | bytes accessed | tf_op | source)
XLA Modules:
  0.0 89.1 jit_solution(17497089839718451698)
XLA Ops:
  0.6 0.0 copy-start.8
  0.6 0.0 copy-start
  0.7 0.0 copy-start.6
  0.7 0.0 copy-start.1
  0.7 0.0 copy-start.4
  0.7 2.8 %prepare.1 = (f32[400,128]{1,0:T(8,128)}, f32[400,128]{1,0:T(8,128)}, f32[16,128]{1,0:T(8,128)}) custom-call(f32[3,32]{1,0:T(4,128)} %centres_s.3, s32[32]{0:T(128)} %counts_s.5, f32[8,8,8192]{2,1,0:T(8,128)} %basis_ref.5, f32[3,8192]{1,0:T(4,128)} %facets_ref.3, f32[64,128]{1,0:T(8,128)} %bitcast.3), custom_call_target="tpu_custom_call" | custom-call | tf_op jit(solution)/shard_map/prepare/pallas_call | solution.py:404
  3.5 2.4 %collective-permute-start = (f32[400,128]{1,0:T(8,128)}, f32[400,128]{1,0:T(8,128)S(1)}, u32[]{:S(2)}, u32[]{:S(2)}) collective-permute-start(f32[400,128]{1,0:T(8,128)} %get-tuple-element.12), channel_id=1, source_target_pairs={{0,2},{2,4},{4,6},{6,8},{8,10},{10,12},{12,14},{14,16},{16,18},{18... | collective-permute-start | bytes 614408 | tf_op jit(solution)/shard_map/ppermute | solution.py:420
  5.9 1.3 %collective-permute-start.1 = (f32[400,128]{1,0:T(8,128)}, f32[400,128]{1,0:T(8,128)S(1)}, u32[]{:S(2)}, u32[]{:S(2)}) collective-permute-start(f32[400,128]{1,0:T(8,128)} %get-tuple-element.14), channel_id=1, source_target_pairs={{2,0},{4,2},{6,4},{8,6},{10,8},{12,10},{14,12},{16,14},{18,16},{20... | collective-permute-start | bytes 614408 | tf_op jit(solution)/shard_map/ppermute | solution.py:421
  7.2 0.0 copy-done.8
  7.2 0.0 copy-done
  7.2 0.0 copy-done.6
  7.2 0.0 copy-done.1
  7.2 0.0 copy-done.4
  7.2 0.0 copy-start.2
  7.3 0.9 %copy-done.2 = f32[3,8192]{1,0:T(4,128)S(1)} copy-done((f32[3,8192]{1,0:T(4,128)S(1)}, f32[3,8192]{1,0:T(4,128)}, u32[]{:S(2)}) %copy-start.2) | copy-done | bytes 98328
  8.1 0.0 copy-start.3
  8.1 0.0 copy-start.5
  8.2 0.0 copy-start.7
  8.2 33.2 %own.1 = (bf16[8192,128]{1,0:T(8,128)(2,1)S(1)}, f32[256,256]{1,0:T(8,128)S(1)}, f32[8192,128]{1,0:T(8,128)S(1)}) custom-call(f32[3,32]{1,0:T(4,128)S(1)} %copy-done.6, s32[32]{0:T(128)S(1)} %copy-done.8, f32[8,8,8192]{2,1,0:T(8,128)S(1)} %copy-done, f32[3,8192]{1,0:T(4,128)S(1)} %copy-done.1, f32[64,128]{1,0:T(8,128)S(1)} %bitcast.4, f32[3,8192]{1,0:T(4,128)S(1)} %copy-done.2), custom_call_target="tpu_custom_call" | custom-call | tf_op jit(solution)/shard_map/own/pallas_call | solution.py:423
  41.4 0.0 collective-permute-done.prev_ref
  41.4 0.0 collective-permute-done.1.next_ref
  41.4 0.0 copy-done.3
  41.4 0.0 copy-done.5
  41.4 0.0 copy-done.7
  41.4 29.5 %halo.1 = (f32[8,8192]{1,0:T(8,128)S(1)}, f32[16,8,128]{2,1,0:T(8,128)S(1)}) custom-call(f32[3,32]{1,0:T(4,128)S(1)} %copy-done.6, s32[32]{0:T(128)S(1)} %copy-done.8, f32[400,128]{1,0:T(8,128)S(1)} %collective-permute-done.prev_ref, f32[16,128]{1,0:T(8,128)S(1)} %copy-done.7, f32[400,128]{1,0:T(8,128)S(1)} %collective-permute-done.1.next_ref, ...), custom_call_target="tpu_custom_call" | custom-call | tf_op jit(solution)/shard_map/halo/pallas_call | solution.py:436
  71.0 16.0 %all_to_all.5.tiles_ref = f32[16,8,128]{2,1,0:T(8,128)S(1)} all-to-all(f32[16,8,128]{2,1,0:T(8,128)S(1)} %get-tuple-element.18), channel_id=1, replica_groups=mesh['box'=16,'rhs'=2] {'box'}, dimensions={0} | all-to-all | bytes 131072 | tf_op jit(solution)/shard_map/all_to_all | solution.py:456
  87.0 2.1 %finish.1 = (f32[8,8192]{1,0:T(8,128)}, f32[8,9]{1,0:T(8,128)}) custom-call(s32[32]{0:T(128)S(1)} %copy-done.8, f32[16,8,128]{2,1,0:T(8,128)S(1)} %all_to_all.5.tiles_ref, f32[8,8192]{1,0:T(8,128)S(1)} %get-tuple-element.19.image_ref, f32[8,8,8192]{2,1,0:T(8,128)S(1)} %copy-done), custom_call_target="tpu_custom_call" | custom-call | tf_op jit(solution)/shard_map/finish/pallas_call | solution.py:457
Async XLA Ops:
  0.6 6.6 %copy-start.8 = (s32[32]{0:T(128)S(1)}, s32[32]{0:T(128)}, u32[]{:S(2)}) copy-start(s32[32]{0:T(128)} %counts_s.5) | copy-start | bytes 388
  0.6 6.6 %copy-start = (f32[8,8,8192]{2,1,0:T(8,128)S(1)}, f32[8,8,8192]{2,1,0:T(8,128)}, u32[]{:S(2)}) copy-start(f32[8,8,8192]{2,1,0:T(8,128)} %basis_ref.5) | copy-start | bytes 6291460
  0.7 6.6 %copy-start.6 = (f32[3,32]{1,0:T(4,128)S(1)}, f32[3,32]{1,0:T(4,128)}, u32[]{:S(2)}) copy-start(f32[3,32]{1,0:T(4,128)} %centres_s.3) | copy-start | bytes 1156
  0.7 6.6 %copy-start.1 = (f32[3,8192]{1,0:T(4,128)S(1)}, f32[3,8192]{1,0:T(4,128)}, u32[]{:S(2)}) copy-start(f32[3,8192]{1,0:T(4,128)} %facets_ref.3) | copy-start | bytes 294916
  0.7 6.6 %copy-start.4 = (f32[8192]{0:T(1024)S(1)}, f32[8192]{0:T(1024)}, u32[]{:S(2)}) copy-start(f32[8192]{0:T(1024)} %param.12) | copy-start | bytes 98308
  3.5 37.9 %collective-permute-start = (f32[400,128]{1,0:T(8,128)}, f32[400,128]{1,0:T(8,128)S(1)}, u32[]{:S(2)}, u32[]{:S(2)}) collective-permute-start(f32[400,128]{1,0:T(8,128)} %get-tuple-element.12), channel_id=1, source_target_pairs={{0,2},{2,4},{4,6},{6,8},{8,10},{10,12},{12,14},{14,16},{16,18},{18... | collective-permute-start | bytes 614408 | tf_op jit(solution)/shard_map/ppermute | solution.py:420
  5.9 35.5 %collective-permute-start.1 = (f32[400,128]{1,0:T(8,128)}, f32[400,128]{1,0:T(8,128)S(1)}, u32[]{:S(2)}, u32[]{:S(2)}) collective-permute-start(f32[400,128]{1,0:T(8,128)} %get-tuple-element.14), channel_id=1, source_target_pairs={{2,0},{4,2},{6,4},{8,6},{10,8},{12,10},{14,12},{16,14},{18,16},{20... | collective-permute-start | bytes 614408 | tf_op jit(solution)/shard_map/ppermute | solution.py:421
  7.2 0.9 %copy-start.2 = (f32[3,8192]{1,0:T(4,128)S(1)}, f32[3,8192]{1,0:T(4,128)}, u32[]{:S(2)}) copy-start(f32[3,8192]{1,0:T(4,128)} %normals_ref.3) | copy-start | bytes 294916
  8.1 33.3 %copy-start.3 = (f32[3,8192]{1,0:T(4,128)S(1)}, f32[3,8192]{1,0:T(4,128)}, u32[]{:S(2)}) copy-start(f32[3,8192]{1,0:T(4,128)} %normals_ref.3) | copy-start | bytes 294916
  8.1 33.3 %copy-start.5 = (f32[8192]{0:T(1024)S(1)}, f32[8192]{0:T(1024)}, u32[]{:S(2)}) copy-start(f32[8192]{0:T(1024)} %param.13) | copy-start | bytes 98308
  8.2 33.3 %copy-start.7 = (f32[16,128]{1,0:T(8,128)S(1)}, f32[16,128]{1,0:T(8,128)}, u32[]{:S(2)}) copy-start(f32[16,128]{1,0:T(8,128)} %get-tuple-element.13.tail_ref) | copy-start | bytes 24580

commit v8 on v7

--- a/solution.py
+++ b/solution.py
@@ -144,7 +144,7 @@
     return x, y, plane, place, plane * plane_boxes + place
 
 
-def near_planes(sources, geometry, strengths, targets, total):
+def near_planes(sources, geometry, strengths, targets, total, length):
     def near_rows(item, _):
         target_y = (item + 1) // 3
         source_y = target_y + lax.rem(item + 1, 3) - 1
@@ -152,9 +152,12 @@
         for first, planes in sources:
             for x in range(4):
                 for plane in planes:
-                    for near_x in range(max(x - 1, 0), min(x + 2, 4)):
-                        start = (plane * plane_boxes + target_y * 4 + near_x) * per_box
-                        runs.append((first + source_y * 4 + x, pl.ds(pl.multiple_of(start, per_box), per_box)))
+                    low, high = max(x - 1, 0), min(x + 2, 4)
+                    start = (plane * plane_boxes + target_y * 4 + low) * per_box
+                    size = (high - low) * per_box
+                    for part in range(0, size, length):
+                        rows_of = pl.ds(pl.multiple_of(start + part, 128), min(length, size))
+                        runs.append((first + source_y * 4 + x, rows_of))
 
         def distances(box, rows_of):
             weights = geometry[pl.ds(pl.multiple_of(box * depth, depth), depth), :]
@@ -205,7 +208,7 @@
 
     lax.fori_loop(0, boxes, target, 0, unroll=2)
     total[...] = jnp.zeros_like(total)
-    near_planes(((0, (0, 1)), (plane_boxes, (0, 1))), geometry, strengths, targets, total)
+    near_planes(((0, (0, 1)), (plane_boxes, (0, 1))), geometry, strengths, targets, total, 128)
 
 
 def halo_kernel(
@@ -218,7 +221,7 @@
     store_pack_features(prev_ref, origin, geometry, strengths, 0)
     store_pack_features(next_ref, origin, geometry, strengths, plane_boxes)
     total[...] = jnp.zeros_like(total)
-    near_planes(((0, (0,)), (plane_boxes, (1,))), geometry, strengths, targets, total)
+    near_planes(((0, (0,)), (plane_boxes, (1,))), geometry, strengths, targets, total, 768)
 
     def near_field(slot, _):
         rows = pl.ds(pl.multiple_of(slot * per_box, per_box), per_box)

time: 89.3 us -> 90.8 us (1.017)
  Pallas kernels: 67.7 us -> 69.2 us
  transfers between devices with their start and end apart: 2 -> 2, of which waited for: 0 -> 0; matrix products, arithmetic and copies ran while one was open for 0% -> 0% of each run, Pallas kernels for 37% -> 38%
where the time goes in v8:
time: 90.8 us; the launch traced here: 90.6 us
  Pallas kernels  69.2 us (76%)
  blocking collectives  16 us (18%)
  starting transfers between devices  3.66 us (4%)
  local copies, waits for them, and re-layouts  0.93 us (1%)
    pallas_call x1, Pallas kernels, on_device(): pl.pallas_call(own_kernel, out_shape=(jax.ShapeDtypeStruct((slots, depth)...  34 us
    pallas_call x1, Pallas kernels, on_device(): pl.pallas_call(halo_kernel, out_shape=(jax.ShapeDtypeStruct((rhs_local, f...  30.2 us
    all_to_all x1, blocking collectives, on_device(): tiles = lax.all_to_all(tiles, 'box', 0, 0, tiled=True)  16 us
    pallas_call x1, Pallas kernels, on_device(): pl.pallas_call(prep_kernel, out_shape=(pack, pack, jax.ShapeDtypeStruct((...  2.82 us
    ppermute x1, starting transfers between devices, on_device(): below = lax.ppermute(high, 'box', [(i, i + 1) for i in range(count - 1)])  2.37 us
    pallas_call x1, Pallas kernels, on_device(): pl.pallas_call(functools.partial(finish_kernel, total_facets), out_shape=...  2.14 us
  transfers between devices with their start and end apart: 2, of which 0 were waited for; matrix products, arithmetic and copies ran while one was open for 0% of the time, Pallas kernels for 38%

profile of v8, /device:TPU:0, one launch (start us, length us, event | category | flops | bytes accessed | tf_op | source)
XLA Modules:
  0.0 90.6 jit_solution(7860643011140998149)
XLA Ops:
  0.6 0.0 copy-start.8
  0.6 0.0 copy-start
  0.7 0.0 copy-start.6
  0.7 0.0 copy-start.1
  0.7 0.0 copy-start.4
  0.7 2.8 %prepare.1 = (f32[400,128]{1,0:T(8,128)}, f32[400,128]{1,0:T(8,128)}, f32[16,128]{1,0:T(8,128)}) custom-call(f32[3,32]{1,0:T(4,128)} %centres_s.3, s32[32]{0:T(128)} %counts_s.5, f32[8,8,8192]{2,1,0:T(8,128)} %basis_ref.5, f32[3,8192]{1,0:T(4,128)} %facets_ref.3, f32[64,128]{1,0:T(8,128)} %bitcast.3), custom_call_target="tpu_custom_call" | custom-call | tf_op jit(solution)/shard_map/prepare/pallas_call | solution.py:407
  3.5 2.4 %collective-permute-start = (f32[400,128]{1,0:T(8,128)}, f32[400,128]{1,0:T(8,128)S(1)}, u32[]{:S(2)}, u32[]{:S(2)}) collective-permute-start(f32[400,128]{1,0:T(8,128)} %get-tuple-element.12), channel_id=1, source_target_pairs={{0,2},{2,4},{4,6},{6,8},{8,10},{10,12},{12,14},{14,16},{16,18},{18... | collective-permute-start | bytes 614408 | tf_op jit(solution)/shard_map/ppermute | solution.py:423
  5.9 1.3 %collective-permute-start.1 = (f32[400,128]{1,0:T(8,128)}, f32[400,128]{1,0:T(8,128)S(1)}, u32[]{:S(2)}, u32[]{:S(2)}) collective-permute-start(f32[400,128]{1,0:T(8,128)} %get-tuple-element.14), channel_id=1, source_target_pairs={{2,0},{4,2},{6,4},{8,6},{10,8},{12,10},{14,12},{16,14},{18,16},{20... | collective-permute-start | bytes 614408 | tf_op jit(solution)/shard_map/ppermute | solution.py:424
  7.2 0.0 copy-done.8
  7.2 0.0 copy-done
  7.2 0.0 copy-done.6
  7.2 0.0 copy-done.1
  7.2 0.0 copy-done.4
  7.2 0.0 copy-start.2
  7.3 0.9 copy-done.2
  8.1 0.0 copy-start.3
  8.1 0.0 copy-start.5
  8.2 0.0 copy-start.7
  8.2 34.0 %own.1 = (bf16[8192,128]{1,0:T(8,128)(2,1)S(1)}, f32[256,256]{1,0:T(8,128)S(1)}, f32[8192,128]{1,0:T(8,128)S(1)}) custom-call(f32[3,32]{1,0:T(4,128)S(1)} %copy-done.6, s32[32]{0:T(128)S(1)} %copy-done.8, f32[8,8,8192]{2,1,0:T(8,128)S(1)} %copy-done, f32[3,8192]{1,0:T(4,128)S(1)} %copy-done.1, f32[64,128]{1,0:T(8,128)S(1)} %bitcast.4, f32[3,8192]{1,0:T(4,128)S(1)} %copy-done.2), custom_call_target="tpu_custom_call" | custom-call | tf_op jit(solution)/shard_map/own/pallas_call | solution.py:426
  42.2 0.0 collective-permute-done.prev_ref
  42.2 0.0 collective-permute-done.1.next_ref
  42.2 0.0 copy-done.3
  42.2 0.0 copy-done.5
  42.2 0.0 copy-done.7
  42.3 30.2 %halo.1 = (f32[8,8192]{1,0:T(8,128)S(1)}, f32[16,8,128]{2,1,0:T(8,128)S(1)}) custom-call(f32[3,32]{1,0:T(4,128)S(1)} %copy-done.6, s32[32]{0:T(128)S(1)} %copy-done.8, f32[400,128]{1,0:T(8,128)S(1)} %collective-permute-done.prev_ref, f32[16,128]{1,0:T(8,128)S(1)} %copy-done.7, f32[400,128]{1,0:T(8,128)S(1)} %collective-permute-done.1.next_ref, ...), custom_call_target="tpu_custom_call" | custom-call | tf_op jit(solution)/shard_map/halo/pallas_call | solution.py:439
  72.5 16.0 %all_to_all.5.tiles_ref = f32[16,8,128]{2,1,0:T(8,128)S(1)} all-to-all(f32[16,8,128]{2,1,0:T(8,128)S(1)} %get-tuple-element.18), channel_id=1, replica_groups=mesh['box'=16,'rhs'=2] {'box'}, dimensions={0} | all-to-all | bytes 131072 | tf_op jit(solution)/shard_map/all_to_all | solution.py:459
  88.4 2.1 %finish.1 = (f32[8,8192]{1,0:T(8,128)}, f32[8,9]{1,0:T(8,128)}) custom-call(s32[32]{0:T(128)S(1)} %copy-done.8, f32[16,8,128]{2,1,0:T(8,128)S(1)} %all_to_all.5.tiles_ref, f32[8,8192]{1,0:T(8,128)S(1)} %get-tuple-element.19.image_ref, f32[8,8,8192]{2,1,0:T(8,128)S(1)} %copy-done), custom_call_target="tpu_custom_call" | custom-call | tf_op jit(solution)/shard_map/finish/pallas_call | solution.py:460
Async XLA Ops:
  0.6 6.6 %copy-start.8 = (s32[32]{0:T(128)S(1)}, s32[32]{0:T(128)}, u32[]{:S(2)}) copy-start(s32[32]{0:T(128)} %counts_s.5) | copy-start | bytes 388
  0.6 6.6 %copy-start = (f32[8,8,8192]{2,1,0:T(8,128)S(1)}, f32[8,8,8192]{2,1,0:T(8,128)}, u32[]{:S(2)}) copy-start(f32[8,8,8192]{2,1,0:T(8,128)} %basis_ref.5) | copy-start | bytes 6291460
  0.7 6.6 %copy-start.6 = (f32[3,32]{1,0:T(4,128)S(1)}, f32[3,32]{1,0:T(4,128)}, u32[]{:S(2)}) copy-start(f32[3,32]{1,0:T(4,128)} %centres_s.3) | copy-start | bytes 1156
  0.7 6.6 %copy-start.1 = (f32[3,8192]{1,0:T(4,128)S(1)}, f32[3,8192]{1,0:T(4,128)}, u32[]{:S(2)}) copy-start(f32[3,8192]{1,0:T(4,128)} %facets_ref.3) | copy-start | bytes 294916
  0.7 6.6 %copy-start.4 = (f32[8192]{0:T(1024)S(1)}, f32[8192]{0:T(1024)}, u32[]{:S(2)}) copy-start(f32[8192]{0:T(1024)} %param.12) | copy-start | bytes 98308
  3.5 38.7 %collective-permute-start = (f32[400,128]{1,0:T(8,128)}, f32[400,128]{1,0:T(8,128)S(1)}, u32[]{:S(2)}, u32[]{:S(2)}) collective-permute-start(f32[400,128]{1,0:T(8,128)} %get-tuple-element.12), channel_id=1, source_target_pairs={{0,2},{2,4},{4,6},{6,8},{8,10},{10,12},{12,14},{14,16},{16,18},{18... | collective-permute-start | bytes 614408 | tf_op jit(solution)/shard_map/ppermute | solution.py:423
  5.9 36.3 %collective-permute-start.1 = (f32[400,128]{1,0:T(8,128)}, f32[400,128]{1,0:T(8,128)S(1)}, u32[]{:S(2)}, u32[]{:S(2)}) collective-permute-start(f32[400,128]{1,0:T(8,128)} %get-tuple-element.14), channel_id=1, source_target_pairs={{2,0},{4,2},{6,4},{8,6},{10,8},{12,10},{14,12},{16,14},{18,16},{20... | collective-permute-start | bytes 614408 | tf_op jit(solution)/shard_map/ppermute | solution.py:424
  7.2 0.9 %copy-start.2 = (f32[3,8192]{1,0:T(4,128)S(1)}, f32[3,8192]{1,0:T(4,128)}, u32[]{:S(2)}) copy-start(f32[3,8192]{1,0:T(4,128)} %normals_ref.3) | copy-start | bytes 294916
  8.1 34.1 %copy-start.3 = (f32[3,8192]{1,0:T(4,128)S(1)}, f32[3,8192]{1,0:T(4,128)}, u32[]{:S(2)}) copy-start(f32[3,8192]{1,0:T(4,128)} %normals_ref.3) | copy-start | bytes 294916
  8.1 34.1 %copy-start.5 = (f32[8192]{0:T(1024)S(1)}, f32[8192]{0:T(1024)}, u32[]{:S(2)}) copy-start(f32[8192]{0:T(1024)} %param.13) | copy-start | bytes 98308
  8.2 34.1 %copy-start.7 = (f32[16,128]{1,0:T(8,128)S(1)}, f32[16,128]{1,0:T(8,128)}, u32[]{:S(2)}) copy-start(f32[16,128]{1,0:T(8,128)} %get-tuple-element.13.tail_ref) | copy-start | bytes 24580

commit v9 on v8

--- a/solution.py
+++ b/solution.py
@@ -144,7 +144,7 @@
     return x, y, plane, place, plane * plane_boxes + place
 
 
-def near_planes(sources, geometry, strengths, targets, total, length):
+def near_planes(sources, geometry, strengths, targets, total, beside=None):
     def near_rows(item, _):
         target_y = (item + 1) // 3
         source_y = target_y + lax.rem(item + 1, 3) - 1
@@ -155,8 +155,8 @@
                     low, high = max(x - 1, 0), min(x + 2, 4)
                     start = (plane * plane_boxes + target_y * 4 + low) * per_box
                     size = (high - low) * per_box
-                    for part in range(0, size, length):
-                        rows_of = pl.ds(pl.multiple_of(start + part, 128), min(length, size))
+                    for part in range(0, size, per_box):
+                        rows_of = pl.ds(pl.multiple_of(start + part, per_box), per_box)
                         runs.append((first + source_y * 4 + x, rows_of))
 
         def distances(box, rows_of):
@@ -165,6 +165,8 @@
 
         ahead = distances(*runs[0])
         for i, (box, rows_of) in enumerate(runs):
+            if beside is not None and i % 5 == 0:
+                beside(item * 4 + i // 5)
             here = ahead
             if i + 1 < len(runs):
                 ahead = distances(*runs[i + 1])
@@ -208,7 +210,7 @@
 
     lax.fori_loop(0, boxes, target, 0, unroll=2)
     total[...] = jnp.zeros_like(total)
-    near_planes(((0, (0, 1)), (plane_boxes, (0, 1))), geometry, strengths, targets, total, 128)
+    near_planes(((0, (0, 1)), (plane_boxes, (0, 1))), geometry, strengths, targets, total)
 
 
 def halo_kernel(
@@ -221,19 +223,6 @@
     store_pack_features(prev_ref, origin, geometry, strengths, 0)
     store_pack_features(next_ref, origin, geometry, strengths, plane_boxes)
     total[...] = jnp.zeros_like(total)
-    near_planes(((0, (0,)), (plane_boxes, (1,))), geometry, strengths, targets, total, 768)
-
-    def near_field(slot, _):
-        rows = pl.ds(pl.multiple_of(slot * per_box, per_box), per_box)
-        turned = jnp.transpose(total[rows, :] + own_total[rows, :])
-        sums = turned[:32] + (turned[32:64] + turned[64:96])
-        side = planes[pl.ds(pl.multiple_of(slot * 8, 8), 8), :]
-        value = side[3:4] * sums[:8] - side[0:1] * sums[8:16]
-        value = value - side[1:2] * sums[16:24] - side[2:3] * sums[24:32]
-        field[pl.ds(pl.multiple_of(slot * 8, 8), 8), :] = value
-        return 0
-
-    lax.fori_loop(0, boxes, near_field, 0, unroll=2)
 
     tails = (prev_ref[tail:, :], tail_ref[...], next_ref[tail:, :])
     for group in range(3):
@@ -251,7 +240,8 @@
     lane_y = (far_lane >> 2) & 3
     lane_z = 2 * (far_lane >> 7) - 2 + ((far_lane >> 4) & 1)
 
-    def far_box(b, _):
+    def far_box(k):
+        b = jnp.minimum(k, boxes - 1)
         x, y, plane, _, slot = target_place(centres_s, b)
         lanes = pl.ds(pl.multiple_of(b * per_box, per_box), per_box)
         local = facets_ref[:, lanes] - origin
@@ -279,10 +269,21 @@
         picked = jnp.where(near, 0.0, far_both).astype(bf16)
         first = jnp.dot(picked, upper, preferred_element_type=f32)
         second = jnp.dot(picked, lower, preferred_element_type=f32)
-        field[pl.ds(pl.multiple_of(slot * 8, 8), 8), :] += first[:8] + first[8:] + second[:8]
+        field[pl.ds(pl.multiple_of(slot * 8, 8), 8), :] = first[:8] + first[8:] + second[:8]
+
+    near_planes(((0, (0,)), (plane_boxes, (1,))), geometry, strengths, targets, total, far_box)
+
+    def near_field(slot, _):
+        rows = pl.ds(pl.multiple_of(slot * per_box, per_box), per_box)
+        turned = jnp.transpose(total[rows, :] + own_total[rows, :])
+        sums = turned[:32] + (turned[32:64] + turned[64:96])
+        side = planes[pl.ds(pl.multiple_of(slot * 8, 8), 8), :]
+        value = side[3:4] * sums[:8] - side[0:1] * sums[8:16]
+        value = value - side[1:2] * sums[16:24] - side[2:3] * sums[24:32]
+        field[pl.ds(pl.multiple_of(slot * 8, 8), 8), :] += value
         return 0
 
-    lax.fori_loop(0, boxes, far_box, 0, unroll=2)
+    lax.fori_loop(0, boxes, near_field, 0, unroll=2)
 
     def image_box(b, carry):
         _, _, _, _, slot = target_place(centres_s, b)
@@ -314,10 +315,10 @@
 
     gram = lax.fori_loop(0, boxes, gram_box, (zeros,) * len(pairs))
     lane = lax.broadcasted_iota(jnp.int32, (8, 128), 1)
-    total = zeros
+    total_sums = zeros
     for k, value in enumerate([*sums, *gram]):
-        total = jnp.where(lane == k, jnp.sum(value, axis=1, keepdims=True), total)
-    sums_ref[...] = jnp.broadcast_to(total[None], sums_ref.shape)
+        total_sums = jnp.where(lane == k, jnp.sum(value, axis=1, keepdims=True), total_sums)
+    sums_ref[...] = total_sums
 
 
 def two_sum(a, b):
@@ -440,7 +441,7 @@
         halo_kernel,
         out_shape=(
             jax.ShapeDtypeStruct((rhs_local, facet_local), f32),
-            jax.ShapeDtypeStruct((count, 8, 128), f32),
+            jax.ShapeDtypeStruct((8, 128), f32),
         ),
         in_specs=[smem, smem] + [vmem] * 10,
         out_specs=(vmem, vmem),
@@ -456,7 +457,7 @@
     )(
         box_centres, facet_counts, below, own_tail, above, facet_centres, normals, contrast, basis, targets, planes, own_total
     )
-    tiles = lax.all_to_all(tiles, "box", 0, 0, tiled=True)
+    tiles = lax.all_gather(tiles, "box")
     next_vector, hessenberg = pl.pallas_call(
         functools.partial(finish_kernel, total_facets),
         out_shape=(

time: 90.8 us -> 96.3 us (1.061)
  blocking collectives: 16 us -> 25.1 us
  Pallas kernels: 69.2 us -> 65.5 us
    all_gather x0 -> x1, blocking collectives: none -> 25.1 us  [on_device(): tiles = lax.all_gather(tiles, 'box')]
    all_to_all x1 -> x0, blocking collectives: 16 us -> none  [on_device(): tiles = lax.all_to_all(tiles, 'box', 0, 0, tiled=True)]
    pallas_call x1, Pallas kernels: 30.2 us -> 27.3 us  [on_device(): pl.pallas_call(halo_kernel, out_shape=(jax.ShapeDtypeStruct((rhs_local, f...]
  transfers between devices with their start and end apart: 2 -> 2, of which waited for: 0 -> 0; matrix products, arithmetic and copies ran while one was open for 0% -> 0% of each run, Pallas kernels for 38% -> 35%
where the time goes in v9:
time: 96.3 us; the launch traced here: 96.1 us
  Pallas kernels  65.5 us (68%)
  blocking collectives  25.1 us (26%)
  starting transfers between devices  3.66 us (4%)
    pallas_call x1, Pallas kernels, on_device(): pl.pallas_call(own_kernel, out_shape=(jax.ShapeDtypeStruct((slots, depth)...  33.2 us
    pallas_call x1, Pallas kernels, on_device(): pl.pallas_call(halo_kernel, out_shape=(jax.ShapeDtypeStruct((rhs_local, f...  27.3 us
    all_gather x1, blocking collectives, on_device(): tiles = lax.all_gather(tiles, 'box')  25.1 us
    pallas_call x1, Pallas kernels, on_device(): pl.pallas_call(prep_kernel, out_shape=(pack, pack, jax.ShapeDtypeStruct((...  2.82 us
    ppermute x1, starting transfers between devices, on_device(): below = lax.ppermute(high, 'box', [(i, i + 1) for i in range(count - 1)])  2.37 us
    pallas_call x1, Pallas kernels, on_device(): pl.pallas_call(functools.partial(finish_kernel, total_facets), out_shape=...  2.14 us
  transfers between devices with their start and end apart: 2, of which 0 were waited for; matrix products, arithmetic and copies ran while one was open for 0% of the time, Pallas kernels for 35%

profile of v9, /device:TPU:0, one launch (start us, length us, event | category | flops | bytes accessed | tf_op | source)
XLA Modules:
  0.0 96.1 jit_solution(8384211738027291613)
XLA Ops:
  0.6 0.0 copy-start.8
  0.6 0.0 copy-start
  0.7 0.0 copy-start.6
  0.7 0.0 copy-start.1
  0.7 0.0 copy-start.4
  0.7 2.8 %prepare.1 = (f32[400,128]{1,0:T(8,128)}, f32[400,128]{1,0:T(8,128)}, f32[16,128]{1,0:T(8,128)}) custom-call(f32[3,32]{1,0:T(4,128)} %centres_s.3, s32[32]{0:T(128)} %counts_s.5, f32[8,8,8192]{2,1,0:T(8,128)} %basis_ref.5, f32[3,8192]{1,0:T(4,128)} %facets_ref.3, f32[64,128]{1,0:T(8,128)} %bitcast.5), custom_call_target="tpu_custom_call" | custom-call | tf_op jit(solution)/shard_map/prepare/pallas_call | solution.py:408
  3.5 2.4 %collective-permute-start = (f32[400,128]{1,0:T(8,128)}, f32[400,128]{1,0:T(8,128)S(1)}, u32[]{:S(2)}, u32[]{:S(2)}) collective-permute-start(f32[400,128]{1,0:T(8,128)} %get-tuple-element.12), channel_id=1, source_target_pairs={{0,2},{2,4},{4,6},{6,8},{8,10},{10,12},{12,14},{14,16},{16,18},{18... | collective-permute-start | bytes 614408 | tf_op jit(solution)/shard_map/ppermute | solution.py:424
  5.9 1.3 %collective-permute-start.1 = (f32[400,128]{1,0:T(8,128)}, f32[400,128]{1,0:T(8,128)S(1)}, u32[]{:S(2)}, u32[]{:S(2)}) collective-permute-start(f32[400,128]{1,0:T(8,128)} %get-tuple-element.14), channel_id=1, source_target_pairs={{2,0},{4,2},{6,4},{8,6},{10,8},{12,10},{14,12},{16,14},{18,16},{20... | collective-permute-start | bytes 614408 | tf_op jit(solution)/shard_map/ppermute | solution.py:425
  7.2 0.0 copy-done.8
  7.2 0.0 copy-done
  7.2 0.0 copy-done.6
  7.2 0.0 copy-done.1
  7.2 0.0 copy-done.4
  7.2 0.0 copy-start.2
  7.3 0.9 copy-done.2
  8.1 0.0 copy-start.3
  8.1 0.0 copy-start.5
  8.2 0.0 copy-start.7
  8.2 33.2 %own.1 = (bf16[8192,128]{1,0:T(8,128)(2,1)S(1)}, f32[256,256]{1,0:T(8,128)S(1)}, f32[8192,128]{1,0:T(8,128)S(1)}) custom-call(f32[3,32]{1,0:T(4,128)S(1)} %copy-done.6, s32[32]{0:T(128)S(1)} %copy-done.8, f32[8,8,8192]{2,1,0:T(8,128)S(1)} %copy-done, f32[3,8192]{1,0:T(4,128)S(1)} %copy-done.1, f32[64,128]{1,0:T(8,128)S(1)} %bitcast.6, f32[3,8192]{1,0:T(4,128)S(1)} %copy-done.2), custom_call_target="tpu_custom_call" | custom-call | tf_op jit(solution)/shard_map/own/pallas_call | solution.py:427
  41.4 0.0 collective-permute-done.prev_ref
  41.4 0.0 collective-permute-done.1.next_ref
  41.4 0.0 copy-done.3
  41.4 0.0 copy-done.5
  41.4 0.0 copy-done.7
  41.5 27.3 %halo.1 = (f32[8,8192]{1,0:T(8,128)S(1)}, f32[8,128]{1,0:T(8,128)S(1)}) custom-call(f32[3,32]{1,0:T(4,128)S(1)} %copy-done.6, s32[32]{0:T(128)S(1)} %copy-done.8, f32[400,128]{1,0:T(8,128)S(1)} %collective-permute-done.prev_ref, f32[16,128]{1,0:T(8,128)S(1)} %copy-done.7, f32[400,128]{1,0:T(8,128)S(1)} %collective-permute-done.1.next_ref, ...), custom_call_target="tpu_custom_call" | custom-call | tf_op jit(solution)/shard_map/halo/pallas_call | solution.py:440
  68.8 25.1 %all-gather = f32[128,128]{1,0:T(8,128)S(1)} all-gather(f32[8,128]{1,0:T(8,128)S(1)} %get-tuple-element.18), channel_id=2, replica_groups=mesh['box'=16,'rhs'=2] {'box'}, dimensions={0}, use_global_device_ids=true | all-gather | bytes 69632 | tf_op jit(solution)/shard_map/all_gather | solution.py:460
  93.9 2.1 %finish.1 = (f32[8,8192]{1,0:T(8,128)}, f32[8,9]{1,0:T(8,128)}) custom-call(s32[32]{0:T(128)S(1)} %copy-done.8, f32[16,8,128]{2,1,0:T(8,128)S(1)} %bitcast.4, f32[8,8192]{1,0:T(8,128)S(1)} %get-tuple-element.19.image_ref, f32[8,8,8192]{2,1,0:T(8,128)S(1)} %copy-done), custom_call_target="tpu_custom_call" | custom-call | tf_op jit(solution)/shard_map/finish/pallas_call | solution.py:461
Async XLA Ops:
  0.6 6.6 %copy-start.8 = (s32[32]{0:T(128)S(1)}, s32[32]{0:T(128)}, u32[]{:S(2)}) copy-start(s32[32]{0:T(128)} %counts_s.5) | copy-start | bytes 388
  0.6 6.6 %copy-start = (f32[8,8,8192]{2,1,0:T(8,128)S(1)}, f32[8,8,8192]{2,1,0:T(8,128)}, u32[]{:S(2)}) copy-start(f32[8,8,8192]{2,1,0:T(8,128)} %basis_ref.5) | copy-start | bytes 6291460
  0.7 6.6 %copy-start.6 = (f32[3,32]{1,0:T(4,128)S(1)}, f32[3,32]{1,0:T(4,128)}, u32[]{:S(2)}) copy-start(f32[3,32]{1,0:T(4,128)} %centres_s.3) | copy-start | bytes 1156
  0.7 6.6 %copy-start.1 = (f32[3,8192]{1,0:T(4,128)S(1)}, f32[3,8192]{1,0:T(4,128)}, u32[]{:S(2)}) copy-start(f32[3,8192]{1,0:T(4,128)} %facets_ref.3) | copy-start | bytes 294916
  0.7 6.6 %copy-start.4 = (f32[8192]{0:T(1024)S(1)}, f32[8192]{0:T(1024)}, u32[]{:S(2)}) copy-start(f32[8192]{0:T(1024)} %param.12) | copy-start | bytes 98308
  3.5 37.9 %collective-permute-start = (f32[400,128]{1,0:T(8,128)}, f32[400,128]{1,0:T(8,128)S(1)}, u32[]{:S(2)}, u32[]{:S(2)}) collective-permute-start(f32[400,128]{1,0:T(8,128)} %get-tuple-element.12), channel_id=1, source_target_pairs={{0,2},{2,4},{4,6},{6,8},{8,10},{10,12},{12,14},{14,16},{16,18},{18... | collective-permute-start | bytes 614408 | tf_op jit(solution)/shard_map/ppermute | solution.py:424
  5.9 35.5 %collective-permute-start.1 = (f32[400,128]{1,0:T(8,128)}, f32[400,128]{1,0:T(8,128)S(1)}, u32[]{:S(2)}, u32[]{:S(2)}) collective-permute-start(f32[400,128]{1,0:T(8,128)} %get-tuple-element.14), channel_id=1, source_target_pairs={{2,0},{4,2},{6,4},{8,6},{10,8},{12,10},{14,12},{16,14},{18,16},{20... | collective-permute-start | bytes 614408 | tf_op jit(solution)/shard_map/ppermute | solution.py:425
  7.2 0.9 copy-start.2
  8.1 33.3 %copy-start.3 = (f32[3,8192]{1,0:T(4,128)S(1)}, f32[3,8192]{1,0:T(4,128)}, u32[]{:S(2)}) copy-start(f32[3,8192]{1,0:T(4,128)} %normals_ref.3) | copy-start | bytes 294916
  8.1 33.3 %copy-start.5 = (f32[8192]{0:T(1024)S(1)}, f32[8192]{0:T(1024)}, u32[]{:S(2)}) copy-start(f32[8192]{0:T(1024)} %param.13) | copy-start | bytes 98308
  8.2 33.3 %copy-start.7 = (f32[16,128]{1,0:T(8,128)S(1)}, f32[16,128]{1,0:T(8,128)}, u32[]{:S(2)}) copy-start(f32[16,128]{1,0:T(8,128)} %get-tuple-element.13.tail_ref) | copy-start | bytes 24580

commit v10 on v7

v10 whole, which is shorter than its diff:
```python
import functools

import jax
import jax.numpy as jnp
from jax import lax
from jax.experimental import pallas as pl
from jax.experimental.pallas import tpu as pltpu
from jax.sharding import PartitionSpec as P

soften = 0.0025
epsilon = 1e-06
f32 = jnp.float32
bf16 = jnp.bfloat16
plane_boxes = 16
per_box = 256
depth = 128


def lattice(centres_s, b):
    x = (centres_s[0, b] + 0.5).astype(jnp.int32)
    y = (centres_s[1, b] + 0.5).astype(jnp.int32)
    z = (centres_s[2, b] + 0.5).astype(jnp.int32)
    return x, y, z


def slot_of(centres_s, b):
    x, y, z = lattice(centres_s, b)
    return (z & 1) * plane_boxes + y * 4 + x


def boxes_by_slot(centres_s, boxes_s):
    def one_box(b, _):
        boxes_s[slot_of(centres_s, b)] = b
        return 0

    lax.fori_loop(0, centres_s.shape[1], one_box, 0)


def wide_row(ref, b):
    return jnp.concatenate([ref[pl.ds(2 * b, 1), :], ref[pl.ds(2 * b + 1, 1), :]], axis=1)


def live_row(counts_s, b):
    slots = lax.broadcasted_iota(jnp.int32, (1, per_box), 1)
    return (slots < counts_s[b]).astype(f32)


def prep_kernel(
    centres_h, counts_h, basis_h, facets_h, areas_h, cross_ref, first_ref, second_ref, tail_ref,
    charges_v, places_v, centres_s, counts_s, current_ref, facets_ref, areas_ref, arrived
):
    boxes = counts_s.shape[0]
    moves = [
        (basis_h.at[basis_h.shape[0] - 1], current_ref),
        (facets_h, facets_ref),
        (areas_h, areas_ref),
        (centres_h, centres_s),
        (counts_h, counts_s),
    ]
    copies = [pltpu.make_async_copy(a, b, arrived.at[k]) for k, (a, b) in enumerate(moves)]
    for copy in copies:
        copy.start()
    for copy in copies:
        copy.wait()
    lane = lax.broadcasted_iota(jnp.int32, (8, 128), 1)
    row = lax.broadcasted_iota(jnp.int32, (8, 128), 0)

    def one_box(b, carry):
        moments, centres = carry
        slot = slot_of(centres_s, b)
        lanes = pl.ds(pl.multiple_of(b * per_box, per_box), per_box)
        facets = facets_ref[:, lanes]
        live = live_row(counts_s, b)
        weighted = current_ref[:, lanes] * (wide_row(areas_ref, b) * live / per_box)
        charges = weighted.astype(bf16).astype(f32)
        start = pl.multiple_of(slot * 16, 16)
        charges_v[pl.ds(start, 8), :] = charges[:, :128]
        charges_v[pl.ds(start + 8, 8), :] = charges[:, 128:]
        places_v[pl.ds(pl.multiple_of(slot * 8, 8), 8), :] = jnp.concatenate(
            [facets[:, :128], facets[:, 128:], jnp.zeros((2, 128), f32)], axis=0
        )
        moments += jnp.where(lane == slot, jnp.sum(weighted, axis=1, keepdims=True), 0.0)
        for a in range(3):
            dipole = jnp.sum(weighted * (facets[a : a + 1] - centres_s[a, b]), axis=1, keepdims=True)
            moments += jnp.where(lane == 32 * (a + 1) + slot, dipole, 0.0)
            centres += jnp.where((lane == slot) & (row == a), centres_s[a, b], 0.0)
        return moments, centres

    zeros = jnp.zeros((8, 128), f32)
    moments, centres = lax.fori_loop(0, boxes, one_box, (zeros, zeros), unroll=4)
    half = lax.axis_index("rhs")
    cross_ref[:512] = charges_v[...]
    cross_ref[512:] = moments
    first_ref[:256] = charges_v[pl.ds(pl.multiple_of((1 - half) * 256, 256), 256), :]
    first_ref[256:384] = places_v[pl.ds(pl.multiple_of((1 - half) * 128, 128), 128), :]
    first_ref[384:392] = moments
    first_ref[392:] = centres
    second_ref[:256] = charges_v[pl.ds(pl.multiple_of(half * 256, 256), 256), :]
    second_ref[256:] = moments
    tail_ref[:8] = moments
    tail_ref[8:] = centres


def thirds(x):
    high = x.astype(bf16).astype(f32)
    rest = x - high
    middle = rest.astype(bf16).astype(f32)
    return high, middle, (rest - middle).astype(bf16).astype(f32)


def stacked_rows(parts, width):
    zeros = jnp.zeros((depth - 8 * len(parts), width), f32)
    return jnp.concatenate([*parts, zeros], axis=0)


def slab_origin(centres_s):
    _, _, z = lattice(centres_s, 0)
    base_z = (z - (z & 1)).astype(f32) + 0.5
    axis_row = lax.broadcasted_iota(jnp.int32, (3, 1), 0)
    return jnp.where(axis_row == 2, base_z, 1.5), base_z


def padded(rows):
    return jnp.concatenate([rows, jnp.zeros((8 - rows.shape[0], rows.shape[1]), f32)], axis=0)


def wide_charges(ref, start):
    start = pl.multiple_of(start, 16)
    return jnp.concatenate([ref[pl.ds(start, 8), :], ref[pl.ds(start + 8, 8), :]], axis=1)


def store_source_features(local, charges, box, geometry, strengths):
    row = lax.broadcasted_iota(jnp.int32, (8, per_box), 0)
    square = jnp.sum(local * local, axis=0, keepdims=True)
    features = jnp.where(row == 3, square, jnp.where(row == 4, 1.0, local))
    high, middle, low = thirds(features)
    rows = stacked_rows((high, high, high, middle, middle, low), per_box)
    geometry[pl.ds(pl.multiple_of(box * depth, depth), depth), :] = rows.astype(bf16)
    products = jnp.concatenate([charges] + [charges * local[a : a + 1] for a in range(3)], axis=0)
    rows = jnp.concatenate([*thirds(products), jnp.zeros((64, per_box), f32)], axis=0)
    strengths[pl.ds(pl.multiple_of(box * per_box, per_box), per_box), :] = jnp.transpose(rows).astype(bf16)


def near_planes(sources, geometry, strengths, targets, total, beside=None):
    def near_rows(item, _):
        target_y = (item + 1) // 3
        source_y = target_y + lax.rem(item + 1, 3) - 1
        runs = []
        for first in sources:
            for x in range(4):
                for near_x in range(max(x - 1, 0), min(x + 2, 4)):
                    start = pl.multiple_of((target_y * 4 + near_x) * per_box, per_box)
                    runs.append((first + source_y * 4 + x, pl.ds(start, per_box)))

        def distances(box, rows_of):
            weights = geometry[pl.ds(pl.multiple_of(box * depth, depth), depth), :]
            return jnp.dot(targets[rows_of, :], weights, preferred_element_type=f32)

        ahead = distances(*runs[0])
        for i, (box, rows_of) in enumerate(runs):
            here = ahead
            if i + 1 < len(runs):
                ahead = distances(*runs[i + 1])
            inverse = lax.rsqrt(here)
            cubed = (inverse * inverse * inverse).astype(bf16)
            given = strengths[pl.ds(pl.multiple_of(box * per_box, per_box), per_box), :]
            total[rows_of, :] += jnp.dot(cubed, given, preferred_element_type=f32)
        if beside is not None:
            beside(item)
        return 0

    lax.fori_loop(0, 10, near_rows, 0)


def own_kernel(
    centres_s, counts_s, basis_ref, facets_ref, areas_ref, normals_ref, cross_ref, targets, planes, total,
    geometry, strengths, boxes_s
):
    boxes = counts_s.shape[0]
    krylov = basis_ref.shape[0]
    row = lax.broadcasted_iota(jnp.int32, (8, per_box), 0)
    origin, _ = slab_origin(centres_s)
    boxes_by_slot(centres_s, boxes_s)
    half = lax.axis_index("rhs")

    def source(slot, _):
        b = boxes_s[slot]
        lanes = pl.ds(pl.multiple_of(b * per_box, per_box), per_box)
        live = live_row(counts_s, b)
        weighted = basis_ref[krylov - 1, :, lanes] * (wide_row(areas_ref, b) * live / per_box)
        charges = jnp.concatenate([weighted.astype(bf16).astype(f32), wide_charges(cross_ref, slot * 16)], axis=0)
        store_source_features(padded(facets_ref[:, lanes] - origin), charges, slot, geometry, strengths)
        return 0

    lax.fori_loop(0, boxes, source, 0, unroll=2)

    def target(place, _):
        b = boxes_s[half * plane_boxes + place]
        lanes = pl.ds(pl.multiple_of(b * per_box, per_box), per_box)
        local = padded(facets_ref[:, lanes] - origin)
        normal = padded(normals_ref[:, lanes])
        square = jnp.sum(local * local, axis=0, keepdims=True) + soften
        along = jnp.sum(local * normal, axis=0, keepdims=True)
        distance = jnp.where(row == 3, 1.0, jnp.where(row == 4, square, -2.0 * local))
        high, middle, low = thirds(distance)
        rows = stacked_rows((high, middle, low, high, middle, high), per_box)
        start = pl.multiple_of(place * per_box, per_box)
        targets[pl.ds(start, per_box), :] = jnp.transpose(rows).astype(bf16)
        planes[pl.ds(pl.multiple_of(place * 8, 8), 8), :] = jnp.where(row == 3, along, normal)
        return 0

    lax.fori_loop(0, plane_boxes, target, 0, unroll=2)
    total[...] = jnp.zeros_like(total)
    near_planes((0, plane_boxes), geometry, strengths, targets, total)


def halo_kernel(
    centres_s, first_ref, second_ref, tail_ref, cross_ref, facets_ref, normals_ref, targets, planes, own_total,
    mine_ref, theirs_ref, geometry, strengths, total, far_halo, far_own, far_centres, boxes_s
):
    boxes = centres_s.shape[1]
    origin, base_z = slab_origin(centres_s)
    boxes_by_slot(centres_s, boxes_s)
    half = lax.axis_index("rhs")

    def source(place, _):
        tile = first_ref[pl.ds(pl.multiple_of(256 + place * 8, 8), 8), :]
        local = padded(jnp.concatenate([tile[0:3], tile[3:6]], axis=1) - origin)
        charges = jnp.concatenate([wide_charges(first_ref, place * 16), wide_charges(second_ref, place * 16)], axis=0)
        store_source_features(local, charges, place, geometry, strengths)
        return 0

    lax.fori_loop(0, plane_boxes, source, 0, unroll=2)
    total[...] = own_total[...]

    moments = []
    for group, (centres, mine, theirs) in enumerate(
        (
            (first_ref[392:400], first_ref[384:392], second_ref[256:264]),
            (tail_ref[8:16], tail_ref[:8], cross_ref[512:520]),
        )
    ):
        columns = jnp.transpose(centres)[:32]
        for a in range(3):
            shift = base_z if a == 2 else 1.5
            far_centres[(group * 3 + a) * 32 : (group * 3 + a + 1) * 32, :] = jnp.broadcast_to(
                columns[:, a : a + 1] - shift, (32, 128)
            )
        both = jnp.concatenate([mine, theirs], axis=0)
        high = both.astype(bf16).astype(f32)
        moments.append(jnp.concatenate([high, both - high], axis=0))
    lane = lax.broadcasted_iota(jnp.int32, (1, 128), 1)
    lane_x = lane & 3
    lane_y = (lane >> 2) & 3
    lane_plane = (lane >> 4) & 1

    def far_field(slot, group):
        b = boxes_s[slot]
        x, y, plane = slot & 3, (slot >> 2) & 3, slot >> 4
        lanes = pl.ds(pl.multiple_of(b * per_box, per_box), per_box)
        local = facets_ref[:, lanes] - origin
        normal = normals_ref[:, lanes]
        d = []
        for a in range(3):
            centre = far_centres[(group * 3 + a) * 32 : (group * 3 + a + 1) * 32, :]
            d.append(local[a : a + 1] - jnp.concatenate([centre, centre], axis=1))
        q = d[0] * d[0] + d[1] * d[1] + d[2] * d[2] + soften
        inverse = lax.rsqrt(q)
        inverse_2 = inverse * inverse
        inverse_3 = inverse_2 * inverse
        t = d[0] * normal[0:1] + d[1] * normal[1:2] + d[2] * normal[2:3]
        single = t * inverse_3
        steep = 3.0 * single * inverse_2
        coefficients = [single] + [steep * d[a] - normal[a : a + 1] * inverse_3 for a in range(3)]
        whole = jnp.concatenate(coefficients, axis=0)
        upper = whole.astype(bf16)
        lower = (whole - upper.astype(f32)).astype(bf16)
        lane_z = lane_plane + (4 * half - 2 if group == 0 else 0)
        near = (jnp.abs(lane_x - x) <= 1) & (jnp.abs(lane_y - y) <= 1) & (jnp.abs(lane_z - plane) <= 1)
        picked = jnp.where(near, 0.0, moments[group]).astype(bf16)
        first = jnp.dot(picked, upper, preferred_element_type=f32)
        second = jnp.dot(picked, lower, preferred_element_type=f32)
        return first[:16] + first[16:] + second[:16]

    def far_boxes(item):
        for k in range(4):
            slot = jnp.minimum(item * 4 + k, boxes - 1)
            far_halo[pl.ds(pl.multiple_of(slot * 16, 16), 16), :] = far_field(slot, 0)
        for k in range(2):
            place = jnp.minimum(item * 2 + k, plane_boxes - 1)
            far_own[pl.ds(pl.multiple_of(place * 16, 16), 16), :] = far_field(half * plane_boxes + place, 1)

    near_planes((0,), geometry, strengths, targets, total, far_boxes)

    def near_field(place, _):
        turned = jnp.transpose(total[pl.ds(pl.multiple_of(place * per_box, per_box), per_box), :])
        sums = turned[:64] + (turned[64:128] + turned[128:192])
        side = planes[pl.ds(pl.multiple_of(place * 8, 8), 8), :]
        value = side[3:4] * sums[:16] - side[0:1] * sums[16:32]
        value = value - side[1:2] * sums[32:48] - side[2:3] * sums[48:64]
        slot = half * plane_boxes + place
        rows = pl.ds(pl.multiple_of(slot * 16, 16), 16)
        far_halo[rows, :] += value + far_own[pl.ds(pl.multiple_of(place * 16, 16), 16), :]
        return 0

    lax.fori_loop(0, plane_boxes, near_field, 0, unroll=2)
    for slot in range(boxes):
        mine_ref[slot * 8 : slot * 8 + 8] = far_halo[slot * 16 : slot * 16 + 8]
        theirs_ref[slot * 8 : slot * 8 + 8] = far_halo[slot * 16 + 8 : slot * 16 + 16]


def gram_kernel(counts_s, basis_ref, sums_ref):
    krylov = basis_ref.shape[0]
    pairs = [(m, n) for m in range(krylov) for n in range(m + 1)]

    def one_box(b, carry):
        lanes = pl.ds(pl.multiple_of(b * per_box, per_box), per_box)
        live = live_row(counts_s, b)
        rows = [basis_ref[m, :, lanes] * live for m in range(krylov)]
        out = []
        for k, (m, n) in enumerate(pairs):
            product = rows[m] * rows[n]
            out.append(carry[k] + product[:, :128] + product[:, 128:])
        return tuple(out)

    zeros = jnp.zeros((8, 128), f32)
    gram = lax.fori_loop(0, counts_s.shape[0], one_box, (zeros,) * len(pairs))
    lane = lax.broadcasted_iota(jnp.int32, (8, 128), 1)
    total = zeros
    for k, value in enumerate(gram):
        total = jnp.where(lane == krylov + 1 + k, jnp.sum(value, axis=1, keepdims=True), total)
    sums_ref[...] = total


def image_kernel(centres_s, counts_s, mine_ref, theirs_ref, gram_ref, contrast_ref, basis_ref, image_ref, sums_ref):
    krylov = basis_ref.shape[0]

    def one_box(b, carry):
        lanes = pl.ds(pl.multiple_of(b * per_box, per_box), per_box)
        rows = pl.ds(pl.multiple_of(slot_of(centres_s, b) * 8, 8), 8)
        live = live_row(counts_s, b)
        part = mine_ref[rows, :] + theirs_ref[rows, :]
        image = live * (basis_ref[krylov - 1, :, lanes] - 2.0 * wide_row(contrast_ref, b) * part)
        image_ref[:, lanes] = image
        sums = []
        for m in range(krylov + 1):
            product = image * (basis_ref[m, :, lanes] if m < krylov else image)
            sums.append(carry[m] + product[:, :128] + product[:, 128:])
        return tuple(sums)

    zeros = jnp.zeros((8, 128), f32)
    sums = lax.fori_loop(0, counts_s.shape[0], one_box, (zeros,) * (krylov + 1), unroll=4)
    lane = lax.broadcasted_iota(jnp.int32, (8, 128), 1)
    total = gram_ref[...]
    for k, value in enumerate(sums):
        total = jnp.where(lane == k, jnp.sum(value, axis=1, keepdims=True), total)
    sums_ref[...] = jnp.broadcast_to(total[None], sums_ref.shape)


def two_sum(a, b):
    s = a + b
    c = s - a
    return s, (a - (s - c)) + (b - c)


def halves(a):
    c = a * 4097.0
    high = c - (c - a)
    return high, a - high


def two_product(a, b):
    p = a * b
    a_high, a_low = halves(a)
    b_high, b_low = halves(b)
    return p, ((a_high * b_high - p) + a_high * b_low + a_low * b_high) + a_low * b_low


def finish_kernel(total_facets, counts_s, tiles_ref, image_ref, basis_ref, next_ref, hessenberg_ref):
    boxes = counts_s.shape[0]
    krylov = basis_ref.shape[0]
    lane = lax.broadcasted_iota(jnp.int32, (8, 128), 1)

    def add_tile(i, carry):
        value, error = two_sum(carry[0], tiles_ref[i])
        return value, carry[1] + error

    sums, rest = lax.fori_loop(0, tiles_ref.shape[0], add_tile, (jnp.zeros((8, 128), f32),) * 2, unroll=8)
    exact = sums + rest
    projections = [exact[:, m : m + 1] / total_facets for m in range(krylov)]
    pairs = [(m, n) for m in range(krylov) for n in range(m + 1)]
    first = jnp.where(lane == krylov, 1.0, 0.0)
    second = jnp.where(lane <= krylov, 1.0, 0.0)
    for m in range(krylov):
        first = jnp.where(lane == m, -2.0 * projections[m], first)
    for k, (m, n) in enumerate(pairs):
        at = lane == krylov + 1 + k
        scale = 1.0 if m == n else 2.0
        first = jnp.where(at, scale * projections[m], first)
        second = jnp.where(at, projections[n], second)
    factor, factor_rest = two_product(first, second)
    value, value_rest = two_product(factor, sums)
    value_rest = value_rest + (factor * rest + factor_rest * sums)
    for shift in (64, 32, 16, 8, 4, 2, 1):
        other = pltpu.roll(value, shift, 1)
        other_rest = pltpu.roll(value_rest, shift, 1)
        value, error = two_sum(value, other)
        value_rest = (value_rest + other_rest) + error
    remaining = jnp.maximum(value + value_rest, 0.0)
    norm = jnp.sqrt(remaining / total_facets + epsilon)
    heads = jnp.where(lane == krylov, norm, 0.0)
    for m in range(krylov):
        heads = jnp.where(lane == m, projections[m], heads)
    hessenberg_ref[...] = heads[:, : krylov + 1]
    wide = [jnp.broadcast_to(p, (8, per_box)) for p in projections]
    scale = jnp.concatenate([1.0 / norm] * (per_box // 128), axis=1)

    def one_box(b, _):
        lanes = pl.ds(pl.multiple_of(b * per_box, per_box), per_box)
        live = live_row(counts_s, b)
        sent = wide[0] * basis_ref[0, :, lanes]
        for m in range(1, krylov):
            sent += wide[m] * basis_ref[m, :, lanes]
        next_ref[:, lanes] = (image_ref[:, lanes] - sent * live) * scale
        return 0

    lax.fori_loop(0, boxes, one_box, 0, unroll=4)


smem = pl.BlockSpec(memory_space=pltpu.SMEM)
vmem = pl.BlockSpec(memory_space=pltpu.VMEM)


def on_device(
    basis, facet_centres, normals, areas, contrast, facet_counts, box_centres, near_boxes, far_boxes
):
    krylov, rhs_local, facet_local = basis.shape
    boxes = facet_counts.shape[0]
    count = lax.axis_size("box")
    total_facets = count * facet_local
    areas = areas.reshape(-1, 128)
    contrast = contrast.reshape(-1, 128)

    def rows(number, width=128, dtype=f32):
        return jax.ShapeDtypeStruct((number, width), dtype)

    def limit(mebibytes):
        return pltpu.CompilerParams(vmem_limit_bytes=mebibytes * 1024 * 1024)

    cross, first, second, tail = pl.pallas_call(
        prep_kernel,
        out_shape=(rows(520), rows(400), rows(264), rows(16)),
        in_specs=[pl.BlockSpec(memory_space=pl.ANY)] * 5,
        out_specs=(vmem,) * 4,
        scratch_shapes=[
            pltpu.VMEM((512, 128), f32),
            pltpu.VMEM((256, 128), f32),
            pltpu.SMEM(box_centres.shape, f32),
            pltpu.SMEM(facet_counts.shape, jnp.int32),
            pltpu.VMEM((rhs_local, facet_local), f32),
            pltpu.VMEM(facet_centres.shape, f32),
            pltpu.VMEM(areas.shape, f32),
            pltpu.SemaphoreType.DMA((5,)),
        ],
        name="prepare",
    )(box_centres, facet_counts, basis, facet_centres, areas)
    swap = [(0, 1), (1, 0)]
    ups = range(count - 1)
    cross = lax.ppermute(cross, "rhs", swap)
    first = lax.ppermute(
        first, ("box", "rhs"), [(2 * i, 2 * i + 2) for i in ups] + [(2 * i + 3, 2 * i + 1) for i in ups]
    )
    second = lax.ppermute(
        second, ("box", "rhs"), [(2 * i + 1, 2 * i + 2) for i in ups] + [(2 * i + 2, 2 * i + 1) for i in ups]
    )
    plane_slots = plane_boxes * per_box
    targets, planes, own_total = pl.pallas_call(
        own_kernel,
        out_shape=(rows(plane_slots, depth, bf16), rows(plane_boxes * 8, per_box), rows(plane_slots, 256)),
        in_specs=[smem, smem] + [vmem] * 5,
        out_specs=(vmem,) * 3,
        scratch_shapes=[
            pltpu.VMEM((boxes * depth, per_box), bf16),
            pltpu.VMEM((boxes * per_box, 256), bf16),
            pltpu.SMEM((boxes,), jnp.int32),
        ],
        compiler_params=limit(24),
        name="own",
    )(box_centres, facet_counts, basis, facet_centres, areas, normals, cross)
    mine, theirs = pl.pallas_call(
        halo_kernel,
        out_shape=(rows(boxes * 8, per_box),) * 2,
        in_specs=[smem] + [vmem] * 9,
        out_specs=(vmem, vmem),
        scratch_shapes=[
            pltpu.VMEM((plane_boxes * depth, per_box), bf16),
            pltpu.VMEM((plane_slots, 256), bf16),
            pltpu.VMEM((plane_slots, 256), f32),
            pltpu.VMEM((boxes * 16, per_box), f32),
            pltpu.VMEM((plane_boxes * 16, per_box), f32),
            pltpu.VMEM((6 * 32, 128), f32),
            pltpu.SMEM((boxes,), jnp.int32),
        ],
        compiler_params=limit(24),
        name="halo",
    )(box_centres, first, second, tail, cross, facet_centres, normals, targets, planes, own_total)
    theirs = lax.ppermute(theirs, "rhs", swap)
    gram = pl.pallas_call(
        gram_kernel,
        out_shape=rows(8),
        in_specs=[smem, vmem],
        out_specs=vmem,
        compiler_params=limit(8),
        name="gram",
    )(facet_counts, basis)
    image, tiles = pl.pallas_call(
        image_kernel,
        out_shape=(rows(rhs_local, facet_local), jax.ShapeDtypeStruct((count, 8, 128), f32)),
        in_specs=[smem, smem] + [vmem] * 5,
        out_specs=(vmem, vmem),
        compiler_params=limit(8),
        name="image",
    )(box_centres, facet_counts, mine, theirs, gram, contrast, basis)
    tiles = lax.all_to_all(tiles, "box", 0, 0, tiled=True)
    next_vector, hessenberg = pl.pallas_call(
        functools.partial(finish_kernel, total_facets),
        out_shape=(
            jax.ShapeDtypeStruct((rhs_local, facet_local), f32),
            jax.ShapeDtypeStruct((rhs_local, krylov + 1), f32),
        ),
        in_specs=[smem] + [vmem] * 3,
        out_specs=(vmem, vmem),
        compiler_params=pltpu.CompilerParams(vmem_limit_bytes=16 * 1024 * 1024),
        name="finish",
    )(facet_counts, tiles, image, basis)
    return next_vector, hessenberg.T


def solution(mesh):
    return jax.shard_map(
        on_device,
        mesh=mesh,
        in_specs=(
            P(None, "rhs", "box"),
            P(None, "box"),
            P(None, "box"),
            P("box"),
            P("box"),
            P("box"),
            P(None, "box"),
            P("box", None),
            P("box", None),
        ),
        out_specs=(P("rhs", "box"), P(None, "rhs")),
        check_vma=False,
    )
```

time: 89.3 us -> 82.2 us (0.920)
  Pallas kernels: 67.7 us -> 46.8 us
  waiting for transfers between devices: 0.01 us -> 8.58 us
  local copies, waits for them, and re-layouts: 0.93 us -> 6.19 us
  blocking collectives: 16 us -> 12.5 us
  starting transfers between devices: 3.66 us -> 6.96 us
    pallas_call x3 -> x5, Pallas kernels: 65.6 us -> 44.6 us  [the longest x1 22.3 us: on_device(): pl.pallas_call(own_kernel, out_shape=(rows(plane_slots, depth, bf16), row...]
    ppermute x2 -> x4, waiting for transfers between devices: 0.01 us -> 8.58 us  [the longest x1 4.46 us: on_device(): cross = lax.ppermute(cross, 'rhs', swap)]
    unnamed x18, local copies, waits for them, and re-layouts: 0.93 us -> 6.19 us
    all_to_all x1, blocking collectives: 16 us -> 12.5 us  [on_device(): tiles = lax.all_to_all(tiles, 'box', 0, 0, tiled=True)]
    ppermute x2 -> x4, starting transfers between devices: 3.66 us -> 6.96 us  [the longest x1 3.03 us: on_device(): cross = lax.ppermute(cross, 'rhs', swap)]
  transfers between devices with their start and end apart: 2 -> 4, of which waited for: 0 -> 2; matrix products, arithmetic and copies ran while one was open for 0% -> 0% of each run, Pallas kernels for 37% -> 29%
where the time goes in v10:
time: 82.2 us; the launch traced here: 81.7 us
  Pallas kernels  46.8 us (57%)
  blocking collectives  12.5 us (15%)
  waiting for transfers between devices  8.58 us (10%)
  starting transfers between devices  6.96 us (8%)
  local copies, waits for them, and re-layouts  6.19 us (8%)
    pallas_call x1, Pallas kernels, on_device(): pl.pallas_call(own_kernel, out_shape=(rows(plane_slots, depth, bf16), row...  22.3 us
    pallas_call x1, Pallas kernels, on_device(): pl.pallas_call(halo_kernel, out_shape=(rows(boxes * 8, per_box),) * 2, in...  16.7 us
    all_to_all x1, blocking collectives, on_device(): tiles = lax.all_to_all(tiles, 'box', 0, 0, tiled=True)  12.5 us
    unnamed x18, local copies, waits for them, and re-layouts  6.19 us
    ppermute x1, waiting for transfers between devices, on_device(): cross = lax.ppermute(cross, 'rhs', swap)  4.46 us
    ppermute x1, waiting for transfers between devices, on_device(): theirs = lax.ppermute(theirs, 'rhs', swap)  4.11 us
    ppermute x1, starting transfers between devices, on_device(): cross = lax.ppermute(cross, 'rhs', swap)  3.03 us
    pallas_call x1, Pallas kernels, on_device(): pl.pallas_call(prep_kernel, out_shape=(rows(520), rows(400), rows(264), r...  2.76 us
  transfers between devices with their start and end apart: 4, of which 2 were waited for; matrix products, arithmetic and copies ran while one was open for 0% of the time, Pallas kernels for 29%

profile of v10, /device:TPU:0, one launch (start us, length us, event | category | flops | bytes accessed | tf_op | source)
XLA Modules:
  0.0 81.7 jit_solution(14678439548568801598)
XLA Ops:
  0.6 2.8 %prepare.1 = (f32[520,128]{1,0:T(8,128)}, f32[400,128]{1,0:T(8,128)}, f32[264,128]{1,0:T(8,128)}, f32[16,128]{1,0:T(8,128)}) custom-call(f32[3,32]{1,0:T(4,128)} %centres_s.5, s32[32]{0:T(128)} %counts_s.7, f32[8,8,8192]{2,1,0:T(8,128)} %basis_ref.7, f32[3,8192]{1,0:T(4,128)} %facets_ref.3, f32[64,128]{1,0:T(8,128)} %bitcast.3), custom_call_target="tpu_custom_call" | custom-call | tf_op jit(solution)/shard_map/prepare/pallas_call | solution.py:450
  3.4 3.0 %collective-permute-start.2 = (f32[520,128]{1,0:T(8,128)}, f32[520,128]{1,0:T(8,128)S(1)}, u32[]{:S(2)}, u32[]{:S(2)}) collective-permute-start(f32[520,128]{1,0:T(8,128)} %get-tuple-element.18), channel_id=1, source_target_pairs={{0,1},{1,0},{2,3},{3,2},{4,5},{5,4},{6,7},{7,6},{8,9},{9,8},{10,11... | collective-permute-start | bytes 798728 | tf_op jit(solution)/shard_map/ppermute | solution.py:469
  6.4 1.5 %collective-permute-start = (f32[400,128]{1,0:T(8,128)}, f32[400,128]{1,0:T(8,128)S(1)}, u32[]{:S(2)}, u32[]{:S(2)}) collective-permute-start(f32[400,128]{1,0:T(8,128)} %get-tuple-element.15), channel_id=1, source_target_pairs={{0,2},{2,4},{4,6},{6,8},{8,10},{10,12},{12,14},{14,16},{16,18},{18... | collective-permute-start | bytes 614408 | tf_op jit(solution)/shard_map/ppermute | solution.py:470
  7.9 0.7 collective-permute-start.1
  8.6 4.5 %collective-permute-done.2.cross_ref = f32[520,128]{1,0:T(8,128)S(1)} collective-permute-done((f32[520,128]{1,0:T(8,128)}, f32[520,128]{1,0:T(8,128)S(1)}, u32[]{:S(2)}, u32[]{:S(2)}) %collective-permute-start.2) | collective-permute-done | bytes 266272 | tf_op jit(solution)/shard_map/ppermute | solution.py:469
  13.0 0.0 copy-start
  13.0 1.6 %copy-done = f32[8,8,8192]{2,1,0:T(8,128)S(1)} copy-done((f32[8,8,8192]{2,1,0:T(8,128)S(1)}, f32[8,8,8192]{2,1,0:T(8,128)}, u32[]{:S(2)}) %copy-start) | copy-done | bytes 2097176
  14.6 0.0 copy-start.2
  14.6 0.9 %copy-done.2 = f32[3,8192]{1,0:T(4,128)S(1)} copy-done((f32[3,8192]{1,0:T(4,128)S(1)}, f32[3,8192]{1,0:T(4,128)}, u32[]{:S(2)}) %copy-start.2) | copy-done | bytes 98328
  15.5 0.0 copy-start.3
  15.5 0.9 %copy-done.3 = f32[3,8192]{1,0:T(4,128)S(1)} copy-done((f32[3,8192]{1,0:T(4,128)S(1)}, f32[3,8192]{1,0:T(4,128)}, u32[]{:S(2)}) %copy-start.3) | copy-done | bytes 98328
  16.4 0.0 copy-start.4
  16.4 0.8 copy-done.4
  17.2 0.0 copy-start.6
  17.2 0.7 copy-done.6
  17.9 0.0 copy-start.7
  17.9 0.7 copy-done.7
  18.5 0.0 copy-start.1
  18.5 22.3 %own.1 = (bf16[4096,128]{1,0:T(8,128)(2,1)S(1)}, f32[128,256]{1,0:T(8,128)S(1)}, f32[4096,256]{1,0:T(8,128)S(1)}) custom-call(f32[3,32]{1,0:T(4,128)S(1)} %copy-done.6, s32[32]{0:T(128)S(1)} %copy-done.7, f32[8,8,8192]{2,1,0:T(8,128)S(1)} %copy-done, f32[3,8192]{1,0:T(4,128)S(1)} %copy-done.2, f32[64,128]{1,0:T(8,128)S(1)} %bitcast.4, ...), custom_call_target="tpu_custom_call" | custom-call | tf_op jit(solution)/shard_map/own/pallas_call | solution.py:477
  40.9 0.0 copy-start.5
  40.9 0.0 collective-permute-done.1.second_ref
  40.9 0.0 collective-permute-done.first_ref
  40.9 0.0 copy-start.8
  40.9 0.7 copy-done.8
  41.6 16.7 %halo.1 = (f32[256,256]{1,0:T(8,128)S(1)}, f32[256,256]{1,0:T(8,128)S(1)}) custom-call(f32[3,32]{1,0:T(4,128)S(1)} %copy-done.6, f32[400,128]{1,0:T(8,128)S(1)} %collective-permute-done.first_ref, f32[264,128]{1,0:T(8,128)S(1)} %collective-permute-done.1.second_ref, f32[16,128]{1,0:T(8,128)S(1)} %copy-done.8, ...), custom_call_target="tpu_custom_call" | custom-call | tf_op jit(solution)/shard_map/halo/pallas_call | solution.py:490
  58.3 1.8 %collective-permute-start.3 = (f32[256,256]{1,0:T(8,128)S(1)}, f32[256,256]{1,0:T(8,128)S(1)}, u32[]{:S(2)}, u32[]{:S(2)}) collective-permute-start(f32[256,256]{1,0:T(8,128)S(1)} %get-tuple-element.23), channel_id=1, source_target_pairs={{0,1},{1,0},{2,3},{3,2},{4,5},{5,4},{6,7},{7,6},{8,9},{9,8},{10,11... | collective-permute-start | bytes 786440 | tf_op jit(solution)/shard_map/ppermute | solution.py:507
  60.1 0.0 copy-done.1
  60.1 1.7 %gram.1.gram_ref = f32[8,128]{1,0:T(8,128)S(1)} custom-call(s32[32]{0:T(128)S(1)} %copy-done.7, f32[8,8,8192]{2,1,0:T(8,128)S(1)} %copy-done.1), custom_call_target="tpu_custom_call" | custom-call | tf_op jit(solution)/shard_map/gram/pallas_call | solution.py:508
  61.8 4.1 %collective-permute-done.3.theirs_ref = f32[256,256]{1,0:T(8,128)S(1)} collective-permute-done((f32[256,256]{1,0:T(8,128)S(1)}, f32[256,256]{1,0:T(8,128)S(1)}, u32[]{:S(2)}, u32[]{:S(2)}) %collective-permute-start.3) | collective-permute-done | bytes 262176 | tf_op jit(solution)/shard_map/ppermute | solution.py:507
  65.9 0.0 copy-done.5
  65.9 1.2 %image.1 = (f32[8,8192]{1,0:T(8,128)S(1)}, f32[16,8,128]{2,1,0:T(8,128)S(1)}) custom-call(f32[3,32]{1,0:T(4,128)S(1)} %copy-done.6, s32[32]{0:T(128)S(1)} %copy-done.7, f32[256,256]{1,0:T(8,128)S(1)} %get-tuple-element.22.mine_ref, f32[256,256]{1,0:T(8,128)S(1)} %collective-permute-done.3.theirs_ref, f32[8,128]{1,0:T(8,128)S(1)} %gram.1.gram_ref, ...), custom_call_target="tpu_custom_call" | custom-call | tf_op jit(solution)/shard_map/image/pallas_call | solution.py:516
  67.1 12.5 %all_to_all.5.tiles_ref = f32[16,8,128]{2,1,0:T(8,128)S(1)} all-to-all(f32[16,8,128]{2,1,0:T(8,128)S(1)} %get-tuple-element.24), channel_id=1, replica_groups=mesh['box'=16,'rhs'=2] {'box'}, dimensions={0} | all-to-all | bytes 131072 | tf_op jit(solution)/shard_map/all_to_all | solution.py:524
  79.6 2.1 %finish.1 = (f32[8,8192]{1,0:T(8,128)}, f32[8,9]{1,0:T(8,128)}) custom-call(s32[32]{0:T(128)S(1)} %copy-done.7, f32[16,8,128]{2,1,0:T(8,128)S(1)} %all_to_all.5.tiles_ref, f32[8,8192]{1,0:T(8,128)S(1)} %get-tuple-element.25.image_ref, f32[8,8,8192]{2,1,0:T(8,128)S(1)} %copy-done.1), custom_call_target="tpu_custom_call" | custom-call | tf_op jit(solution)/shard_map/finish/pallas_call | solution.py:525
Async XLA Ops:
  3.4 9.6 %collective-permute-start.2 = (f32[520,128]{1,0:T(8,128)}, f32[520,128]{1,0:T(8,128)S(1)}, u32[]{:S(2)}, u32[]{:S(2)}) collective-permute-start(f32[520,128]{1,0:T(8,128)} %get-tuple-element.18), channel_id=1, source_target_pairs={{0,1},{1,0},{2,3},{3,2},{4,5},{5,4},{6,7},{7,6},{8,9},{9,8},{10,11... | collective-permute-start | bytes 798728 | tf_op jit(solution)/shard_map/ppermute | solution.py:469
  6.4 34.5 %collective-permute-start = (f32[400,128]{1,0:T(8,128)}, f32[400,128]{1,0:T(8,128)S(1)}, u32[]{:S(2)}, u32[]{:S(2)}) collective-permute-start(f32[400,128]{1,0:T(8,128)} %get-tuple-element.15), channel_id=1, source_target_pairs={{0,2},{2,4},{4,6},{6,8},{8,10},{10,12},{12,14},{14,16},{16,18},{18... | collective-permute-start | bytes 614408 | tf_op jit(solution)/shard_map/ppermute | solution.py:470
  7.9 33.0 %collective-permute-start.1 = (f32[264,128]{1,0:T(8,128)}, f32[264,128]{1,0:T(8,128)S(1)}, u32[]{:S(2)}, u32[]{:S(2)}) collective-permute-start(f32[264,128]{1,0:T(8,128)} %get-tuple-element.16), channel_id=1, source_target_pairs={{1,2},{3,4},{5,6},{7,8},{9,10},{11,12},{13,14},{15,16},{17,18},{19... | collective-permute-start | bytes 405512 | tf_op jit(solution)/shard_map/ppermute | solution.py:473
  13.0 1.6 %copy-start = (f32[8,8,8192]{2,1,0:T(8,128)S(1)}, f32[8,8,8192]{2,1,0:T(8,128)}, u32[]{:S(2)}) copy-start(f32[8,8,8192]{2,1,0:T(8,128)} %basis_ref.7) | copy-start | bytes 6291460
  14.6 0.9 %copy-start.2 = (f32[3,8192]{1,0:T(4,128)S(1)}, f32[3,8192]{1,0:T(4,128)}, u32[]{:S(2)}) copy-start(f32[3,8192]{1,0:T(4,128)} %facets_ref.3) | copy-start | bytes 294916
  15.5 0.9 %copy-start.3 = (f32[3,8192]{1,0:T(4,128)S(1)}, f32[3,8192]{1,0:T(4,128)}, u32[]{:S(2)}) copy-start(f32[3,8192]{1,0:T(4,128)} %normals_ref.3) | copy-start | bytes 294916
  16.4 0.8 copy-start.4
  17.2 0.7 copy-start.6
  17.9 0.7 copy-start.7
  18.5 41.6 %copy-start.1 = (f32[8,8,8192]{2,1,0:T(8,128)S(1)}, f32[8,8,8192]{2,1,0:T(8,128)}, u32[]{:S(2)}) copy-start(f32[8,8,8192]{2,1,0:T(8,128)} %basis_ref.7) | copy-start | bytes 6291460
  40.9 25.0 %copy-start.5 = (f32[8192]{0:T(1024)S(1)}, f32[8192]{0:T(1024)}, u32[]{:S(2)}) copy-start(f32[8192]{0:T(1024)} %param.13) | copy-start | bytes 98308
  40.9 0.7 copy-start.8
  58.3 7.6 %collective-permute-start.3 = (f32[256,256]{1,0:T(8,128)S(1)}, f32[256,256]{1,0:T(8,128)S(1)}, u32[]{:S(2)}, u32[]{:S(2)}) collective-permute-start(f32[256,256]{1,0:T(8,128)S(1)} %get-tuple-element.23), channel_id=1, source_target_pairs={{0,1},{1,0},{2,3},{3,2},{4,5},{5,4},{6,7},{7,6},{8,9},{9,8},{10,11... | collective-permute-start | bytes 786440 | tf_op jit(solution)/shard_map/ppermute | solution.py:507

commit v11 on v10

--- a/solution.py
+++ b/solution.py
@@ -28,14 +28,6 @@
     return (z & 1) * plane_boxes + y * 4 + x
 
 
-def boxes_by_slot(centres_s, boxes_s):
-    def one_box(b, _):
-        boxes_s[slot_of(centres_s, b)] = b
-        return 0
-
-    lax.fori_loop(0, centres_s.shape[1], one_box, 0)
-
-
 def wide_row(ref, b):
     return jnp.concatenate([ref[pl.ds(2 * b, 1), :], ref[pl.ds(2 * b + 1, 1), :]], axis=1)
 
@@ -46,14 +38,15 @@
 
 
 def prep_kernel(
-    centres_h, counts_h, basis_h, facets_h, areas_h, cross_ref, first_ref, second_ref, tail_ref,
-    charges_v, places_v, centres_s, counts_s, current_ref, facets_ref, areas_ref, arrived
+    centres_h, counts_h, basis_h, facets_h, areas_h, normals_h, cross_ref, first_ref, second_ref, local_ref,
+    charges_v, centres_s, counts_s, current_ref, facets_ref, areas_ref, normals_ref, arrived
 ):
     boxes = counts_s.shape[0]
     moves = [
         (basis_h.at[basis_h.shape[0] - 1], current_ref),
         (facets_h, facets_ref),
         (areas_h, areas_ref),
+        (normals_h, normals_ref),
         (centres_h, centres_s),
         (counts_h, counts_s),
     ]
@@ -64,20 +57,20 @@
         copy.wait()
     lane = lax.broadcasted_iota(jnp.int32, (8, 128), 1)
     row = lax.broadcasted_iota(jnp.int32, (8, 128), 0)
+    empty = jnp.zeros((2, 128), f32)
 
     def one_box(b, carry):
         moments, centres = carry
         slot = slot_of(centres_s, b)
         lanes = pl.ds(pl.multiple_of(b * per_box, per_box), per_box)
         facets = facets_ref[:, lanes]
+        normals = normals_ref[:, lanes]
         live = live_row(counts_s, b)
         weighted = current_ref[:, lanes] * (wide_row(areas_ref, b) * live / per_box)
-        charges = weighted.astype(bf16).astype(f32)
         start = pl.multiple_of(slot * 16, 16)
-        charges_v[pl.ds(start, 8), :] = charges[:, :128]
-        charges_v[pl.ds(start + 8, 8), :] = charges[:, 128:]
-        places_v[pl.ds(pl.multiple_of(slot * 8, 8), 8), :] = jnp.concatenate(
-            [facets[:, :128], facets[:, 128:], jnp.zeros((2, 128), f32)], axis=0
+        charges_v[pl.ds(start, 16), :] = jnp.concatenate([weighted[:, :128], weighted[:, 128:]], axis=0)
+        local_ref[pl.ds(start, 16), :] = jnp.concatenate(
+            [facets[:, :128], facets[:, 128:], empty, normals[:, :128], normals[:, 128:], empty], axis=0
         )
         moments += jnp.where(lane == slot, jnp.sum(weighted, axis=1, keepdims=True), 0.0)
         for a in range(3):
@@ -88,17 +81,24 @@
 
     zeros = jnp.zeros((8, 128), f32)
     moments, centres = lax.fori_loop(0, boxes, one_box, (zeros, zeros), unroll=4)
+    _, _, z = lattice(centres_s, 0)
+    base_z = (z - (z & 1)).astype(f32) + 0.5
+    centres = jnp.where((row == 3) | (row == 4), 1.5, jnp.where(row == 5, base_z, centres))
     half = lax.axis_index("rhs")
-    cross_ref[:512] = charges_v[...]
-    cross_ref[512:] = moments
-    first_ref[:256] = charges_v[pl.ds(pl.multiple_of((1 - half) * 256, 256), 256), :]
-    first_ref[256:384] = places_v[pl.ds(pl.multiple_of((1 - half) * 128, 128), 128), :]
+    away = pl.multiple_of((1 - half) * 256, 256)
+    here = pl.multiple_of(half * 256, 256)
+    pieces = jnp.concatenate([*thirds(moments), zeros], axis=0).astype(bf16)
+    cross_ref[:512] = charges_v[...].astype(bf16)
+    cross_ref[512:] = pieces
+    second_ref[:256] = charges_v[pl.ds(here, 256), :].astype(bf16)
+    second_ref[256:] = pieces
+    first_ref[:256] = charges_v[pl.ds(away, 256), :].astype(bf16).astype(f32)
+    for place in range(plane_boxes):
+        first_ref[256 + 8 * place : 264 + 8 * place] = local_ref[pl.ds(away + 16 * place, 8), :]
     first_ref[384:392] = moments
     first_ref[392:] = centres
-    second_ref[:256] = charges_v[pl.ds(pl.multiple_of(half * 256, 256), 256), :]
-    second_ref[256:] = moments
-    tail_ref[:8] = moments
-    tail_ref[8:] = centres
+    local_ref[512:520] = moments
+    local_ref[520:] = centres
 
 
 def thirds(x):
@@ -113,20 +113,22 @@
     return jnp.concatenate([*parts, zeros], axis=0)
 
 
-def slab_origin(centres_s):
-    _, _, z = lattice(centres_s, 0)
-    base_z = (z - (z & 1)).astype(f32) + 0.5
-    axis_row = lax.broadcasted_iota(jnp.int32, (3, 1), 0)
-    return jnp.where(axis_row == 2, base_z, 1.5), base_z
-
-
 def padded(rows):
     return jnp.concatenate([rows, jnp.zeros((8 - rows.shape[0], rows.shape[1]), f32)], axis=0)
 
 
-def wide_charges(ref, start):
-    start = pl.multiple_of(start, 16)
-    return jnp.concatenate([ref[pl.ds(start, 8), :], ref[pl.ds(start + 8, 8), :]], axis=1)
+def wide_charges(ref, place):
+    both = ref[pl.ds(pl.multiple_of(place * 16, 16), 16), :].astype(f32)
+    return jnp.concatenate([both[:8], both[8:]], axis=1)
+
+
+def wide_tile(ref, start):
+    tile = ref[pl.ds(pl.multiple_of(start, 8), 8), :]
+    return jnp.concatenate([tile[0:3], tile[3:6]], axis=1)
+
+
+def whole_moments(pieces):
+    return pieces[:8] + (pieces[8:16] + pieces[16:24])
 
 
 def store_source_features(local, charges, box, geometry, strengths):
@@ -138,7 +140,7 @@
     geometry[pl.ds(pl.multiple_of(box * depth, depth), depth), :] = rows.astype(bf16)
     products = jnp.concatenate([charges] + [charges * local[a : a + 1] for a in range(3)], axis=0)
     rows = jnp.concatenate([*thirds(products), jnp.zeros((64, per_box), f32)], axis=0)
-    strengths[pl.ds(pl.multiple_of(box * per_box, per_box), per_box), :] = jnp.transpose(rows).astype(bf16)
+    strengths[pl.ds(pl.multiple_of(box * 256, 256), 256), :] = rows.astype(bf16)
 
 
 def near_planes(sources, geometry, strengths, targets, total, beside=None):
@@ -163,8 +165,10 @@
                 ahead = distances(*runs[i + 1])
             inverse = lax.rsqrt(here)
             cubed = (inverse * inverse * inverse).astype(bf16)
-            given = strengths[pl.ds(pl.multiple_of(box * per_box, per_box), per_box), :]
-            total[rows_of, :] += jnp.dot(cubed, given, preferred_element_type=f32)
+            given = strengths[pl.ds(pl.multiple_of(box * 256, 256), 256), :]
+            total[rows_of, :] += lax.dot_general(
+                cubed, given, (((1,), (1,)), ((), ())), preferred_element_type=f32
+            )
         if beside is not None:
             beside(item)
         return 0
@@ -172,33 +176,35 @@
     lax.fori_loop(0, 10, near_rows, 0)
 
 
-def own_kernel(
-    centres_s, counts_s, basis_ref, facets_ref, areas_ref, normals_ref, cross_ref, targets, planes, total,
-    geometry, strengths, boxes_s
+def field_kernel(
+    local_ref, sent_ref, cross_ref, first_ref, second_ref, mine_ref, theirs_ref,
+    geometry, strengths, targets, planes, total, far_halo, far_own, far_centres
 ):
-    boxes = counts_s.shape[0]
-    krylov = basis_ref.shape[0]
+    boxes = 2 * plane_boxes
+    half = lax.axis_index("rhs")
+    origin = local_ref[523:526, 0:1]
     row = lax.broadcasted_iota(jnp.int32, (8, per_box), 0)
-    origin, _ = slab_origin(centres_s)
-    boxes_by_slot(centres_s, boxes_s)
-    half = lax.axis_index("rhs")
 
     def source(slot, _):
-        b = boxes_s[slot]
-        lanes = pl.ds(pl.multiple_of(b * per_box, per_box), per_box)
-        live = live_row(counts_s, b)
-        weighted = basis_ref[krylov - 1, :, lanes] * (wide_row(areas_ref, b) * live / per_box)
-        charges = jnp.concatenate([weighted.astype(bf16).astype(f32), wide_charges(cross_ref, slot * 16)], axis=0)
-        store_source_features(padded(facets_ref[:, lanes] - origin), charges, slot, geometry, strengths)
+        local = padded(wide_tile(local_ref, slot * 16) - origin)
+        charges = jnp.concatenate([wide_charges(sent_ref, slot), wide_charges(cross_ref, slot)], axis=0)
+        store_source_features(local, charges, slot, geometry, strengths)
         return 0
 
     lax.fori_loop(0, boxes, source, 0, unroll=2)
 
+    def halo_source(place, _):
+        local = padded(wide_tile(first_ref, 256 + place * 8) - origin)
+        charges = jnp.concatenate([wide_charges(first_ref, place), wide_charges(second_ref, place)], axis=0)
+        store_source_features(local, charges, boxes + place, geometry, strengths)
+        return 0
+
+    lax.fori_loop(0, plane_boxes, halo_source, 0, unroll=2)
+
     def target(place, _):
-        b = boxes_s[half * plane_boxes + place]
-        lanes = pl.ds(pl.multiple_of(b * per_box, per_box), per_box)
-        local = padded(facets_ref[:, lanes] - origin)
-        normal = padded(normals_ref[:, lanes])
+        start = (half * plane_boxes + place) * 16
+        local = padded(wide_tile(local_ref, start) - origin)
+        normal = padded(wide_tile(local_ref, start + 8))
         square = jnp.sum(local * local, axis=0, keepdims=True) + soften
         along = jnp.sum(local * normal, axis=0, keepdims=True)
         distance = jnp.where(row == 3, 1.0, jnp.where(row == 4, square, -2.0 * local))
@@ -211,42 +217,20 @@
 
     lax.fori_loop(0, plane_boxes, target, 0, unroll=2)
     total[...] = jnp.zeros_like(total)
-    near_planes((0, plane_boxes), geometry, strengths, targets, total)
-
-
-def halo_kernel(
-    centres_s, first_ref, second_ref, tail_ref, cross_ref, facets_ref, normals_ref, targets, planes, own_total,
-    mine_ref, theirs_ref, geometry, strengths, total, far_halo, far_own, far_centres, boxes_s
-):
-    boxes = centres_s.shape[1]
-    origin, base_z = slab_origin(centres_s)
-    boxes_by_slot(centres_s, boxes_s)
-    half = lax.axis_index("rhs")
-
-    def source(place, _):
-        tile = first_ref[pl.ds(pl.multiple_of(256 + place * 8, 8), 8), :]
-        local = padded(jnp.concatenate([tile[0:3], tile[3:6]], axis=1) - origin)
-        charges = jnp.concatenate([wide_charges(first_ref, place * 16), wide_charges(second_ref, place * 16)], axis=0)
-        store_source_features(local, charges, place, geometry, strengths)
-        return 0
-
-    lax.fori_loop(0, plane_boxes, source, 0, unroll=2)
-    total[...] = own_total[...]
 
     moments = []
     for group, (centres, mine, theirs) in enumerate(
         (
-            (first_ref[392:400], first_ref[384:392], second_ref[256:264]),
-            (tail_ref[8:16], tail_ref[:8], cross_ref[512:520]),
+            (first_ref[392:400], first_ref[384:392], second_ref[256:288]),
+            (local_ref[520:528], local_ref[512:520], cross_ref[512:544]),
         )
     ):
-        columns = jnp.transpose(centres)[:32]
+        columns = jnp.transpose(jnp.concatenate([centres[:3] - origin, centres[3:]], axis=0))[:32]
         for a in range(3):
-            shift = base_z if a == 2 else 1.5
             far_centres[(group * 3 + a) * 32 : (group * 3 + a + 1) * 32, :] = jnp.broadcast_to(
-                columns[:, a : a + 1] - shift, (32, 128)
+                columns[:, a : a + 1], (32, 128)
             )
-        both = jnp.concatenate([mine, theirs], axis=0)
+        both = jnp.concatenate([mine, whole_moments(theirs.astype(f32))], axis=0)
         high = both.astype(bf16).astype(f32)
         moments.append(jnp.concatenate([high, both - high], axis=0))
     lane = lax.broadcasted_iota(jnp.int32, (1, 128), 1)
@@ -255,11 +239,9 @@
     lane_plane = (lane >> 4) & 1
 
     def far_field(slot, group):
-        b = boxes_s[slot]
         x, y, plane = slot & 3, (slot >> 2) & 3, slot >> 4
-        lanes = pl.ds(pl.multiple_of(b * per_box, per_box), per_box)
-        local = facets_ref[:, lanes] - origin
-        normal = normals_ref[:, lanes]
+        local = wide_tile(local_ref, slot * 16) - origin
+        normal = wide_tile(local_ref, slot * 16 + 8)
         d = []
         for a in range(3):
             centre = far_centres[(group * 3 + a) * 32 : (group * 3 + a + 1) * 32, :]
@@ -290,7 +272,7 @@
             place = jnp.minimum(item * 2 + k, plane_boxes - 1)
             far_own[pl.ds(pl.multiple_of(place * 16, 16), 16), :] = far_field(half * plane_boxes + place, 1)
 
-    near_planes((0,), geometry, strengths, targets, total, far_boxes)
+    near_planes((0, plane_boxes, 2 * plane_boxes), geometry, strengths, targets, total, far_boxes)
 
     def near_field(place, _):
         turned = jnp.transpose(total[pl.ds(pl.multiple_of(place * per_box, per_box), per_box), :])
@@ -447,26 +429,26 @@
     def limit(mebibytes):
         return pltpu.CompilerParams(vmem_limit_bytes=mebibytes * 1024 * 1024)
 
-    cross, first, second, tail = pl.pallas_call(
+    sent, first, second, local = pl.pallas_call(
         prep_kernel,
-        out_shape=(rows(520), rows(400), rows(264), rows(16)),
-        in_specs=[pl.BlockSpec(memory_space=pl.ANY)] * 5,
+        out_shape=(rows(544, dtype=bf16), rows(400), rows(288, dtype=bf16), rows(528)),
+        in_specs=[pl.BlockSpec(memory_space=pl.ANY)] * 6,
         out_specs=(vmem,) * 4,
         scratch_shapes=[
             pltpu.VMEM((512, 128), f32),
-            pltpu.VMEM((256, 128), f32),
             pltpu.SMEM(box_centres.shape, f32),
             pltpu.SMEM(facet_counts.shape, jnp.int32),
             pltpu.VMEM((rhs_local, facet_local), f32),
             pltpu.VMEM(facet_centres.shape, f32),
             pltpu.VMEM(areas.shape, f32),
-            pltpu.SemaphoreType.DMA((5,)),
+            pltpu.VMEM(normals.shape, f32),
+            pltpu.SemaphoreType.DMA((6,)),
         ],
         name="prepare",
-    )(box_centres, facet_counts, basis, facet_centres, areas)
+    )(box_centres, facet_counts, basis, facet_centres, areas, normals)
     swap = [(0, 1), (1, 0)]
     ups = range(count - 1)
-    cross = lax.ppermute(cross, "rhs", swap)
+    cross = lax.ppermute(sent, "rhs", swap)
     first = lax.ppermute(
         first, ("box", "rhs"), [(2 * i, 2 * i + 2) for i in ups] + [(2 * i + 3, 2 * i + 1) for i in ups]
     )
@@ -474,36 +456,24 @@
         second, ("box", "rhs"), [(2 * i + 1, 2 * i + 2) for i in ups] + [(2 * i + 2, 2 * i + 1) for i in ups]
     )
     plane_slots = plane_boxes * per_box
-    targets, planes, own_total = pl.pallas_call(
-        own_kernel,
-        out_shape=(rows(plane_slots, depth, bf16), rows(plane_boxes * 8, per_box), rows(plane_slots, 256)),
-        in_specs=[smem, smem] + [vmem] * 5,
-        out_specs=(vmem,) * 3,
-        scratch_shapes=[
-            pltpu.VMEM((boxes * depth, per_box), bf16),
-            pltpu.VMEM((boxes * per_box, 256), bf16),
-            pltpu.SMEM((boxes,), jnp.int32),
-        ],
-        compiler_params=limit(24),
-        name="own",
-    )(box_centres, facet_counts, basis, facet_centres, areas, normals, cross)
     mine, theirs = pl.pallas_call(
-        halo_kernel,
+        field_kernel,
         out_shape=(rows(boxes * 8, per_box),) * 2,
-        in_specs=[smem] + [vmem] * 9,
+        in_specs=[vmem] * 5,
         out_specs=(vmem, vmem),
         scratch_shapes=[
-            pltpu.VMEM((plane_boxes * depth, per_box), bf16),
-            pltpu.VMEM((plane_slots, 256), bf16),
+            pltpu.VMEM((3 * plane_boxes * depth, per_box), bf16),
+            pltpu.VMEM((3 * plane_boxes * 256, per_box), bf16),
+            pltpu.VMEM((plane_slots, depth), bf16),
+            pltpu.VMEM((plane_boxes * 8, per_box), f32),
             pltpu.VMEM((plane_slots, 256), f32),
             pltpu.VMEM((boxes * 16, per_box), f32),
             pltpu.VMEM((plane_boxes * 16, per_box), f32),
             pltpu.VMEM((6 * 32, 128), f32),
-            pltpu.SMEM((boxes,), jnp.int32),
         ],
-        compiler_params=limit(24),
-        name="halo",
-    )(box_centres, first, second, tail, cross, facet_centres, normals, targets, planes, own_total)
+        compiler_params=limit(60),
+        name="fields",
+    )(local, sent, cross, first, second)
     theirs = lax.ppermute(theirs, "rhs", swap)
     gram = pl.pallas_call(
         gram_kernel,

time: 82.2 us -> 75 us (0.912)
  local copies, waits for them, and re-layouts: 6.19 us -> 0.77 us
  Pallas kernels: 46.8 us -> 42 us
  blocking collectives: 12.5 us -> 14.6 us
  starting transfers between devices: 6.96 us -> 8.32 us
    unnamed x18 -> x16, local copies, waits for them, and re-layouts: 6.19 us -> 0.77 us
    pallas_call x3 -> x2, Pallas kernels: 41.8 us -> 37 us  [the longest x1 34 us: on_device(): pl.pallas_call(field_kernel, out_shape=(rows(boxes * 8, per_box),) * 2, i...]
    all_to_all x1, blocking collectives: 12.5 us -> 14.6 us  [on_device(): tiles = lax.all_to_all(tiles, 'box', 0, 0, tiled=True)]
    ppermute x1, starting transfers between devices: 1.8 us -> 3.35 us  [on_device(): theirs = lax.ppermute(theirs, 'rhs', swap)]
    ppermute x1, starting transfers between devices: 3.03 us -> 1.96 us  [on_device(): cross = lax.ppermute(sent, 'rhs', swap)]
    ppermute x1, waiting for transfers between devices: 4.46 us -> 3.54 us  [on_device(): cross = lax.ppermute(sent, 'rhs', swap)]
    ppermute x1, starting transfers between devices: 1.46 us -> 2.37 us  [on_device(): lax.ppermute(first, ('box', 'rhs'), [(2 * i, 2 * i + 2) for i in ups] + [...]
  transfers between devices with their start and end apart: 4 -> 4, of which waited for: 2 -> 2; matrix products, arithmetic and copies ran while one was open for 0% -> 0% of each run, Pallas kernels for 29% -> 2%
where the time goes in v11:
time: 75 us; the launch traced here: 74.7 us
  Pallas kernels  42 us (56%)
  blocking collectives  14.6 us (19%)
  starting transfers between devices  8.32 us (11%)
  waiting for transfers between devices  8.27 us (11%)
  local copies, waits for them, and re-layouts  0.77 us (1%)
    pallas_call x1, Pallas kernels, on_device(): pl.pallas_call(field_kernel, out_shape=(rows(boxes * 8, per_box),) * 2, i...  34 us
    all_to_all x1, blocking collectives, on_device(): tiles = lax.all_to_all(tiles, 'box', 0, 0, tiled=True)  14.6 us
    ppermute x1, waiting for transfers between devices, on_device(): theirs = lax.ppermute(theirs, 'rhs', swap)  4.73 us
    ppermute x1, waiting for transfers between devices, on_device(): cross = lax.ppermute(sent, 'rhs', swap)  3.54 us
    ppermute x1, starting transfers between devices, on_device(): theirs = lax.ppermute(theirs, 'rhs', swap)  3.35 us
    pallas_call x1, Pallas kernels, on_device(): pl.pallas_call(prep_kernel, out_shape=(rows(544, dtype=bf16), rows(400),...  3.04 us
    ppermute x1, starting transfers between devices, on_device(): lax.ppermute(first, ('box', 'rhs'), [(2 * i, 2 * i + 2) for i in ups] + [...  2.37 us
    pallas_call x1, Pallas kernels, on_device(): pl.pallas_call(functools.partial(finish_kernel, total_facets), out_shape=...  2.14 us
  transfers between devices with their start and end apart: 4, of which 2 were waited for; matrix products, arithmetic and copies ran while one was open for 0% of the time, Pallas kernels for 2%

profile of v11, /device:TPU:0, one launch (start us, length us, event | category | flops | bytes accessed | tf_op | source)
XLA Modules:
  0.0 74.7 jit_solution(1028212964216186124)
XLA Ops:
  0.6 0.0 copy-start.4
  0.6 0.0 copy-start
  0.7 0.0 copy-start.2
  0.7 0.0 copy-start.3
  0.7 3.0 %prepare.1 = (bf16[544,128]{1,0:T(8,128)(2,1)}, f32[400,128]{1,0:T(8,128)}, bf16[288,128]{1,0:T(8,128)(2,1)}, f32[528,128]{1,0:T(8,128)}) custom-call(f32[3,32]{1,0:T(4,128)} %centres_s.1, s32[32]{0:T(128)} %counts_s.5, f32[8,8,8192]{2,1,0:T(8,128)} %basis_ref.5, f32[3,8192]{1,0:T(4,128)} %facets_h.1, f32[64,128]{1,0:T(8,128)} %bitcast.4, f32[3,8192]{1,0:T(4,128)} %normals_h.1), custom_call_target="tpu_custom_call" | custom-call | tf_op jit(solution)/shard_map/prepare/pallas_call | solution.py:432
  3.7 2.4 %collective-permute-start.1 = (f32[400,128]{1,0:T(8,128)}, f32[400,128]{1,0:T(8,128)S(1)}, u32[]{:S(2)}, u32[]{:S(2)}) collective-permute-start(f32[400,128]{1,0:T(8,128)} %get-tuple-element.14), channel_id=1, source_target_pairs={{0,2},{2,4},{4,6},{6,8},{8,10},{10,12},{12,14},{14,16},{16,18},{18... | collective-permute-start | bytes 614408 | tf_op jit(solution)/shard_map/ppermute | solution.py:452
  6.1 2.0 %collective-permute-start = (bf16[544,128]{1,0:T(8,128)(2,1)}, bf16[544,128]{1,0:T(8,128)(2,1)S(1)}, u32[]{:S(2)}, u32[]{:S(2)}) collective-permute-start(bf16[544,128]{1,0:T(8,128)(2,1)} %get-tuple-element.13.sent_ref), channel_id=1, source_target_pairs={{0,1},{1,0},{2,3},{3,2},{4,5},{5,4},{6,7},{7,6},{8,9},{9,8},{10,11... | collective-permute-start | bytes 417800 | tf_op jit(solution)/shard_map/ppermute | solution.py:451
  8.1 0.7 collective-permute-start.2
  8.7 0.0 collective-permute-done.2.second_ref
  8.7 0.0 copy-start.7
  8.7 3.5 %collective-permute-done.cross_ref = bf16[544,128]{1,0:T(8,128)(2,1)S(1)} collective-permute-done((bf16[544,128]{1,0:T(8,128)(2,1)}, bf16[544,128]{1,0:T(8,128)(2,1)S(1)}, u32[]{:S(2)}, u32[]{:S(2)}) %collective-permute-start) | collective-permute-done | bytes 139296 | tf_op jit(solution)/shard_map/ppermute | solution.py:451
  12.3 0.0 copy-start.6
  12.3 0.0 collective-permute-done.1.first_ref
  12.3 0.0 copy-start.5
  12.3 0.0 copy-done.7
  12.3 0.6 copy-done.6
  12.9 0.1 copy-done.5
  13.0 34.0 %fields.1 = (f32[256,256]{1,0:T(8,128)}, f32[256,256]{1,0:T(8,128)}) custom-call(f32[528,128]{1,0:T(8,128)} %get-tuple-element.12.local_ref, bf16[544,128]{1,0:T(8,128)(2,1)} %get-tuple-element.13.sent_ref, bf16[544,128]{1,0:T(8,128)(2,1)} %copy-done.6, f32[400,128]{1,0:T(8,128)} %copy-done.5, bf16[288,128]{1,0:T(8,128)(2,1)} %copy-done.7), custom_call_target="tpu_custom_call" | custom-call | tf_op jit(solution)/shard_map/fields/pallas_call | solution.py:459
  47.0 0.0 copy-start.1
  47.0 3.3 %collective-permute-start.3 = (f32[256,256]{1,0:T(8,128)}, f32[256,256]{1,0:T(8,128)S(1)}, u32[]{:S(2)}, u32[]{:S(2)}) collective-permute-start(f32[256,256]{1,0:T(8,128)} %get-tuple-element.17), channel_id=1, source_target_pairs={{0,1},{1,0},{2,3},{3,2},{4,5},{5,4},{6,7},{7,6},{8,9},{9,8},{10,11... | collective-permute-start | bytes 786440 | tf_op jit(solution)/shard_map/ppermute | solution.py:477
  50.4 0.0 copy-done.4
  50.4 0.0 copy-done
  50.4 1.7 %gram.1.gram_ref = f32[8,128]{1,0:T(8,128)S(1)} custom-call(s32[32]{0:T(128)S(1)} %copy-done.4, f32[8,8,8192]{2,1,0:T(8,128)S(1)} %copy-done), custom_call_target="tpu_custom_call" | custom-call | tf_op jit(solution)/shard_map/gram/pallas_call | solution.py:478
  52.0 4.7 %collective-permute-done.3.theirs_ref = f32[256,256]{1,0:T(8,128)S(1)} collective-permute-done((f32[256,256]{1,0:T(8,128)}, f32[256,256]{1,0:T(8,128)S(1)}, u32[]{:S(2)}, u32[]{:S(2)}) %collective-permute-start.3) | collective-permute-done | bytes 262176 | tf_op jit(solution)/shard_map/ppermute | solution.py:477
  56.8 0.0 copy-done.2
  56.8 0.0 copy-done.3
  56.8 0.0 copy-done.1
  56.8 1.2 %image.1 = (f32[8,8192]{1,0:T(8,128)S(1)}, f32[16,8,128]{2,1,0:T(8,128)S(1)}) custom-call(f32[3,32]{1,0:T(4,128)S(1)} %copy-done.3, s32[32]{0:T(128)S(1)} %copy-done.4, f32[256,256]{1,0:T(8,128)S(1)} %copy-done.1, f32[256,256]{1,0:T(8,128)S(1)} %collective-permute-done.3.theirs_ref, f32[8,128]{1,0:T(8,128)S(1)} %gram.1.gram_ref, f32[64,128]{1,0:T(8,128)S(1)} %bitcast.3, ...), custom_call_target="tpu_custom_call" | custom-call | tf_op jit(solution)/shard_map/image/pallas_call | solution.py:486
  58.0 14.6 %all_to_all.5.tiles_ref = f32[16,8,128]{2,1,0:T(8,128)S(1)} all-to-all(f32[16,8,128]{2,1,0:T(8,128)S(1)} %get-tuple-element.18), channel_id=1, replica_groups=mesh['box'=16,'rhs'=2] {'box'}, dimensions={0} | all-to-all | bytes 131072 | tf_op jit(solution)/shard_map/all_to_all | solution.py:494
  72.6 2.1 %finish.1 = (f32[8,8192]{1,0:T(8,128)}, f32[8,9]{1,0:T(8,128)}) custom-call(s32[32]{0:T(128)S(1)} %copy-done.4, f32[16,8,128]{2,1,0:T(8,128)S(1)} %all_to_all.5.tiles_ref, f32[8,8192]{1,0:T(8,128)S(1)} %get-tuple-element.19.image_ref, f32[8,8,8192]{2,1,0:T(8,128)S(1)} %copy-done), custom_call_target="tpu_custom_call" | custom-call | tf_op jit(solution)/shard_map/finish/pallas_call | solution.py:495
Async XLA Ops:
  0.6 49.7 %copy-start.4 = (s32[32]{0:T(128)S(1)}, s32[32]{0:T(128)}, u32[]{:S(2)}) copy-start(s32[32]{0:T(128)} %counts_s.5) | copy-start | bytes 388
  0.6 49.7 %copy-start = (f32[8,8,8192]{2,1,0:T(8,128)S(1)}, f32[8,8,8192]{2,1,0:T(8,128)}, u32[]{:S(2)}) copy-start(f32[8,8,8192]{2,1,0:T(8,128)} %basis_ref.5) | copy-start | bytes 6291460
  0.7 56.1 %copy-start.2 = (f32[8192]{0:T(1024)S(1)}, f32[8192]{0:T(1024)}, u32[]{:S(2)}) copy-start(f32[8192]{0:T(1024)} %param.13) | copy-start | bytes 98308
  0.7 56.1 %copy-start.3 = (f32[3,32]{1,0:T(4,128)S(1)}, f32[3,32]{1,0:T(4,128)}, u32[]{:S(2)}) copy-start(f32[3,32]{1,0:T(4,128)} %centres_s.1) | copy-start | bytes 1156
  3.7 8.6 %collective-permute-start.1 = (f32[400,128]{1,0:T(8,128)}, f32[400,128]{1,0:T(8,128)S(1)}, u32[]{:S(2)}, u32[]{:S(2)}) collective-permute-start(f32[400,128]{1,0:T(8,128)} %get-tuple-element.14), channel_id=1, source_target_pairs={{0,2},{2,4},{4,6},{6,8},{8,10},{10,12},{12,14},{14,16},{16,18},{18... | collective-permute-start | bytes 614408 | tf_op jit(solution)/shard_map/ppermute | solution.py:452
  6.1 6.2 %collective-permute-start = (bf16[544,128]{1,0:T(8,128)(2,1)}, bf16[544,128]{1,0:T(8,128)(2,1)S(1)}, u32[]{:S(2)}, u32[]{:S(2)}) collective-permute-start(bf16[544,128]{1,0:T(8,128)(2,1)} %get-tuple-element.13.sent_ref), channel_id=1, source_target_pairs={{0,1},{1,0},{2,3},{3,2},{4,5},{5,4},{6,7},{7,6},{8,9},{9,8},{10,11... | collective-permute-start | bytes 417800 | tf_op jit(solution)/shard_map/ppermute | solution.py:451
  8.1 0.7 collective-permute-start.2
  8.7 3.6 %copy-start.7 = (bf16[288,128]{1,0:T(8,128)(2,1)}, bf16[288,128]{1,0:T(8,128)(2,1)S(1)}, u32[]{:S(2)}) copy-start(bf16[288,128]{1,0:T(8,128)(2,1)S(1)} %collective-permute-done.2.second_ref) | copy-start | bytes 221188
  12.3 0.7 copy-start.6
  12.3 0.8 %copy-start.5 = (f32[400,128]{1,0:T(8,128)}, f32[400,128]{1,0:T(8,128)S(1)}, u32[]{:S(2)}) copy-start(f32[400,128]{1,0:T(8,128)S(1)} %collective-permute-done.1.first_ref) | copy-start | bytes 614404
  47.0 9.8 %copy-start.1 = (f32[256,256]{1,0:T(8,128)S(1)}, f32[256,256]{1,0:T(8,128)}, u32[]{:S(2)}) copy-start(f32[256,256]{1,0:T(8,128)} %get-tuple-element.16.mine_ref) | copy-start | bytes 786436
  47.0 9.7 %collective-permute-start.3 = (f32[256,256]{1,0:T(8,128)}, f32[256,256]{1,0:T(8,128)S(1)}, u32[]{:S(2)}, u32[]{:S(2)}) collective-permute-start(f32[256,256]{1,0:T(8,128)} %get-tuple-element.17), channel_id=1, source_target_pairs={{0,1},{1,0},{2,3},{3,2},{4,5},{5,4},{6,7},{7,6},{8,9},{9,8},{10,11... | collective-permute-start | bytes 786440 | tf_op jit(solution)/shard_map/ppermute | solution.py:477

commit v12 on v11

--- a/solution.py
+++ b/solution.py
@@ -148,27 +148,36 @@
         target_y = (item + 1) // 3
         source_y = target_y + lax.rem(item + 1, 3) - 1
         runs = []
-        for first in sources:
-            for x in range(4):
-                for near_x in range(max(x - 1, 0), min(x + 2, 4)):
-                    start = pl.multiple_of((target_y * 4 + near_x) * per_box, per_box)
-                    runs.append((first + source_y * 4 + x, pl.ds(start, per_box)))
-
-        def distances(box, rows_of):
+        for near_x in range(4):
+            for first in sources:
+                for x in range(max(near_x - 1, 0), min(near_x + 2, 4)):
+                    runs.append((near_x, first + source_y * 4 + x))
+
+        def distances(near_x, box):
+            start = pl.multiple_of((target_y * 4 + near_x) * per_box, per_box)
             weights = geometry[pl.ds(pl.multiple_of(box * depth, depth), depth), :]
-            return jnp.dot(targets[rows_of, :], weights, preferred_element_type=f32)
+            return jnp.dot(targets[pl.ds(start, per_box), :], weights, preferred_element_type=f32)
 
         ahead = distances(*runs[0])
-        for i, (box, rows_of) in enumerate(runs):
+        cubed = []
+        given = []
+        for i, (near_x, box) in enumerate(runs):
             here = ahead
             if i + 1 < len(runs):
                 ahead = distances(*runs[i + 1])
             inverse = lax.rsqrt(here)
-            cubed = (inverse * inverse * inverse).astype(bf16)
-            given = strengths[pl.ds(pl.multiple_of(box * 256, 256), 256), :]
-            total[rows_of, :] += lax.dot_general(
-                cubed, given, (((1,), (1,)), ((), ())), preferred_element_type=f32
-            )
+            cubed.append((inverse * inverse * inverse).astype(bf16))
+            given.append(strengths[pl.ds(pl.multiple_of(box * 256, 256), 256), :])
+            if i + 1 == len(runs) or runs[i + 1][0] != near_x:
+                rows_of = pl.ds(pl.multiple_of((target_y * 4 + near_x) * per_box, per_box), per_box)
+                total[rows_of, :] += lax.dot_general(
+                    jnp.concatenate(cubed, axis=1),
+                    jnp.concatenate(given, axis=1),
+                    (((1,), (1,)), ((), ())),
+                    preferred_element_type=f32,
+                )
+                cubed = []
+                given = []
         if beside is not None:
             beside(item)
         return 0

time: 75 us -> 73.2 us (0.976)
  Pallas kernels: 42 us -> 40.3 us
    pallas_call x1, Pallas kernels: 34 us -> 32.2 us  [on_device(): pl.pallas_call(field_kernel, out_shape=(rows(boxes * 8, per_box),) * 2, i...]
where the time goes in v12:
time: 73.2 us; the launch traced here: 73 us
  Pallas kernels  40.3 us (55%)
  blocking collectives  14.6 us (20%)
  starting transfers between devices  8.32 us (11%)
  waiting for transfers between devices  8.26 us (11%)
  local copies, waits for them, and re-layouts  0.77 us (1%)
    pallas_call x1, Pallas kernels, on_device(): pl.pallas_call(field_kernel, out_shape=(rows(boxes * 8, per_box),) * 2, i...  32.2 us
    all_to_all x1, blocking collectives, on_device(): tiles = lax.all_to_all(tiles, 'box', 0, 0, tiled=True)  14.6 us
    ppermute x1, waiting for transfers between devices, on_device(): theirs = lax.ppermute(theirs, 'rhs', swap)  4.71 us
    ppermute x1, waiting for transfers between devices, on_device(): cross = lax.ppermute(sent, 'rhs', swap)  3.54 us
    ppermute x1, starting transfers between devices, on_device(): theirs = lax.ppermute(theirs, 'rhs', swap)  3.34 us
    pallas_call x1, Pallas kernels, on_device(): pl.pallas_call(prep_kernel, out_shape=(rows(544, dtype=bf16), rows(400),...  3.04 us
    ppermute x1, starting transfers between devices, on_device(): lax.ppermute(first, ('box', 'rhs'), [(2 * i, 2 * i + 2) for i in ups] + [...  2.37 us
    pallas_call x1, Pallas kernels, on_device(): pl.pallas_call(functools.partial(finish_kernel, total_facets), out_shape=...  2.14 us
  transfers between devices with their start and end apart: 4, of which 2 were waited for; matrix products, arithmetic and copies ran while one was open for 0% of the time, Pallas kernels for 2%

profile of v12, /device:TPU:0, one launch (start us, length us, event | category | flops | bytes accessed | tf_op | source)
XLA Modules:
  0.0 73.0 jit_solution(3706454254058025527)
XLA Ops:
  0.6 0.0 copy-start.4
  0.6 0.0 copy-start
  0.7 0.0 copy-start.2
  0.7 0.0 copy-start.3
  0.7 3.0 %prepare.1 = (bf16[544,128]{1,0:T(8,128)(2,1)}, f32[400,128]{1,0:T(8,128)}, bf16[288,128]{1,0:T(8,128)(2,1)}, f32[528,128]{1,0:T(8,128)}) custom-call(f32[3,32]{1,0:T(4,128)} %centres_s.1, s32[32]{0:T(128)} %counts_s.5, f32[8,8,8192]{2,1,0:T(8,128)} %basis_ref.5, f32[3,8192]{1,0:T(4,128)} %facets_h.1, f32[64,128]{1,0:T(8,128)} %bitcast.4, f32[3,8192]{1,0:T(4,128)} %normals_h.1), custom_call_target="tpu_custom_call" | custom-call | tf_op jit(solution)/shard_map/prepare/pallas_call | solution.py:441
  3.7 2.4 %collective-permute-start.1 = (f32[400,128]{1,0:T(8,128)}, f32[400,128]{1,0:T(8,128)S(1)}, u32[]{:S(2)}, u32[]{:S(2)}) collective-permute-start(f32[400,128]{1,0:T(8,128)} %get-tuple-element.14), channel_id=1, source_target_pairs={{0,2},{2,4},{4,6},{6,8},{8,10},{10,12},{12,14},{14,16},{16,18},{18... | collective-permute-start | bytes 614408 | tf_op jit(solution)/shard_map/ppermute | solution.py:461
  6.1 2.0 %collective-permute-start = (bf16[544,128]{1,0:T(8,128)(2,1)}, bf16[544,128]{1,0:T(8,128)(2,1)S(1)}, u32[]{:S(2)}, u32[]{:S(2)}) collective-permute-start(bf16[544,128]{1,0:T(8,128)(2,1)} %get-tuple-element.13.sent_ref), channel_id=1, source_target_pairs={{0,1},{1,0},{2,3},{3,2},{4,5},{5,4},{6,7},{7,6},{8,9},{9,8},{10,11... | collective-permute-start | bytes 417800 | tf_op jit(solution)/shard_map/ppermute | solution.py:460
  8.1 0.7 collective-permute-start.2
  8.7 0.0 collective-permute-done.2.second_ref
  8.7 0.0 copy-start.7
  8.7 3.5 %collective-permute-done.cross_ref = bf16[544,128]{1,0:T(8,128)(2,1)S(1)} collective-permute-done((bf16[544,128]{1,0:T(8,128)(2,1)}, bf16[544,128]{1,0:T(8,128)(2,1)S(1)}, u32[]{:S(2)}, u32[]{:S(2)}) %collective-permute-start) | collective-permute-done | bytes 139296 | tf_op jit(solution)/shard_map/ppermute | solution.py:460
  12.3 0.0 copy-start.6
  12.3 0.0 collective-permute-done.1.first_ref
  12.3 0.0 copy-start.5
  12.3 0.0 copy-done.7
  12.3 0.6 copy-done.6
  12.9 0.1 copy-done.5
  13.0 32.2 %fields.1 = (f32[256,256]{1,0:T(8,128)}, f32[256,256]{1,0:T(8,128)}) custom-call(f32[528,128]{1,0:T(8,128)} %get-tuple-element.12.local_ref, bf16[544,128]{1,0:T(8,128)(2,1)} %get-tuple-element.13.sent_ref, bf16[544,128]{1,0:T(8,128)(2,1)} %copy-done.6, f32[400,128]{1,0:T(8,128)} %copy-done.5, bf16[288,128]{1,0:T(8,128)(2,1)} %copy-done.7), custom_call_target="tpu_custom_call" | custom-call | tf_op jit(solution)/shard_map/fields/pallas_call | solution.py:468
  45.3 0.0 copy-start.1
  45.3 3.3 %collective-permute-start.3 = (f32[256,256]{1,0:T(8,128)}, f32[256,256]{1,0:T(8,128)S(1)}, u32[]{:S(2)}, u32[]{:S(2)}) collective-permute-start(f32[256,256]{1,0:T(8,128)} %get-tuple-element.17), channel_id=1, source_target_pairs={{0,1},{1,0},{2,3},{3,2},{4,5},{5,4},{6,7},{7,6},{8,9},{9,8},{10,11... | collective-permute-start | bytes 786440 | tf_op jit(solution)/shard_map/ppermute | solution.py:486
  48.6 0.0 copy-done.4
  48.6 0.0 copy-done
  48.6 1.7 %gram.1.gram_ref = f32[8,128]{1,0:T(8,128)S(1)} custom-call(s32[32]{0:T(128)S(1)} %copy-done.4, f32[8,8,8192]{2,1,0:T(8,128)S(1)} %copy-done), custom_call_target="tpu_custom_call" | custom-call | tf_op jit(solution)/shard_map/gram/pallas_call | solution.py:487
  50.3 4.7 %collective-permute-done.3.theirs_ref = f32[256,256]{1,0:T(8,128)S(1)} collective-permute-done((f32[256,256]{1,0:T(8,128)}, f32[256,256]{1,0:T(8,128)S(1)}, u32[]{:S(2)}, u32[]{:S(2)}) %collective-permute-start.3) | collective-permute-done | bytes 262176 | tf_op jit(solution)/shard_map/ppermute | solution.py:486
  55.0 0.0 copy-done.2
  55.0 0.0 copy-done.3
  55.0 0.0 copy-done.1
  55.0 1.2 %image.1 = (f32[8,8192]{1,0:T(8,128)S(1)}, f32[16,8,128]{2,1,0:T(8,128)S(1)}) custom-call(f32[3,32]{1,0:T(4,128)S(1)} %copy-done.3, s32[32]{0:T(128)S(1)} %copy-done.4, f32[256,256]{1,0:T(8,128)S(1)} %copy-done.1, f32[256,256]{1,0:T(8,128)S(1)} %collective-permute-done.3.theirs_ref, f32[8,128]{1,0:T(8,128)S(1)} %gram.1.gram_ref, f32[64,128]{1,0:T(8,128)S(1)} %bitcast.3, ...), custom_call_target="tpu_custom_call" | custom-call | tf_op jit(solution)/shard_map/image/pallas_call | solution.py:495
  56.2 14.6 %all_to_all.5.tiles_ref = f32[16,8,128]{2,1,0:T(8,128)S(1)} all-to-all(f32[16,8,128]{2,1,0:T(8,128)S(1)} %get-tuple-element.18), channel_id=1, replica_groups=mesh['box'=16,'rhs'=2] {'box'}, dimensions={0} | all-to-all | bytes 131072 | tf_op jit(solution)/shard_map/all_to_all | solution.py:503
  70.8 2.1 %finish.1 = (f32[8,8192]{1,0:T(8,128)}, f32[8,9]{1,0:T(8,128)}) custom-call(s32[32]{0:T(128)S(1)} %copy-done.4, f32[16,8,128]{2,1,0:T(8,128)S(1)} %all_to_all.5.tiles_ref, f32[8,8192]{1,0:T(8,128)S(1)} %get-tuple-element.19.image_ref, f32[8,8,8192]{2,1,0:T(8,128)S(1)} %copy-done), custom_call_target="tpu_custom_call" | custom-call | tf_op jit(solution)/shard_map/finish/pallas_call | solution.py:504
Async XLA Ops:
  0.6 48.0 %copy-start.4 = (s32[32]{0:T(128)S(1)}, s32[32]{0:T(128)}, u32[]{:S(2)}) copy-start(s32[32]{0:T(128)} %counts_s.5) | copy-start | bytes 388
  0.6 48.0 %copy-start = (f32[8,8,8192]{2,1,0:T(8,128)S(1)}, f32[8,8,8192]{2,1,0:T(8,128)}, u32[]{:S(2)}) copy-start(f32[8,8,8192]{2,1,0:T(8,128)} %basis_ref.5) | copy-start | bytes 6291460
  0.7 54.3 %copy-start.2 = (f32[8192]{0:T(1024)S(1)}, f32[8192]{0:T(1024)}, u32[]{:S(2)}) copy-start(f32[8192]{0:T(1024)} %param.13) | copy-start | bytes 98308
  0.7 54.3 %copy-start.3 = (f32[3,32]{1,0:T(4,128)S(1)}, f32[3,32]{1,0:T(4,128)}, u32[]{:S(2)}) copy-start(f32[3,32]{1,0:T(4,128)} %centres_s.1) | copy-start | bytes 1156
  3.7 8.6 %collective-permute-start.1 = (f32[400,128]{1,0:T(8,128)}, f32[400,128]{1,0:T(8,128)S(1)}, u32[]{:S(2)}, u32[]{:S(2)}) collective-permute-start(f32[400,128]{1,0:T(8,128)} %get-tuple-element.14), channel_id=1, source_target_pairs={{0,2},{2,4},{4,6},{6,8},{8,10},{10,12},{12,14},{14,16},{16,18},{18... | collective-permute-start | bytes 614408 | tf_op jit(solution)/shard_map/ppermute | solution.py:461
  6.1 6.2 %collective-permute-start = (bf16[544,128]{1,0:T(8,128)(2,1)}, bf16[544,128]{1,0:T(8,128)(2,1)S(1)}, u32[]{:S(2)}, u32[]{:S(2)}) collective-permute-start(bf16[544,128]{1,0:T(8,128)(2,1)} %get-tuple-element.13.sent_ref), channel_id=1, source_target_pairs={{0,1},{1,0},{2,3},{3,2},{4,5},{5,4},{6,7},{7,6},{8,9},{9,8},{10,11... | collective-permute-start | bytes 417800 | tf_op jit(solution)/shard_map/ppermute | solution.py:460
  8.1 0.7 collective-permute-start.2
  8.7 3.6 %copy-start.7 = (bf16[288,128]{1,0:T(8,128)(2,1)}, bf16[288,128]{1,0:T(8,128)(2,1)S(1)}, u32[]{:S(2)}) copy-start(bf16[288,128]{1,0:T(8,128)(2,1)S(1)} %collective-permute-done.2.second_ref) | copy-start | bytes 221188
  12.3 0.7 copy-start.6
  12.3 0.8 %copy-start.5 = (f32[400,128]{1,0:T(8,128)}, f32[400,128]{1,0:T(8,128)S(1)}, u32[]{:S(2)}) copy-start(f32[400,128]{1,0:T(8,128)S(1)} %collective-permute-done.1.first_ref) | copy-start | bytes 614404
  45.3 9.7 %copy-start.1 = (f32[256,256]{1,0:T(8,128)S(1)}, f32[256,256]{1,0:T(8,128)}, u32[]{:S(2)}) copy-start(f32[256,256]{1,0:T(8,128)} %get-tuple-element.16.mine_ref) | copy-start | bytes 786436
  45.3 9.7 %collective-permute-start.3 = (f32[256,256]{1,0:T(8,128)}, f32[256,256]{1,0:T(8,128)S(1)}, u32[]{:S(2)}, u32[]{:S(2)}) collective-permute-start(f32[256,256]{1,0:T(8,128)} %get-tuple-element.17), channel_id=1, source_target_pairs={{0,1},{1,0},{2,3},{3,2},{4,5},{5,4},{6,7},{7,6},{8,9},{9,8},{10,11... | collective-permute-start | bytes 786440 | tf_op jit(solution)/shard_map/ppermute | solution.py:486

commit v13 on v12

--- a/solution.py
+++ b/solution.py
@@ -186,8 +186,8 @@
 
 
 def field_kernel(
-    local_ref, sent_ref, cross_ref, first_ref, second_ref, mine_ref, theirs_ref,
-    geometry, strengths, targets, planes, total, far_halo, far_own, far_centres
+    centres_s, local_ref, sent_ref, cross_ref, first_ref, second_ref, mine_ref, theirs_ref,
+    geometry, strengths, targets, planes, total, far, far_centres, far_moments
 ):
     boxes = 2 * plane_boxes
     half = lax.axis_index("rhs")
@@ -200,7 +200,7 @@
         store_source_features(local, charges, slot, geometry, strengths)
         return 0
 
-    lax.fori_loop(0, boxes, source, 0, unroll=2)
+    lax.fori_loop(0, boxes, source, 0, unroll=4)
 
     def halo_source(place, _):
         local = padded(wide_tile(first_ref, 256 + place * 8) - origin)
@@ -208,7 +208,7 @@
         store_source_features(local, charges, boxes + place, geometry, strengths)
         return 0
 
-    lax.fori_loop(0, plane_boxes, halo_source, 0, unroll=2)
+    lax.fori_loop(0, plane_boxes, halo_source, 0, unroll=4)
 
     def target(place, _):
         start = (half * plane_boxes + place) * 16
@@ -224,10 +224,9 @@
         planes[pl.ds(pl.multiple_of(place * 8, 8), 8), :] = jnp.where(row == 3, along, normal)
         return 0
 
-    lax.fori_loop(0, plane_boxes, target, 0, unroll=2)
+    lax.fori_loop(0, plane_boxes, target, 0, unroll=4)
     total[...] = jnp.zeros_like(total)
 
-    moments = []
     for group, (centres, mine, theirs) in enumerate(
         (
             (first_ref[392:400], first_ref[384:392], second_ref[256:288]),
@@ -241,19 +240,21 @@
             )
         both = jnp.concatenate([mine, whole_moments(theirs.astype(f32))], axis=0)
         high = both.astype(bf16).astype(f32)
-        moments.append(jnp.concatenate([high, both - high], axis=0))
+        far_moments[group * 32 : group * 32 + 32, :] = jnp.concatenate([high, both - high], axis=0)
     lane = lax.broadcasted_iota(jnp.int32, (1, 128), 1)
     lane_x = lane & 3
     lane_y = (lane >> 2) & 3
     lane_plane = (lane >> 4) & 1
 
-    def far_field(slot, group):
+    def far_field(k):
+        group = (k >= boxes).astype(jnp.int32)
+        slot = jnp.where(k < boxes, k, half * plane_boxes + k - boxes)
         x, y, plane = slot & 3, (slot >> 2) & 3, slot >> 4
         local = wide_tile(local_ref, slot * 16) - origin
         normal = wide_tile(local_ref, slot * 16 + 8)
         d = []
         for a in range(3):
-            centre = far_centres[(group * 3 + a) * 32 : (group * 3 + a + 1) * 32, :]
+            centre = far_centres[pl.ds(pl.multiple_of((group * 3 + a) * 32, 32), 32), :]
             d.append(local[a : a + 1] - jnp.concatenate([centre, centre], axis=1))
         q = d[0] * d[0] + d[1] * d[1] + d[2] * d[2] + soften
         inverse = lax.rsqrt(q)
@@ -266,20 +267,17 @@
         whole = jnp.concatenate(coefficients, axis=0)
         upper = whole.astype(bf16)
         lower = (whole - upper.astype(f32)).astype(bf16)
-        lane_z = lane_plane + (4 * half - 2 if group == 0 else 0)
+        lane_z = lane_plane + jnp.where(group == 0, 4 * half - 2, 0)
         near = (jnp.abs(lane_x - x) <= 1) & (jnp.abs(lane_y - y) <= 1) & (jnp.abs(lane_z - plane) <= 1)
-        picked = jnp.where(near, 0.0, moments[group]).astype(bf16)
+        picked = jnp.where(near, 0.0, far_moments[pl.ds(pl.multiple_of(group * 32, 32), 32), :]).astype(bf16)
         first = jnp.dot(picked, upper, preferred_element_type=f32)
         second = jnp.dot(picked, lower, preferred_element_type=f32)
         return first[:16] + first[16:] + second[:16]
 
     def far_boxes(item):
-        for k in range(4):
-            slot = jnp.minimum(item * 4 + k, boxes - 1)
-            far_halo[pl.ds(pl.multiple_of(slot * 16, 16), 16), :] = far_field(slot, 0)
-        for k in range(2):
-            place = jnp.minimum(item * 2 + k, plane_boxes - 1)
-            far_own[pl.ds(pl.multiple_of(place * 16, 16), 16), :] = far_field(half * plane_boxes + place, 1)
+        for i in range(5):
+            k = jnp.minimum(item * 5 + i, 3 * plane_boxes - 1)
+            far[pl.ds(pl.multiple_of(k * 16, 16), 16), :] = far_field(k)
 
     near_planes((0, plane_boxes, 2 * plane_boxes), geometry, strengths, targets, total, far_boxes)
 
@@ -291,22 +289,30 @@
         value = value - side[1:2] * sums[32:48] - side[2:3] * sums[48:64]
         slot = half * plane_boxes + place
         rows = pl.ds(pl.multiple_of(slot * 16, 16), 16)
-        far_halo[rows, :] += value + far_own[pl.ds(pl.multiple_of(place * 16, 16), 16), :]
-        return 0
-
-    lax.fori_loop(0, plane_boxes, near_field, 0, unroll=2)
-    for slot in range(boxes):
-        mine_ref[slot * 8 : slot * 8 + 8] = far_halo[slot * 16 : slot * 16 + 8]
-        theirs_ref[slot * 8 : slot * 8 + 8] = far_halo[slot * 16 + 8 : slot * 16 + 16]
-
-
-def gram_kernel(counts_s, basis_ref, sums_ref):
+        far[rows, :] += value + far[pl.ds(pl.multiple_of((boxes + place) * 16, 16), 16), :]
+        return 0
+
+    lax.fori_loop(0, plane_boxes, near_field, 0, unroll=4)
+
+    def given_back(b, _):
+        start = pl.multiple_of(slot_of(centres_s, b) * 16, 16)
+        rows = pl.ds(pl.multiple_of(b * 8, 8), 8)
+        mine_ref[rows, :] = far[pl.ds(start, 8), :]
+        theirs_ref[rows, :] = far[pl.ds(start + 8, 8), :]
+        return 0
+
+    lax.fori_loop(0, boxes, given_back, 0, unroll=4)
+
+
+def gram_kernel(counts_s, basis_ref, sums_ref, live_ref):
     krylov = basis_ref.shape[0]
     pairs = [(m, n) for m in range(krylov) for n in range(m + 1)]
 
     def one_box(b, carry):
         lanes = pl.ds(pl.multiple_of(b * per_box, per_box), per_box)
         live = live_row(counts_s, b)
+        live_ref[pl.ds(2 * b, 1), :] = live[:, :128]
+        live_ref[pl.ds(2 * b + 1, 1), :] = live[:, 128:]
         rows = [basis_ref[m, :, lanes] * live for m in range(krylov)]
         out = []
         for k, (m, n) in enumerate(pairs):
@@ -323,13 +329,13 @@
     sums_ref[...] = total
 
 
-def image_kernel(centres_s, counts_s, mine_ref, theirs_ref, gram_ref, contrast_ref, basis_ref, image_ref, sums_ref):
+def image_kernel(mine_ref, theirs_ref, gram_ref, live_ref, contrast_ref, basis_ref, image_ref, sums_ref):
     krylov = basis_ref.shape[0]
 
     def one_box(b, carry):
         lanes = pl.ds(pl.multiple_of(b * per_box, per_box), per_box)
-        rows = pl.ds(pl.multiple_of(slot_of(centres_s, b) * 8, 8), 8)
-        live = live_row(counts_s, b)
+        rows = pl.ds(pl.multiple_of(b * 8, 8), 8)
+        live = wide_row(live_ref, b)
         part = mine_ref[rows, :] + theirs_ref[rows, :]
         image = live * (basis_ref[krylov - 1, :, lanes] - 2.0 * wide_row(contrast_ref, b) * part)
         image_ref[:, lanes] = image
@@ -340,7 +346,7 @@
         return tuple(sums)
 
     zeros = jnp.zeros((8, 128), f32)
-    sums = lax.fori_loop(0, counts_s.shape[0], one_box, (zeros,) * (krylov + 1), unroll=4)
+    sums = lax.fori_loop(0, live_ref.shape[0] // 2, one_box, (zeros,) * (krylov + 1), unroll=4)
     lane = lax.broadcasted_iota(jnp.int32, (8, 128), 1)
     total = gram_ref[...]
     for k, value in enumerate(sums):
@@ -367,16 +373,15 @@
     return p, ((a_high * b_high - p) + a_high * b_low + a_low * b_high) + a_low * b_low
 
 
-def finish_kernel(total_facets, counts_s, tiles_ref, image_ref, basis_ref, next_ref, hessenberg_ref):
-    boxes = counts_s.shape[0]
+def finish_kernel(total_facets, tiles_ref, live_ref, image_ref, basis_ref, next_ref, hessenberg_ref):
+    boxes = live_ref.shape[0] // 2
     krylov = basis_ref.shape[0]
     lane = lax.broadcasted_iota(jnp.int32, (8, 128), 1)
 
-    def add_tile(i, carry):
-        value, error = two_sum(carry[0], tiles_ref[i])
-        return value, carry[1] + error
-
-    sums, rest = lax.fori_loop(0, tiles_ref.shape[0], add_tile, (jnp.zeros((8, 128), f32),) * 2, unroll=8)
+    sums, rest = tiles_ref[0, 0], tiles_ref[0, 1]
+    for i in range(1, tiles_ref.shape[0]):
+        sums, error = two_sum(sums, tiles_ref[i, 0])
+        rest = (rest + tiles_ref[i, 1]) + error
     exact = sums + rest
     projections = [exact[:, m : m + 1] / total_facets for m in range(krylov)]
     pairs = [(m, n) for m in range(krylov) for n in range(m + 1)]
@@ -408,7 +413,7 @@
 
     def one_box(b, _):
         lanes = pl.ds(pl.multiple_of(b * per_box, per_box), per_box)
-        live = live_row(counts_s, b)
+        live = wide_row(live_ref, b)
         sent = wide[0] * basis_ref[0, :, lanes]
         for m in range(1, krylov):
             sent += wide[m] * basis_ref[m, :, lanes]
@@ -468,7 +473,7 @@
     mine, theirs = pl.pallas_call(
         field_kernel,
         out_shape=(rows(boxes * 8, per_box),) * 2,
-        in_specs=[vmem] * 5,
+        in_specs=[smem] + [vmem] * 5,
         out_specs=(vmem, vmem),
         scratch_shapes=[
             pltpu.VMEM((3 * plane_boxes * depth, per_box), bf16),
@@ -476,42 +481,50 @@
             pltpu.VMEM((plane_slots, depth), bf16),
             pltpu.VMEM((plane_boxes * 8, per_box), f32),
             pltpu.VMEM((plane_slots, 256), f32),
-            pltpu.VMEM((boxes * 16, per_box), f32),
-            pltpu.VMEM((plane_boxes * 16, per_box), f32),
+            pltpu.VMEM((3 * plane_boxes * 16, per_box), f32),
             pltpu.VMEM((6 * 32, 128), f32),
+            pltpu.VMEM((2 * 32, 128), f32),
         ],
-        compiler_params=limit(60),
+        compiler_params=limit(32),
         name="fields",
-    )(local, sent, cross, first, second)
+    )(box_centres, local, sent, cross, first, second)
     theirs = lax.ppermute(theirs, "rhs", swap)
-    gram = pl.pallas_call(
+    gram, live = pl.pallas_call(
         gram_kernel,
-        out_shape=rows(8),
+        out_shape=(rows(8), rows(2 * boxes)),
         in_specs=[smem, vmem],
-        out_specs=vmem,
+        out_specs=(vmem, vmem),
         compiler_params=limit(8),
         name="gram",
     )(facet_counts, basis)
+    few = 4 if count % 4 == 0 else 1
     image, tiles = pl.pallas_call(
         image_kernel,
-        out_shape=(rows(rhs_local, facet_local), jax.ShapeDtypeStruct((count, 8, 128), f32)),
-        in_specs=[smem, smem] + [vmem] * 5,
+        out_shape=(rows(rhs_local, facet_local), jax.ShapeDtypeStruct((few, 8, 128), f32)),
+        in_specs=[vmem] * 6,
         out_specs=(vmem, vmem),
         compiler_params=limit(8),
         name="image",
-    )(box_centres, facet_counts, mine, theirs, gram, contrast, basis)
-    tiles = lax.all_to_all(tiles, "box", 0, 0, tiled=True)
+    )(mine, theirs, gram, live, contrast, basis)
+    tiles = lax.all_to_all(
+        tiles, "box", 0, 0, axis_index_groups=[[i + k for k in range(few)] for i in range(0, count, few)], tiled=True
+    )
+    value, rest = tiles[0], jnp.zeros_like(tiles[0])
+    for i in range(1, few):
+        value, error = two_sum(value, tiles[i])
+        rest = rest + error
+    tiles = jnp.broadcast_to(jnp.stack([value, rest])[None], (count // few, 2, 8, 128))
+    tiles = lax.all_to_all(
+        tiles, "box", 0, 0, axis_index_groups=[list(range(i, count, few)) for i in range(few)], tiled=True
+    )
     next_vector, hessenberg = pl.pallas_call(
         functools.partial(finish_kernel, total_facets),
-        out_shape=(
-            jax.ShapeDtypeStruct((rhs_local, facet_local), f32),
-            jax.ShapeDtypeStruct((rhs_local, krylov + 1), f32),
-        ),
-        in_specs=[smem] + [vmem] * 3,
+        out_shape=(rows(rhs_local, facet_local), rows(rhs_local, krylov + 1)),
+        in_specs=[vmem] * 4,
         out_specs=(vmem, vmem),
-        compiler_params=pltpu.CompilerParams(vmem_limit_bytes=16 * 1024 * 1024),
+        compiler_params=limit(16),
         name="finish",
-    )(facet_counts, tiles, image, basis)
+    )(tiles, live, image, basis)
     return next_vector, hessenberg.T
 
 

time: 73.2 us -> 73.8 us (level)
  Pallas kernels: 40.3 us -> 35.7 us
  blocking collectives: 14.6 us -> 18.7 us
  local copies, waits for them, and re-layouts: 0.77 us -> 1.88 us
    all_to_all x1 -> x2, blocking collectives: 14.6 us -> 18.7 us  [the longest x1 9.41 us: on_device(): lax.all_to_all(tiles, 'box', 0, 0, axis_index_groups=[list(range(i, count...]
    pallas_call x1, Pallas kernels: 32.2 us -> 29.1 us  [on_device(): pl.pallas_call(field_kernel, out_shape=(rows(boxes * 8, per_box),) * 2, i...]
    unnamed x16 -> x12, local copies, waits for them, and re-layouts: 0.77 us -> 1.88 us
    pallas_call x1, Pallas kernels: 1.21 us -> 0.36 us  [on_device(): pl.pallas_call(image_kernel, out_shape=(rows(rhs_local, facet_local), jax...]
where the time goes in v13:
time: 73.8 us; the launch traced here: 73.5 us
  Pallas kernels  35.7 us (48%)
  blocking collectives  18.7 us (25%)
  starting transfers between devices  8.37 us (11%)
  waiting for transfers between devices  8.07 us (11%)
  local copies, waits for them, and re-layouts  1.88 us (3%)
    pallas_call x1, Pallas kernels, on_device(): pl.pallas_call(field_kernel, out_shape=(rows(boxes * 8, per_box),) * 2, i...  29.1 us
    all_to_all x1, blocking collectives, on_device(): lax.all_to_all(tiles, 'box', 0, 0, axis_index_groups=[list(range(i, count...  9.41 us
    all_to_all x1, blocking collectives, on_device(): lax.all_to_all(tiles, 'box', 0, 0, axis_index_groups=[[i + k for k in ran...  9.31 us
    ppermute x1, waiting for transfers between devices, on_device(): theirs = lax.ppermute(theirs, 'rhs', swap)  4.52 us
    ppermute x1, waiting for transfers between devices, on_device(): cross = lax.ppermute(sent, 'rhs', swap)  3.55 us
    ppermute x1, starting transfers between devices, on_device(): theirs = lax.ppermute(theirs, 'rhs', swap)  3.39 us
    pallas_call x1, Pallas kernels, on_device(): pl.pallas_call(prep_kernel, out_shape=(rows(544, dtype=bf16), rows(400),...  3.03 us
    ppermute x1, starting transfers between devices, on_device(): lax.ppermute(first, ('box', 'rhs'), [(2 * i, 2 * i + 2) for i in ups] + [...  2.37 us
  transfers between devices with their start and end apart: 4, of which 2 were waited for; matrix products, arithmetic and copies ran while one was open for 0% of the time, Pallas kernels for 2%

profile of v13, /device:TPU:0, one launch (start us, length us, event | category | flops | bytes accessed | tf_op | source)
XLA Modules:
  0.0 73.5 jit_solution(14880647464058856203)
XLA Ops:
  0.6 0.0 copy-start.5
  0.6 0.0 copy-start.4
  0.7 0.0 copy-start
  0.7 0.0 copy-start.3
  0.7 3.0 %prepare.1 = (bf16[544,128]{1,0:T(8,128)(2,1)}, f32[400,128]{1,0:T(8,128)}, bf16[288,128]{1,0:T(8,128)(2,1)}, f32[528,128]{1,0:T(8,128)}) custom-call(f32[3,32]{1,0:T(4,128)} %centres_s.1, s32[32]{0:T(128)} %counts_s.1, f32[8,8,8192]{2,1,0:T(8,128)} %basis_ref.5, f32[3,8192]{1,0:T(4,128)} %facets_h.1, f32[64,128]{1,0:T(8,128)} %bitcast.4, f32[3,8192]{1,0:T(4,128)} %normals_h.1), custom_call_target="tpu_custom_call" | custom-call | tf_op jit(solution)/shard_map/prepare/pallas_call | solution.py:446
  3.7 2.4 %collective-permute-start.1 = (f32[400,128]{1,0:T(8,128)}, f32[400,128]{1,0:T(8,128)S(1)}, u32[]{:S(2)}, u32[]{:S(2)}) collective-permute-start(f32[400,128]{1,0:T(8,128)} %get-tuple-element.16), channel_id=1, source_target_pairs={{0,2},{2,4},{4,6},{6,8},{8,10},{10,12},{12,14},{14,16},{16,18},{18... | collective-permute-start | bytes 614408 | tf_op jit(solution)/shard_map/ppermute | solution.py:466
  6.1 2.0 %collective-permute-start = (bf16[544,128]{1,0:T(8,128)(2,1)}, bf16[544,128]{1,0:T(8,128)(2,1)S(1)}, u32[]{:S(2)}, u32[]{:S(2)}) collective-permute-start(bf16[544,128]{1,0:T(8,128)(2,1)} %get-tuple-element.15.sent_ref), channel_id=1, source_target_pairs={{0,1},{1,0},{2,3},{3,2},{4,5},{5,4},{6,7},{7,6},{8,9},{9,8},{10,11... | collective-permute-start | bytes 417800 | tf_op jit(solution)/shard_map/ppermute | solution.py:465
  8.0 0.7 collective-permute-start.2
  8.7 0.0 collective-permute-done.2.second_ref
  8.7 3.6 %collective-permute-done.cross_ref = bf16[544,128]{1,0:T(8,128)(2,1)S(1)} collective-permute-done((bf16[544,128]{1,0:T(8,128)(2,1)}, bf16[544,128]{1,0:T(8,128)(2,1)S(1)}, u32[]{:S(2)}, u32[]{:S(2)}) %collective-permute-start) | collective-permute-done | bytes 139296 | tf_op jit(solution)/shard_map/ppermute | solution.py:465
  12.3 0.0 collective-permute-done.1.first_ref
  12.3 0.0 copy-done.4
  12.3 0.0 copy-start.1
  12.3 1.0 %copy-done.1 = f32[528,128]{1,0:T(8,128)S(1)} copy-done((f32[528,128]{1,0:T(8,128)S(1)}, f32[528,128]{1,0:T(8,128)}, u32[]{:S(2)}) %copy-start.1) | copy-done | bytes 270360
  13.2 0.0 copy-start.2
  13.2 0.9 %copy-done.2 = bf16[544,128]{1,0:T(8,128)(2,1)S(1)} copy-done((bf16[544,128]{1,0:T(8,128)(2,1)S(1)}, bf16[544,128]{1,0:T(8,128)(2,1)}, u32[]{:S(2)}) %copy-start.2) | copy-done | bytes 139288
  14.1 29.1 %fields.1 = (f32[256,256]{1,0:T(8,128)S(1)}, f32[256,256]{1,0:T(8,128)S(1)}) custom-call(f32[3,32]{1,0:T(4,128)S(1)} %copy-done.4, f32[528,128]{1,0:T(8,128)S(1)} %copy-done.1, bf16[544,128]{1,0:T(8,128)(2,1)S(1)} %copy-done.2, bf16[544,128]{1,0:T(8,128)(2,1)S(1)} %collective-permute-done.cross_ref, f32[400,128]{1,0:T(8,128)S(1)} %collective-permute-done.1.first_ref, ...), custom_call_target="tpu_custom_call" | custom-call | tf_op jit(solution)/shard_map/fields/pallas_call | solution.py:473
  43.3 3.4 %collective-permute-start.3 = (f32[256,256]{1,0:T(8,128)S(1)}, f32[256,256]{1,0:T(8,128)S(1)}, u32[]{:S(2)}, u32[]{:S(2)}) collective-permute-start(f32[256,256]{1,0:T(8,128)S(1)} %get-tuple-element.19), channel_id=1, source_target_pairs={{0,1},{1,0},{2,3},{3,2},{4,5},{5,4},{6,7},{7,6},{8,9},{9,8},{10,11... | collective-permute-start | bytes 786440 | tf_op jit(solution)/shard_map/ppermute | solution.py:491
  46.6 0.0 copy-done.5
  46.6 0.0 copy-done
  46.7 1.7 %gram.1 = (f32[8,128]{1,0:T(8,128)S(1)}, f32[64,128]{1,0:T(8,128)S(1)}) custom-call(s32[32]{0:T(128)S(1)} %copy-done.5, f32[8,8,8192]{2,1,0:T(8,128)S(1)} %copy-done), custom_call_target="tpu_custom_call" | custom-call | tf_op jit(solution)/shard_map/gram/pallas_call | solution.py:492
  48.3 4.5 %collective-permute-done.3.theirs_ref = f32[256,256]{1,0:T(8,128)S(1)} collective-permute-done((f32[256,256]{1,0:T(8,128)S(1)}, f32[256,256]{1,0:T(8,128)S(1)}, u32[]{:S(2)}, u32[]{:S(2)}) %collective-permute-start.3) | collective-permute-done | bytes 262176 | tf_op jit(solution)/shard_map/ppermute | solution.py:491
  52.8 0.0 copy-done.3
  52.8 0.4 image.1
  53.2 9.3 %all_to_all.10 = f32[4,8,128]{2,1,0:T(8,128)S(1)} all-to-all(f32[4,8,128]{2,1,0:T(8,128)S(1)} %get-tuple-element.22), channel_id=1, replica_groups={{0,2,4,6},{8,10,12,14},{16,18,20,22},{24,26,28,30},{1,3,5,7},{9,11,13,1..., dimensions={0} | all-to-all | bytes 32768 | tf_op jit(solution)/shard_map/all_to_all | solution.py:509
  62.5 9.4 %all_to_all.11.tiles_ref = f32[4,2,8,128]{3,2,1,0:T(8,128)S(1)} all-to-all(f32[4,2,8,128]{3,2,1,0:T(8,128)S(1)} %broadcast_in_dim.2), channel_id=1, replica_groups={{0,8,16,24},{2,10,18,26},{4,12,20,28},{6,14,22,30},{1,9,17,25},{3,11,19..., dimensions={0} | all-to-all | bytes 65536 | tf_op jit(solution)/shard_map/all_to_all | solution.py:517
  71.9 1.6 %finish.1 = (f32[8,8192]{1,0:T(8,128)}, f32[8,9]{1,0:T(8,128)}) custom-call(f32[4,2,8,128]{3,2,1,0:T(8,128)S(1)} %all_to_all.11.tiles_ref, f32[64,128]{1,0:T(8,128)S(1)} %get-tuple-element.21.live_ref, f32[8,8192]{1,0:T(8,128)S(1)} %get-tuple-element.23.image_ref, f32[8,8,8192]{2,1,0:T(8,128)S(1)} %copy-done), custom_call_target="tpu_custom_call" | custom-call | tf_op jit(solution)/shard_map/finish/pallas_call | solution.py:520
  (3 shorter events, 0.0 us)
Async XLA Ops:
  0.6 46.0 %copy-start.5 = (s32[32]{0:T(128)S(1)}, s32[32]{0:T(128)}, u32[]{:S(2)}) copy-start(s32[32]{0:T(128)} %counts_s.1) | copy-start | bytes 388
  0.6 11.6 %copy-start.4 = (f32[3,32]{1,0:T(4,128)S(1)}, f32[3,32]{1,0:T(4,128)}, u32[]{:S(2)}) copy-start(f32[3,32]{1,0:T(4,128)} %centres_s.1) | copy-start | bytes 1156
  0.7 46.0 %copy-start = (f32[8,8,8192]{2,1,0:T(8,128)S(1)}, f32[8,8,8192]{2,1,0:T(8,128)}, u32[]{:S(2)}) copy-start(f32[8,8,8192]{2,1,0:T(8,128)} %basis_ref.5) | copy-start | bytes 6291460
  0.7 52.2 %copy-start.3 = (f32[8192]{0:T(1024)S(1)}, f32[8192]{0:T(1024)}, u32[]{:S(2)}) copy-start(f32[8192]{0:T(1024)} %param.13) | copy-start | bytes 98308
  3.7 8.6 %collective-permute-start.1 = (f32[400,128]{1,0:T(8,128)}, f32[400,128]{1,0:T(8,128)S(1)}, u32[]{:S(2)}, u32[]{:S(2)}) collective-permute-start(f32[400,128]{1,0:T(8,128)} %get-tuple-element.16), channel_id=1, source_target_pairs={{0,2},{2,4},{4,6},{6,8},{8,10},{10,12},{12,14},{14,16},{16,18},{18... | collective-permute-start | bytes 614408 | tf_op jit(solution)/shard_map/ppermute | solution.py:466
  6.1 6.2 %collective-permute-start = (bf16[544,128]{1,0:T(8,128)(2,1)}, bf16[544,128]{1,0:T(8,128)(2,1)S(1)}, u32[]{:S(2)}, u32[]{:S(2)}) collective-permute-start(bf16[544,128]{1,0:T(8,128)(2,1)} %get-tuple-element.15.sent_ref), channel_id=1, source_target_pairs={{0,1},{1,0},{2,3},{3,2},{4,5},{5,4},{6,7},{7,6},{8,9},{9,8},{10,11... | collective-permute-start | bytes 417800 | tf_op jit(solution)/shard_map/ppermute | solution.py:465
  8.0 0.7 collective-permute-start.2
  12.3 1.0 %copy-start.1 = (f32[528,128]{1,0:T(8,128)S(1)}, f32[528,128]{1,0:T(8,128)}, u32[]{:S(2)}) copy-start(f32[528,128]{1,0:T(8,128)} %get-tuple-element.14.local_ref) | copy-start | bytes 811012
  13.2 0.9 %copy-start.2 = (bf16[544,128]{1,0:T(8,128)(2,1)S(1)}, bf16[544,128]{1,0:T(8,128)(2,1)}, u32[]{:S(2)}) copy-start(bf16[544,128]{1,0:T(8,128)(2,1)} %get-tuple-element.15.sent_ref) | copy-start | bytes 417796
  43.3 9.6 %collective-permute-start.3 = (f32[256,256]{1,0:T(8,128)S(1)}, f32[256,256]{1,0:T(8,128)S(1)}, u32[]{:S(2)}, u32[]{:S(2)}) collective-permute-start(f32[256,256]{1,0:T(8,128)S(1)} %get-tuple-element.19), channel_id=1, source_target_pairs={{0,1},{1,0},{2,3},{3,2},{4,5},{5,4},{6,7},{7,6},{8,9},{9,8},{10,11... | collective-permute-start | bytes 786440 | tf_op jit(solution)/shard_map/ppermute | solution.py:491

commit v14 on v13

--- a/solution.py
+++ b/solution.py
@@ -131,64 +131,22 @@
     return pieces[:8] + (pieces[8:16] + pieces[16:24])
 
 
-def store_source_features(local, charges, box, geometry, strengths):
+def store_geometry(local, box, geometry):
     row = lax.broadcasted_iota(jnp.int32, (8, per_box), 0)
     square = jnp.sum(local * local, axis=0, keepdims=True)
     features = jnp.where(row == 3, square, jnp.where(row == 4, 1.0, local))
     high, middle, low = thirds(features)
     rows = stacked_rows((high, high, high, middle, middle, low), per_box)
     geometry[pl.ds(pl.multiple_of(box * depth, depth), depth), :] = rows.astype(bf16)
+
+
+def store_strengths(local, charges, box, strengths):
     products = jnp.concatenate([charges] + [charges * local[a : a + 1] for a in range(3)], axis=0)
-    rows = jnp.concatenate([*thirds(products), jnp.zeros((64, per_box), f32)], axis=0)
-    strengths[pl.ds(pl.multiple_of(box * 256, 256), 256), :] = rows.astype(bf16)
-
-
-def near_planes(sources, geometry, strengths, targets, total, beside=None):
-    def near_rows(item, _):
-        target_y = (item + 1) // 3
-        source_y = target_y + lax.rem(item + 1, 3) - 1
-        runs = []
-        for near_x in range(4):
-            for first in sources:
-                for x in range(max(near_x - 1, 0), min(near_x + 2, 4)):
-                    runs.append((near_x, first + source_y * 4 + x))
-
-        def distances(near_x, box):
-            start = pl.multiple_of((target_y * 4 + near_x) * per_box, per_box)
-            weights = geometry[pl.ds(pl.multiple_of(box * depth, depth), depth), :]
-            return jnp.dot(targets[pl.ds(start, per_box), :], weights, preferred_element_type=f32)
-
-        ahead = distances(*runs[0])
-        cubed = []
-        given = []
-        for i, (near_x, box) in enumerate(runs):
-            here = ahead
-            if i + 1 < len(runs):
-                ahead = distances(*runs[i + 1])
-            inverse = lax.rsqrt(here)
-            cubed.append((inverse * inverse * inverse).astype(bf16))
-            given.append(strengths[pl.ds(pl.multiple_of(box * 256, 256), 256), :])
-            if i + 1 == len(runs) or runs[i + 1][0] != near_x:
-                rows_of = pl.ds(pl.multiple_of((target_y * 4 + near_x) * per_box, per_box), per_box)
-                total[rows_of, :] += lax.dot_general(
-                    jnp.concatenate(cubed, axis=1),
-                    jnp.concatenate(given, axis=1),
-                    (((1,), (1,)), ((), ())),
-                    preferred_element_type=f32,
-                )
-                cubed = []
-                given = []
-        if beside is not None:
-            beside(item)
-        return 0
-
-    lax.fori_loop(0, 10, near_rows, 0)
-
-
-def field_kernel(
-    centres_s, local_ref, sent_ref, cross_ref, first_ref, second_ref, mine_ref, theirs_ref,
-    geometry, strengths, targets, planes, total, far, far_centres, far_moments
-):
+    rows = jnp.concatenate(thirds(products), axis=0)
+    strengths[pl.ds(pl.multiple_of(box * 96, 96), 96), :] = rows.astype(bf16)
+
+
+def feature_kernel(local_ref, sent_ref, geometry, mine, targets, planes):
     boxes = 2 * plane_boxes
     half = lax.axis_index("rhs")
     origin = local_ref[523:526, 0:1]
@@ -196,19 +154,11 @@
 
     def source(slot, _):
         local = padded(wide_tile(local_ref, slot * 16) - origin)
-        charges = jnp.concatenate([wide_charges(sent_ref, slot), wide_charges(cross_ref, slot)], axis=0)
-        store_source_features(local, charges, slot, geometry, strengths)
+        store_geometry(local, slot, geometry)
+        store_strengths(local, wide_charges(sent_ref, slot), slot, mine)
         return 0
 
     lax.fori_loop(0, boxes, source, 0, unroll=4)
-
-    def halo_source(place, _):
-        local = padded(wide_tile(first_ref, 256 + place * 8) - origin)
-        charges = jnp.concatenate([wide_charges(first_ref, place), wide_charges(second_ref, place)], axis=0)
-        store_source_features(local, charges, boxes + place, geometry, strengths)
-        return 0
-
-    lax.fori_loop(0, plane_boxes, halo_source, 0, unroll=4)
 
     def target(place, _):
         start = (half * plane_boxes + place) * 16
@@ -225,9 +175,80 @@
         return 0
 
     lax.fori_loop(0, plane_boxes, target, 0, unroll=4)
+
+
+def near_planes(sources, targets, total, beside):
+    def near_rows(item, _):
+        target_y = (item + 1) // 3
+        source_y = target_y + lax.rem(item + 1, 3) - 1
+        runs = []
+        for near_x in range(4):
+            for source in sources:
+                for x in range(max(near_x - 1, 0), min(near_x + 2, 4)):
+                    runs.append((near_x, source, source_y * 4 + x))
+
+        def rows_at(pair, place, number):
+            ref, first = pair
+            return ref[pl.ds(pl.multiple_of((first + place) * number, number), number), :]
+
+        def distances(near_x, source, place):
+            start = pl.multiple_of((target_y * 4 + near_x) * per_box, per_box)
+            weights = rows_at(source[0], place, depth)
+            return jnp.dot(targets[pl.ds(start, per_box), :], weights, preferred_element_type=f32)
+
+        ahead = distances(*runs[0])
+        cubed = []
+        given = []
+        empty = jnp.zeros((64, per_box), bf16)
+        for i, (near_x, source, place) in enumerate(runs):
+            here = ahead
+            if i + 1 < len(runs):
+                ahead = distances(*runs[i + 1])
+            inverse = lax.rsqrt(here)
+            cubed.append((inverse * inverse * inverse).astype(bf16))
+            given.append(jnp.concatenate([rows_at(source[1], place, 96), rows_at(source[2], place, 96), empty], axis=0))
+            if i + 1 == len(runs) or runs[i + 1][0] != near_x:
+                rows_of = pl.ds(pl.multiple_of((target_y * 4 + near_x) * per_box, per_box), per_box)
+                total[rows_of, :] += lax.dot_general(
+                    jnp.concatenate(cubed, axis=1),
+                    jnp.concatenate(given, axis=1),
+                    (((1,), (1,)), ((), ())),
+                    preferred_element_type=f32,
+                )
+                cubed = []
+                given = []
+        beside(item)
+        return 0
+
+    lax.fori_loop(0, 10, near_rows, 0)
+
+
+def field_kernel(
+    centres_s, local_ref, cross_ref, first_ref, second_ref, geometry, mine, targets, planes, mine_ref, theirs_ref,
+    halo_geometry, halo_mine, theirs, total, far, far_centres, far_moments
+):
+    boxes = 2 * plane_boxes
+    half = lax.axis_index("rhs")
+    origin = local_ref[523:526, 0:1]
+
+    def source(slot, _):
+        local = wide_tile(local_ref, slot * 16) - origin
+        store_strengths(local, wide_charges(cross_ref, slot), slot, theirs)
+        return 0
+
+    lax.fori_loop(0, boxes, source, 0, unroll=4)
+
+    def halo_source(place, _):
+        local = padded(wide_tile(first_ref, 256 + place * 8) - origin)
+        store_geometry(local, place, halo_geometry)
+        store_strengths(local, wide_charges(first_ref, place), place, halo_mine)
+        store_strengths(local, wide_charges(second_ref, place), boxes + place, theirs)
+        return 0
+
+    lax.fori_loop(0, plane_boxes, halo_source, 0, unroll=4)
     total[...] = jnp.zeros_like(total)
 
-    for group, (centres, mine, theirs) in enumerate(
+    for group, (centres, ours, others) in enumerate(
         (
             (first_ref[392:400], first_ref[384:392], second_ref[256:288]),
             (local_ref[520:528], local_ref[512:520], cross_ref[512:544]),
@@ -238,7 +259,7 @@
             far_centres[(group * 3 + a) * 32 : (group * 3 + a + 1) * 32, :] = jnp.broadcast_to(
                 columns[:, a : a + 1], (32, 128)
             )
-        both = jnp.concatenate([mine, whole_moments(theirs.astype(f32))], axis=0)
+        both = jnp.concatenate([ours, whole_moments(others.astype(f32))], axis=0)
         high = both.astype(bf16).astype(f32)
         far_moments[group * 32 : group * 32 + 32, :] = jnp.concatenate([high, both - high], axis=0)
     lane = lax.broadcasted_iota(jnp.int32, (1, 128), 1)
@@ -279,14 +300,19 @@
             k = jnp.minimum(item * 5 + i, 3 * plane_boxes - 1)
             far[pl.ds(pl.multiple_of(k * 16, 16), 16), :] = far_field(k)
 
-    near_planes((0, plane_boxes, 2 * plane_boxes), geometry, strengths, targets, total, far_boxes)
+    sources = [((geometry, p), (mine, p), (theirs, p)) for p in (0, plane_boxes)]
+    sources.append(((halo_geometry, 0), (halo_mine, 0), (theirs, boxes)))
+    near_planes(sources, targets, total, far_boxes)
 
     def near_field(place, _):
         turned = jnp.transpose(total[pl.ds(pl.multiple_of(place * per_box, per_box), per_box), :])
-        sums = turned[:64] + (turned[64:128] + turned[128:192])
         side = planes[pl.ds(pl.multiple_of(place * 8, 8), 8), :]
-        value = side[3:4] * sums[:16] - side[0:1] * sums[16:32]
-        value = value - side[1:2] * sums[32:48] - side[2:3] * sums[48:64]
+        values = []
+        for start in (0, 96):
+            sums = turned[start : start + 32] + (turned[start + 32 : start + 64] + turned[start + 64 : start + 96])
+            value = side[3:4] * sums[:8] - side[0:1] * sums[8:16]
+            values.append(value - side[1:2] * sums[16:24] - side[2:3] * sums[24:32])
+        value = jnp.concatenate(values, axis=0)
         slot = half * plane_boxes + place
         rows = pl.ds(pl.multiple_of(slot * 16, 16), 16)
         far[rows, :] += value + far[pl.ds(pl.multiple_of((boxes + place) * 16, 16), 16), :]
@@ -378,10 +404,10 @@
     krylov = basis_ref.shape[0]
     lane = lax.broadcasted_iota(jnp.int32, (8, 128), 1)
 
-    sums, rest = tiles_ref[0, 0], tiles_ref[0, 1]
+    sums, rest = tiles_ref[0], jnp.zeros((8, 128), f32)
     for i in range(1, tiles_ref.shape[0]):
-        sums, error = two_sum(sums, tiles_ref[i, 0])
-        rest = (rest + tiles_ref[i, 1]) + error
+        sums, error = two_sum(sums, tiles_ref[i])
+        rest = rest + error
     exact = sums + rest
     projections = [exact[:, m : m + 1] / total_facets for m in range(krylov)]
     pairs = [(m, n) for m in range(krylov) for n in range(m + 1)]
@@ -470,16 +496,28 @@
         second, ("box", "rhs"), [(2 * i + 1, 2 * i + 2) for i in ups] + [(2 * i + 2, 2 * i + 1) for i in ups]
     )
     plane_slots = plane_boxes * per_box
+    geometry, strengths, targets, planes = pl.pallas_call(
+        feature_kernel,
+        out_shape=(
+            rows(boxes * depth, per_box, bf16),
+            rows(boxes * 96, per_box, bf16),
+            rows(plane_slots, depth, bf16),
+            rows(plane_boxes * 8, per_box),
+        ),
+        in_specs=[vmem] * 2,
+        out_specs=(vmem,) * 4,
+        compiler_params=limit(12),
+        name="features",
+    )(local, sent)
     mine, theirs = pl.pallas_call(
         field_kernel,
         out_shape=(rows(boxes * 8, per_box),) * 2,
-        in_specs=[smem] + [vmem] * 5,
+        in_specs=[smem] + [vmem] * 8,
         out_specs=(vmem, vmem),
         scratch_shapes=[
-            pltpu.VMEM((3 * plane_boxes * depth, per_box), bf16),
-            pltpu.VMEM((3 * plane_boxes * 256, per_box), bf16),
-            pltpu.VMEM((plane_slots, depth), bf16),
-            pltpu.VMEM((plane_boxes * 8, per_box), f32),
+            pltpu.VMEM((plane_boxes * depth, per_box), bf16),
+            pltpu.VMEM((plane_boxes * 96, per_box), bf16),
+            pltpu.VMEM((3 * plane_boxes * 96, per_box), bf16),
             pltpu.VMEM((plane_slots, 256), f32),
             pltpu.VMEM((3 * plane_boxes * 16, per_box), f32),
             pltpu.VMEM((6 * 32, 128), f32),
@@ -487,7 +525,7 @@
         ],
         compiler_params=limit(32),
         name="fields",
-    )(box_centres, local, sent, cross, first, second)
+    )(box_centres, local, cross, first, second, geometry, strengths, targets, planes)
     theirs = lax.ppermute(theirs, "rhs", swap)
     gram, live = pl.pallas_call(
         gram_kernel,
@@ -497,26 +535,15 @@
         compiler_params=limit(8),
         name="gram",
     )(facet_counts, basis)
-    few = 4 if count % 4 == 0 else 1
     image, tiles = pl.pallas_call(
         image_kernel,
-        out_shape=(rows(rhs_local, facet_local), jax.ShapeDtypeStruct((few, 8, 128), f32)),
+        out_shape=(rows(rhs_local, facet_local), jax.ShapeDtypeStruct((count, 8, 128), f32)),
         in_specs=[vmem] * 6,
         out_specs=(vmem, vmem),
         compiler_params=limit(8),
         name="image",
     )(mine, theirs, gram, live, contrast, basis)
-    tiles = lax.all_to_all(
-        tiles, "box", 0, 0, axis_index_groups=[[i + k for k in range(few)] for i in range(0, count, few)], tiled=True
-    )
-    value, rest = tiles[0], jnp.zeros_like(tiles[0])
-    for i in range(1, few):
-        value, error = two_sum(value, tiles[i])
-        rest = rest + error
-    tiles = jnp.broadcast_to(jnp.stack([value, rest])[None], (count // few, 2, 8, 128))
-    tiles = lax.all_to_all(
-        tiles, "box", 0, 0, axis_index_groups=[list(range(i, count, few)) for i in range(few)], tiled=True
-    )
+    tiles = lax.all_to_all(tiles, "box", 0, 0, tiled=True)
     next_vector, hessenberg = pl.pallas_call(
         functools.partial(finish_kernel, total_facets),
         out_shape=(rows(rhs_local, facet_local), rows(rhs_local, krylov + 1)),

time: 73.8 us -> 68 us (0.921)
  blocking collectives: 18.7 us -> 13.5 us
  waiting for transfers between devices: 8.07 us -> 5.02 us
  Pallas kernels: 35.7 us -> 36.9 us
  local copies, waits for them, and re-layouts: 1.88 us -> 2.82 us
    all_to_all x2 -> x1, blocking collectives: 18.7 us -> 13.5 us  [on_device(): tiles = lax.all_to_all(tiles, 'box', 0, 0, tiled=True)]
    ppermute x1, waiting for transfers between devices: 3.55 us -> 0.01 us  [on_device(): cross = lax.ppermute(sent, 'rhs', swap)]
    pallas_call x0 -> x1, Pallas kernels: none -> 2.01 us  [on_device(): pl.pallas_call(feature_kernel, out_shape=(rows(boxes * depth, per_box, bf...]
    unnamed x12 -> x14, local copies, waits for them, and re-layouts: 1.88 us -> 2.82 us
  transfers between devices with their start and end apart: 4 -> 4, of which waited for: 2 -> 1; matrix products, arithmetic and copies ran while one was open for 0% -> 0% of each run, Pallas kernels for 2% -> 5%
where the time goes in v14:
time: 68 us; the launch traced here: 67.7 us
  Pallas kernels  36.9 us (54%)
  blocking collectives  13.5 us (20%)
  starting transfers between devices  8.76 us (13%)
  waiting for transfers between devices  5.02 us (7%)
  local copies, waits for them, and re-layouts  2.82 us (4%)
  between operations  0.75 us (1%)
    pallas_call x1, Pallas kernels, on_device(): pl.pallas_call(field_kernel, out_shape=(rows(boxes * 8, per_box),) * 2, i...  28.4 us
    all_to_all x1, blocking collectives, on_device(): tiles = lax.all_to_all(tiles, 'box', 0, 0, tiled=True)  13.5 us
    ppermute x1, waiting for transfers between devices, on_device(): theirs = lax.ppermute(theirs, 'rhs', swap)  5.02 us
    ppermute x1, starting transfers between devices, on_device(): theirs = lax.ppermute(theirs, 'rhs', swap)  3.78 us
    pallas_call x1, Pallas kernels, on_device(): pl.pallas_call(prep_kernel, out_shape=(rows(544, dtype=bf16), rows(400),...  2.89 us
    unnamed x14, local copies, waits for them, and re-layouts  2.82 us
    ppermute x1, starting transfers between devices, on_device(): lax.ppermute(first, ('box', 'rhs'), [(2 * i, 2 * i + 2) for i in ups] + [...  2.37 us
    pallas_call x1, Pallas kernels, on_device(): pl.pallas_call(feature_kernel, out_shape=(rows(boxes * depth, per_box, bf...  2.01 us
  transfers between devices with their start and end apart: 4, of which 1 were waited for; matrix products, arithmetic and copies ran while one was open for 0% of the time, Pallas kernels for 5%

profile of v14, /device:TPU:0, one launch (start us, length us, event | category | flops | bytes accessed | tf_op | source)
XLA Modules:
  0.0 67.7 jit_solution(11091952108567812915)
XLA Ops:
  0.6 0.0 copy-start.5
  0.6 2.9 %prepare.1 = (bf16[544,128]{1,0:T(8,128)(2,1)}, f32[400,128]{1,0:T(8,128)}, bf16[288,128]{1,0:T(8,128)(2,1)}, f32[528,128]{1,0:T(8,128)}) custom-call(f32[3,32]{1,0:T(4,128)} %centres_s.1, s32[32]{0:T(128)} %counts_s.1, f32[8,8,8192]{2,1,0:T(8,128)} %basis_ref.5, f32[3,8192]{1,0:T(4,128)} %facets_h.1, f32[64,128]{1,0:T(8,128)} %bitcast.4, f32[3,8192]{1,0:T(4,128)} %normals_h.1), custom_call_target="tpu_custom_call" | custom-call | tf_op jit(solution)/shard_map/prepare/pallas_call | solution.py:472
  3.5 2.4 %collective-permute-start.1 = (f32[400,128]{1,0:T(8,128)}, f32[400,128]{1,0:T(8,128)S(1)}, u32[]{:S(2)}, u32[]{:S(2)}) collective-permute-start(f32[400,128]{1,0:T(8,128)} %get-tuple-element.20), channel_id=1, source_target_pairs={{0,2},{2,4},{4,6},{6,8},{8,10},{10,12},{12,14},{14,16},{16,18},{18... | collective-permute-start | bytes 614408 | tf_op jit(solution)/shard_map/ppermute | solution.py:492
  5.9 2.0 %collective-permute-start = (bf16[544,128]{1,0:T(8,128)(2,1)}, bf16[544,128]{1,0:T(8,128)(2,1)S(1)}, u32[]{:S(2)}, u32[]{:S(2)}) collective-permute-start(bf16[544,128]{1,0:T(8,128)(2,1)} %get-tuple-element.19.sent_ref), channel_id=1, source_target_pairs={{0,1},{1,0},{2,3},{3,2},{4,5},{5,4},{6,7},{7,6},{8,9},{9,8},{10,11... | collective-permute-start | bytes 417800 | tf_op jit(solution)/shard_map/ppermute | solution.py:491
  7.9 0.7 collective-permute-start.2
  8.5 0.0 copy-start.1
  8.5 0.9 %copy-done.1 = f32[528,128]{1,0:T(8,128)S(1)} copy-done((f32[528,128]{1,0:T(8,128)S(1)}, f32[528,128]{1,0:T(8,128)}, u32[]{:S(2)}) %copy-start.1) | copy-done | bytes 270360
  9.5 0.0 copy-start.3
  9.5 0.9 %copy-done.3 = bf16[544,128]{1,0:T(8,128)(2,1)S(1)} copy-done((bf16[544,128]{1,0:T(8,128)(2,1)S(1)}, bf16[544,128]{1,0:T(8,128)(2,1)}, u32[]{:S(2)}) %copy-start.3) | copy-done | bytes 139288
  10.4 2.0 %features.1 = (bf16[4096,256]{1,0:T(8,128)(2,1)S(1)}, bf16[3072,256]{1,0:T(8,128)(2,1)S(1)}, bf16[4096,128]{1,0:T(8,128)(2,1)S(1)}, f32[128,256]{1,0:T(8,128)S(1)}) custom-call(f32[528,128]{1,0:T(8,128)S(1)} %copy-done.1, bf16[544,128]{1,0:T(8,128)(2,1)S(1)} %copy-done.3), custom_call_target="tpu_custom_call" | custom-call | tf_op jit(solution)/shard_map/features/pallas_call | solution.py:499
  12.4 0.0 collective-permute-done.2.second_ref
  12.4 0.0 collective-permute-done.cross_ref
  12.4 0.0 collective-permute-done.1.first_ref
  12.4 0.0 copy-done.5
  12.4 0.0 copy-start.2
  12.5 0.9 %copy-done.2 = f32[528,128]{1,0:T(8,128)S(1)} copy-done((f32[528,128]{1,0:T(8,128)S(1)}, f32[528,128]{1,0:T(8,128)}, u32[]{:S(2)}) %copy-start.2) | copy-done | bytes 270360
  13.4 0.0 copy-start
  13.4 0.0 copy-start.6
  13.4 28.4 %fields.1 = (f32[256,256]{1,0:T(8,128)S(1)}, f32[256,256]{1,0:T(8,128)S(1)}) custom-call(f32[3,32]{1,0:T(4,128)S(1)} %copy-done.5, f32[528,128]{1,0:T(8,128)S(1)} %copy-done.2, bf16[544,128]{1,0:T(8,128)(2,1)S(1)} %collective-permute-done.cross_ref, f32[400,128]{1,0:T(8,128)S(1)} %collective-permute-done.1.first_ref, ...), custom_call_target="tpu_custom_call" | custom-call | tf_op jit(solution)/shard_map/fields/pallas_call | solution.py:512
  41.8 0.0 copy-start.4
  41.8 3.8 %collective-permute-start.3 = (f32[256,256]{1,0:T(8,128)S(1)}, f32[256,256]{1,0:T(8,128)S(1)}, u32[]{:S(2)}, u32[]{:S(2)}) collective-permute-start(f32[256,256]{1,0:T(8,128)S(1)} %get-tuple-element.27), channel_id=1, source_target_pairs={{0,1},{1,0},{2,3},{3,2},{4,5},{5,4},{6,7},{7,6},{8,9},{9,8},{10,11... | collective-permute-start | bytes 786440 | tf_op jit(solution)/shard_map/ppermute | solution.py:529
  45.6 0.0 copy-done
  45.6 0.0 copy-done.6
  45.6 1.7 %gram.1 = (f32[8,128]{1,0:T(8,128)S(1)}, f32[64,128]{1,0:T(8,128)S(1)}) custom-call(s32[32]{0:T(128)S(1)} %copy-done.6, f32[8,8,8192]{2,1,0:T(8,128)S(1)} %copy-done), custom_call_target="tpu_custom_call" | custom-call | tf_op jit(solution)/shard_map/gram/pallas_call | solution.py:530
  47.3 5.0 %collective-permute-done.3.theirs_ref = f32[256,256]{1,0:T(8,128)S(1)} collective-permute-done((f32[256,256]{1,0:T(8,128)S(1)}, f32[256,256]{1,0:T(8,128)S(1)}, u32[]{:S(2)}, u32[]{:S(2)}) %collective-permute-start.3) | collective-permute-done | bytes 262176 | tf_op jit(solution)/shard_map/ppermute | solution.py:529
  52.3 0.0 copy-done.4
  52.3 0.4 image.1
  52.6 13.5 %all_to_all.5.tiles_ref = f32[16,8,128]{2,1,0:T(8,128)S(1)} all-to-all(f32[16,8,128]{2,1,0:T(8,128)S(1)} %get-tuple-element.30), channel_id=1, replica_groups=mesh['box'=16,'rhs'=2] {'box'}, dimensions={0} | all-to-all | bytes 131072 | tf_op jit(solution)/shard_map/all_to_all | solution.py:546
  66.1 1.6 %finish.1 = (f32[8,8192]{1,0:T(8,128)}, f32[8,9]{1,0:T(8,128)}) custom-call(f32[16,8,128]{2,1,0:T(8,128)S(1)} %all_to_all.5.tiles_ref, f32[64,128]{1,0:T(8,128)S(1)} %get-tuple-element.29.live_ref, f32[8,8192]{1,0:T(8,128)S(1)} %get-tuple-element.31.image_ref, f32[8,8,8192]{2,1,0:T(8,128)S(1)} %copy-done), custom_call_target="tpu_custom_call" | custom-call | tf_op jit(solution)/shard_map/finish/pallas_call | solution.py:547
Async XLA Ops:
  0.6 11.8 %copy-start.5 = (f32[3,32]{1,0:T(4,128)S(1)}, f32[3,32]{1,0:T(4,128)}, u32[]{:S(2)}) copy-start(f32[3,32]{1,0:T(4,128)} %centres_s.1) | copy-start | bytes 1156
  3.5 8.9 %collective-permute-start.1 = (f32[400,128]{1,0:T(8,128)}, f32[400,128]{1,0:T(8,128)S(1)}, u32[]{:S(2)}, u32[]{:S(2)}) collective-permute-start(f32[400,128]{1,0:T(8,128)} %get-tuple-element.20), channel_id=1, source_target_pairs={{0,2},{2,4},{4,6},{6,8},{8,10},{10,12},{12,14},{14,16},{16,18},{18... | collective-permute-start | bytes 614408 | tf_op jit(solution)/shard_map/ppermute | solution.py:492
  5.9 6.5 %collective-permute-start = (bf16[544,128]{1,0:T(8,128)(2,1)}, bf16[544,128]{1,0:T(8,128)(2,1)S(1)}, u32[]{:S(2)}, u32[]{:S(2)}) collective-permute-start(bf16[544,128]{1,0:T(8,128)(2,1)} %get-tuple-element.19.sent_ref), channel_id=1, source_target_pairs={{0,1},{1,0},{2,3},{3,2},{4,5},{5,4},{6,7},{7,6},{8,9},{9,8},{10,11... | collective-permute-start | bytes 417800 | tf_op jit(solution)/shard_map/ppermute | solution.py:491
  7.9 4.5 %collective-permute-start.2 = (bf16[288,128]{1,0:T(8,128)(2,1)}, bf16[288,128]{1,0:T(8,128)(2,1)S(1)}, u32[]{:S(2)}, u32[]{:S(2)}) collective-permute-start(bf16[288,128]{1,0:T(8,128)(2,1)} %get-tuple-element.21), channel_id=1, source_target_pairs={{1,2},{3,4},{5,6},{7,8},{9,10},{11,12},{13,14},{15,16},{17,18},{19... | collective-permute-start | bytes 221192 | tf_op jit(solution)/shard_map/ppermute | solution.py:495
  8.5 1.0 %copy-start.1 = (f32[528,128]{1,0:T(8,128)S(1)}, f32[528,128]{1,0:T(8,128)}, u32[]{:S(2)}) copy-start(f32[528,128]{1,0:T(8,128)} %get-tuple-element.18.local_ref) | copy-start | bytes 811012
  9.5 0.9 %copy-start.3 = (bf16[544,128]{1,0:T(8,128)(2,1)S(1)}, bf16[544,128]{1,0:T(8,128)(2,1)}, u32[]{:S(2)}) copy-start(bf16[544,128]{1,0:T(8,128)(2,1)} %get-tuple-element.19.sent_ref) | copy-start | bytes 417796
  12.4 1.0 %copy-start.2 = (f32[528,128]{1,0:T(8,128)S(1)}, f32[528,128]{1,0:T(8,128)}, u32[]{:S(2)}) copy-start(f32[528,128]{1,0:T(8,128)} %get-tuple-element.18.local_ref) | copy-start | bytes 811012
  13.4 32.2 %copy-start = (f32[8,8,8192]{2,1,0:T(8,128)S(1)}, f32[8,8,8192]{2,1,0:T(8,128)}, u32[]{:S(2)}) copy-start(f32[8,8,8192]{2,1,0:T(8,128)} %basis_ref.5) | copy-start | bytes 6291460
  13.4 32.2 %copy-start.6 = (s32[32]{0:T(128)S(1)}, s32[32]{0:T(128)}, u32[]{:S(2)}) copy-start(s32[32]{0:T(128)} %counts_s.1) | copy-start | bytes 388
  41.8 10.5 %copy-start.4 = (f32[8192]{0:T(1024)S(1)}, f32[8192]{0:T(1024)}, u32[]{:S(2)}) copy-start(f32[8192]{0:T(1024)} %param.13) | copy-start | bytes 98308
  41.8 10.5 %collective-permute-start.3 = (f32[256,256]{1,0:T(8,128)S(1)}, f32[256,256]{1,0:T(8,128)S(1)}, u32[]{:S(2)}, u32[]{:S(2)}) collective-permute-start(f32[256,256]{1,0:T(8,128)S(1)} %get-tuple-element.27), channel_id=1, source_target_pairs={{0,1},{1,0},{2,3},{3,2},{4,5},{5,4},{6,7},{7,6},{8,9},{9,8},{10,11... | collective-permute-start | bytes 786440 | tf_op jit(solution)/shard_map/ppermute | solution.py:529

commit v15 on v14

--- a/solution.py
+++ b/solution.py
@@ -141,12 +141,12 @@
 
 
 def store_strengths(local, charges, box, strengths):
-    products = jnp.concatenate([charges] + [charges * local[a : a + 1] for a in range(3)], axis=0)
-    rows = jnp.concatenate(thirds(products), axis=0)
-    strengths[pl.ds(pl.multiple_of(box * 96, 96), 96), :] = rows.astype(bf16)
-
-
-def feature_kernel(local_ref, sent_ref, geometry, mine, targets, planes):
+    products = jnp.concatenate([charges * local[a : a + 1] for a in range(3)], axis=0)
+    rows = jnp.concatenate([charges, *thirds(products)], axis=0)
+    strengths[pl.ds(pl.multiple_of(box * 80, 80), 80), :] = rows.astype(bf16)
+
+
+def feature_kernel(local_ref, sent_ref, geometry, mine, targets, planes, local_out):
     boxes = 2 * plane_boxes
     half = lax.axis_index("rhs")
     origin = local_ref[523:526, 0:1]
@@ -175,6 +175,7 @@
         return 0
 
     lax.fori_loop(0, plane_boxes, target, 0, unroll=4)
+    local_out[...] = local_ref[...]
 
 
 def near_planes(sources, targets, total, beside):
@@ -199,19 +200,18 @@
         ahead = distances(*runs[0])
         cubed = []
         given = []
-        empty = jnp.zeros((64, per_box), bf16)
         for i, (near_x, source, place) in enumerate(runs):
             here = ahead
             if i + 1 < len(runs):
                 ahead = distances(*runs[i + 1])
             inverse = lax.rsqrt(here)
             cubed.append((inverse * inverse * inverse).astype(bf16))
-            given.append(jnp.concatenate([rows_at(source[1], place, 96), rows_at(source[2], place, 96), empty], axis=0))
+            given.append(jnp.concatenate([rows_at(source[1], place, 80), rows_at(source[2], place, 80)], axis=0))
             if i + 1 == len(runs) or runs[i + 1][0] != near_x:
-                rows_of = pl.ds(pl.multiple_of((target_y * 4 + near_x) * per_box, per_box), per_box)
+                rows_of = pl.ds(pl.multiple_of((target_y * 4 + near_x) * 160, 160), 160)
                 total[rows_of, :] += lax.dot_general(
+                    jnp.concatenate(given, axis=1),
                     jnp.concatenate(cubed, axis=1),
-                    jnp.concatenate(given, axis=1),
                     (((1,), (1,)), ((), ())),
                     preferred_element_type=f32,
                 )
@@ -305,13 +305,15 @@
     near_planes(sources, targets, total, far_boxes)
 
     def near_field(place, _):
-        turned = jnp.transpose(total[pl.ds(pl.multiple_of(place * per_box, per_box), per_box), :])
+        sums = total[pl.ds(pl.multiple_of(place * 160, 160), 160), :]
         side = planes[pl.ds(pl.multiple_of(place * 8, 8), 8), :]
         values = []
-        for start in (0, 96):
-            sums = turned[start : start + 32] + (turned[start + 32 : start + 64] + turned[start + 64 : start + 96])
-            value = side[3:4] * sums[:8] - side[0:1] * sums[8:16]
-            values.append(value - side[1:2] * sums[16:24] - side[2:3] * sums[24:32])
+        for start in (0, 80):
+            value = side[3:4] * sums[start : start + 8]
+            for a in range(3):
+                high, middle, low = (sums[i : i + 8] for i in range(start + 8 + 8 * a, start + 80, 24))
+                value = value - side[a : a + 1] * (high + (middle + low))
+            values.append(value)
         value = jnp.concatenate(values, axis=0)
         slot = half * plane_boxes + place
         rows = pl.ds(pl.multiple_of(slot * 16, 16), 16)
@@ -496,16 +498,17 @@
         second, ("box", "rhs"), [(2 * i + 1, 2 * i + 2) for i in ups] + [(2 * i + 2, 2 * i + 1) for i in ups]
     )
     plane_slots = plane_boxes * per_box
-    geometry, strengths, targets, planes = pl.pallas_call(
+    geometry, strengths, targets, planes, local = pl.pallas_call(
         feature_kernel,
         out_shape=(
             rows(boxes * depth, per_box, bf16),
-            rows(boxes * 96, per_box, bf16),
+            rows(boxes * 80, per_box, bf16),
             rows(plane_slots, depth, bf16),
             rows(plane_boxes * 8, per_box),
+            rows(528),
         ),
         in_specs=[vmem] * 2,
-        out_specs=(vmem,) * 4,
+        out_specs=(vmem,) * 5,
         compiler_params=limit(12),
         name="features",
     )(local, sent)
@@ -516,9 +519,9 @@
         out_specs=(vmem, vmem),
         scratch_shapes=[
             pltpu.VMEM((plane_boxes * depth, per_box), bf16),
-            pltpu.VMEM((plane_boxes * 96, per_box), bf16),
-            pltpu.VMEM((3 * plane_boxes * 96, per_box), bf16),
-            pltpu.VMEM((plane_slots, 256), f32),
+            pltpu.VMEM((plane_boxes * 80, per_box), bf16),
+            pltpu.VMEM((3 * plane_boxes * 80, per_box), bf16),
+            pltpu.VMEM((plane_boxes * 160, per_box), f32),
             pltpu.VMEM((3 * plane_boxes * 16, per_box), f32),
             pltpu.VMEM((6 * 32, 128), f32),
             pltpu.VMEM((2 * 32, 128), f32),

time: 68 us -> 66.3 us (0.975)
  local copies, waits for them, and re-layouts: 2.82 us -> 1.88 us
  Pallas kernels: 36.9 us -> 36.2 us
    unnamed x14 -> x12, local copies, waits for them, and re-layouts: 2.82 us -> 1.88 us
where the time goes in v15:
time: 66.3 us; the launch traced here: 66.1 us
  Pallas kernels  36.2 us (55%)
  blocking collectives  13.5 us (20%)
  starting transfers between devices  8.76 us (13%)
  waiting for transfers between devices  5.02 us (8%)
  local copies, waits for them, and re-layouts  1.88 us (3%)
  between operations  0.76 us (1%)
    pallas_call x1, Pallas kernels, on_device(): pl.pallas_call(field_kernel, out_shape=(rows(boxes * 8, per_box),) * 2, i...  27.7 us
    all_to_all x1, blocking collectives, on_device(): tiles = lax.all_to_all(tiles, 'box', 0, 0, tiled=True)  13.5 us
    ppermute x1, waiting for transfers between devices, on_device(): theirs = lax.ppermute(theirs, 'rhs', swap)  5.02 us
    ppermute x1, starting transfers between devices, on_device(): theirs = lax.ppermute(theirs, 'rhs', swap)  3.78 us
    pallas_call x1, Pallas kernels, on_device(): pl.pallas_call(prep_kernel, out_shape=(rows(544, dtype=bf16), rows(400),...  2.89 us
    ppermute x1, starting transfers between devices, on_device(): lax.ppermute(first, ('box', 'rhs'), [(2 * i, 2 * i + 2) for i in ups] + [...  2.37 us
    ppermute x1, starting transfers between devices, on_device(): cross = lax.ppermute(sent, 'rhs', swap)  1.96 us
    pallas_call x1, Pallas kernels, on_device(): pl.pallas_call(feature_kernel, out_shape=(rows(boxes * depth, per_box, bf...  1.95 us
  transfers between devices with their start and end apart: 4, of which 1 were waited for; matrix products, arithmetic and copies ran while one was open for 0% of the time, Pallas kernels for 5%

profile of v15, /device:TPU:0, one launch (start us, length us, event | category | flops | bytes accessed | tf_op | source)
XLA Modules:
  0.0 66.1 jit_solution(14090530925429887915)
XLA Ops:
  0.6 0.0 copy-start.4
  0.6 2.9 %prepare.1 = (bf16[544,128]{1,0:T(8,128)(2,1)}, f32[400,128]{1,0:T(8,128)}, bf16[288,128]{1,0:T(8,128)(2,1)}, f32[528,128]{1,0:T(8,128)}) custom-call(f32[3,32]{1,0:T(4,128)} %centres_s.1, s32[32]{0:T(128)} %counts_s.1, f32[8,8,8192]{2,1,0:T(8,128)} %basis_ref.5, f32[3,8192]{1,0:T(4,128)} %facets_h.1, f32[64,128]{1,0:T(8,128)} %bitcast.4, f32[3,8192]{1,0:T(4,128)} %normals_h.1), custom_call_target="tpu_custom_call" | custom-call | tf_op jit(solution)/shard_map/prepare/pallas_call | solution.py:474
  3.5 2.4 %collective-permute-start.1 = (f32[400,128]{1,0:T(8,128)}, f32[400,128]{1,0:T(8,128)S(1)}, u32[]{:S(2)}, u32[]{:S(2)}) collective-permute-start(f32[400,128]{1,0:T(8,128)} %get-tuple-element.22), channel_id=1, source_target_pairs={{0,2},{2,4},{4,6},{6,8},{8,10},{10,12},{12,14},{14,16},{16,18},{18... | collective-permute-start | bytes 614408 | tf_op jit(solution)/shard_map/ppermute | solution.py:494
  5.9 2.0 %collective-permute-start = (bf16[544,128]{1,0:T(8,128)(2,1)}, bf16[544,128]{1,0:T(8,128)(2,1)S(1)}, u32[]{:S(2)}, u32[]{:S(2)}) collective-permute-start(bf16[544,128]{1,0:T(8,128)(2,1)} %get-tuple-element.20.sent_ref), channel_id=1, source_target_pairs={{0,1},{1,0},{2,3},{3,2},{4,5},{5,4},{6,7},{7,6},{8,9},{9,8},{10,11... | collective-permute-start | bytes 417800 | tf_op jit(solution)/shard_map/ppermute | solution.py:493
  7.9 0.7 collective-permute-start.2
  8.5 0.0 copy-start.1
  8.5 0.9 %copy-done.1 = f32[528,128]{1,0:T(8,128)S(1)} copy-done((f32[528,128]{1,0:T(8,128)S(1)}, f32[528,128]{1,0:T(8,128)}, u32[]{:S(2)}) %copy-start.1) | copy-done | bytes 270360
  9.5 0.0 copy-start.2
  9.5 0.9 %copy-done.2 = bf16[544,128]{1,0:T(8,128)(2,1)S(1)} copy-done((bf16[544,128]{1,0:T(8,128)(2,1)S(1)}, bf16[544,128]{1,0:T(8,128)(2,1)}, u32[]{:S(2)}) %copy-start.2) | copy-done | bytes 139288
  10.4 2.0 %features.1 = (bf16[4096,256]{1,0:T(8,128)(2,1)S(1)}, bf16[2560,256]{1,0:T(8,128)(2,1)S(1)}, bf16[4096,128]{1,0:T(8,128)(2,1)S(1)}, f32[128,256]{1,0:T(8,128)S(1)}, f32[528,128]{1,0:T(8,128)S(1)}) custom-call(f32[528,128]{1,0:T(8,128)S(1)} %copy-done.1, bf16[544,128]{1,0:T(8,128)(2,1)S(1)} %copy-done.2), custom_call_target="tpu_custom_call" | custom-call | tf_op jit(solution)/shard_map/features/pallas_call | solution.py:501
  12.4 0.0 collective-permute-done.2.second_ref
  12.4 0.0 collective-permute-done.cross_ref
  12.4 0.0 collective-permute-done.1.first_ref
  12.4 0.0 copy-done.4
  12.4 0.0 copy-start
  12.4 0.0 copy-start.5
  12.4 27.7 %fields.1 = (f32[256,256]{1,0:T(8,128)S(1)}, f32[256,256]{1,0:T(8,128)S(1)}) custom-call(f32[3,32]{1,0:T(4,128)S(1)} %copy-done.4, f32[528,128]{1,0:T(8,128)S(1)} %get-tuple-element.21.local_ref, bf16[544,128]{1,0:T(8,128)(2,1)S(1)} %collective-permute-done.cross_ref, f32[400,128]{1,0:T(8,128)S(1)} %collective-permute-done.1.first_ref, ...), custom_call_target="tpu_custom_call" | custom-call | tf_op jit(solution)/shard_map/fields/pallas_call | solution.py:515
  40.2 0.0 copy-start.3
  40.2 3.8 %collective-permute-start.3 = (f32[256,256]{1,0:T(8,128)S(1)}, f32[256,256]{1,0:T(8,128)S(1)}, u32[]{:S(2)}, u32[]{:S(2)}) collective-permute-start(f32[256,256]{1,0:T(8,128)S(1)} %get-tuple-element.29), channel_id=1, source_target_pairs={{0,1},{1,0},{2,3},{3,2},{4,5},{5,4},{6,7},{7,6},{8,9},{9,8},{10,11... | collective-permute-start | bytes 786440 | tf_op jit(solution)/shard_map/ppermute | solution.py:532
  43.9 0.0 copy-done
  44.0 0.0 copy-done.5
  44.0 1.7 %gram.1 = (f32[8,128]{1,0:T(8,128)S(1)}, f32[64,128]{1,0:T(8,128)S(1)}) custom-call(s32[32]{0:T(128)S(1)} %copy-done.5, f32[8,8,8192]{2,1,0:T(8,128)S(1)} %copy-done), custom_call_target="tpu_custom_call" | custom-call | tf_op jit(solution)/shard_map/gram/pallas_call | solution.py:533
  45.6 5.0 %collective-permute-done.3.theirs_ref = f32[256,256]{1,0:T(8,128)S(1)} collective-permute-done((f32[256,256]{1,0:T(8,128)S(1)}, f32[256,256]{1,0:T(8,128)S(1)}, u32[]{:S(2)}, u32[]{:S(2)}) %collective-permute-start.3) | collective-permute-done | bytes 262176 | tf_op jit(solution)/shard_map/ppermute | solution.py:532
  50.6 0.0 copy-done.3
  50.6 0.4 image.1
  51.0 13.5 %all_to_all.5.tiles_ref = f32[16,8,128]{2,1,0:T(8,128)S(1)} all-to-all(f32[16,8,128]{2,1,0:T(8,128)S(1)} %get-tuple-element.32), channel_id=1, replica_groups=mesh['box'=16,'rhs'=2] {'box'}, dimensions={0} | all-to-all | bytes 131072 | tf_op jit(solution)/shard_map/all_to_all | solution.py:549
  64.5 1.6 %finish.1 = (f32[8,8192]{1,0:T(8,128)}, f32[8,9]{1,0:T(8,128)}) custom-call(f32[16,8,128]{2,1,0:T(8,128)S(1)} %all_to_all.5.tiles_ref, f32[64,128]{1,0:T(8,128)S(1)} %get-tuple-element.31.live_ref, f32[8,8192]{1,0:T(8,128)S(1)} %get-tuple-element.33.image_ref, f32[8,8,8192]{2,1,0:T(8,128)S(1)} %copy-done), custom_call_target="tpu_custom_call" | custom-call | tf_op jit(solution)/shard_map/finish/pallas_call | solution.py:550
Async XLA Ops:
  0.6 11.8 %copy-start.4 = (f32[3,32]{1,0:T(4,128)S(1)}, f32[3,32]{1,0:T(4,128)}, u32[]{:S(2)}) copy-start(f32[3,32]{1,0:T(4,128)} %centres_s.1) | copy-start | bytes 1156
  3.5 8.8 %collective-permute-start.1 = (f32[400,128]{1,0:T(8,128)}, f32[400,128]{1,0:T(8,128)S(1)}, u32[]{:S(2)}, u32[]{:S(2)}) collective-permute-start(f32[400,128]{1,0:T(8,128)} %get-tuple-element.22), channel_id=1, source_target_pairs={{0,2},{2,4},{4,6},{6,8},{8,10},{10,12},{12,14},{14,16},{16,18},{18... | collective-permute-start | bytes 614408 | tf_op jit(solution)/shard_map/ppermute | solution.py:494
  5.9 6.5 %collective-permute-start = (bf16[544,128]{1,0:T(8,128)(2,1)}, bf16[544,128]{1,0:T(8,128)(2,1)S(1)}, u32[]{:S(2)}, u32[]{:S(2)}) collective-permute-start(bf16[544,128]{1,0:T(8,128)(2,1)} %get-tuple-element.20.sent_ref), channel_id=1, source_target_pairs={{0,1},{1,0},{2,3},{3,2},{4,5},{5,4},{6,7},{7,6},{8,9},{9,8},{10,11... | collective-permute-start | bytes 417800 | tf_op jit(solution)/shard_map/ppermute | solution.py:493
  7.9 4.5 %collective-permute-start.2 = (bf16[288,128]{1,0:T(8,128)(2,1)}, bf16[288,128]{1,0:T(8,128)(2,1)S(1)}, u32[]{:S(2)}, u32[]{:S(2)}) collective-permute-start(bf16[288,128]{1,0:T(8,128)(2,1)} %get-tuple-element.23), channel_id=1, source_target_pairs={{1,2},{3,4},{5,6},{7,8},{9,10},{11,12},{13,14},{15,16},{17,18},{19... | collective-permute-start | bytes 221192 | tf_op jit(solution)/shard_map/ppermute | solution.py:497
  8.5 1.0 %copy-start.1 = (f32[528,128]{1,0:T(8,128)S(1)}, f32[528,128]{1,0:T(8,128)}, u32[]{:S(2)}) copy-start(f32[528,128]{1,0:T(8,128)} %get-tuple-element.19.local_ref) | copy-start | bytes 811012
  9.5 0.9 %copy-start.2 = (bf16[544,128]{1,0:T(8,128)(2,1)S(1)}, bf16[544,128]{1,0:T(8,128)(2,1)}, u32[]{:S(2)}) copy-start(bf16[544,128]{1,0:T(8,128)(2,1)} %get-tuple-element.20.sent_ref) | copy-start | bytes 417796
  12.4 31.6 %copy-start = (f32[8,8,8192]{2,1,0:T(8,128)S(1)}, f32[8,8,8192]{2,1,0:T(8,128)}, u32[]{:S(2)}) copy-start(f32[8,8,8192]{2,1,0:T(8,128)} %basis_ref.5) | copy-start | bytes 6291460
  12.4 31.5 %copy-start.5 = (s32[32]{0:T(128)S(1)}, s32[32]{0:T(128)}, u32[]{:S(2)}) copy-start(s32[32]{0:T(128)} %counts_s.1) | copy-start | bytes 388
  40.2 10.5 %copy-start.3 = (f32[8192]{0:T(1024)S(1)}, f32[8192]{0:T(1024)}, u32[]{:S(2)}) copy-start(f32[8192]{0:T(1024)} %param.13) | copy-start | bytes 98308
  40.2 10.5 %collective-permute-start.3 = (f32[256,256]{1,0:T(8,128)S(1)}, f32[256,256]{1,0:T(8,128)S(1)}, u32[]{:S(2)}, u32[]{:S(2)}) collective-permute-start(f32[256,256]{1,0:T(8,128)S(1)} %get-tuple-element.29), channel_id=1, source_target_pairs={{0,1},{1,0},{2,3},{3,2},{4,5},{5,4},{6,7},{7,6},{8,9},{9,8},{10,11... | collective-permute-start | bytes 786440 | tf_op jit(solution)/shard_map/ppermute | solution.py:532

commit v16 on v15

--- a/solution.py
+++ b/solution.py
@@ -13,7 +13,7 @@
 bf16 = jnp.bfloat16
 plane_boxes = 16
 per_box = 256
-depth = 128
+depth = 64
 
 
 def lattice(centres_s, b):

time: 66.3 us -> 66.1 us (level)
  no operation moved by 1% of the time
where the time goes in v16:
time: 66.1 us; the launch traced here: 65.8 us
  Pallas kernels  36 us (54%)
  blocking collectives  13.5 us (20%)
  starting transfers between devices  8.76 us (13%)
  waiting for transfers between devices  5.03 us (8%)
  local copies, waits for them, and re-layouts  1.88 us (3%)
  between operations  0.76 us (1%)
    pallas_call x1, Pallas kernels, on_device(): pl.pallas_call(field_kernel, out_shape=(rows(boxes * 8, per_box),) * 2, i...  27.5 us
    all_to_all x1, blocking collectives, on_device(): tiles = lax.all_to_all(tiles, 'box', 0, 0, tiled=True)  13.5 us
    ppermute x1, waiting for transfers between devices, on_device(): theirs = lax.ppermute(theirs, 'rhs', swap)  5.02 us
    ppermute x1, starting transfers between devices, on_device(): theirs = lax.ppermute(theirs, 'rhs', swap)  3.78 us
    pallas_call x1, Pallas kernels, on_device(): pl.pallas_call(prep_kernel, out_shape=(rows(544, dtype=bf16), rows(400),...  2.89 us
    ppermute x1, starting transfers between devices, on_device(): lax.ppermute(first, ('box', 'rhs'), [(2 * i, 2 * i + 2) for i in ups] + [...  2.37 us
    ppermute x1, starting transfers between devices, on_device(): cross = lax.ppermute(sent, 'rhs', swap)  1.96 us
    pallas_call x1, Pallas kernels, on_device(): pl.pallas_call(feature_kernel, out_shape=(rows(boxes * depth, per_box, bf...  1.94 us
  transfers between devices with their start and end apart: 4, of which 1 were waited for; matrix products, arithmetic and copies ran while one was open for 0% of the time, Pallas kernels for 5%

profile of v16, /device:TPU:0, one launch (start us, length us, event | category | flops | bytes accessed | tf_op | source)
XLA Modules:
  0.0 65.8 jit_solution(16488984084632898714)
XLA Ops:
  0.6 0.0 copy-start.4
  0.6 2.9 %prepare.1 = (bf16[544,128]{1,0:T(8,128)(2,1)}, f32[400,128]{1,0:T(8,128)}, bf16[288,128]{1,0:T(8,128)(2,1)}, f32[528,128]{1,0:T(8,128)}) custom-call(f32[3,32]{1,0:T(4,128)} %centres_s.1, s32[32]{0:T(128)} %counts_s.1, f32[8,8,8192]{2,1,0:T(8,128)} %basis_ref.5, f32[3,8192]{1,0:T(4,128)} %facets_h.1, f32[64,128]{1,0:T(8,128)} %bitcast.4, f32[3,8192]{1,0:T(4,128)} %normals_h.1), custom_call_target="tpu_custom_call" | custom-call | tf_op jit(solution)/shard_map/prepare/pallas_call | solution.py:474
  3.5 2.4 %collective-permute-start.1 = (f32[400,128]{1,0:T(8,128)}, f32[400,128]{1,0:T(8,128)S(1)}, u32[]{:S(2)}, u32[]{:S(2)}) collective-permute-start(f32[400,128]{1,0:T(8,128)} %get-tuple-element.22), channel_id=1, source_target_pairs={{0,2},{2,4},{4,6},{6,8},{8,10},{10,12},{12,14},{14,16},{16,18},{18... | collective-permute-start | bytes 614408 | tf_op jit(solution)/shard_map/ppermute | solution.py:494
  5.9 2.0 %collective-permute-start = (bf16[544,128]{1,0:T(8,128)(2,1)}, bf16[544,128]{1,0:T(8,128)(2,1)S(1)}, u32[]{:S(2)}, u32[]{:S(2)}) collective-permute-start(bf16[544,128]{1,0:T(8,128)(2,1)} %get-tuple-element.20.sent_ref), channel_id=1, source_target_pairs={{0,1},{1,0},{2,3},{3,2},{4,5},{5,4},{6,7},{7,6},{8,9},{9,8},{10,11... | collective-permute-start | bytes 417800 | tf_op jit(solution)/shard_map/ppermute | solution.py:493
  7.9 0.7 collective-permute-start.2
  8.5 0.0 copy-start.1
  8.5 0.9 %copy-done.1 = f32[528,128]{1,0:T(8,128)S(1)} copy-done((f32[528,128]{1,0:T(8,128)S(1)}, f32[528,128]{1,0:T(8,128)}, u32[]{:S(2)}) %copy-start.1) | copy-done | bytes 270360
  9.5 0.0 copy-start.2
  9.5 0.9 %copy-done.2 = bf16[544,128]{1,0:T(8,128)(2,1)S(1)} copy-done((bf16[544,128]{1,0:T(8,128)(2,1)S(1)}, bf16[544,128]{1,0:T(8,128)(2,1)}, u32[]{:S(2)}) %copy-start.2) | copy-done | bytes 139288
  10.4 1.9 %features.1 = (bf16[2048,256]{1,0:T(8,128)(2,1)S(1)}, bf16[2560,256]{1,0:T(8,128)(2,1)S(1)}, bf16[4096,64]{1,0:T(8,128)(2,1)S(1)}, f32[128,256]{1,0:T(8,128)S(1)}, f32[528,128]{1,0:T(8,128)S(1)}) custom-call(f32[528,128]{1,0:T(8,128)S(1)} %copy-done.1, bf16[544,128]{1,0:T(8,128)(2,1)S(1)} %copy-done.2), custom_call_target="tpu_custom_call" | custom-call | tf_op jit(solution)/shard_map/features/pallas_call | solution.py:501
  12.3 0.0 collective-permute-done.2.second_ref
  12.4 0.0 collective-permute-done.cross_ref
  12.4 0.0 collective-permute-done.1.first_ref
  12.4 0.0 copy-done.4
  12.4 0.0 copy-start
  12.4 0.0 copy-start.5
  12.4 27.5 %fields.1 = (f32[256,256]{1,0:T(8,128)S(1)}, f32[256,256]{1,0:T(8,128)S(1)}) custom-call(f32[3,32]{1,0:T(4,128)S(1)} %copy-done.4, f32[528,128]{1,0:T(8,128)S(1)} %get-tuple-element.21.local_ref, bf16[544,128]{1,0:T(8,128)(2,1)S(1)} %collective-permute-done.cross_ref, f32[400,128]{1,0:T(8,128)S(1)} %collective-permute-done.1.first_ref, ...), custom_call_target="tpu_custom_call" | custom-call | tf_op jit(solution)/shard_map/fields/pallas_call | solution.py:515
  39.9 0.0 copy-start.3
  39.9 3.8 %collective-permute-start.3 = (f32[256,256]{1,0:T(8,128)S(1)}, f32[256,256]{1,0:T(8,128)S(1)}, u32[]{:S(2)}, u32[]{:S(2)}) collective-permute-start(f32[256,256]{1,0:T(8,128)S(1)} %get-tuple-element.29), channel_id=1, source_target_pairs={{0,1},{1,0},{2,3},{3,2},{4,5},{5,4},{6,7},{7,6},{8,9},{9,8},{10,11... | collective-permute-start | bytes 786440 | tf_op jit(solution)/shard_map/ppermute | solution.py:532
  43.7 0.0 copy-done
  43.7 0.0 copy-done.5
  43.7 1.7 %gram.1 = (f32[8,128]{1,0:T(8,128)S(1)}, f32[64,128]{1,0:T(8,128)S(1)}) custom-call(s32[32]{0:T(128)S(1)} %copy-done.5, f32[8,8,8192]{2,1,0:T(8,128)S(1)} %copy-done), custom_call_target="tpu_custom_call" | custom-call | tf_op jit(solution)/shard_map/gram/pallas_call | solution.py:533
  45.4 5.0 %collective-permute-done.3.theirs_ref = f32[256,256]{1,0:T(8,128)S(1)} collective-permute-done((f32[256,256]{1,0:T(8,128)S(1)}, f32[256,256]{1,0:T(8,128)S(1)}, u32[]{:S(2)}, u32[]{:S(2)}) %collective-permute-start.3) | collective-permute-done | bytes 262176 | tf_op jit(solution)/shard_map/ppermute | solution.py:532
  50.4 0.0 copy-done.3
  50.4 0.4 image.1
  50.8 13.5 %all_to_all.5.tiles_ref = f32[16,8,128]{2,1,0:T(8,128)S(1)} all-to-all(f32[16,8,128]{2,1,0:T(8,128)S(1)} %get-tuple-element.32), channel_id=1, replica_groups=mesh['box'=16,'rhs'=2] {'box'}, dimensions={0} | all-to-all | bytes 131072 | tf_op jit(solution)/shard_map/all_to_all | solution.py:549
  64.2 1.6 %finish.1 = (f32[8,8192]{1,0:T(8,128)}, f32[8,9]{1,0:T(8,128)}) custom-call(f32[16,8,128]{2,1,0:T(8,128)S(1)} %all_to_all.5.tiles_ref, f32[64,128]{1,0:T(8,128)S(1)} %get-tuple-element.31.live_ref, f32[8,8192]{1,0:T(8,128)S(1)} %get-tuple-element.33.image_ref, f32[8,8,8192]{2,1,0:T(8,128)S(1)} %copy-done), custom_call_target="tpu_custom_call" | custom-call | tf_op jit(solution)/shard_map/finish/pallas_call | solution.py:550
Async XLA Ops:
  0.6 11.7 %copy-start.4 = (f32[3,32]{1,0:T(4,128)S(1)}, f32[3,32]{1,0:T(4,128)}, u32[]{:S(2)}) copy-start(f32[3,32]{1,0:T(4,128)} %centres_s.1) | copy-start | bytes 1156
  3.5 8.8 %collective-permute-start.1 = (f32[400,128]{1,0:T(8,128)}, f32[400,128]{1,0:T(8,128)S(1)}, u32[]{:S(2)}, u32[]{:S(2)}) collective-permute-start(f32[400,128]{1,0:T(8,128)} %get-tuple-element.22), channel_id=1, source_target_pairs={{0,2},{2,4},{4,6},{6,8},{8,10},{10,12},{12,14},{14,16},{16,18},{18... | collective-permute-start | bytes 614408 | tf_op jit(solution)/shard_map/ppermute | solution.py:494
  5.9 6.4 %collective-permute-start = (bf16[544,128]{1,0:T(8,128)(2,1)}, bf16[544,128]{1,0:T(8,128)(2,1)S(1)}, u32[]{:S(2)}, u32[]{:S(2)}) collective-permute-start(bf16[544,128]{1,0:T(8,128)(2,1)} %get-tuple-element.20.sent_ref), channel_id=1, source_target_pairs={{0,1},{1,0},{2,3},{3,2},{4,5},{5,4},{6,7},{7,6},{8,9},{9,8},{10,11... | collective-permute-start | bytes 417800 | tf_op jit(solution)/shard_map/ppermute | solution.py:493
  7.9 4.5 %collective-permute-start.2 = (bf16[288,128]{1,0:T(8,128)(2,1)}, bf16[288,128]{1,0:T(8,128)(2,1)S(1)}, u32[]{:S(2)}, u32[]{:S(2)}) collective-permute-start(bf16[288,128]{1,0:T(8,128)(2,1)} %get-tuple-element.23), channel_id=1, source_target_pairs={{1,2},{3,4},{5,6},{7,8},{9,10},{11,12},{13,14},{15,16},{17,18},{19... | collective-permute-start | bytes 221192 | tf_op jit(solution)/shard_map/ppermute | solution.py:497
  8.5 1.0 %copy-start.1 = (f32[528,128]{1,0:T(8,128)S(1)}, f32[528,128]{1,0:T(8,128)}, u32[]{:S(2)}) copy-start(f32[528,128]{1,0:T(8,128)} %get-tuple-element.19.local_ref) | copy-start | bytes 811012
  9.5 0.9 %copy-start.2 = (bf16[544,128]{1,0:T(8,128)(2,1)S(1)}, bf16[544,128]{1,0:T(8,128)(2,1)}, u32[]{:S(2)}) copy-start(bf16[544,128]{1,0:T(8,128)(2,1)} %get-tuple-element.20.sent_ref) | copy-start | bytes 417796
  12.4 31.3 %copy-start = (f32[8,8,8192]{2,1,0:T(8,128)S(1)}, f32[8,8,8192]{2,1,0:T(8,128)}, u32[]{:S(2)}) copy-start(f32[8,8,8192]{2,1,0:T(8,128)} %basis_ref.5) | copy-start | bytes 6291460
  12.4 31.3 %copy-start.5 = (s32[32]{0:T(128)S(1)}, s32[32]{0:T(128)}, u32[]{:S(2)}) copy-start(s32[32]{0:T(128)} %counts_s.1) | copy-start | bytes 388
  39.9 10.5 %copy-start.3 = (f32[8192]{0:T(1024)S(1)}, f32[8192]{0:T(1024)}, u32[]{:S(2)}) copy-start(f32[8192]{0:T(1024)} %param.13) | copy-start | bytes 98308
  39.9 10.5 %collective-permute-start.3 = (f32[256,256]{1,0:T(8,128)S(1)}, f32[256,256]{1,0:T(8,128)S(1)}, u32[]{:S(2)}, u32[]{:S(2)}) collective-permute-start(f32[256,256]{1,0:T(8,128)S(1)} %get-tuple-element.29), channel_id=1, source_target_pairs={{0,1},{1,0},{2,3},{3,2},{4,5},{5,4},{6,7},{7,6},{8,9},{9,8},{10,11... | collective-permute-start | bytes 786440 | tf_op jit(solution)/shard_map/ppermute | solution.py:532

commit v17 on v16

--- a/solution.py
+++ b/solution.py
@@ -178,75 +178,58 @@
     local_out[...] = local_ref[...]
 
 
-def near_planes(sources, targets, total, beside):
-    def near_rows(item, _):
+def near_planes(sources, targets, total):
+    def rows_at(pair, place, number):
+        ref, first = pair
+        return ref[pl.ds(pl.multiple_of((first + place) * number, number), number), :]
+
+    def near_box(item, near_x, source_x, width):
         target_y = (item + 1) // 3
         source_y = target_y + lax.rem(item + 1, 3) - 1
-        runs = []
-        for near_x in range(4):
-            for source in sources:
-                for x in range(max(near_x - 1, 0), min(near_x + 2, 4)):
-                    runs.append((near_x, source, source_y * 4 + x))
-
-        def rows_at(pair, place, number):
-            ref, first = pair
-            return ref[pl.ds(pl.multiple_of((first + place) * number, number), number), :]
-
-        def distances(near_x, source, place):
-            start = pl.multiple_of((target_y * 4 + near_x) * per_box, per_box)
-            weights = rows_at(source[0], place, depth)
-            return jnp.dot(targets[pl.ds(start, per_box), :], weights, preferred_element_type=f32)
+        place = target_y * 4 + near_x
+        facets = targets[pl.ds(pl.multiple_of(place * per_box, per_box), per_box), :]
+        runs = [(source, source_y * 4 + source_x + k) for source in sources for k in range(width)]
+
+        def distances(source, place):
+            return jnp.dot(facets, rows_at(source[0], place, depth), preferred_element_type=f32)
 
         ahead = distances(*runs[0])
         cubed = []
         given = []
-        for i, (near_x, source, place) in enumerate(runs):
+        for i, (source, source_place) in enumerate(runs):
             here = ahead
             if i + 1 < len(runs):
                 ahead = distances(*runs[i + 1])
             inverse = lax.rsqrt(here)
             cubed.append((inverse * inverse * inverse).astype(bf16))
-            given.append(jnp.concatenate([rows_at(source[1], place, 80), rows_at(source[2], place, 80)], axis=0))
-            if i + 1 == len(runs) or runs[i + 1][0] != near_x:
-                rows_of = pl.ds(pl.multiple_of((target_y * 4 + near_x) * 160, 160), 160)
-                total[rows_of, :] += lax.dot_general(
-                    jnp.concatenate(given, axis=1),
-                    jnp.concatenate(cubed, axis=1),
-                    (((1,), (1,)), ((), ())),
-                    preferred_element_type=f32,
-                )
-                cubed = []
-                given = []
-        beside(item)
-        return 0
-
-    lax.fori_loop(0, 10, near_rows, 0)
-
-
-def field_kernel(
-    centres_s, local_ref, cross_ref, first_ref, second_ref, geometry, mine, targets, planes, mine_ref, theirs_ref,
-    halo_geometry, halo_mine, theirs, total, far, far_centres, far_moments
-):
+            given.append(
+                jnp.concatenate([rows_at(source[1], source_place, 80), rows_at(source[2], source_place, 80)], axis=0)
+            )
+        total[pl.ds(pl.multiple_of(place * 160, 160), 160), :] += lax.dot_general(
+            jnp.concatenate(given, axis=1),
+            jnp.concatenate(cubed, axis=1),
+            (((1,), (1,)), ((), ())),
+            preferred_element_type=f32,
+        )
+
+    def inner(step, _):
+        near_x = 1 + lax.rem(step, 2)
+        near_box(step // 2, near_x, near_x - 1, 3)
+        return 0
+
+    def outer(step, _):
+        side = lax.rem(step, 2)
+        near_box(step // 2, 3 * side, 2 * side, 2)
+        return 0
+
+    lax.fori_loop(0, 20, inner, 0)
+    lax.fori_loop(0, 20, outer, 0)
+
+
+def far_kernel(local_ref, cross_ref, first_ref, second_ref, far, far_centres, far_moments):
     boxes = 2 * plane_boxes
     half = lax.axis_index("rhs")
     origin = local_ref[523:526, 0:1]
-
-    def source(slot, _):
-        local = wide_tile(local_ref, slot * 16) - origin
-        store_strengths(local, wide_charges(cross_ref, slot), slot, theirs)
-        return 0
-
-    lax.fori_loop(0, boxes, source, 0, unroll=4)
-
-    def halo_source(place, _):
-        local = padded(wide_tile(first_ref, 256 + place * 8) - origin)
-        store_geometry(local, place, halo_geometry)
-        store_strengths(local, wide_charges(first_ref, place), place, halo_mine)
-        store_strengths(local, wide_charges(second_ref, place), boxes + place, theirs)
-        return 0
-
-    lax.fori_loop(0, plane_boxes, halo_source, 0, unroll=4)
-    total[...] = jnp.zeros_like(total)
 
     for group, (centres, ours, others) in enumerate(
         (
@@ -295,14 +278,42 @@
         second = jnp.dot(picked, lower, preferred_element_type=f32)
         return first[:16] + first[16:] + second[:16]
 
-    def far_boxes(item):
-        for i in range(5):
-            k = jnp.minimum(item * 5 + i, 3 * plane_boxes - 1)
-            far[pl.ds(pl.multiple_of(k * 16, 16), 16), :] = far_field(k)
+    def far_boxes(k, _):
+        far[pl.ds(pl.multiple_of(k * 16, 16), 16), :] = far_field(k)
+        return 0
+
+    lax.fori_loop(0, 3 * plane_boxes, far_boxes, 0, unroll=4)
+
+
+def field_kernel(
+    centres_s, local_ref, cross_ref, first_ref, second_ref, geometry, mine, targets, planes, far_ref,
+    mine_ref, theirs_ref, halo_geometry, halo_mine, theirs, total, far
+):
+    boxes = 2 * plane_boxes
+    half = lax.axis_index("rhs")
+    origin = local_ref[523:526, 0:1]
+
+    def source(slot, _):
+        local = wide_tile(local_ref, slot * 16) - origin
+        store_strengths(local, wide_charges(cross_ref, slot), slot, theirs)
+        return 0
+
+    lax.fori_loop(0, boxes, source, 0, unroll=4)
+
+    def halo_source(place, _):
+        local = padded(wide_tile(first_ref, 256 + place * 8) - origin)
+        store_geometry(local, place, halo_geometry)
+        store_strengths(local, wide_charges(first_ref, place), place, halo_mine)
+        store_strengths(local, wide_charges(second_ref, place), boxes + place, theirs)
+        return 0
+
+    lax.fori_loop(0, plane_boxes, halo_source, 0, unroll=4)
+    total[...] = jnp.zeros_like(total)
+    far[...] = far_ref[: 16 * boxes]
 
     sources = [((geometry, p), (mine, p), (theirs, p)) for p in (0, plane_boxes)]
     sources.append(((halo_geometry, 0), (halo_mine, 0), (theirs, boxes)))
-    near_planes(sources, targets, total, far_boxes)
+    near_planes(sources, targets, total)
 
     def near_field(place, _):
         sums = total[pl.ds(pl.multiple_of(place * 160, 160), 160), :]
@@ -317,7 +328,7 @@
         value = jnp.concatenate(values, axis=0)
         slot = half * plane_boxes + place
         rows = pl.ds(pl.multiple_of(slot * 16, 16), 16)
-        far[rows, :] += value + far[pl.ds(pl.multiple_of((boxes + place) * 16, 16), 16), :]
+        far[rows, :] = value + far_ref[rows, :] + far_ref[pl.ds(pl.multiple_of((boxes + place) * 16, 16), 16), :]
         return 0
 
     lax.fori_loop(0, plane_boxes, near_field, 0, unroll=4)
@@ -512,23 +523,30 @@
         compiler_params=limit(12),
         name="features",
     )(local, sent)
+    far = pl.pallas_call(
+        far_kernel,
+        out_shape=rows(3 * plane_boxes * 16, per_box),
+        in_specs=[vmem] * 4,
+        out_specs=vmem,
+        scratch_shapes=[pltpu.VMEM((6 * 32, 128), f32), pltpu.VMEM((2 * 32, 128), f32)],
+        compiler_params=limit(8),
+        name="far",
+    )(local, cross, first, second)
     mine, theirs = pl.pallas_call(
         field_kernel,
         out_shape=(rows(boxes * 8, per_box),) * 2,
-        in_specs=[smem] + [vmem] * 8,
+        in_specs=[smem] + [vmem] * 9,
         out_specs=(vmem, vmem),
         scratch_shapes=[
             pltpu.VMEM((plane_boxes * depth, per_box), bf16),
             pltpu.VMEM((plane_boxes * 80, per_box), bf16),
             pltpu.VMEM((3 * plane_boxes * 80, per_box), bf16),
             pltpu.VMEM((plane_boxes * 160, per_box), f32),
-            pltpu.VMEM((3 * plane_boxes * 16, per_box), f32),
-            pltpu.VMEM((6 * 32, 128), f32),
-            pltpu.VMEM((2 * 32, 128), f32),
+            pltpu.VMEM((boxes * 16, per_box), f32),
         ],
         compiler_params=limit(32),
         name="fields",
-    )(box_centres, local, cross, first, second, geometry, strengths, targets, planes)
+    )(box_centres, local, cross, first, second, geometry, strengths, targets, planes, far)
     theirs = lax.ppermute(theirs, "rhs", swap)
     gram, live = pl.pallas_call(
         gram_kernel,

time: 66.1 us -> 79.5 us (1.20)
  Pallas kernels: 36 us -> 49.4 us
    pallas_call x1, Pallas kernels: 27.5 us -> 36.7 us  [on_device(): pl.pallas_call(field_kernel, out_shape=(rows(boxes * 8, per_box),) * 2, i...]
    pallas_call x0 -> x1, Pallas kernels: none -> 4.27 us  [on_device(): pl.pallas_call(far_kernel, out_shape=rows(3 * plane_boxes * 16, per_box),...]
where the time goes in v17:
time: 79.5 us; the launch traced here: 79.3 us
  Pallas kernels  49.4 us (62%)
  blocking collectives  13.5 us (17%)
  starting transfers between devices  8.76 us (11%)
  waiting for transfers between devices  5.02 us (6%)
  local copies, waits for them, and re-layouts  1.88 us (2%)
    pallas_call x1, Pallas kernels, on_device(): pl.pallas_call(field_kernel, out_shape=(rows(boxes * 8, per_box),) * 2, i...  36.7 us
    all_to_all x1, blocking collectives, on_device(): tiles = lax.all_to_all(tiles, 'box', 0, 0, tiled=True)  13.5 us
    ppermute x1, waiting for transfers between devices, on_device(): theirs = lax.ppermute(theirs, 'rhs', swap)  5.02 us
    pallas_call x1, Pallas kernels, on_device(): pl.pallas_call(far_kernel, out_shape=rows(3 * plane_boxes * 16, per_box),...  4.27 us
    ppermute x1, starting transfers between devices, on_device(): theirs = lax.ppermute(theirs, 'rhs', swap)  3.78 us
    pallas_call x1, Pallas kernels, on_device(): pl.pallas_call(prep_kernel, out_shape=(rows(544, dtype=bf16), rows(400),...  2.89 us
    ppermute x1, starting transfers between devices, on_device(): lax.ppermute(first, ('box', 'rhs'), [(2 * i, 2 * i + 2) for i in ups] + [...  2.37 us
    ppermute x1, starting transfers between devices, on_device(): cross = lax.ppermute(sent, 'rhs', swap)  1.96 us
  transfers between devices with their start and end apart: 4, of which 1 were waited for; matrix products, arithmetic and copies ran while one was open for 0% of the time, Pallas kernels for 5%

profile of v17, /device:TPU:0, one launch (start us, length us, event | category | flops | bytes accessed | tf_op | source)
XLA Modules:
  0.0 79.3 jit_solution(10846754294956106440)
XLA Ops:
  0.6 0.0 copy-start.4
  0.6 2.9 %prepare.1 = (bf16[544,128]{1,0:T(8,128)(2,1)}, f32[400,128]{1,0:T(8,128)}, bf16[288,128]{1,0:T(8,128)(2,1)}, f32[528,128]{1,0:T(8,128)}) custom-call(f32[3,32]{1,0:T(4,128)} %centres_s.1, s32[32]{0:T(128)} %counts_s.1, f32[8,8,8192]{2,1,0:T(8,128)} %basis_ref.5, f32[3,8192]{1,0:T(4,128)} %facets_h.1, f32[64,128]{1,0:T(8,128)} %bitcast.4, f32[3,8192]{1,0:T(4,128)} %normals_h.1), custom_call_target="tpu_custom_call" | custom-call | tf_op jit(solution)/shard_map/prepare/pallas_call | solution.py:485
  3.5 2.4 %collective-permute-start.1 = (f32[400,128]{1,0:T(8,128)}, f32[400,128]{1,0:T(8,128)S(1)}, u32[]{:S(2)}, u32[]{:S(2)}) collective-permute-start(f32[400,128]{1,0:T(8,128)} %get-tuple-element.22), channel_id=1, source_target_pairs={{0,2},{2,4},{4,6},{6,8},{8,10},{10,12},{12,14},{14,16},{16,18},{18... | collective-permute-start | bytes 614408 | tf_op jit(solution)/shard_map/ppermute | solution.py:505
  5.9 2.0 %collective-permute-start = (bf16[544,128]{1,0:T(8,128)(2,1)}, bf16[544,128]{1,0:T(8,128)(2,1)S(1)}, u32[]{:S(2)}, u32[]{:S(2)}) collective-permute-start(bf16[544,128]{1,0:T(8,128)(2,1)} %get-tuple-element.20.sent_ref), channel_id=1, source_target_pairs={{0,1},{1,0},{2,3},{3,2},{4,5},{5,4},{6,7},{7,6},{8,9},{9,8},{10,11... | collective-permute-start | bytes 417800 | tf_op jit(solution)/shard_map/ppermute | solution.py:504
  7.9 0.7 collective-permute-start.2
  8.5 0.0 copy-start.1
  8.5 0.9 %copy-done.1 = f32[528,128]{1,0:T(8,128)S(1)} copy-done((f32[528,128]{1,0:T(8,128)S(1)}, f32[528,128]{1,0:T(8,128)}, u32[]{:S(2)}) %copy-start.1) | copy-done | bytes 270360
  9.5 0.0 copy-start.2
  9.5 0.9 %copy-done.2 = bf16[544,128]{1,0:T(8,128)(2,1)S(1)} copy-done((bf16[544,128]{1,0:T(8,128)(2,1)S(1)}, bf16[544,128]{1,0:T(8,128)(2,1)}, u32[]{:S(2)}) %copy-start.2) | copy-done | bytes 139288
  10.4 1.9 %features.1 = (bf16[2048,256]{1,0:T(8,128)(2,1)S(1)}, bf16[2560,256]{1,0:T(8,128)(2,1)S(1)}, bf16[4096,64]{1,0:T(8,128)(2,1)S(1)}, f32[128,256]{1,0:T(8,128)S(1)}, f32[528,128]{1,0:T(8,128)S(1)}) custom-call(f32[528,128]{1,0:T(8,128)S(1)} %copy-done.1, bf16[544,128]{1,0:T(8,128)(2,1)S(1)} %copy-done.2), custom_call_target="tpu_custom_call" | custom-call | tf_op jit(solution)/shard_map/features/pallas_call | solution.py:512
  12.3 0.0 collective-permute-done.2.second_ref
  12.4 0.0 collective-permute-done.cross_ref
  12.4 0.0 collective-permute-done.1.first_ref
  12.4 4.3 %far.1.far_ref = f32[768,256]{1,0:T(8,128)S(1)} custom-call(f32[528,128]{1,0:T(8,128)S(1)} %get-tuple-element.21.local_ref, bf16[544,128]{1,0:T(8,128)(2,1)S(1)} %collective-permute-done.cross_ref, f32[400,128]{1,0:T(8,128)S(1)} %collective-permute-done.1.first_ref, bf16[288,128]{1,0:T(8,128)(2,1)S(1)} %collective-permute-done.2.second_ref), custom_call_target="tpu_custom_call" | custom-call | tf_op jit(solution)/shard_map/far/pallas_call | solution.py:526
  16.6 0.0 copy-done.4
  16.7 0.0 copy-start
  16.7 0.0 copy-start.5
  16.7 36.7 %fields.1 = (f32[256,256]{1,0:T(8,128)S(1)}, f32[256,256]{1,0:T(8,128)S(1)}) custom-call(f32[3,32]{1,0:T(4,128)S(1)} %copy-done.4, f32[528,128]{1,0:T(8,128)S(1)} %get-tuple-element.21.local_ref, bf16[544,128]{1,0:T(8,128)(2,1)S(1)} %collective-permute-done.cross_ref, f32[400,128]{1,0:T(8,128)S(1)} %collective-permute-done.1.first_ref, ...), custom_call_target="tpu_custom_call" | custom-call | tf_op jit(solution)/shard_map/fields/pallas_call | solution.py:535
  53.4 0.0 copy-start.3
  53.4 3.8 %collective-permute-start.3 = (f32[256,256]{1,0:T(8,128)S(1)}, f32[256,256]{1,0:T(8,128)S(1)}, u32[]{:S(2)}, u32[]{:S(2)}) collective-permute-start(f32[256,256]{1,0:T(8,128)S(1)} %get-tuple-element.29), channel_id=1, source_target_pairs={{0,1},{1,0},{2,3},{3,2},{4,5},{5,4},{6,7},{7,6},{8,9},{9,8},{10,11... | collective-permute-start | bytes 786440 | tf_op jit(solution)/shard_map/ppermute | solution.py:550
  57.2 0.0 copy-done
  57.2 0.0 copy-done.5
  57.2 1.7 %gram.1 = (f32[8,128]{1,0:T(8,128)S(1)}, f32[64,128]{1,0:T(8,128)S(1)}) custom-call(s32[32]{0:T(128)S(1)} %copy-done.5, f32[8,8,8192]{2,1,0:T(8,128)S(1)} %copy-done), custom_call_target="tpu_custom_call" | custom-call | tf_op jit(solution)/shard_map/gram/pallas_call | solution.py:551
  58.8 5.0 %collective-permute-done.3.theirs_ref = f32[256,256]{1,0:T(8,128)S(1)} collective-permute-done((f32[256,256]{1,0:T(8,128)S(1)}, f32[256,256]{1,0:T(8,128)S(1)}, u32[]{:S(2)}, u32[]{:S(2)}) %collective-permute-start.3) | collective-permute-done | bytes 262176 | tf_op jit(solution)/shard_map/ppermute | solution.py:550
  63.9 0.0 copy-done.3
  63.9 0.4 image.1
  64.2 13.5 %all_to_all.5.tiles_ref = f32[16,8,128]{2,1,0:T(8,128)S(1)} all-to-all(f32[16,8,128]{2,1,0:T(8,128)S(1)} %get-tuple-element.32), channel_id=1, replica_groups=mesh['box'=16,'rhs'=2] {'box'}, dimensions={0} | all-to-all | bytes 131072 | tf_op jit(solution)/shard_map/all_to_all | solution.py:567
  77.7 1.6 %finish.1 = (f32[8,8192]{1,0:T(8,128)}, f32[8,9]{1,0:T(8,128)}) custom-call(f32[16,8,128]{2,1,0:T(8,128)S(1)} %all_to_all.5.tiles_ref, f32[64,128]{1,0:T(8,128)S(1)} %get-tuple-element.31.live_ref, f32[8,8192]{1,0:T(8,128)S(1)} %get-tuple-element.33.image_ref, f32[8,8,8192]{2,1,0:T(8,128)S(1)} %copy-done), custom_call_target="tpu_custom_call" | custom-call | tf_op jit(solution)/shard_map/finish/pallas_call | solution.py:568
Async XLA Ops:
  0.6 16.0 %copy-start.4 = (f32[3,32]{1,0:T(4,128)S(1)}, f32[3,32]{1,0:T(4,128)}, u32[]{:S(2)}) copy-start(f32[3,32]{1,0:T(4,128)} %centres_s.1) | copy-start | bytes 1156
  3.5 8.8 %collective-permute-start.1 = (f32[400,128]{1,0:T(8,128)}, f32[400,128]{1,0:T(8,128)S(1)}, u32[]{:S(2)}, u32[]{:S(2)}) collective-permute-start(f32[400,128]{1,0:T(8,128)} %get-tuple-element.22), channel_id=1, source_target_pairs={{0,2},{2,4},{4,6},{6,8},{8,10},{10,12},{12,14},{14,16},{16,18},{18... | collective-permute-start | bytes 614408 | tf_op jit(solution)/shard_map/ppermute | solution.py:505
  5.9 6.4 %collective-permute-start = (bf16[544,128]{1,0:T(8,128)(2,1)}, bf16[544,128]{1,0:T(8,128)(2,1)S(1)}, u32[]{:S(2)}, u32[]{:S(2)}) collective-permute-start(bf16[544,128]{1,0:T(8,128)(2,1)} %get-tuple-element.20.sent_ref), channel_id=1, source_target_pairs={{0,1},{1,0},{2,3},{3,2},{4,5},{5,4},{6,7},{7,6},{8,9},{9,8},{10,11... | collective-permute-start | bytes 417800 | tf_op jit(solution)/shard_map/ppermute | solution.py:504
  7.9 4.5 %collective-permute-start.2 = (bf16[288,128]{1,0:T(8,128)(2,1)}, bf16[288,128]{1,0:T(8,128)(2,1)S(1)}, u32[]{:S(2)}, u32[]{:S(2)}) collective-permute-start(bf16[288,128]{1,0:T(8,128)(2,1)} %get-tuple-element.23), channel_id=1, source_target_pairs={{1,2},{3,4},{5,6},{7,8},{9,10},{11,12},{13,14},{15,16},{17,18},{19... | collective-permute-start | bytes 221192 | tf_op jit(solution)/shard_map/ppermute | solution.py:508
  8.5 1.0 %copy-start.1 = (f32[528,128]{1,0:T(8,128)S(1)}, f32[528,128]{1,0:T(8,128)}, u32[]{:S(2)}) copy-start(f32[528,128]{1,0:T(8,128)} %get-tuple-element.19.local_ref) | copy-start | bytes 811012
  9.5 0.9 %copy-start.2 = (bf16[544,128]{1,0:T(8,128)(2,1)S(1)}, bf16[544,128]{1,0:T(8,128)(2,1)}, u32[]{:S(2)}) copy-start(bf16[544,128]{1,0:T(8,128)(2,1)} %get-tuple-element.20.sent_ref) | copy-start | bytes 417796
  16.7 40.5 %copy-start = (f32[8,8,8192]{2,1,0:T(8,128)S(1)}, f32[8,8,8192]{2,1,0:T(8,128)}, u32[]{:S(2)}) copy-start(f32[8,8,8192]{2,1,0:T(8,128)} %basis_ref.5) | copy-start | bytes 6291460
  16.7 40.5 %copy-start.5 = (s32[32]{0:T(128)S(1)}, s32[32]{0:T(128)}, u32[]{:S(2)}) copy-start(s32[32]{0:T(128)} %counts_s.1) | copy-start | bytes 388
  53.4 10.5 %copy-start.3 = (f32[8192]{0:T(1024)S(1)}, f32[8192]{0:T(1024)}, u32[]{:S(2)}) copy-start(f32[8192]{0:T(1024)} %param.13) | copy-start | bytes 98308
  53.4 10.5 %collective-permute-start.3 = (f32[256,256]{1,0:T(8,128)S(1)}, f32[256,256]{1,0:T(8,128)S(1)}, u32[]{:S(2)}, u32[]{:S(2)}) collective-permute-start(f32[256,256]{1,0:T(8,128)S(1)} %get-tuple-element.29), channel_id=1, source_target_pairs={{0,1},{1,0},{2,3},{3,2},{4,5},{5,4},{6,7},{7,6},{8,9},{9,8},{10,11... | collective-permute-start | bytes 786440 | tf_op jit(solution)/shard_map/ppermute | solution.py:550

commit v18 on v16

--- a/solution.py
+++ b/solution.py
@@ -13,6 +13,7 @@
 bf16 = jnp.bfloat16
 plane_boxes = 16
 per_box = 256
+step_items = 2
 depth = 64
 
 
@@ -179,36 +180,38 @@
 
 
 def near_planes(sources, targets, total, beside):
-    def near_rows(item, _):
-        target_y = (item + 1) // 3
-        source_y = target_y + lax.rem(item + 1, 3) - 1
+    def near_rows(step, _):
         runs = []
-        for near_x in range(4):
-            for source in sources:
-                for x in range(max(near_x - 1, 0), min(near_x + 2, 4)):
-                    runs.append((near_x, source, source_y * 4 + x))
+        for item in range(step_items):
+            item = step * step_items + item
+            target_y = (item + 1) // 3
+            source_y = target_y + lax.rem(item + 1, 3) - 1
+            for near_x in range(4):
+                target = target_y * 4 + near_x
+                for source in sources:
+                    for x in range(max(near_x - 1, 0), min(near_x + 2, 4)):
+                        runs.append((target, source, source_y * 4 + x))
 
         def rows_at(pair, place, number):
             ref, first = pair
             return ref[pl.ds(pl.multiple_of((first + place) * number, number), number), :]
 
-        def distances(near_x, source, place):
-            start = pl.multiple_of((target_y * 4 + near_x) * per_box, per_box)
-            weights = rows_at(source[0], place, depth)
-            return jnp.dot(targets[pl.ds(start, per_box), :], weights, preferred_element_type=f32)
+        def distances(target, source, place):
+            facets = targets[pl.ds(pl.multiple_of(target * per_box, per_box), per_box), :]
+            return jnp.dot(facets, rows_at(source[0], place, depth), preferred_element_type=f32)
 
         ahead = distances(*runs[0])
         cubed = []
         given = []
-        for i, (near_x, source, place) in enumerate(runs):
+        for i, (target, source, place) in enumerate(runs):
             here = ahead
             if i + 1 < len(runs):
                 ahead = distances(*runs[i + 1])
             inverse = lax.rsqrt(here)
             cubed.append((inverse * inverse * inverse).astype(bf16))
             given.append(jnp.concatenate([rows_at(source[1], place, 80), rows_at(source[2], place, 80)], axis=0))
-            if i + 1 == len(runs) or runs[i + 1][0] != near_x:
-                rows_of = pl.ds(pl.multiple_of((target_y * 4 + near_x) * 160, 160), 160)
+            if i + 1 == len(runs) or runs[i + 1][0] is not target:
+                rows_of = pl.ds(pl.multiple_of(target * 160, 160), 160)
                 total[rows_of, :] += lax.dot_general(
                     jnp.concatenate(given, axis=1),
                     jnp.concatenate(cubed, axis=1),
@@ -217,10 +220,10 @@
                 )
                 cubed = []
                 given = []
-        beside(item)
-        return 0
-
-    lax.fori_loop(0, 10, near_rows, 0)
+        beside(step)
+        return 0
+
+    lax.fori_loop(0, 10 // step_items, near_rows, 0)
 
 
 def field_kernel(
@@ -295,9 +298,9 @@
         second = jnp.dot(picked, lower, preferred_element_type=f32)
         return first[:16] + first[16:] + second[:16]
 
-    def far_boxes(item):
-        for i in range(5):
-            k = jnp.minimum(item * 5 + i, 3 * plane_boxes - 1)
+    def far_boxes(step):
+        for i in range(5 * step_items):
+            k = jnp.minimum(step * 5 * step_items + i, 3 * plane_boxes - 1)
             far[pl.ds(pl.multiple_of(k * 16, 16), 16), :] = far_field(k)
 
     sources = [((geometry, p), (mine, p), (theirs, p)) for p in (0, plane_boxes)]

time: 66.1 us -> 66.3 us (level)
  no operation moved by 1% of the time
where the time goes in v18:
time: 66.3 us; the launch traced here: 66 us
  Pallas kernels  36.1 us (54%)
  blocking collectives  13.4 us (20%)
  starting transfers between devices  8.78 us (13%)
  waiting for transfers between devices  5.04 us (8%)
  local copies, waits for them, and re-layouts  1.88 us (3%)
  between operations  0.76 us (1%)
    pallas_call x1, Pallas kernels, on_device(): pl.pallas_call(field_kernel, out_shape=(rows(boxes * 8, per_box),) * 2, i...  27.7 us
    all_to_all x1, blocking collectives, on_device(): tiles = lax.all_to_all(tiles, 'box', 0, 0, tiled=True)  13.4 us
    ppermute x1, waiting for transfers between devices, on_device(): theirs = lax.ppermute(theirs, 'rhs', swap)  5.04 us
    ppermute x1, starting transfers between devices, on_device(): theirs = lax.ppermute(theirs, 'rhs', swap)  3.8 us
    pallas_call x1, Pallas kernels, on_device(): pl.pallas_call(prep_kernel, out_shape=(rows(544, dtype=bf16), rows(400),...  2.89 us
    ppermute x1, starting transfers between devices, on_device(): lax.ppermute(first, ('box', 'rhs'), [(2 * i, 2 * i + 2) for i in ups] + [...  2.37 us
    ppermute x1, starting transfers between devices, on_device(): cross = lax.ppermute(sent, 'rhs', swap)  1.96 us
    pallas_call x1, Pallas kernels, on_device(): pl.pallas_call(feature_kernel, out_shape=(rows(boxes * depth, per_box, bf...  1.94 us
  transfers between devices with their start and end apart: 4, of which 1 were waited for; matrix products, arithmetic and copies ran while one was open for 0% of the time, Pallas kernels for 5%

profile of v18, /device:TPU:0, one launch (start us, length us, event | category | flops | bytes accessed | tf_op | source)
XLA Modules:
  0.0 66.0 jit_solution(15634371355796078287)
XLA Ops:
  0.6 0.0 copy-start.4
  0.6 2.9 %prepare.1 = (bf16[544,128]{1,0:T(8,128)(2,1)}, f32[400,128]{1,0:T(8,128)}, bf16[288,128]{1,0:T(8,128)(2,1)}, f32[528,128]{1,0:T(8,128)}) custom-call(f32[3,32]{1,0:T(4,128)} %centres_s.1, s32[32]{0:T(128)} %counts_s.1, f32[8,8,8192]{2,1,0:T(8,128)} %basis_ref.5, f32[3,8192]{1,0:T(4,128)} %facets_h.1, f32[64,128]{1,0:T(8,128)} %bitcast.4, f32[3,8192]{1,0:T(4,128)} %normals_h.1), custom_call_target="tpu_custom_call" | custom-call | tf_op jit(solution)/shard_map/prepare/pallas_call | solution.py:477
  3.5 2.4 %collective-permute-start.1 = (f32[400,128]{1,0:T(8,128)}, f32[400,128]{1,0:T(8,128)S(1)}, u32[]{:S(2)}, u32[]{:S(2)}) collective-permute-start(f32[400,128]{1,0:T(8,128)} %get-tuple-element.22), channel_id=1, source_target_pairs={{0,2},{2,4},{4,6},{6,8},{8,10},{10,12},{12,14},{14,16},{16,18},{18... | collective-permute-start | bytes 614408 | tf_op jit(solution)/shard_map/ppermute | solution.py:497
  5.9 2.0 %collective-permute-start = (bf16[544,128]{1,0:T(8,128)(2,1)}, bf16[544,128]{1,0:T(8,128)(2,1)S(1)}, u32[]{:S(2)}, u32[]{:S(2)}) collective-permute-start(bf16[544,128]{1,0:T(8,128)(2,1)} %get-tuple-element.20.sent_ref), channel_id=1, source_target_pairs={{0,1},{1,0},{2,3},{3,2},{4,5},{5,4},{6,7},{7,6},{8,9},{9,8},{10,11... | collective-permute-start | bytes 417800 | tf_op jit(solution)/shard_map/ppermute | solution.py:496
  7.9 0.7 collective-permute-start.2
  8.5 0.0 copy-start.1
  8.5 0.9 %copy-done.1 = f32[528,128]{1,0:T(8,128)S(1)} copy-done((f32[528,128]{1,0:T(8,128)S(1)}, f32[528,128]{1,0:T(8,128)}, u32[]{:S(2)}) %copy-start.1) | copy-done | bytes 270360
  9.5 0.0 copy-start.2
  9.5 0.9 %copy-done.2 = bf16[544,128]{1,0:T(8,128)(2,1)S(1)} copy-done((bf16[544,128]{1,0:T(8,128)(2,1)S(1)}, bf16[544,128]{1,0:T(8,128)(2,1)}, u32[]{:S(2)}) %copy-start.2) | copy-done | bytes 139288
  10.4 1.9 %features.1 = (bf16[2048,256]{1,0:T(8,128)(2,1)S(1)}, bf16[2560,256]{1,0:T(8,128)(2,1)S(1)}, bf16[4096,64]{1,0:T(8,128)(2,1)S(1)}, f32[128,256]{1,0:T(8,128)S(1)}, f32[528,128]{1,0:T(8,128)S(1)}) custom-call(f32[528,128]{1,0:T(8,128)S(1)} %copy-done.1, bf16[544,128]{1,0:T(8,128)(2,1)S(1)} %copy-done.2), custom_call_target="tpu_custom_call" | custom-call | tf_op jit(solution)/shard_map/features/pallas_call | solution.py:504
  12.3 0.0 collective-permute-done.2.second_ref
  12.4 0.0 collective-permute-done.cross_ref
  12.4 0.0 collective-permute-done.1.first_ref
  12.4 0.0 copy-done.4
  12.4 0.0 copy-start
  12.4 0.0 copy-start.5
  12.4 27.7 %fields.1 = (f32[256,256]{1,0:T(8,128)S(1)}, f32[256,256]{1,0:T(8,128)S(1)}) custom-call(f32[3,32]{1,0:T(4,128)S(1)} %copy-done.4, f32[528,128]{1,0:T(8,128)S(1)} %get-tuple-element.21.local_ref, bf16[544,128]{1,0:T(8,128)(2,1)S(1)} %collective-permute-done.cross_ref, f32[400,128]{1,0:T(8,128)S(1)} %collective-permute-done.1.first_ref, ...), custom_call_target="tpu_custom_call" | custom-call | tf_op jit(solution)/shard_map/fields/pallas_call | solution.py:518
  40.1 0.0 copy-start.3
  40.1 3.8 %collective-permute-start.3 = (f32[256,256]{1,0:T(8,128)S(1)}, f32[256,256]{1,0:T(8,128)S(1)}, u32[]{:S(2)}, u32[]{:S(2)}) collective-permute-start(f32[256,256]{1,0:T(8,128)S(1)} %get-tuple-element.29), channel_id=1, source_target_pairs={{0,1},{1,0},{2,3},{3,2},{4,5},{5,4},{6,7},{7,6},{8,9},{9,8},{10,11... | collective-permute-start | bytes 786440 | tf_op jit(solution)/shard_map/ppermute | solution.py:535
  43.9 0.0 copy-done
  43.9 0.0 copy-done.5
  43.9 1.7 %gram.1 = (f32[8,128]{1,0:T(8,128)S(1)}, f32[64,128]{1,0:T(8,128)S(1)}) custom-call(s32[32]{0:T(128)S(1)} %copy-done.5, f32[8,8,8192]{2,1,0:T(8,128)S(1)} %copy-done), custom_call_target="tpu_custom_call" | custom-call | tf_op jit(solution)/shard_map/gram/pallas_call | solution.py:536
  45.6 5.0 %collective-permute-done.3.theirs_ref = f32[256,256]{1,0:T(8,128)S(1)} collective-permute-done((f32[256,256]{1,0:T(8,128)S(1)}, f32[256,256]{1,0:T(8,128)S(1)}, u32[]{:S(2)}, u32[]{:S(2)}) %collective-permute-start.3) | collective-permute-done | bytes 262176 | tf_op jit(solution)/shard_map/ppermute | solution.py:535
  50.6 0.0 copy-done.3
  50.6 0.4 image.1
  51.0 13.4 %all_to_all.5.tiles_ref = f32[16,8,128]{2,1,0:T(8,128)S(1)} all-to-all(f32[16,8,128]{2,1,0:T(8,128)S(1)} %get-tuple-element.32), channel_id=1, replica_groups=mesh['box'=16,'rhs'=2] {'box'}, dimensions={0} | all-to-all | bytes 131072 | tf_op jit(solution)/shard_map/all_to_all | solution.py:552
  64.4 1.6 %finish.1 = (f32[8,8192]{1,0:T(8,128)}, f32[8,9]{1,0:T(8,128)}) custom-call(f32[16,8,128]{2,1,0:T(8,128)S(1)} %all_to_all.5.tiles_ref, f32[64,128]{1,0:T(8,128)S(1)} %get-tuple-element.31.live_ref, f32[8,8192]{1,0:T(8,128)S(1)} %get-tuple-element.33.image_ref, f32[8,8,8192]{2,1,0:T(8,128)S(1)} %copy-done), custom_call_target="tpu_custom_call" | custom-call | tf_op jit(solution)/shard_map/finish/pallas_call | solution.py:553
Async XLA Ops:
  0.6 11.7 %copy-start.4 = (f32[3,32]{1,0:T(4,128)S(1)}, f32[3,32]{1,0:T(4,128)}, u32[]{:S(2)}) copy-start(f32[3,32]{1,0:T(4,128)} %centres_s.1) | copy-start | bytes 1156
  3.5 8.8 %collective-permute-start.1 = (f32[400,128]{1,0:T(8,128)}, f32[400,128]{1,0:T(8,128)S(1)}, u32[]{:S(2)}, u32[]{:S(2)}) collective-permute-start(f32[400,128]{1,0:T(8,128)} %get-tuple-element.22), channel_id=1, source_target_pairs={{0,2},{2,4},{4,6},{6,8},{8,10},{10,12},{12,14},{14,16},{16,18},{18... | collective-permute-start | bytes 614408 | tf_op jit(solution)/shard_map/ppermute | solution.py:497
  5.9 6.4 %collective-permute-start = (bf16[544,128]{1,0:T(8,128)(2,1)}, bf16[544,128]{1,0:T(8,128)(2,1)S(1)}, u32[]{:S(2)}, u32[]{:S(2)}) collective-permute-start(bf16[544,128]{1,0:T(8,128)(2,1)} %get-tuple-element.20.sent_ref), channel_id=1, source_target_pairs={{0,1},{1,0},{2,3},{3,2},{4,5},{5,4},{6,7},{7,6},{8,9},{9,8},{10,11... | collective-permute-start | bytes 417800 | tf_op jit(solution)/shard_map/ppermute | solution.py:496
  7.9 4.5 %collective-permute-start.2 = (bf16[288,128]{1,0:T(8,128)(2,1)}, bf16[288,128]{1,0:T(8,128)(2,1)S(1)}, u32[]{:S(2)}, u32[]{:S(2)}) collective-permute-start(bf16[288,128]{1,0:T(8,128)(2,1)} %get-tuple-element.23), channel_id=1, source_target_pairs={{1,2},{3,4},{5,6},{7,8},{9,10},{11,12},{13,14},{15,16},{17,18},{19... | collective-permute-start | bytes 221192 | tf_op jit(solution)/shard_map/ppermute | solution.py:500
  8.5 1.0 %copy-start.1 = (f32[528,128]{1,0:T(8,128)S(1)}, f32[528,128]{1,0:T(8,128)}, u32[]{:S(2)}) copy-start(f32[528,128]{1,0:T(8,128)} %get-tuple-element.19.local_ref) | copy-start | bytes 811012
  9.5 0.9 %copy-start.2 = (bf16[544,128]{1,0:T(8,128)(2,1)S(1)}, bf16[544,128]{1,0:T(8,128)(2,1)}, u32[]{:S(2)}) copy-start(bf16[544,128]{1,0:T(8,128)(2,1)} %get-tuple-element.20.sent_ref) | copy-start | bytes 417796
  12.4 31.5 %copy-start = (f32[8,8,8192]{2,1,0:T(8,128)S(1)}, f32[8,8,8192]{2,1,0:T(8,128)}, u32[]{:S(2)}) copy-start(f32[8,8,8192]{2,1,0:T(8,128)} %basis_ref.5) | copy-start | bytes 6291460
  12.4 31.5 %copy-start.5 = (s32[32]{0:T(128)S(1)}, s32[32]{0:T(128)}, u32[]{:S(2)}) copy-start(s32[32]{0:T(128)} %counts_s.1) | copy-start | bytes 388
  40.1 10.5 %copy-start.3 = (f32[8192]{0:T(1024)S(1)}, f32[8192]{0:T(1024)}, u32[]{:S(2)}) copy-start(f32[8192]{0:T(1024)} %param.13) | copy-start | bytes 98308
  40.1 10.5 %collective-permute-start.3 = (f32[256,256]{1,0:T(8,128)S(1)}, f32[256,256]{1,0:T(8,128)S(1)}, u32[]{:S(2)}, u32[]{:S(2)}) collective-permute-start(f32[256,256]{1,0:T(8,128)S(1)} %get-tuple-element.29), channel_id=1, source_target_pairs={{0,1},{1,0},{2,3},{3,2},{4,5},{5,4},{6,7},{7,6},{8,9},{9,8},{10,11... | collective-permute-start | bytes 786440 | tf_op jit(solution)/shard_map/ppermute | solution.py:535

commit v19 on v16

--- a/solution.py
+++ b/solution.py
@@ -200,6 +200,7 @@
         ahead = distances(*runs[0])
         cubed = []
         given = []
+        part = None
         for i, (near_x, source, place) in enumerate(runs):
             here = ahead
             if i + 1 < len(runs):
@@ -207,16 +208,20 @@
             inverse = lax.rsqrt(here)
             cubed.append((inverse * inverse * inverse).astype(bf16))
             given.append(jnp.concatenate([rows_at(source[1], place, 80), rows_at(source[2], place, 80)], axis=0))
-            if i + 1 == len(runs) or runs[i + 1][0] != near_x:
-                rows_of = pl.ds(pl.multiple_of((target_y * 4 + near_x) * 160, 160), 160)
-                total[rows_of, :] += lax.dot_general(
+            last = i + 1 == len(runs) or runs[i + 1][0] != near_x
+            if last or runs[i + 1][1] is not source:
+                sums = lax.dot_general(
                     jnp.concatenate(given, axis=1),
                     jnp.concatenate(cubed, axis=1),
                     (((1,), (1,)), ((), ())),
                     preferred_element_type=f32,
                 )
+                part = sums if part is None else part + sums
                 cubed = []
                 given = []
+            if last:
+                total[pl.ds(pl.multiple_of((target_y * 4 + near_x) * 160, 160), 160), :] += part
+                part = None
         beside(item)
         return 0
 

time: 66.1 us -> 69.3 us (1.048)
  Pallas kernels: 36 us -> 39.2 us
    pallas_call x1, Pallas kernels: 27.5 us -> 30.7 us  [on_device(): pl.pallas_call(field_kernel, out_shape=(rows(boxes * 8, per_box),) * 2, i...]
where the time goes in v19:
time: 69.3 us; the launch traced here: 69 us
  Pallas kernels  39.2 us (57%)
  blocking collectives  13.4 us (19%)
  starting transfers between devices  8.77 us (13%)
  waiting for transfers between devices  5.03 us (7%)
  local copies, waits for them, and re-layouts  1.88 us (3%)
  between operations  0.76 us (1%)
    pallas_call x1, Pallas kernels, on_device(): pl.pallas_call(field_kernel, out_shape=(rows(boxes * 8, per_box),) * 2, i...  30.7 us
    all_to_all x1, blocking collectives, on_device(): tiles = lax.all_to_all(tiles, 'box', 0, 0, tiled=True)  13.4 us
    ppermute x1, waiting for transfers between devices, on_device(): theirs = lax.ppermute(theirs, 'rhs', swap)  5.02 us
    ppermute x1, starting transfers between devices, on_device(): theirs = lax.ppermute(theirs, 'rhs', swap)  3.79 us
    pallas_call x1, Pallas kernels, on_device(): pl.pallas_call(prep_kernel, out_shape=(rows(544, dtype=bf16), rows(400),...  2.89 us
    ppermute x1, starting transfers between devices, on_device(): lax.ppermute(first, ('box', 'rhs'), [(2 * i, 2 * i + 2) for i in ups] + [...  2.37 us
    ppermute x1, starting transfers between devices, on_device(): cross = lax.ppermute(sent, 'rhs', swap)  1.96 us
    pallas_call x1, Pallas kernels, on_device(): pl.pallas_call(feature_kernel, out_shape=(rows(boxes * depth, per_box, bf...  1.94 us
  transfers between devices with their start and end apart: 4, of which 1 were waited for; matrix products, arithmetic and copies ran while one was open for 0% of the time, Pallas kernels for 5%

profile of v19, /device:TPU:0, one launch (start us, length us, event | category | flops | bytes accessed | tf_op | source)
XLA Modules:
  0.0 69.0 jit_solution(9854484927591390959)
XLA Ops:
  0.6 0.0 copy-start.4
  0.6 2.9 %prepare.1 = (bf16[544,128]{1,0:T(8,128)(2,1)}, f32[400,128]{1,0:T(8,128)}, bf16[288,128]{1,0:T(8,128)(2,1)}, f32[528,128]{1,0:T(8,128)}) custom-call(f32[3,32]{1,0:T(4,128)} %centres_s.1, s32[32]{0:T(128)} %counts_s.1, f32[8,8,8192]{2,1,0:T(8,128)} %basis_ref.5, f32[3,8192]{1,0:T(4,128)} %facets_h.1, f32[64,128]{1,0:T(8,128)} %bitcast.4, f32[3,8192]{1,0:T(4,128)} %normals_h.1), custom_call_target="tpu_custom_call" | custom-call | tf_op jit(solution)/shard_map/prepare/pallas_call | solution.py:479
  3.5 2.4 %collective-permute-start.1 = (f32[400,128]{1,0:T(8,128)}, f32[400,128]{1,0:T(8,128)S(1)}, u32[]{:S(2)}, u32[]{:S(2)}) collective-permute-start(f32[400,128]{1,0:T(8,128)} %get-tuple-element.22), channel_id=1, source_target_pairs={{0,2},{2,4},{4,6},{6,8},{8,10},{10,12},{12,14},{14,16},{16,18},{18... | collective-permute-start | bytes 614408 | tf_op jit(solution)/shard_map/ppermute | solution.py:499
  5.9 2.0 %collective-permute-start = (bf16[544,128]{1,0:T(8,128)(2,1)}, bf16[544,128]{1,0:T(8,128)(2,1)S(1)}, u32[]{:S(2)}, u32[]{:S(2)}) collective-permute-start(bf16[544,128]{1,0:T(8,128)(2,1)} %get-tuple-element.20.sent_ref), channel_id=1, source_target_pairs={{0,1},{1,0},{2,3},{3,2},{4,5},{5,4},{6,7},{7,6},{8,9},{9,8},{10,11... | collective-permute-start | bytes 417800 | tf_op jit(solution)/shard_map/ppermute | solution.py:498
  7.9 0.7 collective-permute-start.2
  8.5 0.0 copy-start.1
  8.5 0.9 %copy-done.1 = f32[528,128]{1,0:T(8,128)S(1)} copy-done((f32[528,128]{1,0:T(8,128)S(1)}, f32[528,128]{1,0:T(8,128)}, u32[]{:S(2)}) %copy-start.1) | copy-done | bytes 270360
  9.5 0.0 copy-start.2
  9.5 0.9 %copy-done.2 = bf16[544,128]{1,0:T(8,128)(2,1)S(1)} copy-done((bf16[544,128]{1,0:T(8,128)(2,1)S(1)}, bf16[544,128]{1,0:T(8,128)(2,1)}, u32[]{:S(2)}) %copy-start.2) | copy-done | bytes 139288
  10.4 1.9 %features.1 = (bf16[2048,256]{1,0:T(8,128)(2,1)S(1)}, bf16[2560,256]{1,0:T(8,128)(2,1)S(1)}, bf16[4096,64]{1,0:T(8,128)(2,1)S(1)}, f32[128,256]{1,0:T(8,128)S(1)}, f32[528,128]{1,0:T(8,128)S(1)}) custom-call(f32[528,128]{1,0:T(8,128)S(1)} %copy-done.1, bf16[544,128]{1,0:T(8,128)(2,1)S(1)} %copy-done.2), custom_call_target="tpu_custom_call" | custom-call | tf_op jit(solution)/shard_map/features/pallas_call | solution.py:506
  12.3 0.0 collective-permute-done.2.second_ref
  12.4 0.0 collective-permute-done.cross_ref
  12.4 0.0 collective-permute-done.1.first_ref
  12.4 0.0 copy-done.4
  12.4 0.0 copy-start
  12.4 0.0 copy-start.5
  12.4 30.7 %fields.1 = (f32[256,256]{1,0:T(8,128)S(1)}, f32[256,256]{1,0:T(8,128)S(1)}) custom-call(f32[3,32]{1,0:T(4,128)S(1)} %copy-done.4, f32[528,128]{1,0:T(8,128)S(1)} %get-tuple-element.21.local_ref, bf16[544,128]{1,0:T(8,128)(2,1)S(1)} %collective-permute-done.cross_ref, f32[400,128]{1,0:T(8,128)S(1)} %collective-permute-done.1.first_ref, ...), custom_call_target="tpu_custom_call" | custom-call | tf_op jit(solution)/shard_map/fields/pallas_call | solution.py:520
  43.1 0.0 copy-start.3
  43.1 3.8 %collective-permute-start.3 = (f32[256,256]{1,0:T(8,128)S(1)}, f32[256,256]{1,0:T(8,128)S(1)}, u32[]{:S(2)}, u32[]{:S(2)}) collective-permute-start(f32[256,256]{1,0:T(8,128)S(1)} %get-tuple-element.29), channel_id=1, source_target_pairs={{0,1},{1,0},{2,3},{3,2},{4,5},{5,4},{6,7},{7,6},{8,9},{9,8},{10,11... | collective-permute-start | bytes 786440 | tf_op jit(solution)/shard_map/ppermute | solution.py:537
  46.9 0.0 copy-done
  46.9 0.0 copy-done.5
  46.9 1.7 %gram.1 = (f32[8,128]{1,0:T(8,128)S(1)}, f32[64,128]{1,0:T(8,128)S(1)}) custom-call(s32[32]{0:T(128)S(1)} %copy-done.5, f32[8,8,8192]{2,1,0:T(8,128)S(1)} %copy-done), custom_call_target="tpu_custom_call" | custom-call | tf_op jit(solution)/shard_map/gram/pallas_call | solution.py:538
  48.6 5.0 %collective-permute-done.3.theirs_ref = f32[256,256]{1,0:T(8,128)S(1)} collective-permute-done((f32[256,256]{1,0:T(8,128)S(1)}, f32[256,256]{1,0:T(8,128)S(1)}, u32[]{:S(2)}, u32[]{:S(2)}) %collective-permute-start.3) | collective-permute-done | bytes 262176 | tf_op jit(solution)/shard_map/ppermute | solution.py:537
  53.6 0.0 copy-done.3
  53.6 0.4 image.1
  54.0 13.4 %all_to_all.5.tiles_ref = f32[16,8,128]{2,1,0:T(8,128)S(1)} all-to-all(f32[16,8,128]{2,1,0:T(8,128)S(1)} %get-tuple-element.32), channel_id=1, replica_groups=mesh['box'=16,'rhs'=2] {'box'}, dimensions={0} | all-to-all | bytes 131072 | tf_op jit(solution)/shard_map/all_to_all | solution.py:554
  67.4 1.6 %finish.1 = (f32[8,8192]{1,0:T(8,128)}, f32[8,9]{1,0:T(8,128)}) custom-call(f32[16,8,128]{2,1,0:T(8,128)S(1)} %all_to_all.5.tiles_ref, f32[64,128]{1,0:T(8,128)S(1)} %get-tuple-element.31.live_ref, f32[8,8192]{1,0:T(8,128)S(1)} %get-tuple-element.33.image_ref, f32[8,8,8192]{2,1,0:T(8,128)S(1)} %copy-done), custom_call_target="tpu_custom_call" | custom-call | tf_op jit(solution)/shard_map/finish/pallas_call | solution.py:555
Async XLA Ops:
  0.6 11.7 %copy-start.4 = (f32[3,32]{1,0:T(4,128)S(1)}, f32[3,32]{1,0:T(4,128)}, u32[]{:S(2)}) copy-start(f32[3,32]{1,0:T(4,128)} %centres_s.1) | copy-start | bytes 1156
  3.5 8.8 %collective-permute-start.1 = (f32[400,128]{1,0:T(8,128)}, f32[400,128]{1,0:T(8,128)S(1)}, u32[]{:S(2)}, u32[]{:S(2)}) collective-permute-start(f32[400,128]{1,0:T(8,128)} %get-tuple-element.22), channel_id=1, source_target_pairs={{0,2},{2,4},{4,6},{6,8},{8,10},{10,12},{12,14},{14,16},{16,18},{18... | collective-permute-start | bytes 614408 | tf_op jit(solution)/shard_map/ppermute | solution.py:499
  5.9 6.4 %collective-permute-start = (bf16[544,128]{1,0:T(8,128)(2,1)}, bf16[544,128]{1,0:T(8,128)(2,1)S(1)}, u32[]{:S(2)}, u32[]{:S(2)}) collective-permute-start(bf16[544,128]{1,0:T(8,128)(2,1)} %get-tuple-element.20.sent_ref), channel_id=1, source_target_pairs={{0,1},{1,0},{2,3},{3,2},{4,5},{5,4},{6,7},{7,6},{8,9},{9,8},{10,11... | collective-permute-start | bytes 417800 | tf_op jit(solution)/shard_map/ppermute | solution.py:498
  7.9 4.5 %collective-permute-start.2 = (bf16[288,128]{1,0:T(8,128)(2,1)}, bf16[288,128]{1,0:T(8,128)(2,1)S(1)}, u32[]{:S(2)}, u32[]{:S(2)}) collective-permute-start(bf16[288,128]{1,0:T(8,128)(2,1)} %get-tuple-element.23), channel_id=1, source_target_pairs={{1,2},{3,4},{5,6},{7,8},{9,10},{11,12},{13,14},{15,16},{17,18},{19... | collective-permute-start | bytes 221192 | tf_op jit(solution)/shard_map/ppermute | solution.py:502
  8.5 1.0 %copy-start.1 = (f32[528,128]{1,0:T(8,128)S(1)}, f32[528,128]{1,0:T(8,128)}, u32[]{:S(2)}) copy-start(f32[528,128]{1,0:T(8,128)} %get-tuple-element.19.local_ref) | copy-start | bytes 811012
  9.5 0.9 %copy-start.2 = (bf16[544,128]{1,0:T(8,128)(2,1)S(1)}, bf16[544,128]{1,0:T(8,128)(2,1)}, u32[]{:S(2)}) copy-start(bf16[544,128]{1,0:T(8,128)(2,1)} %get-tuple-element.20.sent_ref) | copy-start | bytes 417796
  12.4 34.6 %copy-start = (f32[8,8,8192]{2,1,0:T(8,128)S(1)}, f32[8,8,8192]{2,1,0:T(8,128)}, u32[]{:S(2)}) copy-start(f32[8,8,8192]{2,1,0:T(8,128)} %basis_ref.5) | copy-start | bytes 6291460
  12.4 34.5 %copy-start.5 = (s32[32]{0:T(128)S(1)}, s32[32]{0:T(128)}, u32[]{:S(2)}) copy-start(s32[32]{0:T(128)} %counts_s.1) | copy-start | bytes 388
  43.1 10.5 %copy-start.3 = (f32[8192]{0:T(1024)S(1)}, f32[8192]{0:T(1024)}, u32[]{:S(2)}) copy-start(f32[8192]{0:T(1024)} %param.13) | copy-start | bytes 98308
  43.1 10.5 %collective-permute-start.3 = (f32[256,256]{1,0:T(8,128)S(1)}, f32[256,256]{1,0:T(8,128)S(1)}, u32[]{:S(2)}, u32[]{:S(2)}) collective-permute-start(f32[256,256]{1,0:T(8,128)S(1)} %get-tuple-element.29), channel_id=1, source_target_pairs={{0,1},{1,0},{2,3},{3,2},{4,5},{5,4},{6,7},{7,6},{8,9},{9,8},{10,11... | collective-permute-start | bytes 786440 | tf_op jit(solution)/shard_map/ppermute | solution.py:537

commit v20 on v18

--- a/solution.py
+++ b/solution.py
@@ -13,7 +13,6 @@
 bf16 = jnp.bfloat16
 plane_boxes = 16
 per_box = 256
-step_items = 2
 depth = 64
 
 
@@ -180,21 +179,18 @@
 
 
 def near_planes(sources, targets, total, beside):
-    def near_rows(step, _):
+    def rows_at(pair, place, number):
+        ref, first = pair
+        return ref[pl.ds(pl.multiple_of((first + place) * number, number), number), :]
+
+    def target_row(target_y, source_y, rows):
         runs = []
-        for item in range(step_items):
-            item = step * step_items + item
-            target_y = (item + 1) // 3
-            source_y = target_y + lax.rem(item + 1, 3) - 1
-            for near_x in range(4):
-                target = target_y * 4 + near_x
-                for source in sources:
+        for near_x in range(4):
+            target = target_y * 4 + near_x
+            for source in sources:
+                for k in range(rows):
                     for x in range(max(near_x - 1, 0), min(near_x + 2, 4)):
-                        runs.append((target, source, source_y * 4 + x))
-
-        def rows_at(pair, place, number):
-            ref, first = pair
-            return ref[pl.ds(pl.multiple_of((first + place) * number, number), number), :]
+                        runs.append((target, source, (source_y + k) * 4 + x))
 
         def distances(target, source, place):
             facets = targets[pl.ds(pl.multiple_of(target * per_box, per_box), per_box), :]
@@ -211,8 +207,7 @@
             cubed.append((inverse * inverse * inverse).astype(bf16))
             given.append(jnp.concatenate([rows_at(source[1], place, 80), rows_at(source[2], place, 80)], axis=0))
             if i + 1 == len(runs) or runs[i + 1][0] is not target:
-                rows_of = pl.ds(pl.multiple_of(target * 160, 160), 160)
-                total[rows_of, :] += lax.dot_general(
+                total[pl.ds(pl.multiple_of(target * 160, 160), 160), :] = lax.dot_general(
                     jnp.concatenate(given, axis=1),
                     jnp.concatenate(cubed, axis=1),
                     (((1,), (1,)), ((), ())),
@@ -220,10 +215,19 @@
                 )
                 cubed = []
                 given = []
-        beside(step)
-        return 0
-
-    lax.fori_loop(0, 10 // step_items, near_rows, 0)
+
+    def outer(i, _):
+        target_row(3 * i, 2 * i, 2)
+        beside(i)
+        return 0
+
+    def inner(i, _):
+        target_row(i + 1, i, 3)
+        beside(i + 2)
+        return 0
+
+    lax.fori_loop(0, 2, outer, 0)
+    lax.fori_loop(0, 2, inner, 0)
 
 
 def field_kernel(
@@ -249,7 +253,6 @@
         return 0
 
     lax.fori_loop(0, plane_boxes, halo_source, 0, unroll=4)
-    total[...] = jnp.zeros_like(total)
 
     for group, (centres, ours, others) in enumerate(
         (
@@ -298,9 +301,9 @@
         second = jnp.dot(picked, lower, preferred_element_type=f32)
         return first[:16] + first[16:] + second[:16]
 
-    def far_boxes(step):
-        for i in range(5 * step_items):
-            k = jnp.minimum(step * 5 * step_items + i, 3 * plane_boxes - 1)
+    def far_boxes(i):
+        for k in range(12):
+            k = i * 12 + k
             far[pl.ds(pl.multiple_of(k * 16, 16), 16), :] = far_field(k)
 
     sources = [((geometry, p), (mine, p), (theirs, p)) for p in (0, plane_boxes)]

time: 66.3 us -> 65 us (0.980)
  Pallas kernels: 36.1 us -> 34.8 us
    pallas_call x1, Pallas kernels: 27.7 us -> 26.4 us  [on_device(): pl.pallas_call(field_kernel, out_shape=(rows(boxes * 8, per_box),) * 2, i...]
  transfers between devices with their start and end apart: 4 -> 4, of which waited for: 1 -> 1; matrix products, arithmetic and copies ran while one was open for 0% -> 0% of each run, Pallas kernels for 5% -> 6%
where the time goes in v20:
time: 65 us; the launch traced here: 64.7 us
  Pallas kernels  34.8 us (54%)
  blocking collectives  13.5 us (21%)
  starting transfers between devices  8.76 us (13%)
  waiting for transfers between devices  5.02 us (8%)
  local copies, waits for them, and re-layouts  1.88 us (3%)
  between operations  0.76 us (1%)
    pallas_call x1, Pallas kernels, on_device(): pl.pallas_call(field_kernel, out_shape=(rows(boxes * 8, per_box),) * 2, i...  26.4 us
    all_to_all x1, blocking collectives, on_device(): tiles = lax.all_to_all(tiles, 'box', 0, 0, tiled=True)  13.5 us
    ppermute x1, waiting for transfers between devices, on_device(): theirs = lax.ppermute(theirs, 'rhs', swap)  5.02 us
    ppermute x1, starting transfers between devices, on_device(): theirs = lax.ppermute(theirs, 'rhs', swap)  3.78 us
    pallas_call x1, Pallas kernels, on_device(): pl.pallas_call(prep_kernel, out_shape=(rows(544, dtype=bf16), rows(400),...  2.89 us
    ppermute x1, starting transfers between devices, on_device(): lax.ppermute(first, ('box', 'rhs'), [(2 * i, 2 * i + 2) for i in ups] + [...  2.37 us
    ppermute x1, starting transfers between devices, on_device(): cross = lax.ppermute(sent, 'rhs', swap)  1.96 us
    pallas_call x1, Pallas kernels, on_device(): pl.pallas_call(feature_kernel, out_shape=(rows(boxes * depth, per_box, bf...  1.94 us
  transfers between devices with their start and end apart: 4, of which 1 were waited for; matrix products, arithmetic and copies ran while one was open for 0% of the time, Pallas kernels for 6%

profile of v20, /device:TPU:0, one launch (start us, length us, event | category | flops | bytes accessed | tf_op | source)
XLA Modules:
  0.0 64.7 jit_solution(8536776210032246591)
XLA Ops:
  0.6 0.0 copy-start.4
  0.6 2.9 %prepare.1 = (bf16[544,128]{1,0:T(8,128)(2,1)}, f32[400,128]{1,0:T(8,128)}, bf16[288,128]{1,0:T(8,128)(2,1)}, f32[528,128]{1,0:T(8,128)}) custom-call(f32[3,32]{1,0:T(4,128)} %centres_s.1, s32[32]{0:T(128)} %counts_s.1, f32[8,8,8192]{2,1,0:T(8,128)} %basis_ref.5, f32[3,8192]{1,0:T(4,128)} %facets_h.1, f32[64,128]{1,0:T(8,128)} %bitcast.4, f32[3,8192]{1,0:T(4,128)} %normals_h.1), custom_call_target="tpu_custom_call" | custom-call | tf_op jit(solution)/shard_map/prepare/pallas_call | solution.py:480
  3.5 2.4 %collective-permute-start.1 = (f32[400,128]{1,0:T(8,128)}, f32[400,128]{1,0:T(8,128)S(1)}, u32[]{:S(2)}, u32[]{:S(2)}) collective-permute-start(f32[400,128]{1,0:T(8,128)} %get-tuple-element.22), channel_id=1, source_target_pairs={{0,2},{2,4},{4,6},{6,8},{8,10},{10,12},{12,14},{14,16},{16,18},{18... | collective-permute-start | bytes 614408 | tf_op jit(solution)/shard_map/ppermute | solution.py:500
  5.9 2.0 %collective-permute-start = (bf16[544,128]{1,0:T(8,128)(2,1)}, bf16[544,128]{1,0:T(8,128)(2,1)S(1)}, u32[]{:S(2)}, u32[]{:S(2)}) collective-permute-start(bf16[544,128]{1,0:T(8,128)(2,1)} %get-tuple-element.20.sent_ref), channel_id=1, source_target_pairs={{0,1},{1,0},{2,3},{3,2},{4,5},{5,4},{6,7},{7,6},{8,9},{9,8},{10,11... | collective-permute-start | bytes 417800 | tf_op jit(solution)/shard_map/ppermute | solution.py:499
  7.9 0.7 %collective-permute-start.2 = (bf16[288,128]{1,0:T(8,128)(2,1)}, bf16[288,128]{1,0:T(8,128)(2,1)S(1)}, u32[]{:S(2)}, u32[]{:S(2)}) collective-permute-start(bf16[288,128]{1,0:T(8,128)(2,1)} %get-tuple-element.23), channel_id=1, source_target_pairs={{1,2},{3,4},{5,6},{7,8},{9,10},{11,12},{13,14},{15,16},{17,18},{19... | collective-permute-start | bytes 221192 | tf_op jit(solution)/shard_map/ppermute | solution.py:503
  8.5 0.0 copy-start.1
  8.5 0.9 %copy-done.1 = f32[528,128]{1,0:T(8,128)S(1)} copy-done((f32[528,128]{1,0:T(8,128)S(1)}, f32[528,128]{1,0:T(8,128)}, u32[]{:S(2)}) %copy-start.1) | copy-done | bytes 270360
  9.5 0.0 copy-start.2
  9.5 0.9 %copy-done.2 = bf16[544,128]{1,0:T(8,128)(2,1)S(1)} copy-done((bf16[544,128]{1,0:T(8,128)(2,1)S(1)}, bf16[544,128]{1,0:T(8,128)(2,1)}, u32[]{:S(2)}) %copy-start.2) | copy-done | bytes 139288
  10.4 1.9 %features.1 = (bf16[2048,256]{1,0:T(8,128)(2,1)S(1)}, bf16[2560,256]{1,0:T(8,128)(2,1)S(1)}, bf16[4096,64]{1,0:T(8,128)(2,1)S(1)}, f32[128,256]{1,0:T(8,128)S(1)}, f32[528,128]{1,0:T(8,128)S(1)}) custom-call(f32[528,128]{1,0:T(8,128)S(1)} %copy-done.1, bf16[544,128]{1,0:T(8,128)(2,1)S(1)} %copy-done.2), custom_call_target="tpu_custom_call" | custom-call | tf_op jit(solution)/shard_map/features/pallas_call | solution.py:507
  12.3 0.0 collective-permute-done.2.second_ref
  12.4 0.0 collective-permute-done.cross_ref
  12.4 0.0 collective-permute-done.1.first_ref
  12.4 0.0 copy-done.4
  12.4 0.0 copy-start
  12.4 0.0 copy-start.5
  12.4 26.4 %fields.1 = (f32[256,256]{1,0:T(8,128)S(1)}, f32[256,256]{1,0:T(8,128)S(1)}) custom-call(f32[3,32]{1,0:T(4,128)S(1)} %copy-done.4, f32[528,128]{1,0:T(8,128)S(1)} %get-tuple-element.21.local_ref, bf16[544,128]{1,0:T(8,128)(2,1)S(1)} %collective-permute-done.cross_ref, f32[400,128]{1,0:T(8,128)S(1)} %collective-permute-done.1.first_ref, ...), custom_call_target="tpu_custom_call" | custom-call | tf_op jit(solution)/shard_map/fields/pallas_call | solution.py:521
  38.8 0.0 copy-start.3
  38.8 3.8 %collective-permute-start.3 = (f32[256,256]{1,0:T(8,128)S(1)}, f32[256,256]{1,0:T(8,128)S(1)}, u32[]{:S(2)}, u32[]{:S(2)}) collective-permute-start(f32[256,256]{1,0:T(8,128)S(1)} %get-tuple-element.29), channel_id=1, source_target_pairs={{0,1},{1,0},{2,3},{3,2},{4,5},{5,4},{6,7},{7,6},{8,9},{9,8},{10,11... | collective-permute-start | bytes 786440 | tf_op jit(solution)/shard_map/ppermute | solution.py:538
  42.6 0.0 copy-done
  42.6 0.0 copy-done.5
  42.6 1.7 %gram.1 = (f32[8,128]{1,0:T(8,128)S(1)}, f32[64,128]{1,0:T(8,128)S(1)}) custom-call(s32[32]{0:T(128)S(1)} %copy-done.5, f32[8,8,8192]{2,1,0:T(8,128)S(1)} %copy-done), custom_call_target="tpu_custom_call" | custom-call | tf_op jit(solution)/shard_map/gram/pallas_call | solution.py:539
  44.3 5.0 %collective-permute-done.3.theirs_ref = f32[256,256]{1,0:T(8,128)S(1)} collective-permute-done((f32[256,256]{1,0:T(8,128)S(1)}, f32[256,256]{1,0:T(8,128)S(1)}, u32[]{:S(2)}, u32[]{:S(2)}) %collective-permute-start.3) | collective-permute-done | bytes 262176 | tf_op jit(solution)/shard_map/ppermute | solution.py:538
  49.3 0.0 copy-done.3
  49.3 0.4 image.1
  49.7 13.5 %all_to_all.5.tiles_ref = f32[16,8,128]{2,1,0:T(8,128)S(1)} all-to-all(f32[16,8,128]{2,1,0:T(8,128)S(1)} %get-tuple-element.32), channel_id=1, replica_groups=mesh['box'=16,'rhs'=2] {'box'}, dimensions={0} | all-to-all | bytes 131072 | tf_op jit(solution)/shard_map/all_to_all | solution.py:555
  63.1 1.6 %finish.1 = (f32[8,8192]{1,0:T(8,128)}, f32[8,9]{1,0:T(8,128)}) custom-call(f32[16,8,128]{2,1,0:T(8,128)S(1)} %all_to_all.5.tiles_ref, f32[64,128]{1,0:T(8,128)S(1)} %get-tuple-element.31.live_ref, f32[8,8192]{1,0:T(8,128)S(1)} %get-tuple-element.33.image_ref, f32[8,8,8192]{2,1,0:T(8,128)S(1)} %copy-done), custom_call_target="tpu_custom_call" | custom-call | tf_op jit(solution)/shard_map/finish/pallas_call | solution.py:556
Async XLA Ops:
  0.6 11.7 %copy-start.4 = (f32[3,32]{1,0:T(4,128)S(1)}, f32[3,32]{1,0:T(4,128)}, u32[]{:S(2)}) copy-start(f32[3,32]{1,0:T(4,128)} %centres_s.1) | copy-start | bytes 1156
  3.5 8.8 %collective-permute-start.1 = (f32[400,128]{1,0:T(8,128)}, f32[400,128]{1,0:T(8,128)S(1)}, u32[]{:S(2)}, u32[]{:S(2)}) collective-permute-start(f32[400,128]{1,0:T(8,128)} %get-tuple-element.22), channel_id=1, source_target_pairs={{0,2},{2,4},{4,6},{6,8},{8,10},{10,12},{12,14},{14,16},{16,18},{18... | collective-permute-start | bytes 614408 | tf_op jit(solution)/shard_map/ppermute | solution.py:500
  5.9 6.4 %collective-permute-start = (bf16[544,128]{1,0:T(8,128)(2,1)}, bf16[544,128]{1,0:T(8,128)(2,1)S(1)}, u32[]{:S(2)}, u32[]{:S(2)}) collective-permute-start(bf16[544,128]{1,0:T(8,128)(2,1)} %get-tuple-element.20.sent_ref), channel_id=1, source_target_pairs={{0,1},{1,0},{2,3},{3,2},{4,5},{5,4},{6,7},{7,6},{8,9},{9,8},{10,11... | collective-permute-start | bytes 417800 | tf_op jit(solution)/shard_map/ppermute | solution.py:499
  7.9 4.5 %collective-permute-start.2 = (bf16[288,128]{1,0:T(8,128)(2,1)}, bf16[288,128]{1,0:T(8,128)(2,1)S(1)}, u32[]{:S(2)}, u32[]{:S(2)}) collective-permute-start(bf16[288,128]{1,0:T(8,128)(2,1)} %get-tuple-element.23), channel_id=1, source_target_pairs={{1,2},{3,4},{5,6},{7,8},{9,10},{11,12},{13,14},{15,16},{17,18},{19... | collective-permute-start | bytes 221192 | tf_op jit(solution)/shard_map/ppermute | solution.py:503
  8.5 1.0 %copy-start.1 = (f32[528,128]{1,0:T(8,128)S(1)}, f32[528,128]{1,0:T(8,128)}, u32[]{:S(2)}) copy-start(f32[528,128]{1,0:T(8,128)} %get-tuple-element.19.local_ref) | copy-start | bytes 811012
  9.5 0.9 %copy-start.2 = (bf16[544,128]{1,0:T(8,128)(2,1)S(1)}, bf16[544,128]{1,0:T(8,128)(2,1)}, u32[]{:S(2)}) copy-start(bf16[544,128]{1,0:T(8,128)(2,1)} %get-tuple-element.20.sent_ref) | copy-start | bytes 417796
  12.4 30.2 %copy-start = (f32[8,8,8192]{2,1,0:T(8,128)S(1)}, f32[8,8,8192]{2,1,0:T(8,128)}, u32[]{:S(2)}) copy-start(f32[8,8,8192]{2,1,0:T(8,128)} %basis_ref.5) | copy-start | bytes 6291460
  12.4 30.2 %copy-start.5 = (s32[32]{0:T(128)S(1)}, s32[32]{0:T(128)}, u32[]{:S(2)}) copy-start(s32[32]{0:T(128)} %counts_s.1) | copy-start | bytes 388
  38.8 10.5 %copy-start.3 = (f32[8192]{0:T(1024)S(1)}, f32[8192]{0:T(1024)}, u32[]{:S(2)}) copy-start(f32[8192]{0:T(1024)} %param.13) | copy-start | bytes 98308
  38.8 10.5 %collective-permute-start.3 = (f32[256,256]{1,0:T(8,128)S(1)}, f32[256,256]{1,0:T(8,128)S(1)}, u32[]{:S(2)}, u32[]{:S(2)}) collective-permute-start(f32[256,256]{1,0:T(8,128)S(1)} %get-tuple-element.29), channel_id=1, source_target_pairs={{0,1},{1,0},{2,3},{3,2},{4,5},{5,4},{6,7},{7,6},{8,9},{9,8},{10,11... | collective-permute-start | bytes 786440 | tf_op jit(solution)/shard_map/ppermute | solution.py:538

commit v21 on v20

--- a/solution.py
+++ b/solution.py
@@ -137,7 +137,9 @@
     features = jnp.where(row == 3, square, jnp.where(row == 4, 1.0, local))
     high, middle, low = thirds(features)
     rows = stacked_rows((high, high, high, middle, middle, low), per_box)
-    geometry[pl.ds(pl.multiple_of(box * depth, depth), depth), :] = rows.astype(bf16)
+    start = pl.multiple_of((box // 4) * depth, depth)
+    lanes = pl.multiple_of(lax.rem(box, 4) * per_box, per_box)
+    geometry[pl.ds(start, depth), pl.ds(lanes, per_box)] = rows.astype(bf16)
 
 
 def store_strengths(local, charges, box, strengths):
@@ -189,23 +191,27 @@
             target = target_y * 4 + near_x
             for source in sources:
                 for k in range(rows):
-                    for x in range(max(near_x - 1, 0), min(near_x + 2, 4)):
-                        runs.append((target, source, (source_y + k) * 4 + x))
-
-        def distances(target, source, place):
+                    runs.append((target, source, source_y + k, max(near_x - 1, 0), min(near_x + 2, 4)))
+
+        def distances(target, source, y, low, high):
             facets = targets[pl.ds(pl.multiple_of(target * per_box, per_box), per_box), :]
-            return jnp.dot(facets, rows_at(source[0], place, depth), preferred_element_type=f32)
+            ref, first = source[0]
+            start = pl.multiple_of((first // 4 + y) * depth, depth)
+            weights = ref[pl.ds(start, depth), low * per_box : high * per_box]
+            return jnp.dot(facets, weights, preferred_element_type=f32)
 
         ahead = distances(*runs[0])
         cubed = []
         given = []
-        for i, (target, source, place) in enumerate(runs):
+        for i, (target, source, y, low, high) in enumerate(runs):
             here = ahead
             if i + 1 < len(runs):
                 ahead = distances(*runs[i + 1])
             inverse = lax.rsqrt(here)
             cubed.append((inverse * inverse * inverse).astype(bf16))
-            given.append(jnp.concatenate([rows_at(source[1], place, 80), rows_at(source[2], place, 80)], axis=0))
+            for x in range(low, high):
+                both = [rows_at(half, y * 4 + x, 80) for half in source[1:]]
+                given.append(jnp.concatenate(both, axis=0))
             if i + 1 == len(runs) or runs[i + 1][0] is not target:
                 total[pl.ds(pl.multiple_of(target * 160, 160), 160), :] = lax.dot_general(
                     jnp.concatenate(given, axis=1),
@@ -507,7 +513,7 @@
     geometry, strengths, targets, planes, local = pl.pallas_call(
         feature_kernel,
         out_shape=(
-            rows(boxes * depth, per_box, bf16),
+            rows(boxes // 4 * depth, 4 * per_box, bf16),
             rows(boxes * 80, per_box, bf16),
             rows(plane_slots, depth, bf16),
             rows(plane_boxes * 8, per_box),
@@ -524,7 +530,7 @@
         in_specs=[smem] + [vmem] * 8,
         out_specs=(vmem, vmem),
         scratch_shapes=[
-            pltpu.VMEM((plane_boxes * depth, per_box), bf16),
+            pltpu.VMEM((plane_boxes // 4 * depth, 4 * per_box), bf16),
             pltpu.VMEM((plane_boxes * 80, per_box), bf16),
             pltpu.VMEM((3 * plane_boxes * 80, per_box), bf16),
             pltpu.VMEM((plane_boxes * 160, per_box), f32),

time: 65 us -> 65.9 us (1.014)
  Pallas kernels: 34.8 us -> 35.8 us
    pallas_call x1, Pallas kernels: 26.4 us -> 27.3 us  [on_device(): pl.pallas_call(field_kernel, out_shape=(rows(boxes * 8, per_box),) * 2, i...]
where the time goes in v21:
time: 65.9 us; the launch traced here: 65.6 us
  Pallas kernels  35.8 us (54%)
  blocking collectives  13.4 us (20%)
  starting transfers between devices  8.77 us (13%)
  waiting for transfers between devices  5.03 us (8%)
  local copies, waits for them, and re-layouts  1.88 us (3%)
  between operations  0.76 us (1%)
    pallas_call x1, Pallas kernels, on_device(): pl.pallas_call(field_kernel, out_shape=(rows(boxes * 8, per_box),) * 2, i...  27.3 us
    all_to_all x1, blocking collectives, on_device(): tiles = lax.all_to_all(tiles, 'box', 0, 0, tiled=True)  13.4 us
    ppermute x1, waiting for transfers between devices, on_device(): theirs = lax.ppermute(theirs, 'rhs', swap)  5.02 us
    ppermute x1, starting transfers between devices, on_device(): theirs = lax.ppermute(theirs, 'rhs', swap)  3.79 us
    pallas_call x1, Pallas kernels, on_device(): pl.pallas_call(prep_kernel, out_shape=(rows(544, dtype=bf16), rows(400),...  2.89 us
    ppermute x1, starting transfers between devices, on_device(): lax.ppermute(first, ('box', 'rhs'), [(2 * i, 2 * i + 2) for i in ups] + [...  2.37 us
    ppermute x1, starting transfers between devices, on_device(): cross = lax.ppermute(sent, 'rhs', swap)  1.96 us
    pallas_call x1, Pallas kernels, on_device(): pl.pallas_call(feature_kernel, out_shape=(rows(boxes // 4 * depth, 4 * pe...  1.95 us
  transfers between devices with their start and end apart: 4, of which 1 were waited for; matrix products, arithmetic and copies ran while one was open for 0% of the time, Pallas kernels for 6%

profile of v21, /device:TPU:0, one launch (start us, length us, event | category | flops | bytes accessed | tf_op | source)
XLA Modules:
  0.0 65.6 jit_solution(16676994742255463096)
XLA Ops:
  0.6 0.0 copy-start.4
  0.6 2.9 %prepare.1 = (bf16[544,128]{1,0:T(8,128)(2,1)}, f32[400,128]{1,0:T(8,128)}, bf16[288,128]{1,0:T(8,128)(2,1)}, f32[528,128]{1,0:T(8,128)}) custom-call(f32[3,32]{1,0:T(4,128)} %centres_s.1, s32[32]{0:T(128)} %counts_s.1, f32[8,8,8192]{2,1,0:T(8,128)} %basis_ref.5, f32[3,8192]{1,0:T(4,128)} %facets_h.1, f32[64,128]{1,0:T(8,128)} %bitcast.4, f32[3,8192]{1,0:T(4,128)} %normals_h.1), custom_call_target="tpu_custom_call" | custom-call | tf_op jit(solution)/shard_map/prepare/pallas_call | solution.py:486
  3.5 2.4 %collective-permute-start.1 = (f32[400,128]{1,0:T(8,128)}, f32[400,128]{1,0:T(8,128)S(1)}, u32[]{:S(2)}, u32[]{:S(2)}) collective-permute-start(f32[400,128]{1,0:T(8,128)} %get-tuple-element.22), channel_id=1, source_target_pairs={{0,2},{2,4},{4,6},{6,8},{8,10},{10,12},{12,14},{14,16},{16,18},{18... | collective-permute-start | bytes 614408 | tf_op jit(solution)/shard_map/ppermute | solution.py:506
  5.9 2.0 %collective-permute-start = (bf16[544,128]{1,0:T(8,128)(2,1)}, bf16[544,128]{1,0:T(8,128)(2,1)S(1)}, u32[]{:S(2)}, u32[]{:S(2)}) collective-permute-start(bf16[544,128]{1,0:T(8,128)(2,1)} %get-tuple-element.20.sent_ref), channel_id=1, source_target_pairs={{0,1},{1,0},{2,3},{3,2},{4,5},{5,4},{6,7},{7,6},{8,9},{9,8},{10,11... | collective-permute-start | bytes 417800 | tf_op jit(solution)/shard_map/ppermute | solution.py:505
  7.9 0.7 collective-permute-start.2
  8.5 0.0 copy-start.1
  8.5 0.9 %copy-done.1 = f32[528,128]{1,0:T(8,128)S(1)} copy-done((f32[528,128]{1,0:T(8,128)S(1)}, f32[528,128]{1,0:T(8,128)}, u32[]{:S(2)}) %copy-start.1) | copy-done | bytes 270360
  9.5 0.0 copy-start.2
  9.5 0.9 %copy-done.2 = bf16[544,128]{1,0:T(8,128)(2,1)S(1)} copy-done((bf16[544,128]{1,0:T(8,128)(2,1)S(1)}, bf16[544,128]{1,0:T(8,128)(2,1)}, u32[]{:S(2)}) %copy-start.2) | copy-done | bytes 139288
  10.4 1.9 %features.1 = (bf16[512,1024]{1,0:T(8,128)(2,1)S(1)}, bf16[2560,256]{1,0:T(8,128)(2,1)S(1)}, bf16[4096,64]{1,0:T(8,128)(2,1)S(1)}, f32[128,256]{1,0:T(8,128)S(1)}, f32[528,128]{1,0:T(8,128)S(1)}) custom-call(f32[528,128]{1,0:T(8,128)S(1)} %copy-done.1, bf16[544,128]{1,0:T(8,128)(2,1)S(1)} %copy-done.2), custom_call_target="tpu_custom_call" | custom-call | tf_op jit(solution)/shard_map/features/pallas_call | solution.py:513
  12.4 0.0 collective-permute-done.2.second_ref
  12.4 0.0 collective-permute-done.cross_ref
  12.4 0.0 collective-permute-done.1.first_ref
  12.4 0.0 copy-done.4
  12.4 0.0 copy-start
  12.4 0.0 copy-start.5
  12.4 27.3 %fields.1 = (f32[256,256]{1,0:T(8,128)S(1)}, f32[256,256]{1,0:T(8,128)S(1)}) custom-call(f32[3,32]{1,0:T(4,128)S(1)} %copy-done.4, f32[528,128]{1,0:T(8,128)S(1)} %get-tuple-element.21.local_ref, bf16[544,128]{1,0:T(8,128)(2,1)S(1)} %collective-permute-done.cross_ref, f32[400,128]{1,0:T(8,128)S(1)} %collective-permute-done.1.first_ref, ...), custom_call_target="tpu_custom_call" | custom-call | tf_op jit(solution)/shard_map/fields/pallas_call | solution.py:527
  39.7 0.0 copy-start.3
  39.8 3.8 %collective-permute-start.3 = (f32[256,256]{1,0:T(8,128)S(1)}, f32[256,256]{1,0:T(8,128)S(1)}, u32[]{:S(2)}, u32[]{:S(2)}) collective-permute-start(f32[256,256]{1,0:T(8,128)S(1)} %get-tuple-element.29), channel_id=1, source_target_pairs={{0,1},{1,0},{2,3},{3,2},{4,5},{5,4},{6,7},{7,6},{8,9},{9,8},{10,11... | collective-permute-start | bytes 786440 | tf_op jit(solution)/shard_map/ppermute | solution.py:544
  43.5 0.0 copy-done
  43.5 0.0 copy-done.5
  43.6 1.7 %gram.1 = (f32[8,128]{1,0:T(8,128)S(1)}, f32[64,128]{1,0:T(8,128)S(1)}) custom-call(s32[32]{0:T(128)S(1)} %copy-done.5, f32[8,8,8192]{2,1,0:T(8,128)S(1)} %copy-done), custom_call_target="tpu_custom_call" | custom-call | tf_op jit(solution)/shard_map/gram/pallas_call | solution.py:545
  45.2 5.0 %collective-permute-done.3.theirs_ref = f32[256,256]{1,0:T(8,128)S(1)} collective-permute-done((f32[256,256]{1,0:T(8,128)S(1)}, f32[256,256]{1,0:T(8,128)S(1)}, u32[]{:S(2)}, u32[]{:S(2)}) %collective-permute-start.3) | collective-permute-done | bytes 262176 | tf_op jit(solution)/shard_map/ppermute | solution.py:544
  50.2 0.0 copy-done.3
  50.2 0.4 image.1
  50.6 13.4 %all_to_all.5.tiles_ref = f32[16,8,128]{2,1,0:T(8,128)S(1)} all-to-all(f32[16,8,128]{2,1,0:T(8,128)S(1)} %get-tuple-element.32), channel_id=1, replica_groups=mesh['box'=16,'rhs'=2] {'box'}, dimensions={0} | all-to-all | bytes 131072 | tf_op jit(solution)/shard_map/all_to_all | solution.py:561
  64.1 1.6 %finish.1 = (f32[8,8192]{1,0:T(8,128)}, f32[8,9]{1,0:T(8,128)}) custom-call(f32[16,8,128]{2,1,0:T(8,128)S(1)} %all_to_all.5.tiles_ref, f32[64,128]{1,0:T(8,128)S(1)} %get-tuple-element.31.live_ref, f32[8,8192]{1,0:T(8,128)S(1)} %get-tuple-element.33.image_ref, f32[8,8,8192]{2,1,0:T(8,128)S(1)} %copy-done), custom_call_target="tpu_custom_call" | custom-call | tf_op jit(solution)/shard_map/finish/pallas_call | solution.py:562
Async XLA Ops:
  0.6 11.8 %copy-start.4 = (f32[3,32]{1,0:T(4,128)S(1)}, f32[3,32]{1,0:T(4,128)}, u32[]{:S(2)}) copy-start(f32[3,32]{1,0:T(4,128)} %centres_s.1) | copy-start | bytes 1156
  3.5 8.8 %collective-permute-start.1 = (f32[400,128]{1,0:T(8,128)}, f32[400,128]{1,0:T(8,128)S(1)}, u32[]{:S(2)}, u32[]{:S(2)}) collective-permute-start(f32[400,128]{1,0:T(8,128)} %get-tuple-element.22), channel_id=1, source_target_pairs={{0,2},{2,4},{4,6},{6,8},{8,10},{10,12},{12,14},{14,16},{16,18},{18... | collective-permute-start | bytes 614408 | tf_op jit(solution)/shard_map/ppermute | solution.py:506
  5.9 6.5 %collective-permute-start = (bf16[544,128]{1,0:T(8,128)(2,1)}, bf16[544,128]{1,0:T(8,128)(2,1)S(1)}, u32[]{:S(2)}, u32[]{:S(2)}) collective-permute-start(bf16[544,128]{1,0:T(8,128)(2,1)} %get-tuple-element.20.sent_ref), channel_id=1, source_target_pairs={{0,1},{1,0},{2,3},{3,2},{4,5},{5,4},{6,7},{7,6},{8,9},{9,8},{10,11... | collective-permute-start | bytes 417800 | tf_op jit(solution)/shard_map/ppermute | solution.py:505
  7.9 4.5 %collective-permute-start.2 = (bf16[288,128]{1,0:T(8,128)(2,1)}, bf16[288,128]{1,0:T(8,128)(2,1)S(1)}, u32[]{:S(2)}, u32[]{:S(2)}) collective-permute-start(bf16[288,128]{1,0:T(8,128)(2,1)} %get-tuple-element.23), channel_id=1, source_target_pairs={{1,2},{3,4},{5,6},{7,8},{9,10},{11,12},{13,14},{15,16},{17,18},{19... | collective-permute-start | bytes 221192 | tf_op jit(solution)/shard_map/ppermute | solution.py:509
  8.5 1.0 %copy-start.1 = (f32[528,128]{1,0:T(8,128)S(1)}, f32[528,128]{1,0:T(8,128)}, u32[]{:S(2)}) copy-start(f32[528,128]{1,0:T(8,128)} %get-tuple-element.19.local_ref) | copy-start | bytes 811012
  9.5 0.9 %copy-start.2 = (bf16[544,128]{1,0:T(8,128)(2,1)S(1)}, bf16[544,128]{1,0:T(8,128)(2,1)}, u32[]{:S(2)}) copy-start(bf16[544,128]{1,0:T(8,128)(2,1)} %get-tuple-element.20.sent_ref) | copy-start | bytes 417796
  12.4 31.2 %copy-start = (f32[8,8,8192]{2,1,0:T(8,128)S(1)}, f32[8,8,8192]{2,1,0:T(8,128)}, u32[]{:S(2)}) copy-start(f32[8,8,8192]{2,1,0:T(8,128)} %basis_ref.5) | copy-start | bytes 6291460
  12.4 31.1 %copy-start.5 = (s32[32]{0:T(128)S(1)}, s32[32]{0:T(128)}, u32[]{:S(2)}) copy-start(s32[32]{0:T(128)} %counts_s.1) | copy-start | bytes 388
  39.7 10.5 %copy-start.3 = (f32[8192]{0:T(1024)S(1)}, f32[8192]{0:T(1024)}, u32[]{:S(2)}) copy-start(f32[8192]{0:T(1024)} %param.13) | copy-start | bytes 98308
  39.8 10.5 %collective-permute-start.3 = (f32[256,256]{1,0:T(8,128)S(1)}, f32[256,256]{1,0:T(8,128)S(1)}, u32[]{:S(2)}, u32[]{:S(2)}) collective-permute-start(f32[256,256]{1,0:T(8,128)S(1)} %get-tuple-element.29), channel_id=1, source_target_pairs={{0,1},{1,0},{2,3},{3,2},{4,5},{5,4},{6,7},{7,6},{8,9},{9,8},{10,11... | collective-permute-start | bytes 786440 | tf_op jit(solution)/shard_map/ppermute | solution.py:544

commit v22 on v20

--- a/solution.py
+++ b/solution.py
@@ -183,7 +183,7 @@
         ref, first = pair
         return ref[pl.ds(pl.multiple_of((first + place) * number, number), number), :]
 
-    def target_row(target_y, source_y, rows):
+    def target_row(target_y, source_y, rows, step):
         runs = []
         for near_x in range(4):
             target = target_y * 4 + near_x
@@ -215,15 +215,16 @@
                 )
                 cubed = []
                 given = []
+            turn, rest = divmod(i, len(runs) // 12)
+            if turn < 12 and rest == len(runs) // 24:
+                beside(step * 12 + turn)
 
     def outer(i, _):
-        target_row(3 * i, 2 * i, 2)
-        beside(i)
+        target_row(3 * i, 2 * i, 2, i)
         return 0
 
     def inner(i, _):
-        target_row(i + 1, i, 3)
-        beside(i + 2)
+        target_row(i + 1, i, 3, i + 2)
         return 0
 
     lax.fori_loop(0, 2, outer, 0)
@@ -301,10 +302,8 @@
         second = jnp.dot(picked, lower, preferred_element_type=f32)
         return first[:16] + first[16:] + second[:16]
 
-    def far_boxes(i):
-        for k in range(12):
-            k = i * 12 + k
-            far[pl.ds(pl.multiple_of(k * 16, 16), 16), :] = far_field(k)
+    def far_boxes(k):
+        far[pl.ds(pl.multiple_of(k * 16, 16), 16), :] = far_field(k)
 
     sources = [((geometry, p), (mine, p), (theirs, p)) for p in (0, plane_boxes)]
     sources.append(((halo_geometry, 0), (halo_mine, 0), (theirs, boxes)))

time: 65 us -> 65.1 us (level)
  no operation moved by 1% of the time
where the time goes in v22:
time: 65.1 us; the launch traced here: 64.9 us
  Pallas kernels  35 us (54%)
  blocking collectives  13.4 us (21%)
  starting transfers between devices  8.77 us (13%)
  waiting for transfers between devices  5.03 us (8%)
  local copies, waits for them, and re-layouts  1.88 us (3%)
  between operations  0.76 us (1%)
    pallas_call x1, Pallas kernels, on_device(): pl.pallas_call(field_kernel, out_shape=(rows(boxes * 8, per_box),) * 2, i...  26.6 us
    all_to_all x1, blocking collectives, on_device(): tiles = lax.all_to_all(tiles, 'box', 0, 0, tiled=True)  13.4 us
    ppermute x1, waiting for transfers between devices, on_device(): theirs = lax.ppermute(theirs, 'rhs', swap)  5.02 us
    ppermute x1, starting transfers between devices, on_device(): theirs = lax.ppermute(theirs, 'rhs', swap)  3.79 us
    pallas_call x1, Pallas kernels, on_device(): pl.pallas_call(prep_kernel, out_shape=(rows(544, dtype=bf16), rows(400),...  2.89 us
    ppermute x1, starting transfers between devices, on_device(): lax.ppermute(first, ('box', 'rhs'), [(2 * i, 2 * i + 2) for i in ups] + [...  2.37 us
    ppermute x1, starting transfers between devices, on_device(): cross = lax.ppermute(sent, 'rhs', swap)  1.96 us
    pallas_call x1, Pallas kernels, on_device(): pl.pallas_call(feature_kernel, out_shape=(rows(boxes * depth, per_box, bf...  1.94 us
  transfers between devices with their start and end apart: 4, of which 1 were waited for; matrix products, arithmetic and copies ran while one was open for 0% of the time, Pallas kernels for 6%

profile of v22, /device:TPU:0, one launch (start us, length us, event | category | flops | bytes accessed | tf_op | source)
XLA Modules:
  0.0 64.9 jit_solution(9883537689769435634)
XLA Ops:
  0.6 0.0 copy-start.4
  0.6 2.9 %prepare.1 = (bf16[544,128]{1,0:T(8,128)(2,1)}, f32[400,128]{1,0:T(8,128)}, bf16[288,128]{1,0:T(8,128)(2,1)}, f32[528,128]{1,0:T(8,128)}) custom-call(f32[3,32]{1,0:T(4,128)} %centres_s.1, s32[32]{0:T(128)} %counts_s.1, f32[8,8,8192]{2,1,0:T(8,128)} %basis_ref.5, f32[3,8192]{1,0:T(4,128)} %facets_h.1, f32[64,128]{1,0:T(8,128)} %bitcast.4, f32[3,8192]{1,0:T(4,128)} %normals_h.1), custom_call_target="tpu_custom_call" | custom-call | tf_op jit(solution)/shard_map/prepare/pallas_call | solution.py:479
  3.5 2.4 %collective-permute-start.1 = (f32[400,128]{1,0:T(8,128)}, f32[400,128]{1,0:T(8,128)S(1)}, u32[]{:S(2)}, u32[]{:S(2)}) collective-permute-start(f32[400,128]{1,0:T(8,128)} %get-tuple-element.22), channel_id=1, source_target_pairs={{0,2},{2,4},{4,6},{6,8},{8,10},{10,12},{12,14},{14,16},{16,18},{18... | collective-permute-start | bytes 614408 | tf_op jit(solution)/shard_map/ppermute | solution.py:499
  5.9 2.0 %collective-permute-start = (bf16[544,128]{1,0:T(8,128)(2,1)}, bf16[544,128]{1,0:T(8,128)(2,1)S(1)}, u32[]{:S(2)}, u32[]{:S(2)}) collective-permute-start(bf16[544,128]{1,0:T(8,128)(2,1)} %get-tuple-element.20.sent_ref), channel_id=1, source_target_pairs={{0,1},{1,0},{2,3},{3,2},{4,5},{5,4},{6,7},{7,6},{8,9},{9,8},{10,11... | collective-permute-start | bytes 417800 | tf_op jit(solution)/shard_map/ppermute | solution.py:498
  7.9 0.7 %collective-permute-start.2 = (bf16[288,128]{1,0:T(8,128)(2,1)}, bf16[288,128]{1,0:T(8,128)(2,1)S(1)}, u32[]{:S(2)}, u32[]{:S(2)}) collective-permute-start(bf16[288,128]{1,0:T(8,128)(2,1)} %get-tuple-element.23), channel_id=1, source_target_pairs={{1,2},{3,4},{5,6},{7,8},{9,10},{11,12},{13,14},{15,16},{17,18},{19... | collective-permute-start | bytes 221192 | tf_op jit(solution)/shard_map/ppermute | solution.py:502
  8.5 0.0 copy-start.1
  8.5 0.9 %copy-done.1 = f32[528,128]{1,0:T(8,128)S(1)} copy-done((f32[528,128]{1,0:T(8,128)S(1)}, f32[528,128]{1,0:T(8,128)}, u32[]{:S(2)}) %copy-start.1) | copy-done | bytes 270360
  9.5 0.0 copy-start.2
  9.5 0.9 %copy-done.2 = bf16[544,128]{1,0:T(8,128)(2,1)S(1)} copy-done((bf16[544,128]{1,0:T(8,128)(2,1)S(1)}, bf16[544,128]{1,0:T(8,128)(2,1)}, u32[]{:S(2)}) %copy-start.2) | copy-done | bytes 139288
  10.4 1.9 %features.1 = (bf16[2048,256]{1,0:T(8,128)(2,1)S(1)}, bf16[2560,256]{1,0:T(8,128)(2,1)S(1)}, bf16[4096,64]{1,0:T(8,128)(2,1)S(1)}, f32[128,256]{1,0:T(8,128)S(1)}, f32[528,128]{1,0:T(8,128)S(1)}) custom-call(f32[528,128]{1,0:T(8,128)S(1)} %copy-done.1, bf16[544,128]{1,0:T(8,128)(2,1)S(1)} %copy-done.2), custom_call_target="tpu_custom_call" | custom-call | tf_op jit(solution)/shard_map/features/pallas_call | solution.py:506
  12.3 0.0 collective-permute-done.2.second_ref
  12.4 0.0 collective-permute-done.cross_ref
  12.4 0.0 collective-permute-done.1.first_ref
  12.4 0.0 copy-done.4
  12.4 0.0 copy-start
  12.4 0.0 copy-start.5
  12.4 26.6 %fields.1 = (f32[256,256]{1,0:T(8,128)S(1)}, f32[256,256]{1,0:T(8,128)S(1)}) custom-call(f32[3,32]{1,0:T(4,128)S(1)} %copy-done.4, f32[528,128]{1,0:T(8,128)S(1)} %get-tuple-element.21.local_ref, bf16[544,128]{1,0:T(8,128)(2,1)S(1)} %collective-permute-done.cross_ref, f32[400,128]{1,0:T(8,128)S(1)} %collective-permute-done.1.first_ref, ...), custom_call_target="tpu_custom_call" | custom-call | tf_op jit(solution)/shard_map/fields/pallas_call | solution.py:520
  39.0 0.0 copy-start.3
  39.0 3.8 %collective-permute-start.3 = (f32[256,256]{1,0:T(8,128)S(1)}, f32[256,256]{1,0:T(8,128)S(1)}, u32[]{:S(2)}, u32[]{:S(2)}) collective-permute-start(f32[256,256]{1,0:T(8,128)S(1)} %get-tuple-element.29), channel_id=1, source_target_pairs={{0,1},{1,0},{2,3},{3,2},{4,5},{5,4},{6,7},{7,6},{8,9},{9,8},{10,11... | collective-permute-start | bytes 786440 | tf_op jit(solution)/shard_map/ppermute | solution.py:537
  42.8 0.0 copy-done
  42.8 0.0 copy-done.5
  42.8 1.7 %gram.1 = (f32[8,128]{1,0:T(8,128)S(1)}, f32[64,128]{1,0:T(8,128)S(1)}) custom-call(s32[32]{0:T(128)S(1)} %copy-done.5, f32[8,8,8192]{2,1,0:T(8,128)S(1)} %copy-done), custom_call_target="tpu_custom_call" | custom-call | tf_op jit(solution)/shard_map/gram/pallas_call | solution.py:538
  44.4 5.0 %collective-permute-done.3.theirs_ref = f32[256,256]{1,0:T(8,128)S(1)} collective-permute-done((f32[256,256]{1,0:T(8,128)S(1)}, f32[256,256]{1,0:T(8,128)S(1)}, u32[]{:S(2)}, u32[]{:S(2)}) %collective-permute-start.3) | collective-permute-done | bytes 262176 | tf_op jit(solution)/shard_map/ppermute | solution.py:537
  49.5 0.0 copy-done.3
  49.5 0.4 image.1
  49.8 13.4 %all_to_all.5.tiles_ref = f32[16,8,128]{2,1,0:T(8,128)S(1)} all-to-all(f32[16,8,128]{2,1,0:T(8,128)S(1)} %get-tuple-element.32), channel_id=1, replica_groups=mesh['box'=16,'rhs'=2] {'box'}, dimensions={0} | all-to-all | bytes 131072 | tf_op jit(solution)/shard_map/all_to_all | solution.py:554
  63.3 1.6 %finish.1 = (f32[8,8192]{1,0:T(8,128)}, f32[8,9]{1,0:T(8,128)}) custom-call(f32[16,8,128]{2,1,0:T(8,128)S(1)} %all_to_all.5.tiles_ref, f32[64,128]{1,0:T(8,128)S(1)} %get-tuple-element.31.live_ref, f32[8,8192]{1,0:T(8,128)S(1)} %get-tuple-element.33.image_ref, f32[8,8,8192]{2,1,0:T(8,128)S(1)} %copy-done), custom_call_target="tpu_custom_call" | custom-call | tf_op jit(solution)/shard_map/finish/pallas_call | solution.py:555
Async XLA Ops:
  0.6 11.7 %copy-start.4 = (f32[3,32]{1,0:T(4,128)S(1)}, f32[3,32]{1,0:T(4,128)}, u32[]{:S(2)}) copy-start(f32[3,32]{1,0:T(4,128)} %centres_s.1) | copy-start | bytes 1156
  3.5 8.8 %collective-permute-start.1 = (f32[400,128]{1,0:T(8,128)}, f32[400,128]{1,0:T(8,128)S(1)}, u32[]{:S(2)}, u32[]{:S(2)}) collective-permute-start(f32[400,128]{1,0:T(8,128)} %get-tuple-element.22), channel_id=1, source_target_pairs={{0,2},{2,4},{4,6},{6,8},{8,10},{10,12},{12,14},{14,16},{16,18},{18... | collective-permute-start | bytes 614408 | tf_op jit(solution)/shard_map/ppermute | solution.py:499
  5.9 6.4 %collective-permute-start = (bf16[544,128]{1,0:T(8,128)(2,1)}, bf16[544,128]{1,0:T(8,128)(2,1)S(1)}, u32[]{:S(2)}, u32[]{:S(2)}) collective-permute-start(bf16[544,128]{1,0:T(8,128)(2,1)} %get-tuple-element.20.sent_ref), channel_id=1, source_target_pairs={{0,1},{1,0},{2,3},{3,2},{4,5},{5,4},{6,7},{7,6},{8,9},{9,8},{10,11... | collective-permute-start | bytes 417800 | tf_op jit(solution)/shard_map/ppermute | solution.py:498
  7.9 4.5 %collective-permute-start.2 = (bf16[288,128]{1,0:T(8,128)(2,1)}, bf16[288,128]{1,0:T(8,128)(2,1)S(1)}, u32[]{:S(2)}, u32[]{:S(2)}) collective-permute-start(bf16[288,128]{1,0:T(8,128)(2,1)} %get-tuple-element.23), channel_id=1, source_target_pairs={{1,2},{3,4},{5,6},{7,8},{9,10},{11,12},{13,14},{15,16},{17,18},{19... | collective-permute-start | bytes 221192 | tf_op jit(solution)/shard_map/ppermute | solution.py:502
  8.5 1.0 %copy-start.1 = (f32[528,128]{1,0:T(8,128)S(1)}, f32[528,128]{1,0:T(8,128)}, u32[]{:S(2)}) copy-start(f32[528,128]{1,0:T(8,128)} %get-tuple-element.19.local_ref) | copy-start | bytes 811012
  9.5 0.9 %copy-start.2 = (bf16[544,128]{1,0:T(8,128)(2,1)S(1)}, bf16[544,128]{1,0:T(8,128)(2,1)}, u32[]{:S(2)}) copy-start(bf16[544,128]{1,0:T(8,128)(2,1)} %get-tuple-element.20.sent_ref) | copy-start | bytes 417796
  12.4 30.4 %copy-start = (f32[8,8,8192]{2,1,0:T(8,128)S(1)}, f32[8,8,8192]{2,1,0:T(8,128)}, u32[]{:S(2)}) copy-start(f32[8,8,8192]{2,1,0:T(8,128)} %basis_ref.5) | copy-start | bytes 6291460
  12.4 30.4 %copy-start.5 = (s32[32]{0:T(128)S(1)}, s32[32]{0:T(128)}, u32[]{:S(2)}) copy-start(s32[32]{0:T(128)} %counts_s.1) | copy-start | bytes 388
  39.0 10.5 %copy-start.3 = (f32[8192]{0:T(1024)S(1)}, f32[8192]{0:T(1024)}, u32[]{:S(2)}) copy-start(f32[8192]{0:T(1024)} %param.13) | copy-start | bytes 98308
  39.0 10.5 %collective-permute-start.3 = (f32[256,256]{1,0:T(8,128)S(1)}, f32[256,256]{1,0:T(8,128)S(1)}, u32[]{:S(2)}, u32[]{:S(2)}) collective-permute-start(f32[256,256]{1,0:T(8,128)S(1)} %get-tuple-element.29), channel_id=1, source_target_pairs={{0,1},{1,0},{2,3},{3,2},{4,5},{5,4},{6,7},{7,6},{8,9},{9,8},{10,11... | collective-permute-start | bytes 786440 | tf_op jit(solution)/shard_map/ppermute | solution.py:537

commit v23 on v20

--- a/solution.py
+++ b/solution.py
@@ -193,8 +193,9 @@
                         runs.append((target, source, (source_y + k) * 4 + x))
 
         def distances(target, source, place):
-            facets = targets[pl.ds(pl.multiple_of(target * per_box, per_box), per_box), :]
-            return jnp.dot(facets, rows_at(source[0], place, depth), preferred_element_type=f32)
+            weights = rows_at(source[0], place, depth)
+            starts = [pl.multiple_of(target * per_box + k, 128) for k in (0, 128)]
+            return [jnp.dot(targets[pl.ds(start, 128), :], weights, preferred_element_type=f32) for start in starts]
 
         ahead = distances(*runs[0])
         cubed = []
@@ -203,8 +204,11 @@
             here = ahead
             if i + 1 < len(runs):
                 ahead = distances(*runs[i + 1])
-            inverse = lax.rsqrt(here)
-            cubed.append((inverse * inverse * inverse).astype(bf16))
+            parts = []
+            for square in here:
+                inverse = lax.rsqrt(square)
+                parts.append((inverse * inverse * inverse).astype(bf16))
+            cubed.append(jnp.concatenate(parts, axis=0))
             given.append(jnp.concatenate([rows_at(source[1], place, 80), rows_at(source[2], place, 80)], axis=0))
             if i + 1 == len(runs) or runs[i + 1][0] is not target:
                 total[pl.ds(pl.multiple_of(target * 160, 160), 160), :] = lax.dot_general(

time: 65 us -> 65.9 us (1.014)
  Pallas kernels: 34.8 us -> 35.7 us
    pallas_call x1, Pallas kernels: 26.4 us -> 27.3 us  [on_device(): pl.pallas_call(field_kernel, out_shape=(rows(boxes * 8, per_box),) * 2, i...]
  transfers between devices with their start and end apart: 4 -> 4, of which waited for: 1 -> 1; matrix products, arithmetic and copies ran while one was open for 0% -> 0% of each run, Pallas kernels for 6% -> 5%
where the time goes in v23:
time: 65.9 us; the launch traced here: 65.6 us
  Pallas kernels  35.7 us (54%)
  blocking collectives  13.4 us (20%)
  starting transfers between devices  8.77 us (13%)
  waiting for transfers between devices  5.04 us (8%)
  local copies, waits for them, and re-layouts  1.88 us (3%)
  between operations  0.76 us (1%)
    pallas_call x1, Pallas kernels, on_device(): pl.pallas_call(field_kernel, out_shape=(rows(boxes * 8, per_box),) * 2, i...  27.3 us
    all_to_all x1, blocking collectives, on_device(): tiles = lax.all_to_all(tiles, 'box', 0, 0, tiled=True)  13.4 us
    ppermute x1, waiting for transfers between devices, on_device(): theirs = lax.ppermute(theirs, 'rhs', swap)  5.04 us
    ppermute x1, starting transfers between devices, on_device(): theirs = lax.ppermute(theirs, 'rhs', swap)  3.79 us
    pallas_call x1, Pallas kernels, on_device(): pl.pallas_call(prep_kernel, out_shape=(rows(544, dtype=bf16), rows(400),...  2.89 us
    ppermute x1, starting transfers between devices, on_device(): lax.ppermute(first, ('box', 'rhs'), [(2 * i, 2 * i + 2) for i in ups] + [...  2.37 us
    ppermute x1, starting transfers between devices, on_device(): cross = lax.ppermute(sent, 'rhs', swap)  1.96 us
    pallas_call x1, Pallas kernels, on_device(): pl.pallas_call(feature_kernel, out_shape=(rows(boxes * depth, per_box, bf...  1.94 us
  transfers between devices with their start and end apart: 4, of which 1 were waited for; matrix products, arithmetic and copies ran while one was open for 0% of the time, Pallas kernels for 5%

profile of v23, /device:TPU:0, one launch (start us, length us, event | category | flops | bytes accessed | tf_op | source)
XLA Modules:
  0.0 65.6 jit_solution(4319122454996993123)
XLA Ops:
  0.6 0.0 copy-start.4
  0.6 2.9 %prepare.1 = (bf16[544,128]{1,0:T(8,128)(2,1)}, f32[400,128]{1,0:T(8,128)}, bf16[288,128]{1,0:T(8,128)(2,1)}, f32[528,128]{1,0:T(8,128)}) custom-call(f32[3,32]{1,0:T(4,128)} %centres_s.1, s32[32]{0:T(128)} %counts_s.1, f32[8,8,8192]{2,1,0:T(8,128)} %basis_ref.5, f32[3,8192]{1,0:T(4,128)} %facets_h.1, f32[64,128]{1,0:T(8,128)} %bitcast.4, f32[3,8192]{1,0:T(4,128)} %normals_h.1), custom_call_target="tpu_custom_call" | custom-call | tf_op jit(solution)/shard_map/prepare/pallas_call | solution.py:484
  3.5 2.4 %collective-permute-start.1 = (f32[400,128]{1,0:T(8,128)}, f32[400,128]{1,0:T(8,128)S(1)}, u32[]{:S(2)}, u32[]{:S(2)}) collective-permute-start(f32[400,128]{1,0:T(8,128)} %get-tuple-element.22), channel_id=1, source_target_pairs={{0,2},{2,4},{4,6},{6,8},{8,10},{10,12},{12,14},{14,16},{16,18},{18... | collective-permute-start | bytes 614408 | tf_op jit(solution)/shard_map/ppermute | solution.py:504
  5.9 2.0 %collective-permute-start = (bf16[544,128]{1,0:T(8,128)(2,1)}, bf16[544,128]{1,0:T(8,128)(2,1)S(1)}, u32[]{:S(2)}, u32[]{:S(2)}) collective-permute-start(bf16[544,128]{1,0:T(8,128)(2,1)} %get-tuple-element.20.sent_ref), channel_id=1, source_target_pairs={{0,1},{1,0},{2,3},{3,2},{4,5},{5,4},{6,7},{7,6},{8,9},{9,8},{10,11... | collective-permute-start | bytes 417800 | tf_op jit(solution)/shard_map/ppermute | solution.py:503
  7.9 0.7 collective-permute-start.2
  8.5 0.0 copy-start.1
  8.5 0.9 %copy-done.1 = f32[528,128]{1,0:T(8,128)S(1)} copy-done((f32[528,128]{1,0:T(8,128)S(1)}, f32[528,128]{1,0:T(8,128)}, u32[]{:S(2)}) %copy-start.1) | copy-done | bytes 270360
  9.5 0.0 copy-start.2
  9.5 0.9 %copy-done.2 = bf16[544,128]{1,0:T(8,128)(2,1)S(1)} copy-done((bf16[544,128]{1,0:T(8,128)(2,1)S(1)}, bf16[544,128]{1,0:T(8,128)(2,1)}, u32[]{:S(2)}) %copy-start.2) | copy-done | bytes 139288
  10.4 1.9 %features.1 = (bf16[2048,256]{1,0:T(8,128)(2,1)S(1)}, bf16[2560,256]{1,0:T(8,128)(2,1)S(1)}, bf16[4096,64]{1,0:T(8,128)(2,1)S(1)}, f32[128,256]{1,0:T(8,128)S(1)}, f32[528,128]{1,0:T(8,128)S(1)}) custom-call(f32[528,128]{1,0:T(8,128)S(1)} %copy-done.1, bf16[544,128]{1,0:T(8,128)(2,1)S(1)} %copy-done.2), custom_call_target="tpu_custom_call" | custom-call | tf_op jit(solution)/shard_map/features/pallas_call | solution.py:511
  12.3 0.0 collective-permute-done.2.second_ref
  12.4 0.0 collective-permute-done.cross_ref
  12.4 0.0 collective-permute-done.1.first_ref
  12.4 0.0 copy-done.4
  12.4 0.0 copy-start
  12.4 0.0 copy-start.5
  12.4 27.3 %fields.1 = (f32[256,256]{1,0:T(8,128)S(1)}, f32[256,256]{1,0:T(8,128)S(1)}) custom-call(f32[3,32]{1,0:T(4,128)S(1)} %copy-done.4, f32[528,128]{1,0:T(8,128)S(1)} %get-tuple-element.21.local_ref, bf16[544,128]{1,0:T(8,128)(2,1)S(1)} %collective-permute-done.cross_ref, f32[400,128]{1,0:T(8,128)S(1)} %collective-permute-done.1.first_ref, ...), custom_call_target="tpu_custom_call" | custom-call | tf_op jit(solution)/shard_map/fields/pallas_call | solution.py:525
  39.7 0.0 copy-start.3
  39.7 3.8 %collective-permute-start.3 = (f32[256,256]{1,0:T(8,128)S(1)}, f32[256,256]{1,0:T(8,128)S(1)}, u32[]{:S(2)}, u32[]{:S(2)}) collective-permute-start(f32[256,256]{1,0:T(8,128)S(1)} %get-tuple-element.29), channel_id=1, source_target_pairs={{0,1},{1,0},{2,3},{3,2},{4,5},{5,4},{6,7},{7,6},{8,9},{9,8},{10,11... | collective-permute-start | bytes 786440 | tf_op jit(solution)/shard_map/ppermute | solution.py:542
  43.5 0.0 copy-done
  43.5 0.0 copy-done.5
  43.5 1.7 %gram.1 = (f32[8,128]{1,0:T(8,128)S(1)}, f32[64,128]{1,0:T(8,128)S(1)}) custom-call(s32[32]{0:T(128)S(1)} %copy-done.5, f32[8,8,8192]{2,1,0:T(8,128)S(1)} %copy-done), custom_call_target="tpu_custom_call" | custom-call | tf_op jit(solution)/shard_map/gram/pallas_call | solution.py:543
  45.2 5.0 %collective-permute-done.3.theirs_ref = f32[256,256]{1,0:T(8,128)S(1)} collective-permute-done((f32[256,256]{1,0:T(8,128)S(1)}, f32[256,256]{1,0:T(8,128)S(1)}, u32[]{:S(2)}, u32[]{:S(2)}) %collective-permute-start.3) | collective-permute-done | bytes 262176 | tf_op jit(solution)/shard_map/ppermute | solution.py:542
  50.2 0.0 copy-done.3
  50.2 0.4 image.1
  50.6 13.4 %all_to_all.5.tiles_ref = f32[16,8,128]{2,1,0:T(8,128)S(1)} all-to-all(f32[16,8,128]{2,1,0:T(8,128)S(1)} %get-tuple-element.32), channel_id=1, replica_groups=mesh['box'=16,'rhs'=2] {'box'}, dimensions={0} | all-to-all | bytes 131072 | tf_op jit(solution)/shard_map/all_to_all | solution.py:559
  64.0 1.6 %finish.1 = (f32[8,8192]{1,0:T(8,128)}, f32[8,9]{1,0:T(8,128)}) custom-call(f32[16,8,128]{2,1,0:T(8,128)S(1)} %all_to_all.5.tiles_ref, f32[64,128]{1,0:T(8,128)S(1)} %get-tuple-element.31.live_ref, f32[8,8192]{1,0:T(8,128)S(1)} %get-tuple-element.33.image_ref, f32[8,8,8192]{2,1,0:T(8,128)S(1)} %copy-done), custom_call_target="tpu_custom_call" | custom-call | tf_op jit(solution)/shard_map/finish/pallas_call | solution.py:560
Async XLA Ops:
  0.6 11.7 %copy-start.4 = (f32[3,32]{1,0:T(4,128)S(1)}, f32[3,32]{1,0:T(4,128)}, u32[]{:S(2)}) copy-start(f32[3,32]{1,0:T(4,128)} %centres_s.1) | copy-start | bytes 1156
  3.5 8.8 %collective-permute-start.1 = (f32[400,128]{1,0:T(8,128)}, f32[400,128]{1,0:T(8,128)S(1)}, u32[]{:S(2)}, u32[]{:S(2)}) collective-permute-start(f32[400,128]{1,0:T(8,128)} %get-tuple-element.22), channel_id=1, source_target_pairs={{0,2},{2,4},{4,6},{6,8},{8,10},{10,12},{12,14},{14,16},{16,18},{18... | collective-permute-start | bytes 614408 | tf_op jit(solution)/shard_map/ppermute | solution.py:504
  5.9 6.4 %collective-permute-start = (bf16[544,128]{1,0:T(8,128)(2,1)}, bf16[544,128]{1,0:T(8,128)(2,1)S(1)}, u32[]{:S(2)}, u32[]{:S(2)}) collective-permute-start(bf16[544,128]{1,0:T(8,128)(2,1)} %get-tuple-element.20.sent_ref), channel_id=1, source_target_pairs={{0,1},{1,0},{2,3},{3,2},{4,5},{5,4},{6,7},{7,6},{8,9},{9,8},{10,11... | collective-permute-start | bytes 417800 | tf_op jit(solution)/shard_map/ppermute | solution.py:503
  7.9 4.5 %collective-permute-start.2 = (bf16[288,128]{1,0:T(8,128)(2,1)}, bf16[288,128]{1,0:T(8,128)(2,1)S(1)}, u32[]{:S(2)}, u32[]{:S(2)}) collective-permute-start(bf16[288,128]{1,0:T(8,128)(2,1)} %get-tuple-element.23), channel_id=1, source_target_pairs={{1,2},{3,4},{5,6},{7,8},{9,10},{11,12},{13,14},{15,16},{17,18},{19... | collective-permute-start | bytes 221192 | tf_op jit(solution)/shard_map/ppermute | solution.py:507
  8.5 1.0 %copy-start.1 = (f32[528,128]{1,0:T(8,128)S(1)}, f32[528,128]{1,0:T(8,128)}, u32[]{:S(2)}) copy-start(f32[528,128]{1,0:T(8,128)} %get-tuple-element.19.local_ref) | copy-start | bytes 811012
  9.5 0.9 %copy-start.2 = (bf16[544,128]{1,0:T(8,128)(2,1)S(1)}, bf16[544,128]{1,0:T(8,128)(2,1)}, u32[]{:S(2)}) copy-start(bf16[544,128]{1,0:T(8,128)(2,1)} %get-tuple-element.20.sent_ref) | copy-start | bytes 417796
  12.4 31.1 %copy-start = (f32[8,8,8192]{2,1,0:T(8,128)S(1)}, f32[8,8,8192]{2,1,0:T(8,128)}, u32[]{:S(2)}) copy-start(f32[8,8,8192]{2,1,0:T(8,128)} %basis_ref.5) | copy-start | bytes 6291460
  12.4 31.1 %copy-start.5 = (s32[32]{0:T(128)S(1)}, s32[32]{0:T(128)}, u32[]{:S(2)}) copy-start(s32[32]{0:T(128)} %counts_s.1) | copy-start | bytes 388
  39.7 10.5 %copy-start.3 = (f32[8192]{0:T(1024)S(1)}, f32[8192]{0:T(1024)}, u32[]{:S(2)}) copy-start(f32[8192]{0:T(1024)} %param.13) | copy-start | bytes 98308
  39.7 10.5 %collective-permute-start.3 = (f32[256,256]{1,0:T(8,128)S(1)}, f32[256,256]{1,0:T(8,128)S(1)}, u32[]{:S(2)}, u32[]{:S(2)}) collective-permute-start(f32[256,256]{1,0:T(8,128)S(1)} %get-tuple-element.29), channel_id=1, source_target_pairs={{0,1},{1,0},{2,3},{3,2},{4,5},{5,4},{6,7},{7,6},{8,9},{9,8},{10,11... | collective-permute-start | bytes 786440 | tf_op jit(solution)/shard_map/ppermute | solution.py:542

commit v24 on v20

--- a/solution.py
+++ b/solution.py
@@ -80,7 +80,7 @@
         return moments, centres
 
     zeros = jnp.zeros((8, 128), f32)
-    moments, centres = lax.fori_loop(0, boxes, one_box, (zeros, zeros), unroll=4)
+    moments, centres = lax.fori_loop(0, boxes, one_box, (zeros, zeros), unroll=8)
     _, _, z = lattice(centres_s, 0)
     base_z = (z - (z & 1)).astype(f32) + 0.5
     centres = jnp.where((row == 3) | (row == 4), 1.5, jnp.where(row == 5, base_z, centres))
@@ -98,7 +98,8 @@
     first_ref[384:392] = moments
     first_ref[392:] = centres
     local_ref[512:520] = moments
-    local_ref[520:] = centres
+    local_ref[520:528] = centres
+    local_ref[528:] = charges_v[...].astype(bf16).astype(f32)
 
 
 def thirds(x):
@@ -146,7 +147,7 @@
     strengths[pl.ds(pl.multiple_of(box * 80, 80), 80), :] = rows.astype(bf16)
 
 
-def feature_kernel(local_ref, sent_ref, geometry, mine, targets, planes, local_out):
+def feature_kernel(local_ref, geometry, mine, targets, planes, local_out):
     boxes = 2 * plane_boxes
     half = lax.axis_index("rhs")
     origin = local_ref[523:526, 0:1]
@@ -155,7 +156,7 @@
     def source(slot, _):
         local = padded(wide_tile(local_ref, slot * 16) - origin)
         store_geometry(local, slot, geometry)
-        store_strengths(local, wide_charges(sent_ref, slot), slot, mine)
+        store_strengths(local, wide_charges(local_ref, 33 + slot), slot, mine)
         return 0
 
     lax.fori_loop(0, boxes, source, 0, unroll=4)
@@ -175,7 +176,7 @@
         return 0
 
     lax.fori_loop(0, plane_boxes, target, 0, unroll=4)
-    local_out[...] = local_ref[...]
+    local_out[...] = local_ref[:528]
 
 
 def near_planes(sources, targets, total, beside):
@@ -479,7 +480,7 @@
 
     sent, first, second, local = pl.pallas_call(
         prep_kernel,
-        out_shape=(rows(544, dtype=bf16), rows(400), rows(288, dtype=bf16), rows(528)),
+        out_shape=(rows(544, dtype=bf16), rows(400), rows(288, dtype=bf16), rows(1040)),
         in_specs=[pl.BlockSpec(memory_space=pl.ANY)] * 6,
         out_specs=(vmem,) * 4,
         scratch_shapes=[
@@ -513,11 +514,11 @@
             rows(plane_boxes * 8, per_box),
             rows(528),
         ),
-        in_specs=[vmem] * 2,
+        in_specs=[vmem],
         out_specs=(vmem,) * 5,
         compiler_params=limit(12),
         name="features",
-    )(local, sent)
+    )(local)
     mine, theirs = pl.pallas_call(
         field_kernel,
         out_shape=(rows(boxes * 8, per_box),) * 2,

time: 65 us -> 64.7 us (level)
  blocking collectives: 13.5 us -> 14.6 us
  local copies, waits for them, and re-layouts: 1.88 us -> 1.06 us
    all_to_all x1, blocking collectives: 13.5 us -> 14.6 us  [on_device(): tiles = lax.all_to_all(tiles, 'box', 0, 0, tiled=True)]
    unnamed x12 -> x10, local copies, waits for them, and re-layouts: 1.88 us -> 1.06 us
  transfers between devices with their start and end apart: 4 -> 4, of which waited for: 1 -> 2; matrix products, arithmetic and copies ran while one was open for 0% -> 0% of each run, Pallas kernels for 6% -> 6%
where the time goes in v24:
time: 64.7 us; the launch traced here: 64.5 us
  Pallas kernels  34.7 us (54%)
  blocking collectives  14.6 us (23%)
  starting transfers between devices  8.39 us (13%)
  waiting for transfers between devices  5.06 us (8%)
  local copies, waits for them, and re-layouts  1.06 us (2%)
  between operations  0.73 us (1%)
    pallas_call x1, Pallas kernels, on_device(): pl.pallas_call(field_kernel, out_shape=(rows(boxes * 8, per_box),) * 2, i...  26.4 us
    all_to_all x1, blocking collectives, on_device(): tiles = lax.all_to_all(tiles, 'box', 0, 0, tiled=True)  14.6 us
    ppermute x1, waiting for transfers between devices, on_device(): theirs = lax.ppermute(theirs, 'rhs', swap)  4.5 us
    ppermute x1, starting transfers between devices, on_device(): theirs = lax.ppermute(theirs, 'rhs', swap)  3.41 us
    pallas_call x1, Pallas kernels, on_device(): pl.pallas_call(prep_kernel, out_shape=(rows(544, dtype=bf16), rows(400),...  2.7 us
    ppermute x1, starting transfers between devices, on_device(): lax.ppermute(first, ('box', 'rhs'), [(2 * i, 2 * i + 2) for i in ups] + [...  2.37 us
    ppermute x1, starting transfers between devices, on_device(): cross = lax.ppermute(sent, 'rhs', swap)  1.96 us
    pallas_call x1, Pallas kernels, on_device(): pl.pallas_call(feature_kernel, out_shape=(rows(boxes * depth, per_box, bf...  1.95 us
  transfers between devices with their start and end apart: 4, of which 2 were waited for; matrix products, arithmetic and copies ran while one was open for 0% of the time, Pallas kernels for 6%

profile of v24, /device:TPU:0, one launch (start us, length us, event | category | flops | bytes accessed | tf_op | source)
XLA Modules:
  0.0 64.5 jit_solution(16564867682503174741)
XLA Ops:
  0.6 0.0 copy-start.3
  0.6 2.7 %prepare.1 = (bf16[544,128]{1,0:T(8,128)(2,1)}, f32[400,128]{1,0:T(8,128)}, bf16[288,128]{1,0:T(8,128)(2,1)}, f32[1040,128]{1,0:T(8,128)}) custom-call(f32[3,32]{1,0:T(4,128)} %centres_s.1, s32[32]{0:T(128)} %counts_s.1, f32[8,8,8192]{2,1,0:T(8,128)} %basis_ref.5, f32[3,8192]{1,0:T(4,128)} %facets_h.1, f32[64,128]{1,0:T(8,128)} %bitcast.4, f32[3,8192]{1,0:T(4,128)} %normals_h.1), custom_call_target="tpu_custom_call" | custom-call | tf_op jit(solution)/shard_map/prepare/pallas_call | solution.py:481
  3.3 2.4 %collective-permute-start.1 = (f32[400,128]{1,0:T(8,128)}, f32[400,128]{1,0:T(8,128)S(1)}, u32[]{:S(2)}, u32[]{:S(2)}) collective-permute-start(f32[400,128]{1,0:T(8,128)} %get-tuple-element.22), channel_id=1, source_target_pairs={{0,2},{2,4},{4,6},{6,8},{8,10},{10,12},{12,14},{14,16},{16,18},{18... | collective-permute-start | bytes 614408 | tf_op jit(solution)/shard_map/ppermute | solution.py:501
  5.7 2.0 %collective-permute-start = (bf16[544,128]{1,0:T(8,128)(2,1)}, bf16[544,128]{1,0:T(8,128)(2,1)S(1)}, u32[]{:S(2)}, u32[]{:S(2)}) collective-permute-start(bf16[544,128]{1,0:T(8,128)(2,1)} %get-tuple-element.21), channel_id=1, source_target_pairs={{0,1},{1,0},{2,3},{3,2},{4,5},{5,4},{6,7},{7,6},{8,9},{9,8},{10,11... | collective-permute-start | bytes 417800 | tf_op jit(solution)/shard_map/ppermute | solution.py:500
  7.7 0.7 %collective-permute-start.2 = (bf16[288,128]{1,0:T(8,128)(2,1)}, bf16[288,128]{1,0:T(8,128)(2,1)S(1)}, u32[]{:S(2)}, u32[]{:S(2)}) collective-permute-start(bf16[288,128]{1,0:T(8,128)(2,1)} %get-tuple-element.23), channel_id=1, source_target_pairs={{1,2},{3,4},{5,6},{7,8},{9,10},{11,12},{13,14},{15,16},{17,18},{19... | collective-permute-start | bytes 221192 | tf_op jit(solution)/shard_map/ppermute | solution.py:504
  8.3 0.0 copy-start.1
  8.3 1.0 %copy-done.1 = f32[1040,128]{1,0:T(8,128)S(1)} copy-done((f32[1040,128]{1,0:T(8,128)S(1)}, f32[1040,128]{1,0:T(8,128)}, u32[]{:S(2)}) %copy-start.1) | copy-done | bytes 532504
  9.4 1.9 %features.1 = (bf16[2048,256]{1,0:T(8,128)(2,1)S(1)}, bf16[2560,256]{1,0:T(8,128)(2,1)S(1)}, bf16[4096,64]{1,0:T(8,128)(2,1)S(1)}, f32[128,256]{1,0:T(8,128)S(1)}, f32[528,128]{1,0:T(8,128)S(1)}) custom-call(f32[1040,128]{1,0:T(8,128)S(1)} %copy-done.1), custom_call_target="tpu_custom_call" | custom-call | tf_op jit(solution)/shard_map/features/pallas_call | solution.py:508
  11.3 0.0 collective-permute-done.2.second_ref
  11.3 0.6 collective-permute-done.cross_ref
  11.9 0.0 collective-permute-done.1.first_ref
  11.9 0.0 copy-done.3
  11.9 0.0 copy-start
  11.9 0.0 copy-start.4
  11.9 26.4 %fields.1 = (f32[256,256]{1,0:T(8,128)S(1)}, f32[256,256]{1,0:T(8,128)S(1)}) custom-call(f32[3,32]{1,0:T(4,128)S(1)} %copy-done.3, f32[528,128]{1,0:T(8,128)S(1)} %get-tuple-element.20.local_ref, bf16[544,128]{1,0:T(8,128)(2,1)S(1)} %collective-permute-done.cross_ref, f32[400,128]{1,0:T(8,128)S(1)} %collective-permute-done.1.first_ref, ...), custom_call_target="tpu_custom_call" | custom-call | tf_op jit(solution)/shard_map/fields/pallas_call | solution.py:522
  38.3 0.0 copy-start.2
  38.3 3.4 %collective-permute-start.3 = (f32[256,256]{1,0:T(8,128)S(1)}, f32[256,256]{1,0:T(8,128)S(1)}, u32[]{:S(2)}, u32[]{:S(2)}) collective-permute-start(f32[256,256]{1,0:T(8,128)S(1)} %get-tuple-element.29), channel_id=1, source_target_pairs={{0,1},{1,0},{2,3},{3,2},{4,5},{5,4},{6,7},{7,6},{8,9},{9,8},{10,11... | collective-permute-start | bytes 786440 | tf_op jit(solution)/shard_map/ppermute | solution.py:539
  41.8 0.0 copy-done
  41.8 0.0 copy-done.4
  41.8 1.7 %gram.1 = (f32[8,128]{1,0:T(8,128)S(1)}, f32[64,128]{1,0:T(8,128)S(1)}) custom-call(s32[32]{0:T(128)S(1)} %copy-done.4, f32[8,8,8192]{2,1,0:T(8,128)S(1)} %copy-done), custom_call_target="tpu_custom_call" | custom-call | tf_op jit(solution)/shard_map/gram/pallas_call | solution.py:540
  43.4 4.5 %collective-permute-done.3.theirs_ref = f32[256,256]{1,0:T(8,128)S(1)} collective-permute-done((f32[256,256]{1,0:T(8,128)S(1)}, f32[256,256]{1,0:T(8,128)S(1)}, u32[]{:S(2)}, u32[]{:S(2)}) %collective-permute-start.3) | collective-permute-done | bytes 262176 | tf_op jit(solution)/shard_map/ppermute | solution.py:539
  47.9 0.0 copy-done.2
  47.9 0.4 image.1
  48.3 14.6 %all_to_all.5.tiles_ref = f32[16,8,128]{2,1,0:T(8,128)S(1)} all-to-all(f32[16,8,128]{2,1,0:T(8,128)S(1)} %get-tuple-element.32), channel_id=1, replica_groups=mesh['box'=16,'rhs'=2] {'box'}, dimensions={0} | all-to-all | bytes 131072 | tf_op jit(solution)/shard_map/all_to_all | solution.py:556
  62.9 1.6 %finish.1 = (f32[8,8192]{1,0:T(8,128)}, f32[8,9]{1,0:T(8,128)}) custom-call(f32[16,8,128]{2,1,0:T(8,128)S(1)} %all_to_all.5.tiles_ref, f32[64,128]{1,0:T(8,128)S(1)} %get-tuple-element.31.live_ref, f32[8,8192]{1,0:T(8,128)S(1)} %get-tuple-element.33.image_ref, f32[8,8,8192]{2,1,0:T(8,128)S(1)} %copy-done), custom_call_target="tpu_custom_call" | custom-call | tf_op jit(solution)/shard_map/finish/pallas_call | solution.py:557
Async XLA Ops:
  0.6 11.3 %copy-start.3 = (f32[3,32]{1,0:T(4,128)S(1)}, f32[3,32]{1,0:T(4,128)}, u32[]{:S(2)}) copy-start(f32[3,32]{1,0:T(4,128)} %centres_s.1) | copy-start | bytes 1156
  3.3 8.6 %collective-permute-start.1 = (f32[400,128]{1,0:T(8,128)}, f32[400,128]{1,0:T(8,128)S(1)}, u32[]{:S(2)}, u32[]{:S(2)}) collective-permute-start(f32[400,128]{1,0:T(8,128)} %get-tuple-element.22), channel_id=1, source_target_pairs={{0,2},{2,4},{4,6},{6,8},{8,10},{10,12},{12,14},{14,16},{16,18},{18... | collective-permute-start | bytes 614408 | tf_op jit(solution)/shard_map/ppermute | solution.py:501
  5.7 6.2 %collective-permute-start = (bf16[544,128]{1,0:T(8,128)(2,1)}, bf16[544,128]{1,0:T(8,128)(2,1)S(1)}, u32[]{:S(2)}, u32[]{:S(2)}) collective-permute-start(bf16[544,128]{1,0:T(8,128)(2,1)} %get-tuple-element.21), channel_id=1, source_target_pairs={{0,1},{1,0},{2,3},{3,2},{4,5},{5,4},{6,7},{7,6},{8,9},{9,8},{10,11... | collective-permute-start | bytes 417800 | tf_op jit(solution)/shard_map/ppermute | solution.py:500
  7.7 3.7 %collective-permute-start.2 = (bf16[288,128]{1,0:T(8,128)(2,1)}, bf16[288,128]{1,0:T(8,128)(2,1)S(1)}, u32[]{:S(2)}, u32[]{:S(2)}) collective-permute-start(bf16[288,128]{1,0:T(8,128)(2,1)} %get-tuple-element.23), channel_id=1, source_target_pairs={{1,2},{3,4},{5,6},{7,8},{9,10},{11,12},{13,14},{15,16},{17,18},{19... | collective-permute-start | bytes 221192 | tf_op jit(solution)/shard_map/ppermute | solution.py:504
  8.3 1.0 %copy-start.1 = (f32[1040,128]{1,0:T(8,128)S(1)}, f32[1040,128]{1,0:T(8,128)}, u32[]{:S(2)}) copy-start(f32[1040,128]{1,0:T(8,128)} %get-tuple-element.19.local_ref) | copy-start | bytes 1597444
  11.9 29.9 %copy-start = (f32[8,8,8192]{2,1,0:T(8,128)S(1)}, f32[8,8,8192]{2,1,0:T(8,128)}, u32[]{:S(2)}) copy-start(f32[8,8,8192]{2,1,0:T(8,128)} %basis_ref.5) | copy-start | bytes 6291460
  11.9 29.9 %copy-start.4 = (s32[32]{0:T(128)S(1)}, s32[32]{0:T(128)}, u32[]{:S(2)}) copy-start(s32[32]{0:T(128)} %counts_s.1) | copy-start | bytes 388
  38.3 9.6 %copy-start.2 = (f32[8192]{0:T(1024)S(1)}, f32[8192]{0:T(1024)}, u32[]{:S(2)}) copy-start(f32[8192]{0:T(1024)} %param.13) | copy-start | bytes 98308
  38.3 9.6 %collective-permute-start.3 = (f32[256,256]{1,0:T(8,128)S(1)}, f32[256,256]{1,0:T(8,128)S(1)}, u32[]{:S(2)}, u32[]{:S(2)}) collective-permute-start(f32[256,256]{1,0:T(8,128)S(1)} %get-tuple-element.29), channel_id=1, source_target_pairs={{0,1},{1,0},{2,3},{3,2},{4,5},{5,4},{6,7},{7,6},{8,9},{9,8},{10,11... | collective-permute-start | bytes 786440 | tf_op jit(solution)/shard_map/ppermute | solution.py:539

commit v25 on v24

--- a/solution.py
+++ b/solution.py
@@ -159,7 +159,7 @@
         store_strengths(local, wide_charges(local_ref, 33 + slot), slot, mine)
         return 0
 
-    lax.fori_loop(0, boxes, source, 0, unroll=4)
+    lax.fori_loop(0, boxes, source, 0, unroll=8)
 
     def target(place, _):
         start = (half * plane_boxes + place) * 16
@@ -179,7 +179,7 @@
     local_out[...] = local_ref[:528]
 
 
-def near_planes(sources, targets, total, beside):
+def near_planes(sources, targets, planes, near, beside):
     def rows_at(pair, place, number):
         ref, first = pair
         return ref[pl.ds(pl.multiple_of((first + place) * number, number), number), :]
@@ -208,12 +208,21 @@
             cubed.append((inverse * inverse * inverse).astype(bf16))
             given.append(jnp.concatenate([rows_at(source[1], place, 80), rows_at(source[2], place, 80)], axis=0))
             if i + 1 == len(runs) or runs[i + 1][0] is not target:
-                total[pl.ds(pl.multiple_of(target * 160, 160), 160), :] = lax.dot_general(
+                sums = lax.dot_general(
                     jnp.concatenate(given, axis=1),
                     jnp.concatenate(cubed, axis=1),
                     (((1,), (1,)), ((), ())),
                     preferred_element_type=f32,
                 )
+                side = planes[pl.ds(pl.multiple_of(target * 8, 8), 8), :]
+                values = []
+                for start in (0, 80):
+                    value = side[3:4] * sums[start : start + 8]
+                    for a in range(3):
+                        high, middle, low = (sums[j : j + 8] for j in range(start + 8 + 8 * a, start + 80, 24))
+                        value = value - side[a : a + 1] * (high + (middle + low))
+                    values.append(value)
+                near[pl.ds(pl.multiple_of(target * 16, 16), 16), :] = jnp.concatenate(values, axis=0)
                 cubed = []
                 given = []
 
@@ -233,7 +242,7 @@
 
 def field_kernel(
     centres_s, local_ref, cross_ref, first_ref, second_ref, geometry, mine, targets, planes, mine_ref, theirs_ref,
-    halo_geometry, halo_mine, theirs, total, far, far_centres, far_moments
+    halo_geometry, halo_mine, theirs, near, far, far_centres, far_moments
 ):
     boxes = 2 * plane_boxes
     half = lax.axis_index("rhs")
@@ -244,7 +253,7 @@
         store_strengths(local, wide_charges(cross_ref, slot), slot, theirs)
         return 0
 
-    lax.fori_loop(0, boxes, source, 0, unroll=4)
+    lax.fori_loop(0, boxes, source, 0, unroll=8)
 
     def halo_source(place, _):
         local = padded(wide_tile(first_ref, 256 + place * 8) - origin)
@@ -253,7 +262,7 @@
         store_strengths(local, wide_charges(second_ref, place), boxes + place, theirs)
         return 0
 
-    lax.fori_loop(0, plane_boxes, halo_source, 0, unroll=4)
+    lax.fori_loop(0, plane_boxes, halo_source, 0, unroll=8)
 
     for group, (centres, ours, others) in enumerate(
         (
@@ -309,19 +318,10 @@
 
     sources = [((geometry, p), (mine, p), (theirs, p)) for p in (0, plane_boxes)]
     sources.append(((halo_geometry, 0), (halo_mine, 0), (theirs, boxes)))
-    near_planes(sources, targets, total, far_boxes)
+    near_planes(sources, targets, planes, near, far_boxes)
 
     def near_field(place, _):
-        sums = total[pl.ds(pl.multiple_of(place * 160, 160), 160), :]
-        side = planes[pl.ds(pl.multiple_of(place * 8, 8), 8), :]
-        values = []
-        for start in (0, 80):
-            value = side[3:4] * sums[start : start + 8]
-            for a in range(3):
-                high, middle, low = (sums[i : i + 8] for i in range(start + 8 + 8 * a, start + 80, 24))
-                value = value - side[a : a + 1] * (high + (middle + low))
-            values.append(value)
-        value = jnp.concatenate(values, axis=0)
+        value = near[pl.ds(pl.multiple_of(place * 16, 16), 16), :]
         slot = half * plane_boxes + place
         rows = pl.ds(pl.multiple_of(slot * 16, 16), 16)
         far[rows, :] += value + far[pl.ds(pl.multiple_of((boxes + place) * 16, 16), 16), :]
@@ -528,7 +528,7 @@
             pltpu.VMEM((plane_boxes * depth, per_box), bf16),
             pltpu.VMEM((plane_boxes * 80, per_box), bf16),
             pltpu.VMEM((3 * plane_boxes * 80, per_box), bf16),
-            pltpu.VMEM((plane_boxes * 160, per_box), f32),
+            pltpu.VMEM((plane_boxes * 16, per_box), f32),
             pltpu.VMEM((3 * plane_boxes * 16, per_box), f32),
             pltpu.VMEM((6 * 32, 128), f32),
             pltpu.VMEM((2 * 32, 128), f32),

time: 64.7 us -> 64 us (0.989)
  Pallas kernels: 34.7 us -> 33.7 us
    pallas_call x1, Pallas kernels: 26.4 us -> 25.7 us  [on_device(): pl.pallas_call(field_kernel, out_shape=(rows(boxes * 8, per_box),) * 2, i...]
  transfers between devices with their start and end apart: 4 -> 4, of which waited for: 2 -> 2; matrix products, arithmetic and copies ran while one was open for 0% -> 0% of each run, Pallas kernels for 6% -> 5%
where the time goes in v25:
time: 64 us; the launch traced here: 63.8 us
  Pallas kernels  33.7 us (53%)
  blocking collectives  14.6 us (23%)
  starting transfers between devices  8.39 us (13%)
  waiting for transfers between devices  5.38 us (8%)
  local copies, waits for them, and re-layouts  1.06 us (2%)
  between operations  0.73 us (1%)
    pallas_call x1, Pallas kernels, on_device(): pl.pallas_call(field_kernel, out_shape=(rows(boxes * 8, per_box),) * 2, i...  25.7 us
    all_to_all x1, blocking collectives, on_device(): tiles = lax.all_to_all(tiles, 'box', 0, 0, tiled=True)  14.6 us
    ppermute x1, waiting for transfers between devices, on_device(): theirs = lax.ppermute(theirs, 'rhs', swap)  4.5 us
    ppermute x1, starting transfers between devices, on_device(): theirs = lax.ppermute(theirs, 'rhs', swap)  3.41 us
    pallas_call x1, Pallas kernels, on_device(): pl.pallas_call(prep_kernel, out_shape=(rows(544, dtype=bf16), rows(400),...  2.7 us
    ppermute x1, starting transfers between devices, on_device(): lax.ppermute(first, ('box', 'rhs'), [(2 * i, 2 * i + 2) for i in ups] + [...  2.37 us
    ppermute x1, starting transfers between devices, on_device(): cross = lax.ppermute(sent, 'rhs', swap)  1.96 us
    pallas_call x1, Pallas kernels, on_device(): pl.pallas_call(gram_kernel, out_shape=(rows(8), rows(2 * boxes)), in_spec...  1.66 us
  transfers between devices with their start and end apart: 4, of which 2 were waited for; matrix products, arithmetic and copies ran while one was open for 0% of the time, Pallas kernels for 5%

profile of v25, /device:TPU:0, one launch (start us, length us, event | category | flops | bytes accessed | tf_op | source)
XLA Modules:
  0.0 63.8 jit_solution(1318986649600431560)
XLA Ops:
  0.6 0.0 copy-start.3
  0.6 2.7 %prepare.1 = (bf16[544,128]{1,0:T(8,128)(2,1)}, f32[400,128]{1,0:T(8,128)}, bf16[288,128]{1,0:T(8,128)(2,1)}, f32[1040,128]{1,0:T(8,128)}) custom-call(f32[3,32]{1,0:T(4,128)} %centres_s.1, s32[32]{0:T(128)} %counts_s.1, f32[8,8,8192]{2,1,0:T(8,128)} %basis_ref.5, f32[3,8192]{1,0:T(4,128)} %facets_h.1, f32[64,128]{1,0:T(8,128)} %bitcast.4, f32[3,8192]{1,0:T(4,128)} %normals_h.1), custom_call_target="tpu_custom_call" | custom-call | tf_op jit(solution)/shard_map/prepare/pallas_call | solution.py:481
  3.3 2.4 %collective-permute-start.1 = (f32[400,128]{1,0:T(8,128)}, f32[400,128]{1,0:T(8,128)S(1)}, u32[]{:S(2)}, u32[]{:S(2)}) collective-permute-start(f32[400,128]{1,0:T(8,128)} %get-tuple-element.22), channel_id=1, source_target_pairs={{0,2},{2,4},{4,6},{6,8},{8,10},{10,12},{12,14},{14,16},{16,18},{18... | collective-permute-start | bytes 614408 | tf_op jit(solution)/shard_map/ppermute | solution.py:501
  5.7 2.0 %collective-permute-start = (bf16[544,128]{1,0:T(8,128)(2,1)}, bf16[544,128]{1,0:T(8,128)(2,1)S(1)}, u32[]{:S(2)}, u32[]{:S(2)}) collective-permute-start(bf16[544,128]{1,0:T(8,128)(2,1)} %get-tuple-element.21), channel_id=1, source_target_pairs={{0,1},{1,0},{2,3},{3,2},{4,5},{5,4},{6,7},{7,6},{8,9},{9,8},{10,11... | collective-permute-start | bytes 417800 | tf_op jit(solution)/shard_map/ppermute | solution.py:500
  7.7 0.7 %collective-permute-start.2 = (bf16[288,128]{1,0:T(8,128)(2,1)}, bf16[288,128]{1,0:T(8,128)(2,1)S(1)}, u32[]{:S(2)}, u32[]{:S(2)}) collective-permute-start(bf16[288,128]{1,0:T(8,128)(2,1)} %get-tuple-element.23), channel_id=1, source_target_pairs={{1,2},{3,4},{5,6},{7,8},{9,10},{11,12},{13,14},{15,16},{17,18},{19... | collective-permute-start | bytes 221192 | tf_op jit(solution)/shard_map/ppermute | solution.py:504
  8.3 0.0 copy-start.1
  8.3 1.0 %copy-done.1 = f32[1040,128]{1,0:T(8,128)S(1)} copy-done((f32[1040,128]{1,0:T(8,128)S(1)}, f32[1040,128]{1,0:T(8,128)}, u32[]{:S(2)}) %copy-start.1) | copy-done | bytes 532504
  9.4 1.6 %features.1 = (bf16[2048,256]{1,0:T(8,128)(2,1)S(1)}, bf16[2560,256]{1,0:T(8,128)(2,1)S(1)}, bf16[4096,64]{1,0:T(8,128)(2,1)S(1)}, f32[128,256]{1,0:T(8,128)S(1)}, f32[528,128]{1,0:T(8,128)S(1)}) custom-call(f32[1040,128]{1,0:T(8,128)S(1)} %copy-done.1), custom_call_target="tpu_custom_call" | custom-call | tf_op jit(solution)/shard_map/features/pallas_call | solution.py:508
  11.0 0.0 collective-permute-done.2.second_ref
  11.0 0.9 %collective-permute-done.cross_ref = bf16[544,128]{1,0:T(8,128)(2,1)S(1)} collective-permute-done((bf16[544,128]{1,0:T(8,128)(2,1)}, bf16[544,128]{1,0:T(8,128)(2,1)S(1)}, u32[]{:S(2)}, u32[]{:S(2)}) %collective-permute-start) | collective-permute-done | bytes 139296 | tf_op jit(solution)/shard_map/ppermute | solution.py:500
  11.9 0.0 collective-permute-done.1.first_ref
  11.9 0.0 copy-done.3
  11.9 0.0 copy-start
  11.9 0.0 copy-start.4
  11.9 25.7 %fields.1 = (f32[256,256]{1,0:T(8,128)S(1)}, f32[256,256]{1,0:T(8,128)S(1)}) custom-call(f32[3,32]{1,0:T(4,128)S(1)} %copy-done.3, f32[528,128]{1,0:T(8,128)S(1)} %get-tuple-element.20.local_ref, bf16[544,128]{1,0:T(8,128)(2,1)S(1)} %collective-permute-done.cross_ref, f32[400,128]{1,0:T(8,128)S(1)} %collective-permute-done.1.first_ref, ...), custom_call_target="tpu_custom_call" | custom-call | tf_op jit(solution)/shard_map/fields/pallas_call | solution.py:522
  37.6 0.0 copy-start.2
  37.7 3.4 %collective-permute-start.3 = (f32[256,256]{1,0:T(8,128)S(1)}, f32[256,256]{1,0:T(8,128)S(1)}, u32[]{:S(2)}, u32[]{:S(2)}) collective-permute-start(f32[256,256]{1,0:T(8,128)S(1)} %get-tuple-element.29), channel_id=1, source_target_pairs={{0,1},{1,0},{2,3},{3,2},{4,5},{5,4},{6,7},{7,6},{8,9},{9,8},{10,11... | collective-permute-start | bytes 786440 | tf_op jit(solution)/shard_map/ppermute | solution.py:539
  41.1 0.0 copy-done
  41.1 0.0 copy-done.4
  41.1 1.7 %gram.1 = (f32[8,128]{1,0:T(8,128)S(1)}, f32[64,128]{1,0:T(8,128)S(1)}) custom-call(s32[32]{0:T(128)S(1)} %copy-done.4, f32[8,8,8192]{2,1,0:T(8,128)S(1)} %copy-done), custom_call_target="tpu_custom_call" | custom-call | tf_op jit(solution)/shard_map/gram/pallas_call | solution.py:540
  42.7 4.5 %collective-permute-done.3.theirs_ref = f32[256,256]{1,0:T(8,128)S(1)} collective-permute-done((f32[256,256]{1,0:T(8,128)S(1)}, f32[256,256]{1,0:T(8,128)S(1)}, u32[]{:S(2)}, u32[]{:S(2)}) %collective-permute-start.3) | collective-permute-done | bytes 262176 | tf_op jit(solution)/shard_map/ppermute | solution.py:539
  47.2 0.0 copy-done.2
  47.2 0.4 image.1
  47.6 14.6 %all_to_all.5.tiles_ref = f32[16,8,128]{2,1,0:T(8,128)S(1)} all-to-all(f32[16,8,128]{2,1,0:T(8,128)S(1)} %get-tuple-element.32), channel_id=1, replica_groups=mesh['box'=16,'rhs'=2] {'box'}, dimensions={0} | all-to-all | bytes 131072 | tf_op jit(solution)/shard_map/all_to_all | solution.py:556
  62.2 1.6 %finish.1 = (f32[8,8192]{1,0:T(8,128)}, f32[8,9]{1,0:T(8,128)}) custom-call(f32[16,8,128]{2,1,0:T(8,128)S(1)} %all_to_all.5.tiles_ref, f32[64,128]{1,0:T(8,128)S(1)} %get-tuple-element.31.live_ref, f32[8,8192]{1,0:T(8,128)S(1)} %get-tuple-element.33.image_ref, f32[8,8,8192]{2,1,0:T(8,128)S(1)} %copy-done), custom_call_target="tpu_custom_call" | custom-call | tf_op jit(solution)/shard_map/finish/pallas_call | solution.py:557
Async XLA Ops:
  0.6 11.3 %copy-start.3 = (f32[3,32]{1,0:T(4,128)S(1)}, f32[3,32]{1,0:T(4,128)}, u32[]{:S(2)}) copy-start(f32[3,32]{1,0:T(4,128)} %centres_s.1) | copy-start | bytes 1156
  3.3 8.6 %collective-permute-start.1 = (f32[400,128]{1,0:T(8,128)}, f32[400,128]{1,0:T(8,128)S(1)}, u32[]{:S(2)}, u32[]{:S(2)}) collective-permute-start(f32[400,128]{1,0:T(8,128)} %get-tuple-element.22), channel_id=1, source_target_pairs={{0,2},{2,4},{4,6},{6,8},{8,10},{10,12},{12,14},{14,16},{16,18},{18... | collective-permute-start | bytes 614408 | tf_op jit(solution)/shard_map/ppermute | solution.py:501
  5.7 6.2 %collective-permute-start = (bf16[544,128]{1,0:T(8,128)(2,1)}, bf16[544,128]{1,0:T(8,128)(2,1)S(1)}, u32[]{:S(2)}, u32[]{:S(2)}) collective-permute-start(bf16[544,128]{1,0:T(8,128)(2,1)} %get-tuple-element.21), channel_id=1, source_target_pairs={{0,1},{1,0},{2,3},{3,2},{4,5},{5,4},{6,7},{7,6},{8,9},{9,8},{10,11... | collective-permute-start | bytes 417800 | tf_op jit(solution)/shard_map/ppermute | solution.py:500
  7.7 3.3 %collective-permute-start.2 = (bf16[288,128]{1,0:T(8,128)(2,1)}, bf16[288,128]{1,0:T(8,128)(2,1)S(1)}, u32[]{:S(2)}, u32[]{:S(2)}) collective-permute-start(bf16[288,128]{1,0:T(8,128)(2,1)} %get-tuple-element.23), channel_id=1, source_target_pairs={{1,2},{3,4},{5,6},{7,8},{9,10},{11,12},{13,14},{15,16},{17,18},{19... | collective-permute-start | bytes 221192 | tf_op jit(solution)/shard_map/ppermute | solution.py:504
  8.3 1.0 %copy-start.1 = (f32[1040,128]{1,0:T(8,128)S(1)}, f32[1040,128]{1,0:T(8,128)}, u32[]{:S(2)}) copy-start(f32[1040,128]{1,0:T(8,128)} %get-tuple-element.19.local_ref) | copy-start | bytes 1597444
  11.9 29.2 %copy-start = (f32[8,8,8192]{2,1,0:T(8,128)S(1)}, f32[8,8,8192]{2,1,0:T(8,128)}, u32[]{:S(2)}) copy-start(f32[8,8,8192]{2,1,0:T(8,128)} %basis_ref.5) | copy-start | bytes 6291460
  11.9 29.2 %copy-start.4 = (s32[32]{0:T(128)S(1)}, s32[32]{0:T(128)}, u32[]{:S(2)}) copy-start(s32[32]{0:T(128)} %counts_s.1) | copy-start | bytes 388
  37.6 9.6 %copy-start.2 = (f32[8192]{0:T(1024)S(1)}, f32[8192]{0:T(1024)}, u32[]{:S(2)}) copy-start(f32[8192]{0:T(1024)} %param.13) | copy-start | bytes 98308
  37.7 9.6 %collective-permute-start.3 = (f32[256,256]{1,0:T(8,128)S(1)}, f32[256,256]{1,0:T(8,128)S(1)}, u32[]{:S(2)}, u32[]{:S(2)}) collective-permute-start(f32[256,256]{1,0:T(8,128)S(1)} %get-tuple-element.29), channel_id=1, source_target_pairs={{0,1},{1,0},{2,3},{3,2},{4,5},{5,4},{6,7},{7,6},{8,9},{9,8},{10,11... | collective-permute-start | bytes 786440 | tf_op jit(solution)/shard_map/ppermute | solution.py:539

commit v26 on v25

--- a/solution.py
+++ b/solution.py
@@ -413,10 +413,14 @@
     krylov = basis_ref.shape[0]
     lane = lax.broadcasted_iota(jnp.int32, (8, 128), 1)
 
-    sums, rest = tiles_ref[0], jnp.zeros((8, 128), f32)
-    for i in range(1, tiles_ref.shape[0]):
-        sums, error = two_sum(sums, tiles_ref[i])
-        rest = rest + error
+    tiles = [(tiles_ref[i], jnp.zeros((8, 128), f32)) for i in range(tiles_ref.shape[0])]
+    while len(tiles) > 1:
+        merged = []
+        for (one, one_rest), (two, two_rest) in zip(tiles[::2], tiles[1::2]):
+            value, error = two_sum(one, two)
+            merged.append((value, (one_rest + two_rest) + error))
+        tiles = merged + tiles[len(tiles) // 2 * 2 :]
+    sums, rest = tiles[0]
     exact = sums + rest
     projections = [exact[:, m : m + 1] / total_facets for m in range(krylov)]
     pairs = [(m, n) for m in range(krylov) for n in range(m + 1)]
@@ -455,7 +459,7 @@
         next_ref[:, lanes] = (image_ref[:, lanes] - sent * live) * scale
         return 0
 
-    lax.fori_loop(0, boxes, one_box, 0, unroll=4)
+    lax.fori_loop(0, boxes, one_box, 0, unroll=8)
 
 
 smem = pl.BlockSpec(memory_space=pltpu.SMEM)

time: 64 us -> 64 us (level)
  no operation moved by 1% of the time
where the time goes in v26:
time: 64 us; the launch traced here: 63.8 us
  Pallas kernels  33.6 us (52%)
  blocking collectives  14.6 us (23%)
  starting transfers between devices  8.39 us (13%)
  waiting for transfers between devices  5.38 us (8%)
  local copies, waits for them, and re-layouts  1.06 us (2%)
  between operations  0.73 us (1%)
    pallas_call x1, Pallas kernels, on_device(): pl.pallas_call(field_kernel, out_shape=(rows(boxes * 8, per_box),) * 2, i...  25.7 us
    all_to_all x1, blocking collectives, on_device(): tiles = lax.all_to_all(tiles, 'box', 0, 0, tiled=True)  14.6 us
    ppermute x1, waiting for transfers between devices, on_device(): theirs = lax.ppermute(theirs, 'rhs', swap)  4.5 us
    ppermute x1, starting transfers between devices, on_device(): theirs = lax.ppermute(theirs, 'rhs', swap)  3.41 us
    pallas_call x1, Pallas kernels, on_device(): pl.pallas_call(prep_kernel, out_shape=(rows(544, dtype=bf16), rows(400),...  2.7 us
    ppermute x1, starting transfers between devices, on_device(): lax.ppermute(first, ('box', 'rhs'), [(2 * i, 2 * i + 2) for i in ups] + [...  2.37 us
    ppermute x1, starting transfers between devices, on_device(): cross = lax.ppermute(sent, 'rhs', swap)  1.96 us
    pallas_call x1, Pallas kernels, on_device(): pl.pallas_call(gram_kernel, out_shape=(rows(8), rows(2 * boxes)), in_spec...  1.66 us
  transfers between devices with their start and end apart: 4, of which 2 were waited for; matrix products, arithmetic and copies ran while one was open for 0% of the time, Pallas kernels for 5%

profile of v26, /device:TPU:0, one launch (start us, length us, event | category | flops | bytes accessed | tf_op | source)
XLA Modules:
  0.0 63.8 jit_solution(2246615861685173956)
XLA Ops:
  0.6 0.0 copy-start.3
  0.6 2.7 %prepare.1 = (bf16[544,128]{1,0:T(8,128)(2,1)}, f32[400,128]{1,0:T(8,128)}, bf16[288,128]{1,0:T(8,128)(2,1)}, f32[1040,128]{1,0:T(8,128)}) custom-call(f32[3,32]{1,0:T(4,128)} %centres_s.1, s32[32]{0:T(128)} %counts_s.1, f32[8,8,8192]{2,1,0:T(8,128)} %basis_ref.5, f32[3,8192]{1,0:T(4,128)} %facets_h.1, f32[64,128]{1,0:T(8,128)} %bitcast.4, f32[3,8192]{1,0:T(4,128)} %normals_h.1), custom_call_target="tpu_custom_call" | custom-call | tf_op jit(solution)/shard_map/prepare/pallas_call | solution.py:485
  3.3 2.4 %collective-permute-start.1 = (f32[400,128]{1,0:T(8,128)}, f32[400,128]{1,0:T(8,128)S(1)}, u32[]{:S(2)}, u32[]{:S(2)}) collective-permute-start(f32[400,128]{1,0:T(8,128)} %get-tuple-element.22), channel_id=1, source_target_pairs={{0,2},{2,4},{4,6},{6,8},{8,10},{10,12},{12,14},{14,16},{16,18},{18... | collective-permute-start | bytes 614408 | tf_op jit(solution)/shard_map/ppermute | solution.py:505
  5.7 2.0 %collective-permute-start = (bf16[544,128]{1,0:T(8,128)(2,1)}, bf16[544,128]{1,0:T(8,128)(2,1)S(1)}, u32[]{:S(2)}, u32[]{:S(2)}) collective-permute-start(bf16[544,128]{1,0:T(8,128)(2,1)} %get-tuple-element.21), channel_id=1, source_target_pairs={{0,1},{1,0},{2,3},{3,2},{4,5},{5,4},{6,7},{7,6},{8,9},{9,8},{10,11... | collective-permute-start | bytes 417800 | tf_op jit(solution)/shard_map/ppermute | solution.py:504
  7.7 0.7 %collective-permute-start.2 = (bf16[288,128]{1,0:T(8,128)(2,1)}, bf16[288,128]{1,0:T(8,128)(2,1)S(1)}, u32[]{:S(2)}, u32[]{:S(2)}) collective-permute-start(bf16[288,128]{1,0:T(8,128)(2,1)} %get-tuple-element.23), channel_id=1, source_target_pairs={{1,2},{3,4},{5,6},{7,8},{9,10},{11,12},{13,14},{15,16},{17,18},{19... | collective-permute-start | bytes 221192 | tf_op jit(solution)/shard_map/ppermute | solution.py:508
  8.3 0.0 copy-start.1
  8.3 1.0 %copy-done.1 = f32[1040,128]{1,0:T(8,128)S(1)} copy-done((f32[1040,128]{1,0:T(8,128)S(1)}, f32[1040,128]{1,0:T(8,128)}, u32[]{:S(2)}) %copy-start.1) | copy-done | bytes 532504
  9.4 1.6 %features.1 = (bf16[2048,256]{1,0:T(8,128)(2,1)S(1)}, bf16[2560,256]{1,0:T(8,128)(2,1)S(1)}, bf16[4096,64]{1,0:T(8,128)(2,1)S(1)}, f32[128,256]{1,0:T(8,128)S(1)}, f32[528,128]{1,0:T(8,128)S(1)}) custom-call(f32[1040,128]{1,0:T(8,128)S(1)} %copy-done.1), custom_call_target="tpu_custom_call" | custom-call | tf_op jit(solution)/shard_map/features/pallas_call | solution.py:512
  11.0 0.0 collective-permute-done.2.second_ref
  11.0 0.9 %collective-permute-done.cross_ref = bf16[544,128]{1,0:T(8,128)(2,1)S(1)} collective-permute-done((bf16[544,128]{1,0:T(8,128)(2,1)}, bf16[544,128]{1,0:T(8,128)(2,1)S(1)}, u32[]{:S(2)}, u32[]{:S(2)}) %collective-permute-start) | collective-permute-done | bytes 139296 | tf_op jit(solution)/shard_map/ppermute | solution.py:504
  11.9 0.0 collective-permute-done.1.first_ref
  11.9 0.0 copy-done.3
  11.9 0.0 copy-start
  11.9 0.0 copy-start.4
  11.9 25.7 %fields.1 = (f32[256,256]{1,0:T(8,128)S(1)}, f32[256,256]{1,0:T(8,128)S(1)}) custom-call(f32[3,32]{1,0:T(4,128)S(1)} %copy-done.3, f32[528,128]{1,0:T(8,128)S(1)} %get-tuple-element.20.local_ref, bf16[544,128]{1,0:T(8,128)(2,1)S(1)} %collective-permute-done.cross_ref, f32[400,128]{1,0:T(8,128)S(1)} %collective-permute-done.1.first_ref, ...), custom_call_target="tpu_custom_call" | custom-call | tf_op jit(solution)/shard_map/fields/pallas_call | solution.py:526
  37.6 0.0 copy-start.2
  37.7 3.4 %collective-permute-start.3 = (f32[256,256]{1,0:T(8,128)S(1)}, f32[256,256]{1,0:T(8,128)S(1)}, u32[]{:S(2)}, u32[]{:S(2)}) collective-permute-start(f32[256,256]{1,0:T(8,128)S(1)} %get-tuple-element.29), channel_id=1, source_target_pairs={{0,1},{1,0},{2,3},{3,2},{4,5},{5,4},{6,7},{7,6},{8,9},{9,8},{10,11... | collective-permute-start | bytes 786440 | tf_op jit(solution)/shard_map/ppermute | solution.py:543
  41.1 0.0 copy-done
  41.1 0.0 copy-done.4
  41.1 1.7 %gram.1 = (f32[8,128]{1,0:T(8,128)S(1)}, f32[64,128]{1,0:T(8,128)S(1)}) custom-call(s32[32]{0:T(128)S(1)} %copy-done.4, f32[8,8,8192]{2,1,0:T(8,128)S(1)} %copy-done), custom_call_target="tpu_custom_call" | custom-call | tf_op jit(solution)/shard_map/gram/pallas_call | solution.py:544
  42.7 4.5 %collective-permute-done.3.theirs_ref = f32[256,256]{1,0:T(8,128)S(1)} collective-permute-done((f32[256,256]{1,0:T(8,128)S(1)}, f32[256,256]{1,0:T(8,128)S(1)}, u32[]{:S(2)}, u32[]{:S(2)}) %collective-permute-start.3) | collective-permute-done | bytes 262176 | tf_op jit(solution)/shard_map/ppermute | solution.py:543
  47.2 0.0 copy-done.2
  47.2 0.4 image.1
  47.6 14.6 %all_to_all.5.tiles_ref = f32[16,8,128]{2,1,0:T(8,128)S(1)} all-to-all(f32[16,8,128]{2,1,0:T(8,128)S(1)} %get-tuple-element.32), channel_id=1, replica_groups=mesh['box'=16,'rhs'=2] {'box'}, dimensions={0} | all-to-all | bytes 131072 | tf_op jit(solution)/shard_map/all_to_all | solution.py:560
  62.2 1.6 %finish.1 = (f32[8,8192]{1,0:T(8,128)}, f32[8,9]{1,0:T(8,128)}) custom-call(f32[16,8,128]{2,1,0:T(8,128)S(1)} %all_to_all.5.tiles_ref, f32[64,128]{1,0:T(8,128)S(1)} %get-tuple-element.31.live_ref, f32[8,8192]{1,0:T(8,128)S(1)} %get-tuple-element.33.image_ref, f32[8,8,8192]{2,1,0:T(8,128)S(1)} %copy-done), custom_call_target="tpu_custom_call" | custom-call | tf_op jit(solution)/shard_map/finish/pallas_call | solution.py:561
Async XLA Ops:
  0.6 11.3 %copy-start.3 = (f32[3,32]{1,0:T(4,128)S(1)}, f32[3,32]{1,0:T(4,128)}, u32[]{:S(2)}) copy-start(f32[3,32]{1,0:T(4,128)} %centres_s.1) | copy-start | bytes 1156
  3.3 8.6 %collective-permute-start.1 = (f32[400,128]{1,0:T(8,128)}, f32[400,128]{1,0:T(8,128)S(1)}, u32[]{:S(2)}, u32[]{:S(2)}) collective-permute-start(f32[400,128]{1,0:T(8,128)} %get-tuple-element.22), channel_id=1, source_target_pairs={{0,2},{2,4},{4,6},{6,8},{8,10},{10,12},{12,14},{14,16},{16,18},{18... | collective-permute-start | bytes 614408 | tf_op jit(solution)/shard_map/ppermute | solution.py:505
  5.7 6.2 %collective-permute-start = (bf16[544,128]{1,0:T(8,128)(2,1)}, bf16[544,128]{1,0:T(8,128)(2,1)S(1)}, u32[]{:S(2)}, u32[]{:S(2)}) collective-permute-start(bf16[544,128]{1,0:T(8,128)(2,1)} %get-tuple-element.21), channel_id=1, source_target_pairs={{0,1},{1,0},{2,3},{3,2},{4,5},{5,4},{6,7},{7,6},{8,9},{9,8},{10,11... | collective-permute-start | bytes 417800 | tf_op jit(solution)/shard_map/ppermute | solution.py:504
  7.7 3.3 %collective-permute-start.2 = (bf16[288,128]{1,0:T(8,128)(2,1)}, bf16[288,128]{1,0:T(8,128)(2,1)S(1)}, u32[]{:S(2)}, u32[]{:S(2)}) collective-permute-start(bf16[288,128]{1,0:T(8,128)(2,1)} %get-tuple-element.23), channel_id=1, source_target_pairs={{1,2},{3,4},{5,6},{7,8},{9,10},{11,12},{13,14},{15,16},{17,18},{19... | collective-permute-start | bytes 221192 | tf_op jit(solution)/shard_map/ppermute | solution.py:508
  8.3 1.0 %copy-start.1 = (f32[1040,128]{1,0:T(8,128)S(1)}, f32[1040,128]{1,0:T(8,128)}, u32[]{:S(2)}) copy-start(f32[1040,128]{1,0:T(8,128)} %get-tuple-element.19.local_ref) | copy-start | bytes 1597444
  11.9 29.2 %copy-start = (f32[8,8,8192]{2,1,0:T(8,128)S(1)}, f32[8,8,8192]{2,1,0:T(8,128)}, u32[]{:S(2)}) copy-start(f32[8,8,8192]{2,1,0:T(8,128)} %basis_ref.5) | copy-start | bytes 6291460
  11.9 29.2 %copy-start.4 = (s32[32]{0:T(128)S(1)}, s32[32]{0:T(128)}, u32[]{:S(2)}) copy-start(s32[32]{0:T(128)} %counts_s.1) | copy-start | bytes 388
  37.6 9.6 %copy-start.2 = (f32[8192]{0:T(1024)S(1)}, f32[8192]{0:T(1024)}, u32[]{:S(2)}) copy-start(f32[8192]{0:T(1024)} %param.13) | copy-start | bytes 98308
  37.7 9.6 %collective-permute-start.3 = (f32[256,256]{1,0:T(8,128)S(1)}, f32[256,256]{1,0:T(8,128)S(1)}, u32[]{:S(2)}, u32[]{:S(2)}) collective-permute-start(f32[256,256]{1,0:T(8,128)S(1)} %get-tuple-element.29), channel_id=1, source_target_pairs={{0,1},{1,0},{2,3},{3,2},{4,5},{5,4},{6,7},{7,6},{8,9},{9,8},{10,11... | collective-permute-start | bytes 786440 | tf_op jit(solution)/shard_map/ppermute | solution.py:543
